TPU v7x, 128 devices: a whole 4x4x4 slice. The times are simulated.
128 devices in a mesh: dp: 16 (over x, z), tp: 8 (over y, core).
Axes of the slice: x: 4, y: 4, z: 4, core: 2. Of those that a mesh axis runs over, the one named last changes fastest.
Arguments:
- queries: bfloat16 [256, 73728], P('dp', 'tp'), may hold values from -6 to 6
- own_latent: bfloat16 [256, 576], P('dp'), may hold values from -11 to 11
- prefix_cache: bfloat16 [2048, 36864], P(('dp', 'tp')), may hold values from -6 to 6
- block_home: int32 [2048], replicated, may hold values from 0 to 2047, as said below
- row_prompt: int32 [256], replicated, may hold values from 0 to 3, as said below
- chosen: int32 [256, 32], replicated, may hold values from 0 to 511, as said below
- value_up: bfloat16 [128, 512, 128], P('tp'), may hold values from -0.25 to 0.25
- out_weight: bfloat16 [16384, 7168], P('tp', 'dp'), may hold values from -0.046875 to 0.046875
- residual: bfloat16 [256, 7168], P(None, 'dp'), may hold values from -0.59765625 to 0.59765625
- norm_gain: bfloat16 [7168], P('dp'), may hold values from 0.099609375 to 1.8984375
- gate_weight: bfloat16 [7168, 18432], P('dp', 'tp'), may hold values from -0.0625 to 0.0625
- up_weight: bfloat16 [7168, 18432], P('dp', 'tp'), may hold values from -0.0625 to 0.0625
Outputs:
- stream: bfloat16 [256, 7168], P(None, 'dp')
- hidden: bfloat16 [256, 18432], P('dp', 'tp')
Inputs may be any that keep to these rules, and one draw needn't show every extreme that they name: A permutation of the stored blocks: block b of prompt p is stored at slot block_home[p * 512 + b], and slots k * 16 to (k + 1) * 16 - 1 lie on the k-th device of dp+tp in mesh order; every device holds the same number of blocks of every prompt. `row_prompt`: the 16 rows of one dp index share one prompt; every prompt serves 4 dp indices. `chosen`: each row names 32 distinct blocks of its prompt. Together the rows of one dp index name at least one and at most 2 distinct blocks stored on any one device; in every draw some dp index names exactly 2 from every device.
All inputs are finite; a program needn't handle non-finite values.
Results may differ from a plain program's by a relative error of at most 0.04.
Values may be sent and summed in bfloat16 or wider, within the bound.
No kernel may reach another device: no remote copies, remote signals or barrier semaphores. Data moves between devices by JAX's collectives and lax.ppermute only.
A program may use at most 192 MiB of HBM per device.

v0:
```python
import math

import jax
import jax.numpy as jnp
from jax import lax
from jax.sharding import PartitionSpec as P

D = 7168
ROPE = 64
QK_NOPE = 128
CAP = 2
PB = 512


EPSILON = 1e-06


def local(
    queries,
    own_latent,
    prefix_cache,
    block_home,
    row_prompt,
    chosen,
    value_up,
    out_weight,
    residual,
    norm_gain,
    gate_weight,
    up_weight,
):
    n_data = lax.axis_size("dp")
    n_lane = lax.axis_size("tp")
    devices = n_data * n_lane
    blk_dev = prefix_cache.shape[0]
    flat_width = prefix_cache.shape[1]
    kv_width = own_latent.shape[1]
    lat_width = value_up.shape[1]
    rows_dev = queries.shape[0]
    heads_dev = value_up.shape[0]
    all_rows = chosen.shape[0]
    replica = lax.axis_index("dp")
    lane_index = lax.axis_index("tp")
    self_index = replica * n_lane + lane_index
    start_row = replica * rows_dev
    slot_ids = block_home[row_prompt[:, None] * PB + chosen]
    holders = slot_ids // blk_dev
    offsets = slot_ids % blk_dev
    owners = jnp.broadcast_to(
        (jnp.arange(all_rows, dtype=jnp.int32) // rows_dev)[:, None], slot_ids.shape
    )
    needed = jnp.zeros((n_data, devices, blk_dev), jnp.int32).at[owners, holders, offsets].set(1)
    rank_table = jnp.cumsum(needed, axis=2)
    own_need = lax.dynamic_index_in_dim(needed, self_index, 1, keepdims=False)
    own_rank = lax.dynamic_index_in_dim(rank_table, self_index, 1, keepdims=False)
    places = jnp.arange(CAP, dtype=jnp.int32)
    matches = (own_need[:, None, :] == 1) & (own_rank[:, None, :] == places[None, :, None] + 1)
    picked = jnp.sum(
        jnp.where(matches, jnp.arange(blk_dev, dtype=jnp.int32)[None, None, :], 0), axis=2
    )
    outgoing = jnp.take(prefix_cache, picked, axis=0)
    copies = jnp.broadcast_to(outgoing[:, None], (n_data, n_lane, CAP, flat_width)).reshape(
        devices, CAP, flat_width
    )
    fetched = lax.all_to_all(copies, ("dp", "tp"), split_axis=0, concat_axis=0, tiled=True).reshape(
        devices * CAP, flat_width
    )
    my_holders = lax.dynamic_slice_in_dim(holders, start_row, rows_dev, 0)
    my_offsets = lax.dynamic_slice_in_dim(offsets, start_row, rows_dev, 0)
    my_ranks = lax.dynamic_index_in_dim(rank_table, replica, 0, keepdims=False)
    positions = my_holders * CAP + my_ranks[my_holders, my_offsets] - 1
    score_scale = 1.0 / math.sqrt(QK_NOPE + ROPE)
    group_rows = 8
    query_blocks = queries.reshape(rows_dev // group_rows, group_rows, heads_dev, kv_width)
    own_blocks = own_latent.reshape(rows_dev // group_rows, group_rows, kv_width)
    place_blocks = positions.reshape(rows_dev // group_rows, group_rows, -1)

    def attend(pieces):
        query_rows, own_rows, place_rows = pieces
        latents = jnp.take(fetched, place_rows, axis=0).reshape(group_rows, -1, kv_width)
        cached = (
            jnp.einsum("rhc,rnc->rhn", query_rows, latents, preferred_element_type=jnp.float32)
            * score_scale
        )
        itself = (
            jnp.einsum("rhc,rc->rh", query_rows, own_rows, preferred_element_type=jnp.float32)
            * score_scale
        )
        highest = jnp.maximum(jnp.max(cached, axis=2), itself)
        cache_raised = jnp.exp(cached - highest[:, :, None])
        own_raised = jnp.exp(itself - highest)
        denominator = jnp.sum(cache_raised, axis=2) + own_raised
        cache_weight = (cache_raised / denominator[:, :, None]).astype(jnp.bfloat16)
        own_weight = (own_raised / denominator).astype(jnp.bfloat16)
        mixture = jnp.einsum(
            "rhn,rnc->rhc",
            cache_weight,
            latents[:, :, :lat_width],
            preferred_element_type=jnp.float32,
        )
        mixture = mixture + own_weight.astype(jnp.float32)[:, :, None] * own_rows[
            :, None, :lat_width
        ].astype(jnp.float32)
        mixture = mixture.astype(jnp.bfloat16)
        lifted = jnp.einsum(
            "rhc,hcv->rhv", mixture, value_up, preferred_element_type=jnp.float32
        ).astype(jnp.bfloat16)
        return lifted.reshape(group_rows, -1)

    per_head = lax.map(attend, (query_blocks, own_blocks, place_blocks)).reshape(rows_dev, -1)
    partial_attn = jnp.dot(
        lax.all_gather(per_head, "dp", axis=0, tiled=True),
        out_weight,
        preferred_element_type=jnp.float32,
    )
    attn = lax.psum(partial_attn.astype(jnp.bfloat16), "tp").astype(jnp.float32)
    stream = (residual.astype(jnp.float32) + attn).astype(jnp.bfloat16)
    stream_wide = stream.astype(jnp.float32)
    part_squares = jnp.sum(stream_wide * stream_wide, axis=1)
    scaled = (stream_wide * norm_gain.astype(jnp.float32)[None, :]).astype(jnp.bfloat16)
    gate_term = jnp.dot(scaled, gate_weight, preferred_element_type=jnp.float32)
    up_term = jnp.dot(scaled, up_weight, preferred_element_type=jnp.float32)
    shares = lax.psum_scatter(
        jnp.concatenate([gate_term, up_term], axis=1).astype(jnp.bfloat16),
        "dp",
        scatter_dimension=0,
        tiled=True,
    ).astype(jnp.float32)
    square_sums = lax.psum(part_squares, "dp")
    row_squares = lax.dynamic_slice_in_dim(square_sums, start_row, rows_dev, 0)
    inverse = lax.rsqrt(row_squares / D + EPSILON)
    ff_dev = gate_weight.shape[1]
    gate_part = shares[:, :ff_dev] * inverse[:, None]
    up_part = shares[:, ff_dev:] * inverse[:, None]
    hidden = (jax.nn.silu(gate_part) * up_part).astype(jnp.bfloat16)
    return (stream, hidden)


def solution(mesh):
    placed = (
        P("dp", "tp"),
        P("dp", None),
        P(("dp", "tp"), None),
        P(),
        P(),
        P(),
        P("tp", None, None),
        P("tp", "dp"),
        P(None, "dp"),
        P("dp"),
        P("dp", "tp"),
        P("dp", "tp"),
    )
    return jax.shard_map(
        local, mesh=mesh, in_specs=placed, out_specs=(P(None, "dp"), P("dp", "tp")), check_vma=False
    )
```

profile of v0, /device:TPU:0, one launch (start us, length us, event | category | flops | bytes accessed | tf_op | source)
XLA Modules:
  0.0 856.6 jit_solution(14196233343610508880)
XLA Ops:
  7.2 0.6 broadcast_compare_fusion.2
  7.8 0.5 iota_add_fusion
  8.3 0.9 copy.89
  9.2 0.7 broadcast_multiply_fusion
  9.8 0.1 compare_select_fusion.4
  10.1 45.5 %gather_fusion.1 = s32[8192]{0:T(1024)S(1)} fusion(s32[2048]{0:T(1024)S(1)} %copy-done.1, s32[8192]{0:T(1024)S(1)} %broadcast_clamp_fusion), kind=kCustom, calls=%fused_computation.1 | custom fusion | bytes 98304 | tf_op jit(solution)/shard_map/gather | solution.py:46
  55.6 0.7 gather.19
  56.4 1.0 compare_select_fusion.3
  57.4 0.7 copy.90
  58.2 0.7 broadcast_select_fusion.3
  58.9 0.8 multiply_reduce_fusion
  59.7 0.1 copy.93
  59.8 0.8 and_reduce_fusion
  60.7 0.7 copy.92
  61.4 0.8 broadcast_select_fusion.2
  62.2 0.7 reshape.307
  62.9 30.7 %scatter_custom_fusion = s32[32768]{0:T(1024)S(1)} fusion(s32[8192]{0:T(1024)} %reshape.307, s32[8192]{0:T(1024)S(1)} %broadcast.355, s32[]{:T(128)} %copy.120), kind=kCustom, calls=%fused_computation.74 | custom fusion | bytes 131584
  93.6 0.8 constant_dynamic-slice_fusion
  94.4 1.1 copy.95
  95.5 0.4 fusion.31
  95.9 0.8 select_reduce_fusion
  96.9 3.5 gather_fusion.3
  100.4 4.6 reshape.300
  105.0 0.1 copy.96
  105.1 3.8 broadcast_select_fusion.1
  108.8 19.0 %broadcast_in_dim.99 = bf16[16,8,2,36864]{3,2,1,0:T(2,128)(2,1)} broadcast(bf16[16,2,36864]{2,1,0:T(2,128)(2,1)S(1)} %broadcast_select_fusion.1), dimensions={0,2,3} | broadcast | bytes 21233664 | tf_op jit(solution)/shard_map/broadcast_in_dim | solution.py:62
  127.8 11.6 %all-to-all-start = ((bf16[128,2,36864]{2,1,0:T(2,128)(2,1)}), bf16[128,2,36864]{2,1,0:T(2,128)(2,1)}, u32[]{:S(2)}, u32[]{:S(2)}) async-start(bf16[128,2,36864]{2,1,0:T(2,128)(2,1)} %bitcast.66), calls=%async_computation | async-start | bytes 37748736 | tf_op jit(solution)/shard_map/all_to_all | solution.py:65
  139.8 3.7 gather_fusion.2
  143.7 0.3 reshape.263
  144.0 254.5 %all-to-all-done = bf16[128,2,36864]{2,1,0:T(2,128)(2,1)} async-done(((bf16[128,2,36864]{2,1,0:T(2,128)(2,1)}), bf16[128,2,36864]{2,1,0:T(2,128)(2,1)}, u32[]{:S(2)}, u32[]{:S(2)}) %all-to-all-start) | async-done | bytes 18874400 | tf_op jit(solution)/shard_map/all_to_all | solution.py:65
  398.5 26.3 %reshape.266 = bf16[256,36864]{1,0:T(8,128)(2,1)} reshape(bf16[128,2,36864]{2,1,0:T(2,128)(2,1)} %all-to-all-done) | data formatting | bytes 37748736 | tf_op jit(solution)/shard_map/reshape | solution.py:65
  424.8 223.1 %while.10 = (s32[]{:T(128)}, bf16[2,8,2048]{2,1,0:T(8,128)(2,1)S(1)}, bf16[2,8,16,576]{3,2,1,0:T(8,128)(2,1)S(1)}, s32[2,8,32]{2,1,0:T(8,128)S(1)}, bf16[256,368...) while((s32[]{:T(128)}, ...), condition=%wide.region_6.7_spmd, body=%wide.region_3.6_spmd.sunk | while | flops 598843520 | bytes 163315840 | solution.py:110
  424.9 39.1 %gather_fusion = bf16[256,36864]{1,0:T(8,128)(2,1)} fusion(bf16[256,36864]{1,0:T(8,128)(2,1)} %get-tuple-element.152, s32[1024]{0:T(1024)S(1)} %pad_clamp_fusion.3), kind=kCustom, calls=%fused_computation.clone.1 | custom fusion | bytes 37749760 | tf_op jit(solution)/shard_map/while/body/eval_jaxpr/jit(_take)/gather | solution.py:80
  464.0 35.5 %gather.32 = bf16[8,2048,576]{2,1,0:T(8,128)(2,1)} reshape(bf16[256,36864]{1,0:T(8,128)(2,1)} %gather_fusion) | data formatting | bytes 37748736 | tf_op jit(solution)/shard_map/while/body/eval_jaxpr/jit(_take)/gather | solution.py:80
  499.5 0.1 broadcast_in_dim.115
  499.6 0.1 broadcast_in_dim.116
  499.7 18.5 %broadcast_select_fusion.5 = bf16[8,2048,576]{2,1,0:T(8,128)(2,1)} fusion(bf16[8,2048,576]{2,1,0:T(8,128)(2,1)} %gather.32, pred[8,2048]{1,0:T(8,128)(4,1)S(1)} %broadcast_in_dim.116), kind=kLoop, calls=%fused_computation.5.clone.1 | loop fusion | flops 9437184 | bytes 37765120 | tf_op jit(solution)/shard_map/while/body/eval_jaxpr/jit(_take)/select_n | solution.py:80
  518.2 9.8 %fusion.69 = (f32[8,16]{1,0:T(8,128)S(1)}, f32[8,16,2048]{2,1,0:T(8,128)S(1)}) fusion(bf16[8,2048,576]{2,1,0:T(8,128)(2,1)} %broadcast_select_fusion.5, bf16[2,8,16,576]{3,2,1,0:T(8,128)(2,1)S(1)} %get-tuple-element.150, s32[]{:T(128)} %get-tuple-element.140), kind=kOutput, calls=%fused_computation.112.clone.1 | convolution fusion | flops 302514048 | bytes 20087300 | tf_op jit(solution)/shard_map/while/body/eval_jaxpr/rhc,rnc->rhn/dot_general | solution.py:82
  528.1 0.2 fusion.70
  528.2 0.3 fusion.71
  528.6 7.3 fusion.73
  535.9 0.4 fusion.74
  536.4 39.1 %gather_fusion = bf16[256,36864]{1,0:T(8,128)(2,1)} fusion(bf16[256,36864]{1,0:T(8,128)(2,1)} %get-tuple-element.152, s32[1024]{0:T(1024)S(1)} %pad_clamp_fusion.3), kind=kCustom, calls=%fused_computation.clone.1 | custom fusion | bytes 37749760 | tf_op jit(solution)/shard_map/while/body/eval_jaxpr/jit(_take)/gather | solution.py:80
  575.5 35.5 %gather.32 = bf16[8,2048,576]{2,1,0:T(8,128)(2,1)} reshape(bf16[256,36864]{1,0:T(8,128)(2,1)} %gather_fusion) | data formatting | bytes 37748736 | tf_op jit(solution)/shard_map/while/body/eval_jaxpr/jit(_take)/gather | solution.py:80
  610.9 0.1 broadcast_in_dim.115
  611.0 0.1 broadcast_in_dim.116
  611.2 18.5 %broadcast_select_fusion.5 = bf16[8,2048,576]{2,1,0:T(8,128)(2,1)} fusion(bf16[8,2048,576]{2,1,0:T(8,128)(2,1)} %gather.32, pred[8,2048]{1,0:T(8,128)(4,1)S(1)} %broadcast_in_dim.116), kind=kLoop, calls=%fused_computation.5.clone.1 | loop fusion | flops 9437184 | bytes 37765120 | tf_op jit(solution)/shard_map/while/body/eval_jaxpr/jit(_take)/select_n | solution.py:80
  629.7 9.8 %fusion.69 = (f32[8,16]{1,0:T(8,128)S(1)}, f32[8,16,2048]{2,1,0:T(8,128)S(1)}) fusion(bf16[8,2048,576]{2,1,0:T(8,128)(2,1)} %broadcast_select_fusion.5, bf16[2,8,16,576]{3,2,1,0:T(8,128)(2,1)S(1)} %get-tuple-element.150, s32[]{:T(128)} %get-tuple-element.140), kind=kOutput, calls=%fused_computation.112.clone.1 | convolution fusion | flops 302514048 | bytes 20087300 | tf_op jit(solution)/shard_map/while/body/eval_jaxpr/rhc,rnc->rhn/dot_general | solution.py:82
  639.5 0.2 fusion.70
  639.7 0.3 fusion.71
  640.1 7.3 fusion.73
  647.4 0.4 fusion.74
  648.0 0.6 copy-done.9
  648.7 58.5 %all-gather.2.cloned.1.call-done = bf16[256,2048]{1,0:T(8,128)(2,1)} async-done(((bf16[16,2048]{1,0:T(8,128)(2,1)}), bf16[256,2048]{1,0:T(8,128)(2,1)}) %all-gather.2.cloned.1.call-update) | async-done | bytes 1048592 | tf_op jit(solution)/shard_map/all_gather | solution.py:112
  707.2 3.2 convolution_convert_fusion.3
  710.5 57.4 %all-reduce.2.cloned.1.call-done = bf16[256,448]{0,1:T(8,128)(2,1)} async-done(((bf16[256,448]{0,1:T(8,128)(2,1)}), bf16[256,448]{0,1:T(8,128)(2,1)}) %all-reduce.2.cloned.1.call-update) | async-done | bytes 229392 | tf_op jit(solution)/shard_map/psum | solution.py:116
  767.9 1.2 fusion.25
  769.1 0.9 convolution_convert_fusion.1
  770.0 0.9 convolution_convert_fusion.2
  770.9 1.6 pad_maximum_fusion
  772.5 40.8 %psum.15 = f32[256]{0:T(256)S(1)} all-reduce(f32[256]{0:T(256)S(1)} %get-tuple-element.61), channel_id=1, replica_groups=mesh['dp'=16,'tp'=8] {'dp'}, use_global_device_ids=true, to_apply=%region_10.11 | all-reduce | flops 256 | bytes 2048 | tf_op jit(solution)/shard_map/psum | solution.py:129
  813.4 35.0 %reduce-scatter.2.cloned.1.call-done = bf16[16,4608]{1,0:T(8,128)(2,1)} async-done(((bf16[256,4608]{1,0:T(8,128)(2,1)}), bf16[16,4608]{1,0:T(8,128)(2,1)}) %reduce-scatter.2.cloned.1.call-update) | async-done | bytes 147472 | tf_op jit(solution)/shard_map/reduce_scatter | solution.py:123
  848.4 0.9 convert_element_type.57
  849.3 0.8 fusion.27
  (71 shorter events, 1.4 us)
Async XLA Ops:
  7.2 761.9 %copy-start = (bf16[448,2304]{1,0:T(8,128)(2,1)S(1)}, bf16[448,2304]{1,0:T(8,128)(2,1)}, u32[]{:S(2)}) copy-start(bf16[448,2304]{1,0:T(8,128)(2,1)} %param.25) | copy-start | bytes 6193156
  7.2 2.9 copy-start.1
  10.1 48.8 %copy-start.12 = (s32[3]{0:T(128)S(1)}, s32[3]{0:T(128)}, u32[]{:S(2)}) copy-start(s32[3]{0:T(128)} %constant.148) | copy-start | bytes 40
  10.1 49.8 %copy-start.11 = (s32[3]{0:T(128)S(1)}, s32[3]{0:T(128)}, u32[]{:S(2)}) copy-start(s32[3]{0:T(128)} %constant.151) | copy-start | bytes 40
  55.6 41.3 %copy-start.2 = (bf16[16,36864]{1,0:T(8,128)(2,1)S(1)}, bf16[16,36864]{1,0:T(8,128)(2,1)}, u32[]{:S(2)}) copy-start(bf16[16,36864]{1,0:T(8,128)(2,1)} %param.16) | copy-start | bytes 3538948
  127.8 270.7 %all-to-all-start = ((bf16[128,2,36864]{2,1,0:T(2,128)(2,1)}), bf16[128,2,36864]{2,1,0:T(2,128)(2,1)}, u32[]{:S(2)}, u32[]{:S(2)}) async-start(bf16[128,2,36864]{2,1,0:T(2,128)(2,1)} %bitcast.66), calls=%async_computation | async-start | bytes 37748736 | tf_op jit(solution)/shard_map/all_to_all | solution.py:65
  139.5 567.8 %all-gather.2.cloned.1.call-start = ((), (), s32[]{:S(2)}) async-start(), calls=%async_computation.2 | async-start | bytes 1114112 | tf_op jit(solution)/shard_map/all_gather | solution.py:112
  139.8 3.8 copy-start.6
  144.0 280.8 %copy-start.8 = (bf16[16,576]{1,0:T(8,128)(2,1)S(1)}, bf16[16,576]{1,0:T(8,128)(2,1)}, u32[]{:S(2)}) copy-start(bf16[16,576]{1,0:T(8,128)(2,1)} %param.15) | copy-start | bytes 55300
  528.6 7.3 copy-start.3
  640.1 7.3 copy-start.3
  648.0 0.6 copy-start.9
  648.0 62.5 %copy-start.10 = (bf16[448]{0:T(512)(128)(2,1)S(1)}, bf16[448]{0:T(512)(128)(2,1)}, u32[]{:S(2)}) copy-start(bf16[448]{0:T(512)(128)(2,1)} %param.23) | copy-start | bytes 2692
  648.0 119.9 %copy-start.7 = (bf16[256,448]{0,1:T(8,128)(2,1)S(1)}, bf16[256,448]{0,1:T(8,128)(2,1)}, u32[]{:S(2)}) copy-start(bf16[256,448]{0,1:T(8,128)(2,1)} %param.22) | copy-start | bytes 688132
  648.6 119.2 %all-reduce.2.cloned.1.call-start = ((), (), s32[]{:S(2)}) async-start(), calls=%async_computation.3 | async-start | bytes 458752 | tf_op jit(solution)/shard_map/psum | solution.py:116
  710.4 137.9 %reduce-scatter.2.cloned.1.call-start = ((), (), s32[]{:S(2)}) async-start(), calls=%async_computation.4 | async-start | bytes 2506752 | tf_op jit(solution)/shard_map/reduce_scatter | solution.py:123
  767.9 2.1 copy-start.4
  769.1 1.8 copy-start.5
Sparse Core Ops, SparseCore 0:
  648.8 58.4 all-gather.1
  710.6 57.2 all-reduce.1
  772.6 75.6 reduce-scatter.1
where the time goes:
time: 860 us; the launch traced here: 857 us
  waiting for transfers between devices  405 us (47%)
  local copies, waits for them, and re-layouts  290 us (34%)
  other arithmetic  53.6 us (6%)
  blocking collectives  40.8 us (5%)
  matrix products  40.4 us (5%)
  between operations  14.1 us (2%)
  starting transfers between devices  11.7 us (1%)
    all_to_all x1, waiting for transfers between devices, local(): lax.all_to_all(copies, ('dp', 'tp'), split_axis=0, concat_axis=0, tiled=T...  255 us
    gather x4, local copies, waits for them, and re-layouts, attend(): jnp.take(fetched, place_rows, axis=0).reshape(group_rows, -1, kv_width)  149 us
    all_gather x1, waiting for transfers between devices, local(): lax.all_gather(per_head, 'dp', axis=0, tiled=True)  58.5 us
    psum x1, waiting for transfers between devices, local(): attn = lax.psum(partial_attn.astype(jnp.bfloat16), 'tp').astype(jnp.float32)  57.4 us
    gather x3, local copies, waits for them, and re-layouts, local(): slot_ids = block_home[row_prompt[:, None] * PB + chosen]  46.4 us
    psum x1, blocking collectives, local(): square_sums = lax.psum(part_squares, 'dp')  40.8 us
    select_n x4, other arithmetic, attend(): jnp.take(fetched, place_rows, axis=0).reshape(group_rows, -1, kv_width)  37 us
    reduce_scatter x1, waiting for transfers between devices, local(): lax.psum_scatter(jnp.concatenate([gate_term, up_term], axis=1).astype(jnp...  35 us
  transfers between devices with their start and end apart: 4, of which 4 were waited for; matrix products, arithmetic and copies ran while one was open for 1% of the time, Pallas kernels for 0%

commit v1 on v0

v1 whole, which is shorter than its diff:
```python
import math

import jax
import jax.numpy as jnp
from jax import lax
from jax.experimental import pallas as pl
from jax.experimental.pallas import tpu as pltpu
from jax.sharding import PartitionSpec as P

D = 7168
LAT = 512
ROPE = 64
QK_NOPE = 128
CAP = 2
PB = 512
BS = 64
KV = LAT + ROPE
EPSILON = 1e-06
SCALE = 1.0 / math.sqrt(QK_NOPE + ROPE)
NEG = -1e30
f32 = jnp.float32
bf16 = jnp.bfloat16


def send(x, axis, to, n):
    return lax.ppermute(x, axis, [(i, to(i)) for i in range(n)])


def swap_core(x):
    return send(x, "tp", lambda i: i ^ 1, 8)


def send_y(x, k):
    return send(x, "tp", lambda i: i ^ (2 * k), 8)


def send_x(x, k):
    return send(x, "dp", lambda i: ((i // 4 + k) % 4) * 4 + i % 4, 16)


def send_z(x, k):
    return send(x, "dp", lambda i: (i // 4) * 4 + (i % 4 + k) % 4, 16)


def fetch_kernel(picks, blocks, out, sem):
    n = out.shape[0]

    def start(i, c):
        pltpu.make_async_copy(blocks.at[picks[i]], out.at[i], sem.at[i]).start()
        return c

    def wait(i, c):
        pltpu.make_async_copy(blocks.at[picks[i]], out.at[i], sem.at[i]).wait()
        return c

    lax.fori_loop(0, n, start, 0, unroll=True)
    lax.fori_loop(0, n, wait, 0, unroll=True)


def fetch(picks, blocks):
    n = picks.shape[0]
    return pl.pallas_call(
        fetch_kernel,
        out_shape=jax.ShapeDtypeStruct((n,) + blocks.shape[1:], blocks.dtype),
        grid_spec=pltpu.PrefetchScalarGridSpec(
            num_scalar_prefetch=1,
            grid=(),
            in_specs=[pl.BlockSpec(memory_space=pl.ANY)],
            out_specs=pl.BlockSpec(memory_space=pl.ANY),
            scratch_shapes=[pltpu.SemaphoreType.DMA((n,))],
        ),
        name="fetch",
    )(picks, blocks)


def token_half(ref, half):
    n = ref.shape[0]
    parts = [
        ref[:, c * BS + half * 32 : c * BS + half * 32 + 32, :].reshape(n * 32, 128)
        for c in range(4)
    ]
    return jnp.concatenate(parts, axis=1)


def token_rope(ref, half):
    n = ref.shape[0]
    rope = ref[:, 4 * BS : 4 * BS + 32, :].reshape(n * 32, 128)
    lane = lax.broadcasted_iota(jnp.int32, rope.shape, 1)
    keep = (lane < ROPE) if half == 0 else (lane >= ROPE)
    return jnp.where(keep, rope, jnp.zeros_like(rope))


def attend_kernel(q_ref, a_ref, b_ref, bias_ref, out_ref, s_ref):
    q = q_ref[...]
    m_rows = q.shape[0]
    step = a_ref.shape[0] * 32
    top = None
    for i in range(4):
        ref, half = (a_ref, b_ref)[i // 2], i % 2
        keys = jnp.concatenate([token_half(ref, half), token_rope(ref, half)], axis=1)
        s = lax.dot_general(q, keys, (((1,), (1,)), ((), ())), preferred_element_type=f32)
        s = s.reshape(m_rows // 16, 16, step) + bias_ref[:, i * step : (i + 1) * step][None]
        s = s.reshape(m_rows, step)
        s_ref[i] = s
        high = jnp.max(s, axis=1, keepdims=True)
        top = high if top is None else jnp.maximum(top, high)
    acc = None
    total = None
    for i in range(4):
        ref, half = (a_ref, b_ref)[i // 2], i % 2
        p = jnp.exp((s_ref[i] - top) * SCALE)
        part = jnp.sum(p, axis=1, keepdims=True)
        o = jnp.dot(p.astype(bf16), token_half(ref, half), preferred_element_type=f32)
        acc = o if acc is None else acc + o
        total = part if total is None else total + part
    out_ref[:, :LAT] = (acc / total).astype(bf16)
    lse = top * SCALE + jnp.log(total)
    hi = lse.astype(bf16).astype(f32)
    mid = (lse - hi).astype(bf16).astype(f32)
    low = lse - hi - mid
    lane = lax.broadcasted_iota(jnp.int32, (m_rows, 128), 1)
    stats = jnp.where(lane == 0, hi, jnp.where(lane == 1, mid, jnp.where(lane == 2, low, 0.0)))
    out_ref[:, LAT:] = stats.astype(bf16)


def attend(q, a, b, bias):
    m_rows = q.shape[0]
    step = a.shape[0] * 32
    return pl.pallas_call(
        attend_kernel,
        out_shape=jax.ShapeDtypeStruct((m_rows, LAT + 128), bf16),
        in_specs=[pl.BlockSpec(memory_space=pltpu.VMEM)] * 4,
        out_specs=pl.BlockSpec(memory_space=pltpu.VMEM),
        scratch_shapes=[pltpu.VMEM((4, m_rows, step), f32)],
        compiler_params=pltpu.CompilerParams(vmem_limit_bytes=40 * 1024 * 1024),
        cost_estimate=pl.CostEstimate(
            flops=2 * m_rows * 4 * step * (640 + 512),
            bytes_accessed=2 * a.size * 2,
            transcendentals=m_rows * 4 * step,
        ),
        name="attend",
    )(q, a, b, bias)


def merge_kernel(o0, o1, o2, o3, q_ref, own_ref, up_ref, out_ref):
    heads, rows = 16, 16
    own = own_ref[...].astype(f32)
    q = q_ref[...].astype(f32).reshape(heads, rows, 640)
    lane = lax.broadcasted_iota(jnp.int32, (rows, 640), 1)
    key = jnp.where(lane < KV, own, 0.0)
    s_own = jnp.sum(q * key[None], axis=2, keepdims=True).reshape(heads * rows, 1) * SCALE
    lses = []
    for o in (o0, o1, o2, o3):
        lses.append(jnp.sum(o[:, LAT:].astype(f32), axis=1, keepdims=True))
    top = s_own
    for v in lses:
        top = jnp.maximum(top, v)
    e_own = jnp.exp(s_own - top)
    es = [jnp.exp(v - top) for v in lses]
    den = e_own + ((es[0] + es[1]) + (es[2] + es[3]))
    mix = (e_own / den).reshape(heads, rows, 1) * own[None, :, :LAT]
    mix = mix.reshape(heads * rows, LAT)
    for o, e in zip((o0, o1, o2, o3), es):
        mix = mix + (e / den) * o[:, :LAT].astype(f32)
    mix = mix.astype(bf16)
    for h in range(heads):
        out_ref[:, h * 128 : (h + 1) * 128] = jnp.dot(
            mix[h * rows : (h + 1) * rows], up_ref[h], preferred_element_type=f32
        ).astype(bf16)


def merge(parts, q, own, value_up):
    return pl.pallas_call(
        merge_kernel,
        out_shape=jax.ShapeDtypeStruct((16, 2048), bf16),
        in_specs=[pl.BlockSpec(memory_space=pltpu.VMEM)] * 7,
        out_specs=pl.BlockSpec(memory_space=pltpu.VMEM),
        compiler_params=pltpu.CompilerParams(vmem_limit_bytes=24 * 1024 * 1024),
        name="merge",
    )(*parts, q, own, value_up)


def local(
    queries,
    own_latent,
    prefix_cache,
    block_home,
    row_prompt,
    chosen,
    value_up,
    out_weight,
    residual,
    norm_gain,
    gate_weight,
    up_weight,
):
    replica = lax.axis_index("dp")
    lane = lax.axis_index("tp")
    me = replica * 8 + lane
    i32 = jnp.int32

    tokens = prefix_cache.reshape(16, BS, KV)
    lat = tokens[:, :, :LAT].reshape(16, BS, 4, 128).transpose(0, 2, 1, 3).reshape(16, 256, 128)
    rope = tokens[:, :, LAT:]
    rope = jnp.concatenate([rope[:, :32], rope[:, 32:]], axis=2)
    blocks = jnp.concatenate([lat, rope], axis=1)

    slots = me * 16 + jnp.arange(16, dtype=i32)
    ids = jnp.arange(2048, dtype=i32)
    held = jnp.sum(jnp.where(block_home[None, :] == slots[:, None], ids[None, :], 0), axis=1)
    wanted = (row_prompt[:, None] * PB + chosen).reshape(16, 512)
    needed = jnp.any(wanted[:, None, :] == held[None, :, None], axis=2)
    offs = jnp.arange(16, dtype=i32)
    before = jnp.sum(
        jnp.where(needed[:, None, :] & (offs[None, :] < offs[:, None])[None], 1, 0), axis=2
    )
    places = jnp.arange(CAP, dtype=i32)
    picks = jnp.sum(
        jnp.where(needed[:, None, :] & (before[:, None, :] == places[None, :, None]), offs, 0),
        axis=2,
    )

    outgoing = fetch(picks.reshape(-1), blocks).reshape(16, CAP, 288, 128)
    arrived = lax.all_to_all(outgoing, "dp", split_axis=0, concat_axis=0, tiled=True)
    mine = arrived.reshape(32, 288, 128)
    other = swap_core(mine)

    prompt = lax.dynamic_slice_in_dim(row_prompt, replica * 16, 1, 0)[0]
    home = lax.dynamic_slice_in_dim(block_home, prompt * PB, PB, 0)
    my_chosen = lax.dynamic_slice_in_dim(chosen, replica * 16, 16, 0)
    sel = jnp.any(my_chosen[:, :, None] == jnp.arange(PB, dtype=i32)[None, None, :], axis=1)
    need = jnp.any(sel, axis=0)
    holder = home // 16
    rank = jnp.sum(
        jnp.where(
            need[None, :] & (holder[None, :] == holder[:, None]) & (home[None, :] < home[:, None]),
            1,
            0,
        ),
        axis=1,
    )
    j = jnp.arange(32, dtype=i32)
    dev = jnp.concatenate([(j // 2) * 8 + lane, (j // 2) * 8 + (lane ^ 1)])
    place = jnp.concatenate([j % 2, j % 2])
    key = jnp.where(need, holder * 2 + rank, -1)
    hit = key[:, None] == (dev * 2 + place)[None, :]
    use = jnp.dot(sel.astype(bf16), hit.astype(bf16), preferred_element_type=f32)
    bias = jnp.where(use > 0.5, 0.0, NEG).reshape(16, 2, 1, 32, 1)
    bias = jnp.broadcast_to(bias, (16, 2, 2, 32, 32)).reshape(16, 4096)

    q = queries.reshape(16, 16, KV).transpose(1, 0, 2).reshape(256, KV)
    q = jnp.concatenate([q, q[:, LAT:]], axis=1)
    own = jnp.concatenate([own_latent, own_latent[:, LAT:]], axis=1)
    q_from = {k: send_y(q, k) for k in (2, 1, 3)}
    parts = []
    for k in (2, 1, 3):
        parts.append(send_y(attend(q_from[k], mine, other, bias), k))
    parts.append(attend(q, mine, other, bias))
    per_head = merge(parts, q, own, value_up)

    gx = jnp.concatenate([per_head] + [send_x(per_head, 4 - k) for k in (1, 2, 3)], axis=0)
    gz = jnp.concatenate([gx] + [send_z(gx, 4 - k) for k in (1, 2, 3)], axis=0)
    partial_attn = jnp.dot(gz, out_weight, preferred_element_type=f32)

    px, pz = replica // 4, replica % 4
    res = residual.reshape(4, 4, 16, 448)
    res = jnp.concatenate([res, res], axis=0)
    res = lax.dynamic_slice_in_dim(res, px, 4, 0)
    res = jnp.concatenate([res, res], axis=1)
    res = lax.dynamic_slice_in_dim(res, pz, 4, 1)
    res = res.transpose(1, 0, 2, 3).reshape(256, 448)

    core = lane % 2
    keep = lax.dynamic_slice_in_dim(partial_attn, core * 128, 128, 0)
    give = lax.dynamic_slice_in_dim(partial_attn, (1 - core) * 128, 128, 0)
    pair = (keep + swap_core(give.astype(bf16)).astype(f32)).astype(bf16)
    t1, t2, t3 = (send_y(pair, k).astype(f32) for k in (1, 2, 3))
    attn = (pair.astype(f32) + t1) + (t2 + t3)
    half = (lax.dynamic_slice_in_dim(res, core * 128, 128, 0).astype(f32) + attn).astype(bf16)
    half_other = swap_core(half)
    first = jnp.where(core == 0, half, half_other)
    second = jnp.where(core == 0, half_other, half)
    stream = jnp.concatenate([first, second], axis=0)

    wide = stream.astype(f32)
    squares = jnp.sum(wide * wide, axis=1)
    hi = lax.reduce_precision(squares, 8, 7)
    low = squares - hi
    col = lax.broadcasted_iota(i32, (256, 128), 1)
    tail = jnp.where(
        col == 0, hi[:, None], jnp.where(col == 1, low[:, None], 0.0)
    ).astype(bf16)
    scaled = (wide * norm_gain.astype(f32)[None, :]).astype(bf16)
    gate = jnp.dot(scaled, gate_weight, preferred_element_type=f32).astype(bf16)
    up = jnp.dot(scaled, up_weight, preferred_element_type=f32).astype(bf16)
    gate = jnp.concatenate([gate, tail], axis=1).reshape(4, 4, 16, 2304 + 128)
    up = up.reshape(4, 4, 16, 2304)

    g_in = [send_x(gate[:, k], k) for k in (2, 1, 3)]
    u_in = [send_z(up[k], k) for k in (2, 1, 3)]

    def add(own_part, got):
        return (own_part.astype(f32) + got[0].astype(f32)) + (
            got[1].astype(f32) + got[2].astype(f32)
        )

    g1 = add(gate[:, 0], g_in)
    u1 = add(up[0], u_in).astype(bf16)
    sq1 = g1[:, :, 2304:2305] + g1[:, :, 2305:2306]
    hi1 = lax.reduce_precision(sq1, 8, 7)
    col1 = lax.broadcasted_iota(i32, (4, 16, 128), 2)
    tail1 = jnp.where(col1 == 0, hi1, jnp.where(col1 == 1, sq1 - hi1, 0.0))
    g1 = jnp.concatenate([g1[:, :, :2304], tail1], axis=2).astype(bf16)
    g_in = [send_z(g1[k], k) for k in (2, 1, 3)]
    u_in = [send_x(u1[k], k) for k in (2, 1, 3)]
    g2 = add(g1[0], g_in)
    u2 = add(u1[0], u_in)
    sq = g2[:, 2304:2305] + g2[:, 2305:2306]
    inverse = lax.rsqrt(sq / D + EPSILON)
    gate_part = g2[:, :2304] * inverse
    up_part = u2 * inverse
    hidden = (jax.nn.silu(gate_part) * up_part).astype(bf16)

    out = stream.reshape(4, 4, 16, 448)
    out = jnp.concatenate([out, out], axis=0)
    out = lax.dynamic_slice_in_dim(out, 4 - pz, 4, 0)
    out = jnp.concatenate([out, out], axis=1)
    out = lax.dynamic_slice_in_dim(out, 4 - px, 4, 1)
    out = out.transpose(1, 0, 2, 3).reshape(256, 448)
    return (out, hidden)


def solution(mesh):
    placed = (
        P("dp", "tp"),
        P("dp", None),
        P(("dp", "tp"), None),
        P(),
        P(),
        P(),
        P("tp", None, None),
        P("tp", "dp"),
        P(None, "dp"),
        P("dp"),
        P("dp", "tp"),
        P("dp", "tp"),
    )
    return jax.shard_map(
        local, mesh=mesh, in_specs=placed, out_specs=(P(None, "dp"), P("dp", "tp")), check_vma=False
    )
```

time: 860 us -> 246 us (0.29)
  waiting for transfers between devices: 405 us -> 41.7 us
  local copies, waits for them, and re-layouts: 290 us -> 17.8 us
  Pallas kernels: 0 us -> 99.3 us
  other arithmetic: 53.6 us -> 9.15 us
  matrix products: 40.4 us -> 2.7 us
  starting transfers between devices: 11.7 us -> 34.1 us
  between operations: 14.1 us -> 1.84 us
    all_to_all x1 -> x0, waiting for transfers between devices: 255 us -> none  [local(): lax.all_to_all(copies, ('dp', 'tp'), split_axis=0, concat_axis=0, tiled=T...]
    gather x11 -> x0, local copies, waits for them, and re-layouts: 207 us -> none  [the longest x4 149 us: attend(): jnp.take(fetched, place_rows, axis=0).reshape(group_rows, -1, kv_width)]
    pallas_call x0 -> x6, Pallas kernels: none -> 99.3 us  [the longest x1 73.5 us: fetch(): pl.pallas_call(fetch_kernel, out_shape=jax.ShapeDtypeStruct((n,) + blocks...]
    all_gather x1 -> x0, waiting for transfers between devices: 58.5 us -> none  [local(): lax.all_gather(per_head, 'dp', axis=0, tiled=True)]
    psum x1 -> x0, waiting for transfers between devices: 57.4 us -> none  [local(): attn = lax.psum(partial_attn.astype(jnp.bfloat16), 'tp').astype(jnp.float32)]
    select_n x10 -> x4, other arithmetic: 42.7 us -> 0.12 us  [the longest x1 0.08 us: local(): holder = home // 16]
    ppermute x0 -> x30, waiting for transfers between devices: none -> 41.7 us  [send(): return lax.ppermute(x, axis, [(i, to(i)) for i in range(n)])]
    psum x1 -> x0, blocking collectives: 40.8 us -> none  [local(): square_sums = lax.psum(part_squares, 'dp')]
  transfers between devices with their start and end apart: 4 -> 30, of which waited for: 4 -> 19; matrix products, arithmetic and copies ran while one was open for 1% -> 7% of each run, Pallas kernels for 0% -> 10%
where the time goes in v1:
time: 246 us
  Pallas kernels  99.3 us (40%)
  waiting for transfers between devices  41.7 us (17%)
  blocking collectives  39.3 us (16%)
  starting transfers between devices  34.1 us (14%)
  local copies, waits for them, and re-layouts  17.8 us (7%)
  other arithmetic  9.15 us (4%)
  matrix products  2.7 us (1%)
    pallas_call x1, Pallas kernels, fetch(): pl.pallas_call(fetch_kernel, out_shape=jax.ShapeDtypeStruct((n,) + blocks...  73.5 us
    ppermute x30, waiting for transfers between devices, send(): return lax.ppermute(x, axis, [(i, to(i)) for i in range(n)])  41.7 us
    all_to_all x1, blocking collectives, local(): lax.all_to_all(outgoing, 'dp', split_axis=0, concat_axis=0, tiled=True)  39.3 us
    ppermute x30, starting transfers between devices, send(): return lax.ppermute(x, axis, [(i, to(i)) for i in range(n)])  34.1 us
    pallas_call x4, Pallas kernels, attend(): pl.pallas_call(attend_kernel, out_shape=jax.ShapeDtypeStruct((m_rows, LAT...  25.2 us
  transfers between devices with their start and end apart: 30, of which 19 were waited for; matrix products, arithmetic and copies ran while one was open for 7% of the time, Pallas kernels for 10%

profile of v1, /device:TPU:0, one launch (start us, length us, event | category | flops | bytes accessed | tf_op | source)
XLA Modules:
  0.0 245.9 jit_solution(18293096823548133053)
XLA Ops:
  0.7 2.8 %reshape.134 = bf16[16,64,576]{2,1,0:T(8,128)(2,1)S(1)} reshape(bf16[16,36864]{1,0:T(8,128)(2,1)} %param.14) | data formatting | bytes 2359296 | tf_op jit(solution)/shard_map/reshape | solution.py:202
  3.5 0.7 fusion.41
  4.2 1.1 slice.117
  7.3 1.4 reshape.135
  9.0 1.2 maximum_maximum_fusion.blocks
  10.2 73.5 %fetch.1 = bf16[32,288,128]{2,1,0:T(8,128)(2,1)} custom-call(s32[32]{0:T(128)} %reshape.133.picks, bf16[16,288,128]{2,1,0:T(8,128)(2,1)} %maximum_maximum_fusion.blocks), custom_call_target="tpu_custom_call" | custom-call | tf_op jit(solution)/shard_map/fetch/pallas_call | solution.py:62
  83.7 39.3 %all_to_all.5 = bf16[16,2,288,128]{3,2,1,0:T(8,128)(2,1)} all-to-all(bf16[16,2,288,128]{3,2,1,0:T(8,128)(2,1)} %bitcast.70), channel_id=1, replica_groups=mesh['dp'=16,'tp'=8] {'dp'}, dimensions={0} | all-to-all | bytes 4718592 | tf_op jit(solution)/shard_map/all_to_all | solution.py:224
  123.5 3.3 %collective-permute-start = (bf16[256,640]{1,0:T(8,128)(2,1)S(1)}, bf16[256,640]{1,0:T(8,128)(2,1)}, u32[]{:S(2)}, u32[]{:S(2)}) collective-permute-start(bf16[256,640]{1,0:T(8,128)(2,1)S(1)} %pad_maximum_fusion.1.q_ref), channel_id=1, source_target_pairs={{0,4},{1,5},{2,6},{3,7},{4,0},{5,1},{6,2},{7,3},{8,12},{9,13},{10,... | collective-permute-start | bytes 983048 | tf_op jit(solution)/shard_map/ppermute | solution.py:26
  126.8 0.7 collective-permute-start.3
  130.6 1.2 broadcast_in_dim.132
  131.8 1.7 reshape.139.bias_ref
  133.6 0.8 copy.38
  134.4 1.1 fusion.13
  135.7 6.3 %attend.4 = bf16[256,640]{1,0:T(8,128)(2,1)S(1)} custom-call(bf16[256,640]{1,0:T(8,128)(2,1)} %collective-permute-done.q_ref, bf16[32,288,128]{2,1,0:T(8,128)(2,1)} %bitcast.9.a_ref, bf16[32,288,128]{2,1,0:T(8,128)(2,1)} %collective-permute-done.1.b_ref, f32[16,4096]{1,0:T(8,128)S(1)} %reshape.139.bias_ref), custom_call_target="tpu_custom_call" | custom-call | flops 2415919104 | bytes 4718592 | tf_op jit(solution)/shard_map/attend/pallas_call | solution.py:129
  142.1 3.5 %collective-permute-start.2 = (bf16[256,640]{1,0:T(8,128)(2,1)S(1)}, bf16[256,640]{1,0:T(8,128)(2,1)S(1)}, u32[]{:S(2)}, u32[]{:S(2)}) collective-permute-start(bf16[256,640]{1,0:T(8,128)(2,1)S(1)} %attend.4), channel_id=1, source_target_pairs={{0,4},{1,5},{2,6},{3,7},{4,0},{5,1},{6,2},{7,3},{8,12},{9,13},{10,... | collective-permute-start | bytes 983048 | tf_op jit(solution)/shard_map/ppermute | solution.py:26
  145.5 6.2 %attend.5 = bf16[256,640]{1,0:T(8,128)(2,1)S(1)} custom-call(bf16[256,640]{1,0:T(8,128)(2,1)S(1)} %collective-permute-done.3.q_ref, bf16[32,288,128]{2,1,0:T(8,128)(2,1)} %bitcast.9.a_ref, bf16[32,288,128]{2,1,0:T(8,128)(2,1)} %collective-permute-done.1.b_ref, f32[16,4096]{1,0:T(8,128)S(1)} %reshape.139.bias_ref), custom_call_target="tpu_custom_call" | custom-call | flops 2415919104 | bytes 4718592 | tf_op jit(solution)/shard_map/attend/pallas_call | solution.py:129
  151.8 0.8 collective-permute-start.4
  152.6 6.2 %attend.6 = bf16[256,640]{1,0:T(8,128)(2,1)S(1)} custom-call(bf16[256,640]{1,0:T(8,128)(2,1)S(1)} %collective-permute-done.5.q_ref, bf16[32,288,128]{2,1,0:T(8,128)(2,1)} %bitcast.9.a_ref, bf16[32,288,128]{2,1,0:T(8,128)(2,1)} %collective-permute-done.1.b_ref, f32[16,4096]{1,0:T(8,128)S(1)} %reshape.139.bias_ref), custom_call_target="tpu_custom_call" | custom-call | flops 2415919104 | bytes 4718592 | tf_op jit(solution)/shard_map/attend/pallas_call | solution.py:129
  159.3 6.4 %attend.7.o3 = bf16[256,640]{1,0:T(8,128)(2,1)S(1)} custom-call(bf16[256,640]{1,0:T(8,128)(2,1)S(1)} %pad_maximum_fusion.1.q_ref, bf16[32,288,128]{2,1,0:T(8,128)(2,1)} %bitcast.9.a_ref, bf16[32,288,128]{2,1,0:T(8,128)(2,1)} %collective-permute-done.1.b_ref, f32[16,4096]{1,0:T(8,128)S(1)} %reshape.139.bias_ref), custom_call_target="tpu_custom_call" | custom-call | flops 2415919104 | bytes 4718592 | tf_op jit(solution)/shard_map/attend/pallas_call | solution.py:129
  165.8 2.7 %collective-permute-done.6.o2 = bf16[256,640]{1,0:T(8,128)(2,1)S(1)} collective-permute-done((bf16[256,640]{1,0:T(8,128)(2,1)S(1)}, bf16[256,640]{1,0:T(8,128)(2,1)S(1)}, u32[]{:S(2)}, u32[]{:S(2)}) %collective-permute-start.6) | collective-permute-done | bytes 327712 | tf_op jit(solution)/shard_map/ppermute | solution.py:26
  168.5 0.6 merge.1
  169.1 1.3 collective-permute-start.7
  170.4 1.3 collective-permute-start.8
  172.0 1.4 collective-permute-done.7
  173.4 2.7 %collective-permute-done.8 = bf16[16,2048]{1,0:T(8,128)(2,1)S(1)} collective-permute-done((bf16[16,2048]{1,0:T(8,128)(2,1)S(1)}, bf16[16,2048]{1,0:T(8,128)(2,1)S(1)}, u32[]{:S(2)}, u32[]{:S(2)}) %collective-permute-start.8) | collective-permute-done | bytes 65568 | tf_op jit(solution)/shard_map/ppermute | solution.py:26
  176.2 1.0 collective-permute-done.9
  177.2 1.1 collective-permute-start.10
  178.3 1.4 collective-permute-start.11
  180.3 4.1 %collective-permute-done.10 = bf16[64,2048]{1,0:T(8,128)(2,1)S(1)} collective-permute-done((bf16[64,2048]{1,0:T(8,128)(2,1)S(1)}, bf16[64,2048]{1,0:T(8,128)(2,1)S(1)}, u32[]{:S(2)}, u32[]{:S(2)}) %collective-permute-start.10) | collective-permute-done | bytes 262176 | tf_op jit(solution)/shard_map/ppermute | solution.py:26
  184.4 2.4 collective-permute-done.11
  186.8 2.7 %collective-permute-done.12 = bf16[64,2048]{1,0:T(8,128)(2,1)S(1)} collective-permute-done((bf16[64,2048]{1,0:T(8,128)(2,1)S(1)}, bf16[64,2048]{1,0:T(8,128)(2,1)S(1)}, u32[]{:S(2)}, u32[]{:S(2)}) %collective-permute-start.12) | collective-permute-done | bytes 262176 | tf_op jit(solution)/shard_map/ppermute | solution.py:26
  189.5 0.7 fusion.44
  190.5 1.1 collective-permute-done.13
  191.7 1.0 collective-permute-start.16
  192.7 1.3 collective-permute-start.15
  194.0 1.9 collective-permute-start.14
  196.0 4.6 %collective-permute-done.16 = bf16[128,448]{0,1:T(8,128)(2,1)S(1)} collective-permute-done((bf16[128,448]{0,1:T(8,128)(2,1)S(1)}, bf16[128,448]{0,1:T(8,128)(2,1)S(1)}, u32[]{:S(2)}, u32[]{:S(2)}) %collective-permute-start.16) | collective-permute-done | bytes 114720 | tf_op jit(solution)/shard_map/ppermute | solution.py:26
  200.7 0.6 collective-permute-done.14
  201.5 1.3 collective-permute-done.17
  202.9 0.9 convolution_convert_fusion
  203.8 1.1 fusion.42
  205.5 1.4 collective-permute-start.25
  206.9 1.6 collective-permute-start.24
  208.4 0.9 convolution_convert_fusion.1
  209.6 1.0 slice_bitcast_fusion.2
  210.6 0.9 copy.46
  211.4 1.1 fusion.10
  212.6 0.7 copy.47
  213.3 1.8 copy.52
  215.1 0.8 collective-permute-start.20
  216.0 1.2 collective-permute-start.19
  217.2 1.4 collective-permute-start.18
  218.6 3.5 %collective-permute-done.25 = bf16[4,16,2304]{2,1,0:T(8,128)(2,1)} collective-permute-done((bf16[4,16,2304]{2,1,0:T(8,128)(2,1)}, bf16[4,16,2304]{2,1,0:T(8,128)(2,1)}, u32[]{:S(2)}, u32[]{:S(2)}) %collective-permute-start.25) | collective-permute-done | bytes 294944 | tf_op jit(solution)/shard_map/ppermute | solution.py:26
  222.1 1.4 fusion.5
  223.5 2.2 collective-permute-done.20
  225.6 6.7 %collective-permute-done.19 = bf16[4,16,2432]{2,1,0:T(8,128)(2,1)S(1)} collective-permute-done((bf16[4,16,2432]{2,1,0:T(8,128)(2,1)}, bf16[4,16,2432]{2,1,0:T(8,128)(2,1)S(1)}, u32[]{:S(2)}, u32[]{:S(2)}) %collective-permute-start.19) | collective-permute-done | bytes 311328 | tf_op jit(solution)/shard_map/ppermute | solution.py:26
  232.8 1.7 collective-permute-start.23
  234.9 2.3 collective-permute-start.21
  237.2 0.7 collective-permute-start.29
  237.9 1.4 collective-permute-start.28
  239.3 1.2 collective-permute-start.27
  241.6 1.8 collective-permute-done.28
  243.5 1.7 collective-permute-done.27
  245.2 0.8 fusion.19
  (113 shorter events, 10.8 us)
Async XLA Ops:
  0.6 202.3 %copy-start = (bf16[448,2304]{1,0:T(8,128)(2,1)S(1)}, bf16[448,2304]{1,0:T(8,128)(2,1)}, u32[]{:S(2)}) copy-start(bf16[448,2304]{1,0:T(8,128)(2,1)} %param.23) | copy-start | bytes 6193156
  3.5 1.8 copy-start.12
  3.5 1.8 copy-start.7
  3.5 2.0 copy-start.10
  7.3 1.7 copy-start.4
  83.7 39.3 %copy-start.5 = (bf16[16,9216]{1,0:T(8,128)(2,1)S(1)}, bf16[16,9216]{1,0:T(8,128)(2,1)}, u32[]{:S(2)}) copy-start(bf16[16,9216]{1,0:T(8,128)(2,1)} %param.12) | copy-start | bytes 884740
  123.0 5.4 %copy-start.8 = (s32[256,32]{0,1:T(8,128)S(1)}, s32[256,32]{0,1:T(8,128)}, u32[]{:S(2)}) copy-start(s32[256,32]{0,1:T(8,128)} %param.17) | copy-start | bytes 98308
  123.0 12.7 %collective-permute-start.1 = (bf16[32,288,128]{2,1,0:T(8,128)(2,1)}, bf16[32,288,128]{2,1,0:T(8,128)(2,1)}, u32[]{:S(2)}, u32[]{:S(2)}) collective-permute-start(bf16[32,288,128]{2,1,0:T(8,128)(2,1)} %bitcast.9.a_ref), channel_id=1, source_target_pairs={{0,1},{1,0},{2,3},{3,2},{4,5},{5,4},{6,7},{7,6},{8,9},{9,8},{10,11... | collective-permute-start | bytes 7077896 | tf_op jit(solution)/shard_map/ppermute | solution.py:26
  123.4 10.2 %copy-start.6 = (bf16[256,448]{0,1:T(8,128)(2,1)S(1)}, bf16[256,448]{0,1:T(8,128)(2,1)}, u32[]{:S(2)}) copy-start(bf16[256,448]{0,1:T(8,128)(2,1)} %param.20) | copy-start | bytes 688132
  123.5 12.2 %collective-permute-start = (bf16[256,640]{1,0:T(8,128)(2,1)S(1)}, bf16[256,640]{1,0:T(8,128)(2,1)}, u32[]{:S(2)}, u32[]{:S(2)}) collective-permute-start(bf16[256,640]{1,0:T(8,128)(2,1)S(1)} %pad_maximum_fusion.1.q_ref), channel_id=1, source_target_pairs={{0,4},{1,5},{2,6},{3,7},{4,0},{5,1},{6,2},{7,3},{8,12},{9,13},{10,... | collective-permute-start | bytes 983048 | tf_op jit(solution)/shard_map/ppermute | solution.py:26
  126.8 18.8 %collective-permute-start.3 = (bf16[256,640]{1,0:T(8,128)(2,1)S(1)}, bf16[256,640]{1,0:T(8,128)(2,1)S(1)}, u32[]{:S(2)}, u32[]{:S(2)}) collective-permute-start(bf16[256,640]{1,0:T(8,128)(2,1)S(1)} %pad_maximum_fusion.1.q_ref), channel_id=1, source_target_pairs={{0,2},{1,3},{2,0},{3,1},{4,6},{5,7},{6,4},{7,5},{8,10},{9,11},{10,... | collective-permute-start | bytes 983048 | tf_op jit(solution)/shard_map/ppermute | solution.py:26
  127.4 25.1 %collective-permute-start.5 = (bf16[256,640]{1,0:T(8,128)(2,1)S(1)}, bf16[256,640]{1,0:T(8,128)(2,1)S(1)}, u32[]{:S(2)}, u32[]{:S(2)}) collective-permute-start(bf16[256,640]{1,0:T(8,128)(2,1)S(1)} %pad_maximum_fusion.1.q_ref), channel_id=1, source_target_pairs={{0,6},{1,7},{2,4},{3,5},{4,2},{5,3},{6,0},{7,1},{8,14},{9,15},{10,... | collective-permute-start | bytes 983048 | tf_op jit(solution)/shard_map/ppermute | solution.py:26
  142.1 23.7 %collective-permute-start.2 = (bf16[256,640]{1,0:T(8,128)(2,1)S(1)}, bf16[256,640]{1,0:T(8,128)(2,1)S(1)}, u32[]{:S(2)}, u32[]{:S(2)}) collective-permute-start(bf16[256,640]{1,0:T(8,128)(2,1)S(1)} %attend.4), channel_id=1, source_target_pairs={{0,4},{1,5},{2,6},{3,7},{4,0},{5,1},{6,2},{7,3},{8,12},{9,13},{10,... | collective-permute-start | bytes 983048 | tf_op jit(solution)/shard_map/ppermute | solution.py:26
  151.8 7.5 %copy-start.9 = (bf16[16,576]{1,0:T(8,128)(2,1)S(1)}, bf16[16,576]{1,0:T(8,128)(2,1)}, u32[]{:S(2)}) copy-start(bf16[16,576]{1,0:T(8,128)(2,1)} %param.13) | copy-start | bytes 55300
  151.8 7.5 %slice-start = ((bf16[16,576]{1,0:T(8,128)(2,1)}), bf16[16,64]{1,0:T(8,128)(2,1)S(1)}, s32[]{:S(2)}) async-start(bf16[16,576]{1,0:T(8,128)(2,1)} %param.13), calls=%async_computation.1 | async-start | bytes 8192 | tf_op jit(solution)/shard_map/slice | solution.py:253
  151.8 14.0 %collective-permute-start.4 = (bf16[256,640]{1,0:T(8,128)(2,1)S(1)}, bf16[256,640]{1,0:T(8,128)(2,1)S(1)}, u32[]{:S(2)}, u32[]{:S(2)}) collective-permute-start(bf16[256,640]{1,0:T(8,128)(2,1)S(1)} %attend.5), channel_id=1, source_target_pairs={{0,2},{1,3},{2,0},{3,1},{4,6},{5,7},{6,4},{7,5},{8,10},{9,11},{10,... | collective-permute-start | bytes 983048 | tf_op jit(solution)/shard_map/ppermute | solution.py:26
  158.8 9.7 %collective-permute-start.6 = (bf16[256,640]{1,0:T(8,128)(2,1)S(1)}, bf16[256,640]{1,0:T(8,128)(2,1)S(1)}, u32[]{:S(2)}, u32[]{:S(2)}) collective-permute-start(bf16[256,640]{1,0:T(8,128)(2,1)S(1)} %attend.6), channel_id=1, source_target_pairs={{0,6},{1,7},{2,4},{3,5},{4,2},{5,3},{6,0},{7,1},{8,14},{9,15},{10,... | collective-permute-start | bytes 983048 | tf_op jit(solution)/shard_map/ppermute | solution.py:26
  159.3 9.1 %copy-start.1 = (bf16[16,512,128]{2,1,0:T(8,128)(2,1)S(1)}, bf16[16,512,128]{2,1,0:T(8,128)(2,1)}, u32[]{:S(2)}) copy-start(bf16[16,512,128]{2,1,0:T(8,128)(2,1)} %up_ref.1) | copy-start | bytes 6291460
  169.1 20.4 %copy-start.3 = (bf16[2048,448]{0,1:T(8,128)(2,1)S(1)}, bf16[2048,448]{0,1:T(8,128)(2,1)}, u32[]{:S(2)}) copy-start(bf16[2048,448]{0,1:T(8,128)(2,1)} %param.19) | copy-start | bytes 5505028
  169.1 4.3 %collective-permute-start.7 = (bf16[16,2048]{1,0:T(8,128)(2,1)S(1)}, bf16[16,2048]{1,0:T(8,128)(2,1)S(1)}, u32[]{:S(2)}, u32[]{:S(2)}) collective-permute-start(bf16[16,2048]{1,0:T(8,128)(2,1)S(1)} %merge.1), channel_id=1, source_target_pairs={{0,96},{8,104},{16,112},{24,120},{32,0},{40,8},{48,16},{56,24},{64... | collective-permute-start | bytes 196616 | tf_op jit(solution)/shard_map/ppermute | solution.py:26
  170.4 5.8 %collective-permute-start.8 = (bf16[16,2048]{1,0:T(8,128)(2,1)S(1)}, bf16[16,2048]{1,0:T(8,128)(2,1)S(1)}, u32[]{:S(2)}, u32[]{:S(2)}) collective-permute-start(bf16[16,2048]{1,0:T(8,128)(2,1)S(1)} %merge.1), channel_id=1, source_target_pairs={{0,64},{8,72},{16,80},{24,88},{32,96},{40,104},{48,112},{56,120},{... | collective-permute-start | bytes 196616 | tf_op jit(solution)/shard_map/ppermute | solution.py:26
  171.7 5.5 %collective-permute-start.9 = (bf16[16,2048]{1,0:T(8,128)(2,1)S(1)}, bf16[16,2048]{1,0:T(8,128)(2,1)S(1)}, u32[]{:S(2)}, u32[]{:S(2)}) collective-permute-start(bf16[16,2048]{1,0:T(8,128)(2,1)S(1)} %merge.1), channel_id=1, source_target_pairs={{0,32},{8,40},{16,48},{24,56},{32,64},{40,72},{48,80},{56,88},{64,... | collective-permute-start | bytes 196616 | tf_op jit(solution)/shard_map/ppermute | solution.py:26
  177.2 7.2 %collective-permute-start.10 = (bf16[64,2048]{1,0:T(8,128)(2,1)S(1)}, bf16[64,2048]{1,0:T(8,128)(2,1)S(1)}, u32[]{:S(2)}, u32[]{:S(2)}) collective-permute-start(bf16[64,2048]{1,0:T(8,128)(2,1)S(1)} %pad_maximum_fusion.2), channel_id=1, source_target_pairs={{0,24},{8,0},{16,8},{24,16},{32,56},{40,32},{48,40},{56,48},{64,88... | collective-permute-start | bytes 786440 | tf_op jit(solution)/shard_map/ppermute | solution.py:26
  178.3 8.5 %collective-permute-start.11 = (bf16[64,2048]{1,0:T(8,128)(2,1)S(1)}, bf16[64,2048]{1,0:T(8,128)(2,1)S(1)}, u32[]{:S(2)}, u32[]{:S(2)}) collective-permute-start(bf16[64,2048]{1,0:T(8,128)(2,1)S(1)} %pad_maximum_fusion.2), channel_id=1, source_target_pairs={{0,16},{8,24},{16,0},{24,8},{32,48},{40,56},{48,32},{56,40},{64,80... | collective-permute-start | bytes 786440 | tf_op jit(solution)/shard_map/ppermute | solution.py:26
  179.7 9.8 %collective-permute-start.12 = (bf16[64,2048]{1,0:T(8,128)(2,1)S(1)}, bf16[64,2048]{1,0:T(8,128)(2,1)S(1)}, u32[]{:S(2)}, u32[]{:S(2)}) collective-permute-start(bf16[64,2048]{1,0:T(8,128)(2,1)S(1)} %pad_maximum_fusion.2), channel_id=1, source_target_pairs={{0,8},{8,16},{16,24},{24,0},{32,40},{40,48},{48,56},{56,32},{64,72... | collective-permute-start | bytes 786440 | tf_op jit(solution)/shard_map/ppermute | solution.py:26
  190.2 11.2 %copy-start.11 = (bf16[448]{0:T(512)(128)(2,1)S(1)}, bf16[448]{0:T(512)(128)(2,1)}, u32[]{:S(2)}) copy-start(bf16[448]{0:T(512)(128)(2,1)} %param.21) | copy-start | bytes 2692
  190.3 1.4 collective-permute-start.13
  191.7 8.9 %collective-permute-start.16 = (bf16[128,448]{0,1:T(8,128)(2,1)S(1)}, bf16[128,448]{0,1:T(8,128)(2,1)S(1)}, u32[]{:S(2)}, u32[]{:S(2)}) collective-permute-start(bf16[128,448]{0,1:T(8,128)(2,1)S(1)} %add_convert_fusion.1), channel_id=1, source_target_pairs={{0,6},{1,7},{2,4},{3,5},{4,2},{5,3},{6,0},{7,1},{8,14},{9,15},{10,... | collective-permute-start | bytes 344072 | tf_op jit(solution)/shard_map/ppermute | solution.py:26
  192.7 7.9 %collective-permute-start.15 = (bf16[128,448]{0,1:T(8,128)(2,1)S(1)}, bf16[128,448]{0,1:T(8,128)(2,1)S(1)}, u32[]{:S(2)}, u32[]{:S(2)}) collective-permute-start(bf16[128,448]{0,1:T(8,128)(2,1)S(1)} %add_convert_fusion.1), channel_id=1, source_target_pairs={{0,4},{1,5},{2,6},{3,7},{4,0},{5,1},{6,2},{7,3},{8,12},{9,13},{10,... | collective-permute-start | bytes 344072 | tf_op jit(solution)/shard_map/ppermute | solution.py:26
  194.0 7.3 %collective-permute-start.14 = (bf16[128,448]{0,1:T(8,128)(2,1)S(1)}, bf16[128,448]{0,1:T(8,128)(2,1)S(1)}, u32[]{:S(2)}, u32[]{:S(2)}) collective-permute-start(bf16[128,448]{0,1:T(8,128)(2,1)S(1)} %add_convert_fusion.1), channel_id=1, source_target_pairs={{0,2},{1,3},{2,0},{3,1},{4,6},{5,7},{6,4},{7,5},{8,10},{9,11},{10,... | collective-permute-start | bytes 344072 | tf_op jit(solution)/shard_map/ppermute | solution.py:26
  201.4 1.4 collective-permute-start.17
  203.8 4.7 %copy-start.2 = (bf16[448,2304]{1,0:T(8,128)(2,1)S(1)}, bf16[448,2304]{1,0:T(8,128)(2,1)}, u32[]{:S(2)}) copy-start(bf16[448,2304]{1,0:T(8,128)(2,1)} %param.22) | copy-start | bytes 6193156
  204.9 12.3 %collective-permute-start.26 = (bf16[4,16,2304]{2,1,0:T(8,128)(2,1)}, bf16[4,16,2304]{2,1,0:T(8,128)(2,1)}, u32[]{:S(2)}, u32[]{:S(2)}) collective-permute-start(bf16[4,16,2304]{2,1,0:T(8,128)(2,1)} %bitcast.26), channel_id=1, source_target_pairs={{0,24},{8,0},{16,8},{24,16},{32,56},{40,32},{48,40},{56,48},{64,88... | collective-permute-start | bytes 884744 | tf_op jit(solution)/shard_map/ppermute | solution.py:26
  205.5 16.6 %collective-permute-start.25 = (bf16[4,16,2304]{2,1,0:T(8,128)(2,1)}, bf16[4,16,2304]{2,1,0:T(8,128)(2,1)}, u32[]{:S(2)}, u32[]{:S(2)}) collective-permute-start(bf16[4,16,2304]{2,1,0:T(8,128)(2,1)} %bitcast.25), channel_id=1, source_target_pairs={{0,8},{8,16},{16,24},{24,0},{32,40},{40,48},{48,56},{56,32},{64,72... | collective-permute-start | bytes 884744 | tf_op jit(solution)/shard_map/ppermute | solution.py:26
  206.9 15.2 %collective-permute-start.24 = (bf16[4,16,2304]{2,1,0:T(8,128)(2,1)}, bf16[4,16,2304]{2,1,0:T(8,128)(2,1)}, u32[]{:S(2)}, u32[]{:S(2)}) collective-permute-start(bf16[4,16,2304]{2,1,0:T(8,128)(2,1)} %bitcast.24), channel_id=1, source_target_pairs={{0,16},{8,24},{16,0},{24,8},{32,48},{40,56},{48,32},{56,40},{64,80... | collective-permute-start | bytes 884744 | tf_op jit(solution)/shard_map/ppermute | solution.py:26
  215.1 10.5 %collective-permute-start.20 = (bf16[4,16,2432]{2,1,0:T(8,128)(2,1)}, bf16[4,16,2432]{2,1,0:T(8,128)(2,1)S(1)}, u32[]{:S(2)}, u32[]{:S(2)}) collective-permute-start(bf16[4,16,2432]{2,1,0:T(8,128)(2,1)} %get-tuple-element.16), channel_id=1, source_target_pairs={{0,96},{8,104},{16,112},{24,120},{32,0},{40,8},{48,16},{56,24},{64... | collective-permute-start | bytes 933896 | tf_op jit(solution)/shard_map/ppermute | solution.py:26
  216.0 16.4 %collective-permute-start.19 = (bf16[4,16,2432]{2,1,0:T(8,128)(2,1)}, bf16[4,16,2432]{2,1,0:T(8,128)(2,1)S(1)}, u32[]{:S(2)}, u32[]{:S(2)}) collective-permute-start(bf16[4,16,2432]{2,1,0:T(8,128)(2,1)} %get-tuple-element.15), channel_id=1, source_target_pairs={{0,32},{8,40},{16,48},{24,56},{32,64},{40,72},{48,80},{56,88},{64,... | collective-permute-start | bytes 933896 | tf_op jit(solution)/shard_map/ppermute | solution.py:26
  217.2 15.2 %collective-permute-start.18 = (bf16[4,16,2432]{2,1,0:T(8,128)(2,1)}, bf16[4,16,2432]{2,1,0:T(8,128)(2,1)S(1)}, u32[]{:S(2)}, u32[]{:S(2)}) collective-permute-start(bf16[4,16,2432]{2,1,0:T(8,128)(2,1)} %get-tuple-element.14), channel_id=1, source_target_pairs={{0,64},{8,72},{16,80},{24,88},{32,96},{40,104},{48,112},{56,120},{... | collective-permute-start | bytes 933896 | tf_op jit(solution)/shard_map/ppermute | solution.py:26
  232.8 6.5 %collective-permute-start.23 = (bf16[16,2432]{1,0:T(8,128)(2,1)S(1)}, bf16[16,2432]{1,0:T(8,128)(2,1)S(1)}, u32[]{:S(2)}, u32[]{:S(2)}) collective-permute-start(bf16[16,2432]{1,0:T(8,128)(2,1)S(1)} %get-tuple-element.22), channel_id=1, source_target_pairs={{0,24},{8,0},{16,8},{24,16},{32,56},{40,32},{48,40},{56,48},{64,88... | collective-permute-start | bytes 233480 | tf_op jit(solution)/shard_map/ppermute | solution.py:26
  234.6 6.4 %collective-permute-start.22 = (bf16[16,2432]{1,0:T(8,128)(2,1)S(1)}, bf16[16,2432]{1,0:T(8,128)(2,1)S(1)}, u32[]{:S(2)}, u32[]{:S(2)}) collective-permute-start(bf16[16,2432]{1,0:T(8,128)(2,1)S(1)} %get-tuple-element.23), channel_id=1, source_target_pairs={{0,8},{8,16},{16,24},{24,0},{32,40},{40,48},{48,56},{56,32},{64,72... | collective-permute-start | bytes 233480 | tf_op jit(solution)/shard_map/ppermute | solution.py:26
  234.9 6.1 %collective-permute-start.21 = (bf16[16,2432]{1,0:T(8,128)(2,1)S(1)}, bf16[16,2432]{1,0:T(8,128)(2,1)S(1)}, u32[]{:S(2)}, u32[]{:S(2)}) collective-permute-start(bf16[16,2432]{1,0:T(8,128)(2,1)S(1)} %get-tuple-element.21), channel_id=1, source_target_pairs={{0,16},{8,24},{16,0},{24,8},{32,48},{40,56},{48,32},{56,40},{64,80... | collective-permute-start | bytes 233480 | tf_op jit(solution)/shard_map/ppermute | solution.py:26
  237.2 4.4 %collective-permute-start.29 = (bf16[16,2304]{1,0:T(8,128)(2,1)S(1)}, bf16[16,2304]{1,0:T(8,128)(2,1)S(1)}, u32[]{:S(2)}, u32[]{:S(2)}) collective-permute-start(bf16[16,2304]{1,0:T(8,128)(2,1)S(1)} %get-tuple-element.25), channel_id=1, source_target_pairs={{0,96},{8,104},{16,112},{24,120},{32,0},{40,8},{48,16},{56,24},{64... | collective-permute-start | bytes 221192 | tf_op jit(solution)/shard_map/ppermute | solution.py:26
  237.9 5.6 %collective-permute-start.28 = (bf16[16,2304]{1,0:T(8,128)(2,1)S(1)}, bf16[16,2304]{1,0:T(8,128)(2,1)S(1)}, u32[]{:S(2)}, u32[]{:S(2)}) collective-permute-start(bf16[16,2304]{1,0:T(8,128)(2,1)S(1)} %get-tuple-element.26), channel_id=1, source_target_pairs={{0,32},{8,40},{16,48},{24,56},{32,64},{40,72},{48,80},{56,88},{64,... | collective-permute-start | bytes 221192 | tf_op jit(solution)/shard_map/ppermute | solution.py:26
  239.3 5.9 %collective-permute-start.27 = (bf16[16,2304]{1,0:T(8,128)(2,1)S(1)}, bf16[16,2304]{1,0:T(8,128)(2,1)S(1)}, u32[]{:S(2)}, u32[]{:S(2)}) collective-permute-start(bf16[16,2304]{1,0:T(8,128)(2,1)S(1)} %get-tuple-element.24), channel_id=1, source_target_pairs={{0,64},{8,72},{16,80},{24,88},{32,96},{40,104},{48,112},{56,120},{... | collective-permute-start | bytes 221192 | tf_op jit(solution)/shard_map/ppermute | solution.py:26

commit v2 on v1

v2 whole, which is shorter than its diff:
```python
import functools
import math

import jax
import jax.numpy as jnp
from jax import lax
from jax.experimental import pallas as pl
from jax.experimental.pallas import tpu as pltpu
from jax.sharding import PartitionSpec as P

D = 7168
LAT = 512
ROPE = 64
QK_NOPE = 128
CAP = 2
PB = 512
BS = 64
KV = LAT + ROPE
EPSILON = 1e-06
SCALE = 1.0 / math.sqrt(QK_NOPE + ROPE)
SCALE2 = SCALE / math.log(2.0)
NEG = -1e30
f32 = jnp.float32
bf16 = jnp.bfloat16


def send(x, axis, to, n):
    return lax.ppermute(x, axis, [(i, to(i)) for i in range(n)])


def swap_core(x):
    return send(x, "tp", lambda i: i ^ 1, 8)


def send_y(x, k):
    return send(x, "tp", lambda i: i ^ (2 * k), 8)


def send_x(x, k):
    return send(x, "dp", lambda i: ((i // 4 + k) % 4) * 4 + i % 4, 16)


def send_z(x, k):
    return send(x, "dp", lambda i: (i // 4) * 4 + (i % 4 + k) % 4, 16)


def fetch_kernel(picks, tokens, *outs):
    px, pz = picks[32] // 4, picks[32] % 4
    for place in range(CAP):
        for first in range(4):
            for second in range(4):
                kx, kz = (first, second) if place == 0 else (second, first)
                dest = ((px + kx) % 4) * 4 + (pz + kz) % 4
                pick = picks[dest * CAP + place]
                out = outs[place * 4 + first]
                for c in range(4):
                    out[second, c * BS : (c + 1) * BS, :] = tokens[pick, :, c * 128 : (c + 1) * 128]
                rope = tokens[pick, :, LAT:KV]
                out[second, 4 * BS :, :] = jnp.concatenate([rope[:32], rope[32:]], axis=1)


def fetch(picks, tokens):
    return pl.pallas_call(
        fetch_kernel,
        out_shape=[jax.ShapeDtypeStruct((4, 288, 128), bf16)] * 8,
        grid_spec=pltpu.PrefetchScalarGridSpec(
            num_scalar_prefetch=1,
            grid=(),
            in_specs=[pl.BlockSpec(memory_space=pltpu.VMEM)],
            out_specs=[pl.BlockSpec(memory_space=pltpu.VMEM)] * 8,
        ),
        compiler_params=pltpu.CompilerParams(vmem_limit_bytes=16 * 1024 * 1024),
        name="fetch",
    )(picks, tokens)


def half_latent(refs, half):
    rows = []
    for ref in refs:
        parts = [
            ref[:, c * BS + half * 32 : c * BS + half * 32 + 32, :].reshape(-1, 128)
            for c in range(4)
        ]
        rows.append(jnp.concatenate(parts, axis=1))
    return jnp.concatenate(rows, axis=0)


def half_rope(refs, half):
    rope = jnp.concatenate(
        [ref[:, 4 * BS : 4 * BS + 32, :].reshape(-1, 128) for ref in refs], axis=0
    )
    lane = lax.broadcasted_iota(jnp.int32, rope.shape, 1)
    keep = (lane < ROPE) if half == 0 else (lane >= ROPE)
    return jnp.where(keep, rope, jnp.zeros_like(rope))


def attend_kernel(groups, resume, last, *refs):
    q_ref, bias_ref = refs[0], refs[1]
    pieces = refs[2 : 2 + 4 * groups]
    refs = refs[2 + 4 * groups :]
    if resume:
        acc_in, stat_in = refs[0], refs[1]
        refs = refs[2:]
    q = q_ref[...]
    m_rows = q.shape[0]

    def values(g):
        mine = pieces[4 * g : 4 * g + 4]
        return jnp.concatenate([half_latent(mine, 0), half_latent(mine, 1)], axis=0)

    def scores(g):
        mine = pieces[4 * g : 4 * g + 4]
        ropes = jnp.concatenate([half_rope(mine, 0), half_rope(mine, 1)], axis=0)
        keys = jnp.concatenate([values(g), ropes], axis=1)
        s = lax.dot_general(q, keys, (((1,), (1,)), ((), ())), preferred_element_type=f32)
        n = s.shape[1]
        s = s.reshape(m_rows // 16, 16, n) + bias_ref[:, g * n : (g + 1) * n][None]
        return s.reshape(m_rows, n)

    top = total = acc = None
    if resume:
        top, total, acc = stat_in[:, 0:1], stat_in[:, 64:65], acc_in[...]
    s = scores(0)
    for g in range(groups):
        ahead = scores(g + 1) if g + 1 < groups else None
        high = jnp.max(s, axis=1, keepdims=True)
        new = high if top is None else jnp.maximum(top, high)
        p = jnp.exp2((s - new) * SCALE2)
        part = jnp.sum(p, axis=1, keepdims=True)
        o = jnp.dot(p.astype(bf16), values(g), preferred_element_type=f32)
        if top is None:
            acc, total = o, part
        else:
            fade = jnp.exp2((top - new) * SCALE2)
            acc, total = acc * fade + o, total * fade + part
        top, s = new, ahead
    lane = lax.broadcasted_iota(jnp.int32, (m_rows, 128), 1)
    if not last:
        refs[0][...] = acc
        refs[1][...] = jnp.where(lane < 64, top, total)
        return
    out_ref = refs[0]
    out_ref[:, :LAT] = (acc / total).astype(bf16)
    lse = top * SCALE + jnp.log(total)
    hi = lse.astype(bf16).astype(f32)
    mid = (lse - hi).astype(bf16).astype(f32)
    low = lse - hi - mid
    stats = jnp.where(lane == 0, hi, jnp.where(lane == 1, mid, jnp.where(lane == 2, low, 0.0)))
    out_ref[:, LAT:] = stats.astype(bf16)


def attend(q, bias, pieces, carry=(), last=True):
    m_rows = q.shape[0]
    groups = len(pieces) // 4
    if last:
        shape = jax.ShapeDtypeStruct((m_rows, LAT + 128), bf16)
    else:
        shape = [
            jax.ShapeDtypeStruct((m_rows, LAT), f32),
            jax.ShapeDtypeStruct((m_rows, 128), f32),
        ]
    vmem = pl.BlockSpec(memory_space=pltpu.VMEM)
    return pl.pallas_call(
        functools.partial(attend_kernel, groups, bool(carry), last),
        out_shape=shape,
        in_specs=[vmem] * (2 + len(pieces) + len(carry)),
        out_specs=vmem if last else [vmem] * 2,
        compiler_params=pltpu.CompilerParams(vmem_limit_bytes=20 * 1024 * 1024),
        cost_estimate=pl.CostEstimate(
            flops=2 * m_rows * groups * 1024 * (768 + 512) * 2,
            bytes_accessed=groups * 4 * 4 * 288 * 128 * 2,
            transcendentals=m_rows * groups * 1024,
        ),
        name="attend",
    )(q, bias, *pieces, *carry)


def merge_kernel(o0, o1, o2, o3, q_ref, own_ref, up_ref, out_ref):
    heads, rows = 16, 16
    own = own_ref[...].astype(f32)
    q = q_ref[...].astype(f32).reshape(heads, rows, 640)
    lane = lax.broadcasted_iota(jnp.int32, (rows, 640), 1)
    key = jnp.where(lane < KV, own, 0.0)
    s_own = jnp.sum(q * key[None], axis=2, keepdims=True).reshape(heads * rows, 1) * SCALE
    lses = []
    for o in (o0, o1, o2, o3):
        lses.append(jnp.sum(o[:, LAT:].astype(f32), axis=1, keepdims=True))
    top = s_own
    for v in lses:
        top = jnp.maximum(top, v)
    e_own = jnp.exp(s_own - top)
    es = [jnp.exp(v - top) for v in lses]
    den = e_own + ((es[0] + es[1]) + (es[2] + es[3]))
    mix = (e_own / den).reshape(heads, rows, 1) * own[None, :, :LAT]
    mix = mix.reshape(heads * rows, LAT)
    for o, e in zip((o0, o1, o2, o3), es):
        mix = mix + (e / den) * o[:, :LAT].astype(f32)
    mix = mix.astype(bf16)
    for h in range(heads):
        out_ref[:, h * 128 : (h + 1) * 128] = jnp.dot(
            mix[h * rows : (h + 1) * rows], up_ref[h], preferred_element_type=f32
        ).astype(bf16)


def merge(parts, q, own, value_up):
    return pl.pallas_call(
        merge_kernel,
        out_shape=jax.ShapeDtypeStruct((16, 2048), bf16),
        in_specs=[pl.BlockSpec(memory_space=pltpu.VMEM)] * 7,
        out_specs=pl.BlockSpec(memory_space=pltpu.VMEM),
        compiler_params=pltpu.CompilerParams(vmem_limit_bytes=24 * 1024 * 1024),
        name="merge",
    )(*parts, q, own, value_up)


def ffn_kernel(core_ref, half_ref, other_ref, gain_ref, wg_ref, wu_ref, stream_ref, *outs):
    core = core_ref[0]
    half, other = half_ref[...].astype(f32), other_ref[...].astype(f32)
    wide = jnp.concatenate(
        [jnp.where(core == 0, half, other), jnp.where(core == 0, other, half)], axis=0
    )
    stream_ref[...] = wide.astype(bf16)
    squares = jnp.sum(wide * wide, axis=1, keepdims=True)
    hi = squares.astype(bf16).astype(f32)
    lane = lax.broadcasted_iota(jnp.int32, (256, 128), 1)
    tail = jnp.where(lane == 0, hi, jnp.where(lane == 1, squares - hi, 0.0)).astype(bf16)
    scaled = (wide * gain_ref[...].astype(f32)).astype(bf16)
    gate = jnp.dot(scaled, wg_ref[...], preferred_element_type=f32).astype(bf16)
    gate = gate.reshape(4, 4, 16, 2304)
    tail = tail.reshape(4, 4, 16, 128)
    for k in range(4):
        outs[k][:, :, :2304] = gate[:, k]
        outs[k][:, :, 2304:] = tail[:, k]
    up = jnp.dot(scaled, wu_ref[...], preferred_element_type=f32).astype(bf16)
    up = up.reshape(4, 4, 16, 2304)
    for k in range(4):
        outs[4 + k][...] = up[k]


def ffn(core, half, other, gain, wg, wu):
    vmem = pl.BlockSpec(memory_space=pltpu.VMEM)
    return pl.pallas_call(
        ffn_kernel,
        out_shape=[jax.ShapeDtypeStruct((256, 448), bf16)]
        + [jax.ShapeDtypeStruct((4, 16, 2304 + 128), bf16)] * 4
        + [jax.ShapeDtypeStruct((4, 16, 2304), bf16)] * 4,
        in_specs=[pl.BlockSpec(memory_space=pltpu.SMEM)] + [vmem] * 5,
        out_specs=[vmem] * 9,
        compiler_params=pltpu.CompilerParams(vmem_limit_bytes=24 * 1024 * 1024),
        name="ffn",
    )(core, half, other, gain, wg, wu)


def add4(a, b, c, d):
    return (a.astype(f32) + b.astype(f32)) + (c.astype(f32) + d.astype(f32))


def local(
    queries,
    own_latent,
    prefix_cache,
    block_home,
    row_prompt,
    chosen,
    value_up,
    out_weight,
    residual,
    norm_gain,
    gate_weight,
    up_weight,
):
    replica = lax.axis_index("dp")
    lane = lax.axis_index("tp")
    px, pz = replica // 4, replica % 4
    core = lane % 2
    me = replica * 8 + lane
    i32 = jnp.int32

    q = queries.reshape(16, 16, KV).transpose(1, 0, 2).reshape(256, KV)
    q = jnp.concatenate([q, q[:, LAT:]], axis=1)
    own = jnp.concatenate([own_latent, own_latent[:, LAT:]], axis=1)
    q_from = {k: send_y(q, k) for k in (2, 1, 3)}
    q_from[0] = q

    slots = me * 16 + jnp.arange(16, dtype=i32)
    ids = jnp.arange(2048, dtype=i32)
    held = jnp.sum(jnp.where(block_home[None, :] == slots[:, None], ids[None, :], 0), axis=1)
    wanted = (row_prompt[:, None] * PB + chosen).reshape(16, 512)
    needed = jnp.any(wanted[:, None, :] == held[None, :, None], axis=2)
    offs = jnp.arange(16, dtype=i32)
    before = jnp.sum(
        jnp.where(needed[:, None, :] & (offs[None, :] < offs[:, None])[None], 1, 0), axis=2
    )
    places = jnp.arange(CAP, dtype=i32)
    picks = jnp.sum(
        jnp.where(needed[:, None, :] & (before[:, None, :] == places[None, :, None]), offs, 0),
        axis=2,
    )
    picks = jnp.concatenate([picks.reshape(-1), replica.reshape(1)])

    sent = fetch(picks, prefix_cache.reshape(16, BS, KV))
    a_got = [sent[0]] + [None] * 3
    b_got = [sent[4]] + [None] * 3
    for k in (2, 1, 3):
        a_got[k] = send_x(sent[k], k)
        b_got[k] = send_z(sent[4 + k], k)
    a_next = jnp.stack(a_got, axis=1)
    b_next = jnp.stack(b_got, axis=1)
    a_in = [a_next[0]] + [None] * 3
    b_in = [b_next[0]] + [None] * 3
    for k in (2, 1, 3):
        a_in[k] = send_z(a_next[k], k)
        b_in[k] = send_x(b_next[k], k)
    pieces = []
    for k in (0, 2, 1, 3):
        pieces += [a_in[k], b_in[k], swap_core(a_in[k]), swap_core(b_in[k])]

    prompt = lax.dynamic_slice_in_dim(row_prompt, replica * 16, 1, 0)[0]
    home = lax.dynamic_slice_in_dim(block_home, prompt * PB, PB, 0)
    my_chosen = lax.dynamic_slice_in_dim(chosen, replica * 16, 16, 0)
    sel = jnp.any(my_chosen[:, :, None] == jnp.arange(PB, dtype=i32)[None, None, :], axis=1)
    need = jnp.any(sel, axis=0)
    holder = home // 16
    rank = jnp.sum(
        jnp.where(
            need[None, :] & (holder[None, :] == holder[:, None]) & (home[None, :] < home[:, None]),
            1,
            0,
        ),
        axis=1,
    )
    g = jnp.array([0, 2, 1, 3], i32)[:, None, None, None]
    sib = jnp.array([0, 1], i32)[None, :, None, None]
    place = jnp.array([0, 1], i32)[None, None, :, None]
    j = jnp.arange(4, dtype=i32)[None, None, None, :]
    kx = jnp.where(place == 0, j, g)
    kz = jnp.where(place == 0, g, j)
    dev = (((px - kx) % 4) * 4 + (pz - kz) % 4) * 8 + (lane ^ sib)
    want_key = (dev * 2 + place).reshape(64)
    key = jnp.where(need, holder * 2 + rank, -1)
    hit = key[:, None] == want_key[None, :]
    use = jnp.dot(sel.astype(bf16), hit.astype(bf16), preferred_element_type=f32)
    bias = jnp.where(use > 0.5, 0.0, NEG).reshape(16, 4, 1, 16, 1)
    bias = jnp.broadcast_to(bias, (16, 4, 2, 16, 32)).reshape(16, 4096)

    parts = [send_y(attend(q_from[k], bias, pieces), k) for k in (2, 1, 3)]
    parts.append(attend(q, bias, pieces))
    per_head = merge(parts, q, own, value_up)

    gx = jnp.concatenate([per_head] + [send_x(per_head, 4 - k) for k in (1, 2, 3)], axis=0)
    gz = jnp.concatenate([gx] + [send_z(gx, 4 - k) for k in (1, 2, 3)], axis=0)
    partial_attn = jnp.dot(gz, out_weight, preferred_element_type=f32)

    res = residual.reshape(4, 4, 16, 448)
    res = jnp.concatenate([res, res], axis=0)
    res = lax.dynamic_slice_in_dim(res, px, 4, 0)
    res = jnp.concatenate([res, res], axis=1)
    res = lax.dynamic_slice_in_dim(res, pz, 4, 1)
    res = res.transpose(1, 0, 2, 3).reshape(256, 448)
    res = lax.dynamic_slice_in_dim(res, core * 128, 128, 0)

    keep = lax.dynamic_slice_in_dim(partial_attn, core * 128, 128, 0)
    give = lax.dynamic_slice_in_dim(partial_attn, (1 - core) * 128, 128, 0)
    pair = (keep + swap_core(give.astype(bf16)).astype(f32)).astype(bf16)
    t = [send_y(pair, k) for k in (1, 2, 3)]
    half = (res.astype(f32) + add4(pair, *t)).astype(bf16)
    half_other = swap_core(half)
    stream, *terms = ffn(
        core.reshape(1), half, half_other, norm_gain.reshape(1, 448), gate_weight, up_weight
    )

    g_in = [send_x(terms[k], k) for k in (2, 1, 3)]
    u_in = [send_z(terms[4 + k], k) for k in (2, 1, 3)]
    g1 = add4(terms[0], *g_in)
    u1 = add4(terms[4], *u_in).astype(bf16)
    sq1 = g1[:, :, 2304:2305] + g1[:, :, 2305:2306]
    hi1 = lax.reduce_precision(sq1, 8, 7)
    col1 = lax.broadcasted_iota(i32, (4, 16, 128), 2)
    tail1 = jnp.where(col1 == 0, hi1, jnp.where(col1 == 1, sq1 - hi1, 0.0))
    g1 = jnp.concatenate([g1[:, :, :2304], tail1], axis=2).astype(bf16)
    stream, g1 = lax.optimization_barrier((stream, g1))
    g_in = [send_z(g1[k], k) for k in (2, 1, 3)]
    u_in = [send_x(u1[k], k) for k in (2, 1, 3)]
    g2 = add4(g1[0], *g_in)
    u2 = add4(u1[0], *u_in)
    sq = g2[:, 2304:2305] + g2[:, 2305:2306]
    inverse = lax.rsqrt(sq / D + EPSILON)
    gate_part = g2[:, :2304] * inverse
    up_part = u2 * inverse
    hidden = (jax.nn.silu(gate_part) * up_part).astype(bf16)

    out = stream.reshape(4, 4, 16, 448)
    out = jnp.concatenate([out, out], axis=0)
    out = lax.dynamic_slice_in_dim(out, 4 - pz, 4, 0)
    out = jnp.concatenate([out, out], axis=1)
    out = lax.dynamic_slice_in_dim(out, 4 - px, 4, 1)
    out = out.transpose(1, 0, 2, 3).reshape(256, 448)
    return (out, hidden)


def solution(mesh):
    placed = (
        P("dp", "tp"),
        P("dp", None),
        P(("dp", "tp"), None),
        P(),
        P(),
        P(),
        P("tp", None, None),
        P("tp", "dp"),
        P(None, "dp"),
        P("dp"),
        P("dp", "tp"),
        P("dp", "tp"),
    )
    return jax.shard_map(
        local, mesh=mesh, in_specs=placed, out_specs=(P(None, "dp"), P("dp", "tp")), check_vma=False
    )
```

time: 246 us -> 178 us (0.72)
  Pallas kernels: 99.3 us -> 26 us
  blocking collectives: 39.3 us -> 0 us
  starting transfers between devices: 34.1 us -> 66.8 us
  waiting for transfers between devices: 41.7 us -> 54.5 us
    pallas_call x5 -> x6, Pallas kernels: 98.7 us -> 25.4 us  [the longest x4 21.1 us: attend(): pl.pallas_call(functools.partial(attend_kernel, groups, bool(carry), last...]
    all_to_all x1 -> x0, blocking collectives: 39.3 us -> none  [local(): lax.all_to_all(outgoing, 'dp', split_axis=0, concat_axis=0, tiled=True)]
    ppermute x30 -> x49, starting transfers between devices: 34.1 us -> 66.8 us  [send(): return lax.ppermute(x, axis, [(i, to(i)) for i in range(n)])]
    ppermute x30 -> x49, waiting for transfers between devices: 41.7 us -> 54.5 us  [send(): return lax.ppermute(x, axis, [(i, to(i)) for i in range(n)])]
    unnamed x35 -> x55, local copies, waits for them, and re-layouts: 2.88 us -> 8.07 us
    slice x3 -> x0, local copies, waits for them, and re-layouts: 2.84 us -> none  [the longest x1 1.08 us: local(): tokens[:, :, :LAT].reshape(16, BS, 4, 128).transpose(0, 2, 1, 3)]
  transfers between devices with their start and end apart: 30 -> 49, of which waited for: 19 -> 23; matrix products, arithmetic and copies ran while one was open for 7% -> 10% of each run, Pallas kernels for 10% -> 13%
where the time goes in v2:
time: 178 us
  starting transfers between devices  66.8 us (38%)
  waiting for transfers between devices  54.5 us (31%)
  Pallas kernels  26 us (15%)
  local copies, waits for them, and re-layouts  18.9 us (11%)
  other arithmetic  8.67 us (5%)
  between operations  1.91 us (1%)
    ppermute x49, starting transfers between devices, send(): return lax.ppermute(x, axis, [(i, to(i)) for i in range(n)])  66.8 us
    ppermute x49, waiting for transfers between devices, send(): return lax.ppermute(x, axis, [(i, to(i)) for i in range(n)])  54.5 us
    pallas_call x4, Pallas kernels, attend(): pl.pallas_call(functools.partial(attend_kernel, groups, bool(carry), last...  21.1 us
    unnamed x55, local copies, waits for them, and re-layouts  8.07 us
  transfers between devices with their start and end apart: 49, of which 23 were waited for; matrix products, arithmetic and copies ran while one was open for 10% of the time, Pallas kernels for 13%

profile of v2, /device:TPU:0, one launch (start us, length us, event | category | flops | bytes accessed | tf_op | source)
XLA Modules:
  0.0 177.8 jit_solution(10666611034169783000)
XLA Ops:
  0.7 1.4 reshape.170
  2.2 3.4 %collective-permute-start = (bf16[256,640]{1,0:T(8,128)(2,1)S(1)}, bf16[256,640]{1,0:T(8,128)(2,1)}, u32[]{:S(2)}, u32[]{:S(2)}) collective-permute-start(bf16[256,640]{1,0:T(8,128)(2,1)S(1)} %pad_maximum_fusion.2.refs_0_.q_ref), channel_id=1, source_target_pairs={{0,4},{1,5},{2,6},{3,7},{4,0},{5,1},{6,2},{7,3},{8,12},{9,13},{10,... | collective-permute-start | bytes 983048 | tf_op jit(solution)/shard_map/ppermute | solution.py:28
  7.2 2.7 %reshape.175.tokens = bf16[16,64,576]{2,1,0:T(8,128)(2,1)S(1)} reshape(bf16[16,36864]{1,0:T(8,128)(2,1)} %param.17) | data formatting | bytes 2359296 | tf_op jit(solution)/shard_map/reshape | solution.py:301
  9.9 1.9 %fetch.1 = (bf16[4,288,128]{2,1,0:T(8,128)(2,1)S(1)}, bf16[4,288,128]{2,1,0:T(8,128)(2,1)}, bf16[4,288,128]{2,1,0:T(8,128)(2,1)}, bf16[4,288,128]{2,1,0:T(8,128)...) custom-call(s32[33]{0:T(128)S(1)} %pad_add_fusion.picks, ...), custom_call_target="tpu_custom_call" | custom-call | tf_op jit(solution)/shard_map/fetch/pallas_call | solution.py:63
  14.7 2.8 %collective-permute-start.3 = (bf16[4,288,128]{2,1,0:T(8,128)(2,1)}, bf16[4,288,128]{2,1,0:T(8,128)(2,1)S(1)}, u32[]{:S(2)}, u32[]{:S(2)}) collective-permute-start(bf16[4,288,128]{2,1,0:T(8,128)(2,1)} %get-tuple-element.24), channel_id=1, source_target_pairs={{0,96},{8,104},{16,112},{24,120},{32,0},{40,8},{48,16},{56,24},{64... | collective-permute-start | bytes 884744 | tf_op jit(solution)/shard_map/ppermute | solution.py:28
  18.2 0.9 collective-permute-start.1
  19.1 4.0 %collective-permute-start.6 = (bf16[4,288,128]{2,1,0:T(8,128)(2,1)}, bf16[4,288,128]{2,1,0:T(8,128)(2,1)S(1)}, u32[]{:S(2)}, u32[]{:S(2)}) collective-permute-start(bf16[4,288,128]{2,1,0:T(8,128)(2,1)} %get-tuple-element.28), channel_id=1, source_target_pairs={{0,24},{8,0},{16,8},{24,16},{32,56},{40,32},{48,40},{56,48},{64,88... | collective-permute-start | bytes 884744 | tf_op jit(solution)/shard_map/ppermute | solution.py:28
  25.1 5.0 %collective-permute-done.3 = bf16[4,288,128]{2,1,0:T(8,128)(2,1)S(1)} collective-permute-done((bf16[4,288,128]{2,1,0:T(8,128)(2,1)}, bf16[4,288,128]{2,1,0:T(8,128)(2,1)S(1)}, u32[]{:S(2)}, u32[]{:S(2)}) %collective-permute-start.3) | collective-permute-done | bytes 294944 | tf_op jit(solution)/shard_map/ppermute | solution.py:28
  30.1 3.9 %collective-permute-start.5 = (bf16[4,288,128]{2,1,0:T(8,128)(2,1)}, bf16[4,288,128]{2,1,0:T(8,128)(2,1)S(1)}, u32[]{:S(2)}, u32[]{:S(2)}) collective-permute-start(bf16[4,288,128]{2,1,0:T(8,128)(2,1)} %copy-done.14), channel_id=1, source_target_pairs={{0,16},{8,24},{16,0},{24,8},{32,48},{40,56},{48,32},{56,40},{64,80... | collective-permute-start | bytes 884744 | tf_op jit(solution)/shard_map/ppermute | solution.py:28
  34.0 1.0 collective-permute-start.4
  35.0 1.1 pad_maximum_fusion
  36.9 2.0 %collective-permute-done.5 = bf16[4,288,128]{2,1,0:T(8,128)(2,1)S(1)} collective-permute-done((bf16[4,288,128]{2,1,0:T(8,128)(2,1)}, bf16[4,288,128]{2,1,0:T(8,128)(2,1)S(1)}, u32[]{:S(2)}, u32[]{:S(2)}) %collective-permute-start.5) | collective-permute-done | bytes 294944 | tf_op jit(solution)/shard_map/ppermute | solution.py:28
  38.9 3.2 %collective-permute-done.4 = bf16[4,288,128]{2,1,0:T(8,128)(2,1)S(1)} collective-permute-done((bf16[4,288,128]{2,1,0:T(8,128)(2,1)}, bf16[4,288,128]{2,1,0:T(8,128)(2,1)S(1)}, u32[]{:S(2)}, u32[]{:S(2)}) %collective-permute-start.4) | collective-permute-done | bytes 294944 | tf_op jit(solution)/shard_map/ppermute | solution.py:28
  42.3 0.9 slice_bitcast_fusion
  43.7 3.0 %collective-permute-start.9 = (bf16[4,288,128]{2,1,0:T(8,128)(2,1)S(1)}, bf16[4,288,128]{2,1,0:T(8,128)(2,1)}, u32[]{:S(2)}, u32[]{:S(2)}) collective-permute-start(bf16[4,288,128]{2,1,0:T(8,128)(2,1)S(1)} %get-tuple-element.56), channel_id=1, source_target_pairs={{0,16},{8,24},{16,0},{24,8},{32,48},{40,56},{48,32},{56,40},{64,80... | collective-permute-start | bytes 884744 | tf_op jit(solution)/shard_map/ppermute | solution.py:28
  47.6 3.8 %collective-permute-start.14 = (bf16[4,288,128]{2,1,0:T(8,128)(2,1)}, bf16[4,288,128]{2,1,0:T(8,128)(2,1)}, u32[]{:S(2)}, u32[]{:S(2)}) collective-permute-start(bf16[4,288,128]{2,1,0:T(8,128)(2,1)} %get-tuple-element.51), channel_id=1, source_target_pairs={{0,32},{8,40},{16,48},{24,56},{32,64},{40,72},{48,80},{56,88},{64,... | collective-permute-start | bytes 884744 | tf_op jit(solution)/shard_map/ppermute | solution.py:28
  52.1 3.1 %collective-permute-start.17 = (bf16[4,288,128]{2,1,0:T(8,128)(2,1)S(1)}, bf16[4,288,128]{2,1,0:T(8,128)(2,1)}, u32[]{:S(2)}, u32[]{:S(2)}) collective-permute-start(bf16[4,288,128]{2,1,0:T(8,128)(2,1)S(1)} %get-tuple-element.54), channel_id=1, source_target_pairs={{0,24},{8,0},{16,8},{24,16},{32,56},{40,32},{48,40},{56,48},{64,88... | collective-permute-start | bytes 884744 | tf_op jit(solution)/shard_map/ppermute | solution.py:28
  55.3 4.7 %collective-permute-start.18 = (bf16[4,288,128]{2,1,0:T(8,128)(2,1)}, bf16[4,288,128]{2,1,0:T(8,128)(2,1)}, u32[]{:S(2)}, u32[]{:S(2)}) collective-permute-start(bf16[4,288,128]{2,1,0:T(8,128)(2,1)} %get-tuple-element.50), channel_id=1, source_target_pairs={{0,96},{8,104},{16,112},{24,120},{32,0},{40,8},{48,16},{56,24},{64... | collective-permute-start | bytes 884744 | tf_op jit(solution)/shard_map/ppermute | solution.py:28
  61.2 2.1 %collective-permute-done.14.refs_11_ = bf16[4,288,128]{2,1,0:T(8,128)(2,1)} collective-permute-done((bf16[4,288,128]{2,1,0:T(8,128)(2,1)}, bf16[4,288,128]{2,1,0:T(8,128)(2,1)}, u32[]{:S(2)}, u32[]{:S(2)}) %collective-permute-start.14) | collective-permute-done | bytes 294944 | tf_op jit(solution)/shard_map/ppermute | solution.py:28
  63.8 1.1 collective-permute-done.18.refs_15_
  65.7 1.2 broadcast_in_dim.154
  66.9 1.7 reshape.172.refs_1_
  70.3 0.9 collective-permute-start.22
  71.7 1.0 copy-done.11
  72.7 5.3 %attend.4 = bf16[256,640]{1,0:T(8,128)(2,1)S(1)} custom-call(bf16[256,640]{1,0:T(8,128)(2,1)} %collective-permute-done.refs_0_, f32[16,4096]{1,0:T(8,128)S(1)} %reshape.172.refs_1_, bf16[4,288,128]{2,1,0:T(8,128)(2,1)S(1)} %get-tuple-element.57.refs_2_, bf16[4,288,128]{2,1,0:T(8,128)(2,1)S(1)} %get-tuple-element.53.refs_3_, ...), custom_call_target="tpu_custom_call" | custom-call | flops 5368709120 | bytes 4718592 | tf_op jit(solution)/shard_map/attend/pallas_call | solution.py:163
  78.0 3.0 %collective-permute-start.21 = (bf16[256,640]{1,0:T(8,128)(2,1)S(1)}, bf16[256,640]{1,0:T(8,128)(2,1)S(1)}, u32[]{:S(2)}, u32[]{:S(2)}) collective-permute-start(bf16[256,640]{1,0:T(8,128)(2,1)S(1)} %attend.4), channel_id=1, source_target_pairs={{0,4},{1,5},{2,6},{3,7},{4,0},{5,1},{6,2},{7,3},{8,12},{9,13},{10,... | collective-permute-start | bytes 983048 | tf_op jit(solution)/shard_map/ppermute | solution.py:28
  81.0 5.2 %attend.5 = bf16[256,640]{1,0:T(8,128)(2,1)S(1)} custom-call(bf16[256,640]{1,0:T(8,128)(2,1)S(1)} %collective-permute-done.22.refs_0_, f32[16,4096]{1,0:T(8,128)S(1)} %reshape.172.refs_1_, bf16[4,288,128]{2,1,0:T(8,128)(2,1)S(1)} %get-tuple-element.57.refs_2_, bf16[4,288,128]{2,1,0:T(8,128)(2,1)S(1)} %get-tuple-element.53.refs_3_, ...), custom_call_target="tpu_custom_call" | custom-call | flops 5368709120 | bytes 4718592 | tf_op jit(solution)/shard_map/attend/pallas_call | solution.py:163
  87.0 0.9 copy-done.8
  87.9 5.2 %attend.6 = bf16[256,640]{1,0:T(8,128)(2,1)S(1)} custom-call(bf16[256,640]{1,0:T(8,128)(2,1)S(1)} %collective-permute-done.24.refs_0_, f32[16,4096]{1,0:T(8,128)S(1)} %copy-done.8, bf16[4,288,128]{2,1,0:T(8,128)(2,1)S(1)} %get-tuple-element.57.refs_2_, bf16[4,288,128]{2,1,0:T(8,128)(2,1)S(1)} %get-tuple-element.53.refs_3_, ...), custom_call_target="tpu_custom_call" | custom-call | flops 5368709120 | bytes 4718592 | tf_op jit(solution)/shard_map/attend/pallas_call | solution.py:163
  94.0 5.4 %attend.7.o3 = bf16[256,640]{1,0:T(8,128)(2,1)S(1)} custom-call(bf16[256,640]{1,0:T(8,128)(2,1)S(1)} %pad_maximum_fusion.2.refs_0_.q_ref, f32[16,4096]{1,0:T(8,128)S(1)} %copy-done.8, bf16[4,288,128]{2,1,0:T(8,128)(2,1)S(1)} %get-tuple-element.57.refs_2_, bf16[4,288,128]{2,1,0:T(8,128)(2,1)S(1)} %get-tuple-element.53.refs_3_, ...), custom_call_target="tpu_custom_call" | custom-call | flops 5368709120 | bytes 4718592 | tf_op jit(solution)/shard_map/attend/pallas_call | solution.py:163
  99.4 3.8 %collective-permute-done.25.o2 = bf16[256,640]{1,0:T(8,128)(2,1)S(1)} collective-permute-done((bf16[256,640]{1,0:T(8,128)(2,1)S(1)}, bf16[256,640]{1,0:T(8,128)(2,1)S(1)}, u32[]{:S(2)}, u32[]{:S(2)}) %collective-permute-start.25) | collective-permute-done | bytes 327712 | tf_op jit(solution)/shard_map/ppermute | solution.py:28
  103.8 3.8 %collective-permute-start.26 = (bf16[16,2048]{1,0:T(8,128)(2,1)S(1)}, bf16[16,2048]{1,0:T(8,128)(2,1)S(1)}, u32[]{:S(2)}, u32[]{:S(2)}) collective-permute-start(bf16[16,2048]{1,0:T(8,128)(2,1)S(1)} %merge.1), channel_id=1, source_target_pairs={{0,96},{8,104},{16,112},{24,120},{32,0},{40,8},{48,16},{56,24},{64... | collective-permute-start | bytes 196616 | tf_op jit(solution)/shard_map/ppermute | solution.py:28
  107.6 0.9 collective-permute-start.28
  108.6 1.6 collective-permute-done.26
  110.1 3.4 %collective-permute-done.27 = bf16[16,2048]{1,0:T(8,128)(2,1)S(1)} collective-permute-done((bf16[16,2048]{1,0:T(8,128)(2,1)S(1)}, bf16[16,2048]{1,0:T(8,128)(2,1)S(1)}, u32[]{:S(2)}, u32[]{:S(2)}) %collective-permute-start.27) | collective-permute-done | bytes 65568 | tf_op jit(solution)/shard_map/ppermute | solution.py:28
  113.8 0.9 collective-permute-start.29
  114.8 2.1 %collective-permute-start.30 = (bf16[64,2048]{1,0:T(8,128)(2,1)S(1)}, bf16[64,2048]{1,0:T(8,128)(2,1)S(1)}, u32[]{:S(2)}, u32[]{:S(2)}) collective-permute-start(bf16[64,2048]{1,0:T(8,128)(2,1)S(1)} %pad_maximum_fusion.4), channel_id=1, source_target_pairs={{0,16},{8,24},{16,0},{24,8},{32,48},{40,56},{48,32},{56,40},{64,80... | collective-permute-start | bytes 786440 | tf_op jit(solution)/shard_map/ppermute | solution.py:28
  117.2 4.2 %collective-permute-done.29 = bf16[64,2048]{1,0:T(8,128)(2,1)S(1)} collective-permute-done((bf16[64,2048]{1,0:T(8,128)(2,1)S(1)}, bf16[64,2048]{1,0:T(8,128)(2,1)S(1)}, u32[]{:S(2)}, u32[]{:S(2)}) %collective-permute-start.29) | collective-permute-done | bytes 262176 | tf_op jit(solution)/shard_map/ppermute | solution.py:28
  121.5 2.2 %collective-permute-done.30 = bf16[64,2048]{1,0:T(8,128)(2,1)S(1)} collective-permute-done((bf16[64,2048]{1,0:T(8,128)(2,1)S(1)}, bf16[64,2048]{1,0:T(8,128)(2,1)S(1)}, u32[]{:S(2)}, u32[]{:S(2)}) %collective-permute-start.30) | collective-permute-done | bytes 262176 | tf_op jit(solution)/shard_map/ppermute | solution.py:28
  123.7 2.7 %collective-permute-done.31 = bf16[64,2048]{1,0:T(8,128)(2,1)S(1)} collective-permute-done((bf16[64,2048]{1,0:T(8,128)(2,1)S(1)}, bf16[64,2048]{1,0:T(8,128)(2,1)S(1)}, u32[]{:S(2)}, u32[]{:S(2)}) %collective-permute-start.31) | collective-permute-done | bytes 262176 | tf_op jit(solution)/shard_map/ppermute | solution.py:28
  127.5 1.1 collective-permute-done.32
  128.6 1.1 collective-permute-start.35
  129.7 1.2 collective-permute-start.34
  130.9 1.9 %collective-permute-start.33 = (bf16[128,448]{1,0:T(8,128)(2,1)S(1)}, bf16[128,448]{1,0:T(8,128)(2,1)S(1)}, u32[]{:S(2)}, u32[]{:S(2)}) collective-permute-start(bf16[128,448]{1,0:T(8,128)(2,1)S(1)} %add_convert_fusion.2), channel_id=1, source_target_pairs={{0,2},{1,3},{2,0},{3,1},{4,6},{5,7},{6,4},{7,5},{8,10},{9,11},{10,... | collective-permute-start | bytes 344072 | tf_op jit(solution)/shard_map/ppermute | solution.py:28
  132.9 5.3 %collective-permute-done.35 = bf16[128,448]{1,0:T(8,128)(2,1)S(1)} collective-permute-done((bf16[128,448]{1,0:T(8,128)(2,1)S(1)}, bf16[128,448]{1,0:T(8,128)(2,1)S(1)}, u32[]{:S(2)}, u32[]{:S(2)}) %collective-permute-start.35) | collective-permute-done | bytes 114720 | tf_op jit(solution)/shard_map/ppermute | solution.py:28
  139.1 1.3 collective-permute-done.36.other_ref
  140.4 2.4 %ffn.1 = (bf16[256,448]{1,0:T(8,128)(2,1)S(1)}, bf16[4,16,2432]{2,1,0:T(8,128)(2,1)S(1)}, bf16[4,16,2432]{2,1,0:T(8,128)(2,1)S(1)}, bf16[4,16,2432]{2,1,0:T(8,12...) custom-call(s32[1]{0:T(128)} %bitcast.core_ref, ...), custom_call_target="tpu_custom_call" | custom-call | tf_op jit(solution)/shard_map/ffn/pallas_call | solution.py:242
  144.1 1.4 collective-permute-start.44
  145.5 1.7 collective-permute-start.43
  147.3 0.9 collective-permute-start.39
  148.1 1.2 collective-permute-start.38
  149.3 4.4 %collective-permute-done.45 = bf16[4,16,2304]{2,1,0:T(8,128)(2,1)} collective-permute-done((bf16[4,16,2304]{2,1,0:T(8,128)(2,1)}, bf16[4,16,2304]{2,1,0:T(8,128)(2,1)}, u32[]{:S(2)}, u32[]{:S(2)}) %collective-permute-start.45) | collective-permute-done | bytes 294944 | tf_op jit(solution)/shard_map/ppermute | solution.py:28
  153.7 1.3 collective-permute-start.37
  155.6 5.2 %collective-permute-done.43 = bf16[4,16,2304]{2,1,0:T(8,128)(2,1)} collective-permute-done((bf16[4,16,2304]{2,1,0:T(8,128)(2,1)}, bf16[4,16,2304]{2,1,0:T(8,128)(2,1)}, u32[]{:S(2)}, u32[]{:S(2)}) %collective-permute-start.43) | collective-permute-done | bytes 294944 | tf_op jit(solution)/shard_map/ppermute | solution.py:28
  160.8 1.3 add_convert_fusion
  162.8 0.9 collective-permute-start.48
  163.6 1.2 collective-permute-start.47
  165.3 1.2 collective-permute-start.42
  166.5 0.9 collective-permute-start.41
  167.4 1.7 collective-permute-start.40
  170.3 1.2 collective-permute-start.46
  172.1 1.2 collective-permute-done.40
  173.6 2.6 %collective-permute-done.46 = bf16[16,2304]{1,0:T(8,128)(2,1)S(1)} collective-permute-done((bf16[16,2304]{1,0:T(8,128)(2,1)S(1)}, bf16[16,2304]{1,0:T(8,128)(2,1)S(1)}, u32[]{:S(2)}, u32[]{:S(2)}) %collective-permute-start.46) | collective-permute-done | bytes 73760 | tf_op jit(solution)/shard_map/ppermute | solution.py:28
  176.2 1.6 fusion.13
  (161 shorter events, 24.6 us)
Async XLA Ops:
  0.6 125.7 %copy-start = (bf16[2048,448]{0,1:T(8,128)(2,1)S(1)}, bf16[2048,448]{0,1:T(8,128)(2,1)}, u32[]{:S(2)}) copy-start(bf16[2048,448]{0,1:T(8,128)(2,1)} %param.22) | copy-start | bytes 5505028
  0.6 5.0 %copy-start.21 = (s32[256]{0:T(256)S(1)}, s32[256]{0:T(256)}, u32[]{:S(2)}) copy-start(s32[256]{0:T(256)} %param.19) | copy-start | bytes 3076
  0.7 5.0 %copy-start.18 = (s32[256,32]{0,1:T(8,128)S(1)}, s32[256,32]{0,1:T(8,128)}, u32[]{:S(2)}) copy-start(s32[256,32]{0,1:T(8,128)} %param.20) | copy-start | bytes 98308
  0.7 5.2 %copy-start.19 = (s32[2048]{0:T(1024)S(1)}, s32[2048]{0:T(1024)}, u32[]{:S(2)}) copy-start(s32[2048]{0:T(1024)} %param.18) | copy-start | bytes 24580
  2.2 45.3 %collective-permute-start = (bf16[256,640]{1,0:T(8,128)(2,1)S(1)}, bf16[256,640]{1,0:T(8,128)(2,1)}, u32[]{:S(2)}, u32[]{:S(2)}) collective-permute-start(bf16[256,640]{1,0:T(8,128)(2,1)S(1)} %pad_maximum_fusion.2.refs_0_.q_ref), channel_id=1, source_target_pairs={{0,4},{1,5},{2,6},{3,7},{4,0},{5,1},{6,2},{7,3},{8,12},{9,13},{10,... | collective-permute-start | bytes 983048 | tf_op jit(solution)/shard_map/ppermute | solution.py:28
  9.8 15.2 %copy-start.22 = (s32[4]{0:T(128)S(1)}, s32[4]{0:T(128)}, u32[]{:S(2)}) copy-start(s32[4]{0:T(128)} %constant.115.clone) | copy-start | bytes 52
  14.7 15.4 %collective-permute-start.3 = (bf16[4,288,128]{2,1,0:T(8,128)(2,1)}, bf16[4,288,128]{2,1,0:T(8,128)(2,1)S(1)}, u32[]{:S(2)}, u32[]{:S(2)}) collective-permute-start(bf16[4,288,128]{2,1,0:T(8,128)(2,1)} %get-tuple-element.24), channel_id=1, source_target_pairs={{0,96},{8,104},{16,112},{24,120},{32,0},{40,8},{48,16},{56,24},{64... | collective-permute-start | bytes 884744 | tf_op jit(solution)/shard_map/ppermute | solution.py:28
  17.4 16.5 %collective-permute-start.2 = (bf16[4,288,128]{2,1,0:T(8,128)(2,1)}, bf16[4,288,128]{2,1,0:T(8,128)(2,1)S(1)}, u32[]{:S(2)}, u32[]{:S(2)}) collective-permute-start(bf16[4,288,128]{2,1,0:T(8,128)(2,1)} %get-tuple-element.23), channel_id=1, source_target_pairs={{0,64},{8,72},{16,80},{24,88},{32,96},{40,104},{48,112},{56,120},{... | collective-permute-start | bytes 884744 | tf_op jit(solution)/shard_map/ppermute | solution.py:28
  18.2 16.8 %collective-permute-start.1 = (bf16[4,288,128]{2,1,0:T(8,128)(2,1)}, bf16[4,288,128]{2,1,0:T(8,128)(2,1)S(1)}, u32[]{:S(2)}, u32[]{:S(2)}) collective-permute-start(bf16[4,288,128]{2,1,0:T(8,128)(2,1)} %get-tuple-element.22), channel_id=1, source_target_pairs={{0,32},{8,40},{16,48},{24,56},{32,64},{40,72},{48,80},{56,88},{64,... | collective-permute-start | bytes 884744 | tf_op jit(solution)/shard_map/ppermute | solution.py:28
  19.1 17.8 %collective-permute-start.6 = (bf16[4,288,128]{2,1,0:T(8,128)(2,1)}, bf16[4,288,128]{2,1,0:T(8,128)(2,1)S(1)}, u32[]{:S(2)}, u32[]{:S(2)}) collective-permute-start(bf16[4,288,128]{2,1,0:T(8,128)(2,1)} %get-tuple-element.28), channel_id=1, source_target_pairs={{0,24},{8,0},{16,8},{24,16},{32,56},{40,32},{48,40},{56,48},{64,88... | collective-permute-start | bytes 884744 | tf_op jit(solution)/shard_map/ppermute | solution.py:28
  30.1 8.8 %collective-permute-start.5 = (bf16[4,288,128]{2,1,0:T(8,128)(2,1)}, bf16[4,288,128]{2,1,0:T(8,128)(2,1)S(1)}, u32[]{:S(2)}, u32[]{:S(2)}) collective-permute-start(bf16[4,288,128]{2,1,0:T(8,128)(2,1)} %copy-done.14), channel_id=1, source_target_pairs={{0,16},{8,24},{16,0},{24,8},{32,48},{40,56},{48,32},{56,40},{64,80... | collective-permute-start | bytes 884744 | tf_op jit(solution)/shard_map/ppermute | solution.py:28
  34.0 8.1 %collective-permute-start.4 = (bf16[4,288,128]{2,1,0:T(8,128)(2,1)}, bf16[4,288,128]{2,1,0:T(8,128)(2,1)S(1)}, u32[]{:S(2)}, u32[]{:S(2)}) collective-permute-start(bf16[4,288,128]{2,1,0:T(8,128)(2,1)} %copy-done.13), channel_id=1, source_target_pairs={{0,8},{8,16},{16,24},{24,0},{32,40},{40,48},{48,56},{56,32},{64,72... | collective-permute-start | bytes 884744 | tf_op jit(solution)/shard_map/ppermute | solution.py:28
  36.1 6.0 %copy-start.5 = (bf16[4,288,128]{2,1,0:T(8,128)(2,1)S(1)}, bf16[4,288,128]{2,1,0:T(8,128)(2,1)}, u32[]{:S(2)}) copy-start(bf16[4,288,128]{2,1,0:T(8,128)(2,1)} %copy-done.4) | copy-start | bytes 884740
  43.2 4.4 %collective-permute-start.7 = (bf16[4,288,128]{2,1,0:T(8,128)(2,1)S(1)}, bf16[4,288,128]{2,1,0:T(8,128)(2,1)S(1)}, u32[]{:S(2)}, u32[]{:S(2)}) collective-permute-start(bf16[4,288,128]{2,1,0:T(8,128)(2,1)S(1)} %get-tuple-element.57.refs_2_), channel_id=1, source_target_pairs={{0,1},{1,0},{2,3},{3,2},{4,5},{5,4},{6,7},{7,6},{8,9},{9,8},{10,11... | collective-permute-start | bytes 884744 | tf_op jit(solution)/shard_map/ppermute | solution.py:28
  43.2 8.2 %collective-permute-start.8 = (bf16[4,288,128]{2,1,0:T(8,128)(2,1)S(1)}, bf16[4,288,128]{2,1,0:T(8,128)(2,1)S(1)}, u32[]{:S(2)}, u32[]{:S(2)}) collective-permute-start(bf16[4,288,128]{2,1,0:T(8,128)(2,1)S(1)} %get-tuple-element.53.refs_3_), channel_id=1, source_target_pairs={{0,1},{1,0},{2,3},{3,2},{4,5},{5,4},{6,7},{7,6},{8,9},{9,8},{10,11... | collective-permute-start | bytes 884744 | tf_op jit(solution)/shard_map/ppermute | solution.py:28
  43.7 11.5 %collective-permute-start.9 = (bf16[4,288,128]{2,1,0:T(8,128)(2,1)S(1)}, bf16[4,288,128]{2,1,0:T(8,128)(2,1)}, u32[]{:S(2)}, u32[]{:S(2)}) collective-permute-start(bf16[4,288,128]{2,1,0:T(8,128)(2,1)S(1)} %get-tuple-element.56), channel_id=1, source_target_pairs={{0,16},{8,24},{16,0},{24,8},{32,48},{40,56},{48,32},{56,40},{64,80... | collective-permute-start | bytes 884744 | tf_op jit(solution)/shard_map/ppermute | solution.py:28
  46.7 13.2 %collective-permute-start.10 = (bf16[4,288,128]{2,1,0:T(8,128)(2,1)S(1)}, bf16[4,288,128]{2,1,0:T(8,128)(2,1)}, u32[]{:S(2)}, u32[]{:S(2)}) collective-permute-start(bf16[4,288,128]{2,1,0:T(8,128)(2,1)S(1)} %get-tuple-element.52), channel_id=1, source_target_pairs={{0,64},{8,72},{16,80},{24,88},{32,96},{40,104},{48,112},{56,120},{... | collective-permute-start | bytes 884744 | tf_op jit(solution)/shard_map/ppermute | solution.py:28
  47.5 13.1 %collective-permute-start.13 = (bf16[4,288,128]{2,1,0:T(8,128)(2,1)}, bf16[4,288,128]{2,1,0:T(8,128)(2,1)}, u32[]{:S(2)}, u32[]{:S(2)}) collective-permute-start(bf16[4,288,128]{2,1,0:T(8,128)(2,1)} %get-tuple-element.55), channel_id=1, source_target_pairs={{0,8},{8,16},{16,24},{24,0},{32,40},{40,48},{48,56},{56,32},{64,72... | collective-permute-start | bytes 884744 | tf_op jit(solution)/shard_map/ppermute | solution.py:28
  47.6 15.7 %collective-permute-start.14 = (bf16[4,288,128]{2,1,0:T(8,128)(2,1)}, bf16[4,288,128]{2,1,0:T(8,128)(2,1)}, u32[]{:S(2)}, u32[]{:S(2)}) collective-permute-start(bf16[4,288,128]{2,1,0:T(8,128)(2,1)} %get-tuple-element.51), channel_id=1, source_target_pairs={{0,32},{8,40},{16,48},{24,56},{32,64},{40,72},{48,80},{56,88},{64,... | collective-permute-start | bytes 884744 | tf_op jit(solution)/shard_map/ppermute | solution.py:28
  52.1 11.2 %collective-permute-start.17 = (bf16[4,288,128]{2,1,0:T(8,128)(2,1)S(1)}, bf16[4,288,128]{2,1,0:T(8,128)(2,1)}, u32[]{:S(2)}, u32[]{:S(2)}) collective-permute-start(bf16[4,288,128]{2,1,0:T(8,128)(2,1)S(1)} %get-tuple-element.54), channel_id=1, source_target_pairs={{0,24},{8,0},{16,8},{24,16},{32,56},{40,32},{48,40},{56,48},{64,88... | collective-permute-start | bytes 884744 | tf_op jit(solution)/shard_map/ppermute | solution.py:28
  55.3 9.6 %collective-permute-start.18 = (bf16[4,288,128]{2,1,0:T(8,128)(2,1)}, bf16[4,288,128]{2,1,0:T(8,128)(2,1)}, u32[]{:S(2)}, u32[]{:S(2)}) collective-permute-start(bf16[4,288,128]{2,1,0:T(8,128)(2,1)} %get-tuple-element.50), channel_id=1, source_target_pairs={{0,96},{8,104},{16,112},{24,120},{32,0},{40,8},{48,16},{56,24},{64... | collective-permute-start | bytes 884744 | tf_op jit(solution)/shard_map/ppermute | solution.py:28
  59.9 4.9 %collective-permute-start.11 = (bf16[4,288,128]{2,1,0:T(8,128)(2,1)}, bf16[4,288,128]{2,1,0:T(8,128)(2,1)}, u32[]{:S(2)}, u32[]{:S(2)}) collective-permute-start(bf16[4,288,128]{2,1,0:T(8,128)(2,1)} %collective-permute-done.9.refs_6_), channel_id=1, source_target_pairs={{0,1},{1,0},{2,3},{3,2},{4,5},{5,4},{6,7},{7,6},{8,9},{9,8},{10,11... | collective-permute-start | bytes 884744 | tf_op jit(solution)/shard_map/ppermute | solution.py:28
  60.6 9.7 %collective-permute-start.12 = (bf16[4,288,128]{2,1,0:T(8,128)(2,1)}, bf16[4,288,128]{2,1,0:T(8,128)(2,1)}, u32[]{:S(2)}, u32[]{:S(2)}) collective-permute-start(bf16[4,288,128]{2,1,0:T(8,128)(2,1)} %collective-permute-done.10.refs_7_), channel_id=1, source_target_pairs={{0,1},{1,0},{2,3},{3,2},{4,5},{5,4},{6,7},{7,6},{8,9},{9,8},{10,11... | collective-permute-start | bytes 884744 | tf_op jit(solution)/shard_map/ppermute | solution.py:28
  63.3 7.9 %collective-permute-start.15 = (bf16[4,288,128]{2,1,0:T(8,128)(2,1)}, bf16[4,288,128]{2,1,0:T(8,128)(2,1)}, u32[]{:S(2)}, u32[]{:S(2)}) collective-permute-start(bf16[4,288,128]{2,1,0:T(8,128)(2,1)} %collective-permute-done.13.refs_10_), channel_id=1, source_target_pairs={{0,1},{1,0},{2,3},{3,2},{4,5},{5,4},{6,7},{7,6},{8,9},{9,8},{10,11... | collective-permute-start | bytes 884744 | tf_op jit(solution)/shard_map/ppermute | solution.py:28
  63.3 8.4 %collective-permute-start.16 = (bf16[4,288,128]{2,1,0:T(8,128)(2,1)}, bf16[4,288,128]{2,1,0:T(8,128)(2,1)}, u32[]{:S(2)}, u32[]{:S(2)}) collective-permute-start(bf16[4,288,128]{2,1,0:T(8,128)(2,1)} %collective-permute-done.14.refs_11_), channel_id=1, source_target_pairs={{0,1},{1,0},{2,3},{3,2},{4,5},{5,4},{6,7},{7,6},{8,9},{9,8},{10,11... | collective-permute-start | bytes 884744 | tf_op jit(solution)/shard_map/ppermute | solution.py:28
  64.9 6.8 %collective-permute-start.19 = (bf16[4,288,128]{2,1,0:T(8,128)(2,1)}, bf16[4,288,128]{2,1,0:T(8,128)(2,1)}, u32[]{:S(2)}, u32[]{:S(2)}) collective-permute-start(bf16[4,288,128]{2,1,0:T(8,128)(2,1)} %collective-permute-done.17.refs_14_), channel_id=1, source_target_pairs={{0,1},{1,0},{2,3},{3,2},{4,5},{5,4},{6,7},{7,6},{8,9},{9,8},{10,11... | collective-permute-start | bytes 884744 | tf_op jit(solution)/shard_map/ppermute | solution.py:28
  64.9 6.8 %collective-permute-start.20 = (bf16[4,288,128]{2,1,0:T(8,128)(2,1)}, bf16[4,288,128]{2,1,0:T(8,128)(2,1)}, u32[]{:S(2)}, u32[]{:S(2)}) collective-permute-start(bf16[4,288,128]{2,1,0:T(8,128)(2,1)} %collective-permute-done.18.refs_15_), channel_id=1, source_target_pairs={{0,1},{1,0},{2,3},{3,2},{4,5},{5,4},{6,7},{7,6},{8,9},{9,8},{10,11... | collective-permute-start | bytes 884744 | tf_op jit(solution)/shard_map/ppermute | solution.py:28
  65.7 2.9 %copy-start.17 = (bf16[256,448]{0,1:T(8,128)(2,1)S(1)}, bf16[256,448]{0,1:T(8,128)(2,1)}, u32[]{:S(2)}) copy-start(bf16[256,448]{0,1:T(8,128)(2,1)} %param.23) | copy-start | bytes 688132
  66.9 2.6 %slice-start = ((bf16[16,576]{1,0:T(8,128)(2,1)}), bf16[16,64]{1,0:T(8,128)(2,1)S(1)}, s32[]{:S(2)}) async-start(bf16[16,576]{1,0:T(8,128)(2,1)} %param.16), calls=%async_computation | async-start | bytes 8192 | tf_op jit(solution)/shard_map/slice | solution.py:281
  68.7 12.3 %copy-start.7 = (f32[16,4096]{1,0:T(8,128)}, f32[16,4096]{1,0:T(8,128)S(1)}, u32[]{:S(2)}) copy-start(f32[16,4096]{1,0:T(8,128)S(1)} %reshape.172.refs_1_) | copy-start | bytes 786436
  70.3 10.7 %collective-permute-start.22 = (bf16[256,640]{1,0:T(8,128)(2,1)S(1)}, bf16[256,640]{1,0:T(8,128)(2,1)S(1)}, u32[]{:S(2)}, u32[]{:S(2)}) collective-permute-start(bf16[256,640]{1,0:T(8,128)(2,1)S(1)} %pad_maximum_fusion.2.refs_0_.q_ref), channel_id=1, source_target_pairs={{0,2},{1,3},{2,0},{3,1},{4,6},{5,7},{6,4},{7,5},{8,10},{9,11},{10,... | collective-permute-start | bytes 983048 | tf_op jit(solution)/shard_map/ppermute | solution.py:28
  71.2 15.8 %collective-permute-start.24 = (bf16[256,640]{1,0:T(8,128)(2,1)S(1)}, bf16[256,640]{1,0:T(8,128)(2,1)S(1)}, u32[]{:S(2)}, u32[]{:S(2)}) collective-permute-start(bf16[256,640]{1,0:T(8,128)(2,1)S(1)} %pad_maximum_fusion.2.refs_0_.q_ref), channel_id=1, source_target_pairs={{0,6},{1,7},{2,4},{3,5},{4,2},{5,3},{6,0},{7,1},{8,14},{9,15},{10,... | collective-permute-start | bytes 983048 | tf_op jit(solution)/shard_map/ppermute | solution.py:28
  78.0 9.0 %copy-start.12 = (bf16[4,288,128]{2,1,0:T(8,128)(2,1)S(1)}, bf16[4,288,128]{2,1,0:T(8,128)(2,1)}, u32[]{:S(2)}) copy-start(bf16[4,288,128]{2,1,0:T(8,128)(2,1)} %copy-done.10) | copy-start | bytes 884740
  78.0 21.4 %collective-permute-start.21 = (bf16[256,640]{1,0:T(8,128)(2,1)S(1)}, bf16[256,640]{1,0:T(8,128)(2,1)S(1)}, u32[]{:S(2)}, u32[]{:S(2)}) collective-permute-start(bf16[256,640]{1,0:T(8,128)(2,1)S(1)} %attend.4), channel_id=1, source_target_pairs={{0,4},{1,5},{2,6},{3,7},{4,0},{5,1},{6,2},{7,3},{8,12},{9,13},{10,... | collective-permute-start | bytes 983048 | tf_op jit(solution)/shard_map/ppermute | solution.py:28
  86.2 13.1 %collective-permute-start.23 = (bf16[256,640]{1,0:T(8,128)(2,1)S(1)}, bf16[256,640]{1,0:T(8,128)(2,1)S(1)}, u32[]{:S(2)}, u32[]{:S(2)}) collective-permute-start(bf16[256,640]{1,0:T(8,128)(2,1)S(1)} %attend.5), channel_id=1, source_target_pairs={{0,2},{1,3},{2,0},{3,1},{4,6},{5,7},{6,4},{7,5},{8,10},{9,11},{10,... | collective-permute-start | bytes 983048 | tf_op jit(solution)/shard_map/ppermute | solution.py:28
  93.2 10.0 %collective-permute-start.25 = (bf16[256,640]{1,0:T(8,128)(2,1)S(1)}, bf16[256,640]{1,0:T(8,128)(2,1)S(1)}, u32[]{:S(2)}, u32[]{:S(2)}) collective-permute-start(bf16[256,640]{1,0:T(8,128)(2,1)S(1)} %attend.6), channel_id=1, source_target_pairs={{0,6},{1,7},{2,4},{3,5},{4,2},{5,3},{6,0},{7,1},{8,14},{9,15},{10,... | collective-permute-start | bytes 983048 | tf_op jit(solution)/shard_map/ppermute | solution.py:28
  94.0 9.2 %copy-start.1 = (bf16[16,512,128]{2,1,0:T(8,128)(2,1)S(1)}, bf16[16,512,128]{2,1,0:T(8,128)(2,1)}, u32[]{:S(2)}) copy-start(bf16[16,512,128]{2,1,0:T(8,128)(2,1)} %up_ref.1) | copy-start | bytes 6291460
  103.8 6.3 %collective-permute-start.26 = (bf16[16,2048]{1,0:T(8,128)(2,1)S(1)}, bf16[16,2048]{1,0:T(8,128)(2,1)S(1)}, u32[]{:S(2)}, u32[]{:S(2)}) collective-permute-start(bf16[16,2048]{1,0:T(8,128)(2,1)S(1)} %merge.1), channel_id=1, source_target_pairs={{0,96},{8,104},{16,112},{24,120},{32,0},{40,8},{48,16},{56,24},{64... | collective-permute-start | bytes 196616 | tf_op jit(solution)/shard_map/ppermute | solution.py:28
  107.6 5.9 %collective-permute-start.27 = (bf16[16,2048]{1,0:T(8,128)(2,1)S(1)}, bf16[16,2048]{1,0:T(8,128)(2,1)S(1)}, u32[]{:S(2)}, u32[]{:S(2)}) collective-permute-start(bf16[16,2048]{1,0:T(8,128)(2,1)S(1)} %merge.1), channel_id=1, source_target_pairs={{0,64},{8,72},{16,80},{24,88},{32,96},{40,104},{48,112},{56,120},{... | collective-permute-start | bytes 196616 | tf_op jit(solution)/shard_map/ppermute | solution.py:28
  107.6 6.2 %collective-permute-start.28 = (bf16[16,2048]{1,0:T(8,128)(2,1)S(1)}, bf16[16,2048]{1,0:T(8,128)(2,1)S(1)}, u32[]{:S(2)}, u32[]{:S(2)}) collective-permute-start(bf16[16,2048]{1,0:T(8,128)(2,1)S(1)} %merge.1), channel_id=1, source_target_pairs={{0,32},{8,40},{16,48},{24,56},{32,64},{40,72},{48,80},{56,88},{64,... | collective-permute-start | bytes 196616 | tf_op jit(solution)/shard_map/ppermute | solution.py:28
  113.8 7.6 %collective-permute-start.29 = (bf16[64,2048]{1,0:T(8,128)(2,1)S(1)}, bf16[64,2048]{1,0:T(8,128)(2,1)S(1)}, u32[]{:S(2)}, u32[]{:S(2)}) collective-permute-start(bf16[64,2048]{1,0:T(8,128)(2,1)S(1)} %pad_maximum_fusion.4), channel_id=1, source_target_pairs={{0,24},{8,0},{16,8},{24,16},{32,56},{40,32},{48,40},{56,48},{64,88... | collective-permute-start | bytes 786440 | tf_op jit(solution)/shard_map/ppermute | solution.py:28
  114.8 8.9 %collective-permute-start.30 = (bf16[64,2048]{1,0:T(8,128)(2,1)S(1)}, bf16[64,2048]{1,0:T(8,128)(2,1)S(1)}, u32[]{:S(2)}, u32[]{:S(2)}) collective-permute-start(bf16[64,2048]{1,0:T(8,128)(2,1)S(1)} %pad_maximum_fusion.4), channel_id=1, source_target_pairs={{0,16},{8,24},{16,0},{24,8},{32,48},{40,56},{48,32},{56,40},{64,80... | collective-permute-start | bytes 786440 | tf_op jit(solution)/shard_map/ppermute | solution.py:28
  116.8 9.5 %collective-permute-start.31 = (bf16[64,2048]{1,0:T(8,128)(2,1)S(1)}, bf16[64,2048]{1,0:T(8,128)(2,1)S(1)}, u32[]{:S(2)}, u32[]{:S(2)}) collective-permute-start(bf16[64,2048]{1,0:T(8,128)(2,1)S(1)} %pad_maximum_fusion.4), channel_id=1, source_target_pairs={{0,8},{8,16},{16,24},{24,0},{32,40},{40,48},{48,56},{56,32},{64,72... | collective-permute-start | bytes 786440 | tf_op jit(solution)/shard_map/ppermute | solution.py:28
  126.4 14.0 %copy-start.3 = (bf16[448,2304]{1,0:T(8,128)(2,1)S(1)}, bf16[448,2304]{1,0:T(8,128)(2,1)}, u32[]{:S(2)}) copy-start(bf16[448,2304]{1,0:T(8,128)(2,1)} %wu_ref.1) | copy-start | bytes 6193156
  127.2 1.4 collective-permute-start.32
  127.4 11.6 %copy-start.20 = (bf16[448]{0:T(512)(128)(2,1)S(1)}, bf16[448]{0:T(512)(128)(2,1)}, u32[]{:S(2)}) copy-start(bf16[448]{0:T(512)(128)(2,1)} %param.24) | copy-start | bytes 2692
  127.4 13.0 %copy-start.2 = (bf16[448,2304]{1,0:T(8,128)(2,1)S(1)}, bf16[448,2304]{1,0:T(8,128)(2,1)}, u32[]{:S(2)}) copy-start(bf16[448,2304]{1,0:T(8,128)(2,1)} %wg_ref.1) | copy-start | bytes 6193156
  128.6 9.6 %collective-permute-start.35 = (bf16[128,448]{1,0:T(8,128)(2,1)S(1)}, bf16[128,448]{1,0:T(8,128)(2,1)S(1)}, u32[]{:S(2)}, u32[]{:S(2)}) collective-permute-start(bf16[128,448]{1,0:T(8,128)(2,1)S(1)} %add_convert_fusion.2), channel_id=1, source_target_pairs={{0,6},{1,7},{2,4},{3,5},{4,2},{5,3},{6,0},{7,1},{8,14},{9,15},{10,... | collective-permute-start | bytes 344072 | tf_op jit(solution)/shard_map/ppermute | solution.py:28
  129.7 8.5 %collective-permute-start.34 = (bf16[128,448]{1,0:T(8,128)(2,1)S(1)}, bf16[128,448]{1,0:T(8,128)(2,1)S(1)}, u32[]{:S(2)}, u32[]{:S(2)}) collective-permute-start(bf16[128,448]{1,0:T(8,128)(2,1)S(1)} %add_convert_fusion.2), channel_id=1, source_target_pairs={{0,4},{1,5},{2,6},{3,7},{4,0},{5,1},{6,2},{7,3},{8,12},{9,13},{10,... | collective-permute-start | bytes 344072 | tf_op jit(solution)/shard_map/ppermute | solution.py:28
  130.9 8.0 %collective-permute-start.33 = (bf16[128,448]{1,0:T(8,128)(2,1)S(1)}, bf16[128,448]{1,0:T(8,128)(2,1)S(1)}, u32[]{:S(2)}, u32[]{:S(2)}) collective-permute-start(bf16[128,448]{1,0:T(8,128)(2,1)S(1)} %add_convert_fusion.2), channel_id=1, source_target_pairs={{0,2},{1,3},{2,0},{3,1},{4,6},{5,7},{6,4},{7,5},{8,10},{9,11},{10,... | collective-permute-start | bytes 344072 | tf_op jit(solution)/shard_map/ppermute | solution.py:28
  139.0 1.4 collective-permute-start.36
  143.5 10.2 %collective-permute-start.45 = (bf16[4,16,2304]{2,1,0:T(8,128)(2,1)}, bf16[4,16,2304]{2,1,0:T(8,128)(2,1)}, u32[]{:S(2)}, u32[]{:S(2)}) collective-permute-start(bf16[4,16,2304]{2,1,0:T(8,128)(2,1)} %get-tuple-element.39), channel_id=1, source_target_pairs={{0,24},{8,0},{16,8},{24,16},{32,56},{40,32},{48,40},{56,48},{64,88... | collective-permute-start | bytes 884744 | tf_op jit(solution)/shard_map/ppermute | solution.py:28
  144.1 11.4 %collective-permute-start.44 = (bf16[4,16,2304]{2,1,0:T(8,128)(2,1)}, bf16[4,16,2304]{2,1,0:T(8,128)(2,1)}, u32[]{:S(2)}, u32[]{:S(2)}) collective-permute-start(bf16[4,16,2304]{2,1,0:T(8,128)(2,1)} %get-tuple-element.38), channel_id=1, source_target_pairs={{0,8},{8,16},{16,24},{24,0},{32,40},{40,48},{48,56},{56,32},{64,72... | collective-permute-start | bytes 884744 | tf_op jit(solution)/shard_map/ppermute | solution.py:28
  145.5 15.2 %collective-permute-start.43 = (bf16[4,16,2304]{2,1,0:T(8,128)(2,1)}, bf16[4,16,2304]{2,1,0:T(8,128)(2,1)}, u32[]{:S(2)}, u32[]{:S(2)}) collective-permute-start(bf16[4,16,2304]{2,1,0:T(8,128)(2,1)} %get-tuple-element.37), channel_id=1, source_target_pairs={{0,16},{8,24},{16,0},{24,8},{32,48},{40,56},{48,32},{56,40},{64,80... | collective-permute-start | bytes 884744 | tf_op jit(solution)/shard_map/ppermute | solution.py:28
  147.3 17.5 %collective-permute-start.39 = (bf16[4,16,2432]{2,1,0:T(8,128)(2,1)}, bf16[4,16,2432]{2,1,0:T(8,128)(2,1)S(1)}, u32[]{:S(2)}, u32[]{:S(2)}) collective-permute-start(bf16[4,16,2432]{2,1,0:T(8,128)(2,1)} %copy-done.9), channel_id=1, source_target_pairs={{0,96},{8,104},{16,112},{24,120},{32,0},{40,8},{48,16},{56,24},{64... | collective-permute-start | bytes 933896 | tf_op jit(solution)/shard_map/ppermute | solution.py:28
  148.1 16.7 %collective-permute-start.38 = (bf16[4,16,2432]{2,1,0:T(8,128)(2,1)S(1)}, bf16[4,16,2432]{2,1,0:T(8,128)(2,1)S(1)}, u32[]{:S(2)}, u32[]{:S(2)}) collective-permute-start(bf16[4,16,2432]{2,1,0:T(8,128)(2,1)S(1)} %get-tuple-element.32), channel_id=1, source_target_pairs={{0,32},{8,40},{16,48},{24,56},{32,64},{40,72},{48,80},{56,88},{64,... | collective-permute-start | bytes 933896 | tf_op jit(solution)/shard_map/ppermute | solution.py:28
  153.7 11.1 %collective-permute-start.37 = (bf16[4,16,2432]{2,1,0:T(8,128)(2,1)S(1)}, bf16[4,16,2432]{2,1,0:T(8,128)(2,1)S(1)}, u32[]{:S(2)}, u32[]{:S(2)}) collective-permute-start(bf16[4,16,2432]{2,1,0:T(8,128)(2,1)S(1)} %get-tuple-element.31), channel_id=1, source_target_pairs={{0,64},{8,72},{16,80},{24,88},{32,96},{40,104},{48,112},{56,120},{... | collective-permute-start | bytes 933896 | tf_op jit(solution)/shard_map/ppermute | solution.py:28
  162.0 2.8 %copy-start.15 = (bf16[4,16,2304]{2,1,0:T(8,128)(2,1)}, bf16[4,16,2304]{2,1,0:T(8,128)(2,1)S(1)}, u32[]{:S(2)}) copy-start(bf16[4,16,2304]{2,1,0:T(8,128)(2,1)S(1)} %add_convert_fusion) | copy-start | bytes 884740
  162.8 10.8 %collective-permute-start.48 = (bf16[16,2304]{1,0:T(8,128)(2,1)}, bf16[16,2304]{1,0:T(8,128)(2,1)S(1)}, u32[]{:S(2)}, u32[]{:S(2)}) collective-permute-start(bf16[16,2304]{1,0:T(8,128)(2,1)} %get-tuple-element.62), channel_id=1, source_target_pairs={{0,96},{8,104},{16,112},{24,120},{32,0},{40,8},{48,16},{56,24},{64... | collective-permute-start | bytes 221192 | tf_op jit(solution)/shard_map/ppermute | solution.py:28
  163.6 9.9 %collective-permute-start.47 = (bf16[16,2304]{1,0:T(8,128)(2,1)S(1)}, bf16[16,2304]{1,0:T(8,128)(2,1)S(1)}, u32[]{:S(2)}, u32[]{:S(2)}) collective-permute-start(bf16[16,2304]{1,0:T(8,128)(2,1)S(1)} %get-tuple-element.63), channel_id=1, source_target_pairs={{0,32},{8,40},{16,48},{24,56},{32,64},{40,72},{48,80},{56,88},{64,... | collective-permute-start | bytes 221192 | tf_op jit(solution)/shard_map/ppermute | solution.py:28
  165.3 5.0 %collective-permute-start.42 = (bf16[16,2432]{1,0:T(8,128)(2,1)S(1)}, bf16[16,2432]{1,0:T(8,128)(2,1)S(1)}, u32[]{:S(2)}, u32[]{:S(2)}) collective-permute-start(bf16[16,2432]{1,0:T(8,128)(2,1)S(1)} %get-tuple-element.59), channel_id=1, source_target_pairs={{0,24},{8,0},{16,8},{24,16},{32,56},{40,32},{48,40},{56,48},{64,88... | collective-permute-start | bytes 233480 | tf_op jit(solution)/shard_map/ppermute | solution.py:28
  166.5 5.6 %collective-permute-start.41 = (bf16[16,2432]{1,0:T(8,128)(2,1)S(1)}, bf16[16,2432]{1,0:T(8,128)(2,1)S(1)}, u32[]{:S(2)}, u32[]{:S(2)}) collective-permute-start(bf16[16,2432]{1,0:T(8,128)(2,1)S(1)} %get-tuple-element.60), channel_id=1, source_target_pairs={{0,8},{8,16},{16,24},{24,0},{32,40},{40,48},{48,56},{56,32},{64,72... | collective-permute-start | bytes 233480 | tf_op jit(solution)/shard_map/ppermute | solution.py:28
  167.4 5.9 %collective-permute-start.40 = (bf16[16,2432]{1,0:T(8,128)(2,1)S(1)}, bf16[16,2432]{1,0:T(8,128)(2,1)S(1)}, u32[]{:S(2)}, u32[]{:S(2)}) collective-permute-start(bf16[16,2432]{1,0:T(8,128)(2,1)S(1)} %get-tuple-element.58), channel_id=1, source_target_pairs={{0,16},{8,24},{16,0},{24,8},{32,48},{40,56},{48,32},{56,40},{64,80... | collective-permute-start | bytes 233480 | tf_op jit(solution)/shard_map/ppermute | solution.py:28
  170.3 5.9 %collective-permute-start.46 = (bf16[16,2304]{1,0:T(8,128)(2,1)S(1)}, bf16[16,2304]{1,0:T(8,128)(2,1)S(1)}, u32[]{:S(2)}, u32[]{:S(2)}) collective-permute-start(bf16[16,2304]{1,0:T(8,128)(2,1)S(1)} %get-tuple-element.61), channel_id=1, source_target_pairs={{0,64},{8,72},{16,80},{24,88},{32,96},{40,104},{48,112},{56,120},{... | collective-permute-start | bytes 221192 | tf_op jit(solution)/shard_map/ppermute | solution.py:28
  (9 other events, 7.1 us)

commit v3 on v2

v3 whole, which is shorter than its diff:
```python
import functools
import math

import jax
import jax.numpy as jnp
from jax import lax
from jax.experimental import pallas as pl
from jax.experimental.pallas import tpu as pltpu
from jax.sharding import PartitionSpec as P

D = 7168
LAT = 512
ROPE = 64
QK_NOPE = 128
CAP = 2
PB = 512
BS = 64
KV = LAT + ROPE
EPSILON = 1e-06
FF = 2304
SCALE = 1.0 / math.sqrt(QK_NOPE + ROPE)
SCALE2 = SCALE / math.log(2.0)
NEG = -1e30
f32 = jnp.float32
bf16 = jnp.bfloat16


def send(x, axis, to, n):
    return lax.ppermute(x, axis, [(i, to(i)) for i in range(n)])


def swap_core(x):
    return send(x, "tp", lambda i: i ^ 1, 8)


def send_y(x, k):
    return send(x, "tp", lambda i: i ^ (2 * k), 8)


def send_dp(x, stage, k):
    pairs = []
    for i in range(128):
        dp, tp = i // 8, i % 8
        if tp % 2 == stage:
            to = ((dp // 4 + k) % 4) * 4 + dp % 4
        else:
            to = (dp // 4) * 4 + (dp % 4 + k) % 4
        pairs.append((i, to * 8 + tp))
    return lax.ppermute(x, ("dp", "tp"), pairs)


VMEM = pl.BlockSpec(memory_space=pltpu.VMEM)
SMEM = pl.BlockSpec(memory_space=pltpu.SMEM)


def call(kernel, name, outs, ins, scalars=0, limit=20, **kw):
    return pl.pallas_call(
        kernel,
        out_shape=outs,
        in_specs=[SMEM] * scalars + [VMEM] * (len(ins) - scalars),
        out_specs=[VMEM] * len(outs),
        compiler_params=pltpu.CompilerParams(vmem_limit_bytes=limit * 1024 * 1024),
        name=name,
        **kw,
    )(*ins)


def shape(*dims, dtype=bf16):
    return jax.ShapeDtypeStruct(dims, dtype)


def place_of(where, ka, kb):
    px, pz, core = where[0], where[1], where[2]
    kx = jnp.where(core == 0, ka, kb)
    kz = jnp.where(core == 0, kb, ka)
    return ((px + kx) % 4) * 4 + (pz + kz) % 4


def fetch_kernel(where, picks, tokens, *outs):
    for ka in range(4):
        for kb in range(4):
            dest = place_of(where, ka, kb)
            for rank in range(CAP):
                pick = picks[dest * CAP + rank]
                out = outs[ka]
                at = kb * CAP + rank
                for c in range(4):
                    out[at, c * BS : (c + 1) * BS, :] = tokens[pick, :, c * 128 : (c + 1) * 128]
                rope = tokens[pick, :, LAT:KV]
                out[at, 4 * BS :, :] = jnp.concatenate([rope[:32], rope[32:]], axis=1)


def regroup_kernel(*refs):
    for ka in range(4):
        for kb in range(4):
            refs[4 + kb][ka * CAP : (ka + 1) * CAP] = refs[ka][kb * CAP : (kb + 1) * CAP]


def half_latent(refs, half):
    rows = []
    for ref in refs:
        parts = [
            ref[:, c * BS + half * 32 : c * BS + half * 32 + 32, :].reshape(-1, 128)
            for c in range(4)
        ]
        rows.append(jnp.concatenate(parts, axis=1))
    return jnp.concatenate(rows, axis=0)


def half_rope(refs, half):
    rope = jnp.concatenate(
        [ref[:, 4 * BS : 4 * BS + 32, :].reshape(-1, 128) for ref in refs], axis=0
    )
    lane = lax.broadcasted_iota(jnp.int32, rope.shape, 1)
    keep = (lane < ROPE) if half == 0 else (lane >= ROPE)
    return jnp.where(keep, rope, jnp.zeros_like(rope))


def attend_kernel(groups, resume, last, *refs):
    index, q_ref, bias_ref = refs[:3]
    pieces = refs[3 : 3 + 2 * groups]
    refs = refs[3 + 2 * groups :]
    if resume:
        acc_in, stat_in = refs[0], refs[1]
        refs = refs[2:]
    q = q_ref[index[0]]
    m_rows = q.shape[0]

    def values(g):
        mine = pieces[2 * g : 2 * g + 2]
        return jnp.concatenate([half_latent(mine, 0), half_latent(mine, 1)], axis=0)

    def scores(g):
        mine = pieces[2 * g : 2 * g + 2]
        ropes = jnp.concatenate([half_rope(mine, 0), half_rope(mine, 1)], axis=0)
        keys = jnp.concatenate([values(g), ropes], axis=1)
        s = lax.dot_general(q, keys, (((1,), (1,)), ((), ())), preferred_element_type=f32)
        n = s.shape[1]
        s = s.reshape(m_rows // 16, 16, n) + bias_ref[:, g * n : (g + 1) * n][None]
        return s.reshape(m_rows, n)

    top = total = acc = None
    if resume:
        top, total, acc = stat_in[:, 0:1], stat_in[:, 64:65], acc_in[...]
    s = scores(0)
    for g in range(groups):
        ahead = scores(g + 1) if g + 1 < groups else None
        high = jnp.max(s, axis=1, keepdims=True)
        new = high if top is None else jnp.maximum(top, high)
        p = jnp.exp2((s - new) * SCALE2)
        part = jnp.sum(p, axis=1, keepdims=True)
        o = jnp.dot(p.astype(bf16), values(g), preferred_element_type=f32)
        if top is None:
            acc, total = o, part
        else:
            fade = jnp.exp2((top - new) * SCALE2)
            acc, total = acc * fade + o, total * fade + part
        top, s = new, ahead
    lane = lax.broadcasted_iota(jnp.int32, (m_rows, 128), 1)
    if not last:
        refs[0][...] = acc
        refs[1][...] = jnp.where(lane < 64, top, total)
        return
    out_ref = refs[0]
    out_ref[:, :LAT] = (acc / total).astype(bf16)
    lse = top * SCALE + jnp.log(total)
    hi = lse.astype(bf16).astype(f32)
    mid = (lse - hi).astype(bf16).astype(f32)
    low = lse - hi - mid
    stats = jnp.where(lane == 0, hi, jnp.where(lane == 1, mid, jnp.where(lane == 2, low, 0.0)))
    out_ref[:, LAT:] = stats.astype(bf16)


def attend(index, q, bias, pieces, carry=(), last=True):
    m_rows = q.shape[1]
    groups = len(pieces) // 2
    if last:
        outs = [shape(m_rows, LAT + 128)]
    else:
        outs = [shape(m_rows, LAT, dtype=f32), shape(m_rows, 128, dtype=f32)]
    cost = pl.CostEstimate(
        flops=2 * m_rows * groups * 1024 * (768 + 512) * 2,
        bytes_accessed=groups * 16 * 288 * 128 * 2,
        transcendentals=m_rows * groups * 1024,
    )
    return call(
        functools.partial(attend_kernel, groups, bool(carry), last),
        "attend",
        outs,
        [index, q, bias, *pieces, *carry],
        scalars=1,
        cost_estimate=cost,
    )


def merge_kernel(o0, o1, o2, o3, q_ref, own_ref, up_ref, out_ref):
    heads, rows = 16, 16
    own = own_ref[...].astype(f32)
    q = q_ref[...].astype(f32).reshape(heads, rows, 640)
    lane = lax.broadcasted_iota(jnp.int32, (rows, 640), 1)
    key = jnp.where(lane < KV, own, 0.0)
    s_own = jnp.sum(q * key[None], axis=2, keepdims=True).reshape(heads * rows, 1) * SCALE
    lses = []
    for o in (o0, o1, o2, o3):
        lses.append(jnp.sum(o[:, LAT:].astype(f32), axis=1, keepdims=True))
    top = s_own
    for v in lses:
        top = jnp.maximum(top, v)
    e_own = jnp.exp(s_own - top)
    es = [jnp.exp(v - top) for v in lses]
    den = e_own + ((es[0] + es[1]) + (es[2] + es[3]))
    mix = (e_own / den).reshape(heads, rows, 1) * own[None, :, :LAT]
    mix = mix.reshape(heads * rows, LAT)
    for o, e in zip((o0, o1, o2, o3), es):
        mix = mix + (e / den) * o[:, :LAT].astype(f32)
    mix = mix.astype(bf16)
    for h in range(heads):
        out_ref[:, h * 128 : (h + 1) * 128] = jnp.dot(
            mix[h * rows : (h + 1) * rows], up_ref[h], preferred_element_type=f32
        ).astype(bf16)


def merge(parts, q, own, value_up):
    return pl.pallas_call(
        merge_kernel,
        out_shape=jax.ShapeDtypeStruct((16, 2048), bf16),
        in_specs=[pl.BlockSpec(memory_space=pltpu.VMEM)] * 7,
        out_specs=pl.BlockSpec(memory_space=pltpu.VMEM),
        compiler_params=pltpu.CompilerParams(vmem_limit_bytes=24 * 1024 * 1024),
        name="merge",
    )(*parts, q, own, value_up)


def project_kernel(where, p0, p1, p2, p3, weight, keep_ref, give_ref):
    core = where[2]
    rows = jnp.concatenate([p0[...], p1[...], p2[...], p3[...]], axis=0)
    full = lax.dot_general(
        rows, weight[...], (((1,), (1,)), ((), ())), preferred_element_type=f32
    ).reshape(4, 4, 16, 448)

    @pl.when(core == 0)
    def _():
        keep_ref[...] = full[:2]
        give_ref[...] = full[2:].astype(bf16)

    @pl.when(core == 1)
    def _():
        for i in range(2):
            keep_ref[i] = full[:, 2 + i]
            give_ref[i] = full[:, i].astype(bf16)


def join_kernel(where, pair, t1, t2, t3, residual, out):
    px, pz, core = where[0], where[1], where[2]
    for i in range(2):
        for kx in range(4):
            kz = core * 2 + i
            dp = ((px + kx) % 4) * 4 + (pz + kz) % 4
            attn = (pair[i, kx].astype(f32) + t1[i, kx].astype(f32)) + (
                t2[i, kx].astype(f32) + t3[i, kx].astype(f32)
            )
            out[i, kx] = (residual[dp].astype(f32) + attn).astype(bf16)


def ffn_kernel(where, half_ref, other_ref, gain_ref, wg_ref, wu_ref, stream_ref, *outs):
    px, pz, core = where[0], where[1], where[2]
    half, other = half_ref[...].astype(f32), other_ref[...].astype(f32)
    rows = jnp.concatenate(
        [jnp.where(core == 0, half, other), jnp.where(core == 0, other, half)], axis=0
    )
    for kz in range(4):
        for kx in range(4):
            stream_ref[((px + kx) % 4) * 4 + (pz + kz) % 4] = rows[kz, kx].astype(bf16)
    turned = jnp.stack([rows[:, k] for k in range(4)], axis=0)
    wide = jnp.where(core == 0, rows, turned).reshape(256, 448)
    squares = jnp.sum(wide * wide, axis=1, keepdims=True)
    hi = squares.astype(bf16).astype(f32)
    lane = lax.broadcasted_iota(jnp.int32, (256, 128), 1)
    tail = jnp.where(lane == 0, hi, jnp.where(lane == 1, squares - hi, 0.0)).astype(bf16)
    scaled = (wide * gain_ref[...].astype(f32)).astype(bf16)
    gate = jnp.dot(scaled, wg_ref[...], preferred_element_type=f32).astype(bf16)
    gate = gate.reshape(4, 4, 16, FF)
    tail = tail.reshape(4, 4, 16, 128)
    for k in range(4):
        outs[k][:, :, :FF] = gate[:, k]
        outs[k][:, :, 2 * FF :] = tail[:, k]
    up = jnp.dot(scaled, wu_ref[...], preferred_element_type=f32).astype(bf16)
    up = up.reshape(4, 4, 16, FF)
    for k in range(4):
        outs[k][:, :, FF : 2 * FF] = up[:, k]


def sum4(refs, at):
    a, b, c, d = (ref[at].astype(f32) for ref in refs)
    return (a + b) + (c + d)


def fold_kernel(*refs):
    for kb in range(4):
        s = sum4(refs[:4], kb)
        refs[4 + kb][:, : 2 * FF] = s[:, : 2 * FF].astype(bf16)
        squares = jnp.sum(s[:, 2 * FF :], axis=1, keepdims=True)
        hi = squares.astype(bf16).astype(f32)
        lane = lax.broadcasted_iota(jnp.int32, (16, 128), 1)
        tail = jnp.where(lane == 0, hi, jnp.where(lane == 1, squares - hi, 0.0))
        refs[4 + kb][:, 2 * FF :] = tail.astype(bf16)


def finish_kernel(r0, r1, r2, r3, out):
    s = sum4((r0, r1, r2, r3), ...)
    squares = jnp.sum(s[:, 2 * FF :], axis=1, keepdims=True)
    inverse = lax.rsqrt(squares / D + EPSILON)
    gate = s[:, :FF] * inverse
    up = s[:, FF : 2 * FF] * inverse
    out[...] = (gate / (1.0 + jnp.exp(-gate)) * up).astype(bf16)


def local(
    queries,
    own_latent,
    prefix_cache,
    block_home,
    row_prompt,
    chosen,
    value_up,
    out_weight,
    residual,
    norm_gain,
    gate_weight,
    up_weight,
):
    replica = lax.axis_index("dp")
    lane = lax.axis_index("tp")
    px, pz = replica // 4, replica % 4
    core = lane % 2
    me = replica * 8 + lane
    i32 = jnp.int32
    where = jnp.stack([px, pz, core]).astype(i32)

    q = queries.reshape(16, 16, KV).transpose(1, 0, 2).reshape(256, KV)
    q = jnp.concatenate([q, q[:, LAT:]], axis=1)
    own = jnp.concatenate([own_latent, own_latent[:, LAT:]], axis=1)
    chips = [[c + 2 * y for y in range(4)] for c in range(2)]
    q_all = lax.all_gather(q, "tp", axis_index_groups=chips)

    slots = me * 16 + jnp.arange(16, dtype=i32)
    ids = jnp.arange(2048, dtype=i32)
    held = jnp.sum(jnp.where(block_home[None, :] == slots[:, None], ids[None, :], 0), axis=1)
    wanted = (row_prompt[:, None] * PB + chosen).reshape(16, 512)
    needed = jnp.any(wanted[:, None, :] == held[None, :, None], axis=2)
    offs = jnp.arange(16, dtype=i32)
    before = jnp.sum(
        jnp.where(needed[:, None, :] & (offs[None, :] < offs[:, None])[None], 1, 0), axis=2
    )
    places = jnp.arange(CAP, dtype=i32)
    picks = jnp.sum(
        jnp.where(needed[:, None, :] & (before[:, None, :] == places[None, :, None]), offs, 0),
        axis=2,
    )
    sent = call(
        fetch_kernel,
        "fetch",
        [shape(8, 288, 128)] * 4,
        [where, picks.reshape(-1), prefix_cache.reshape(16, BS, KV)],
        scalars=2,
    )
    got = [sent[0]] + [send_dp(sent[k], 0, k) for k in (1, 2, 3)]
    groups = call(regroup_kernel, "regroup", [shape(8, 288, 128)] * 4, got)
    arrived = {0: groups[0]}
    for k in (2, 1, 3):
        arrived[k] = send_dp(groups[k], 1, k)
    pieces = []
    for k in (0, 2, 1, 3):
        pieces += [arrived[k], swap_core(arrived[k])]

    prompt = lax.dynamic_slice_in_dim(row_prompt, replica * 16, 1, 0)[0]
    home = lax.dynamic_slice_in_dim(block_home, prompt * PB, PB, 0)
    my_chosen = lax.dynamic_slice_in_dim(chosen, replica * 16, 16, 0)
    sel = jnp.any(my_chosen[:, :, None] == jnp.arange(PB, dtype=i32)[None, None, :], axis=1)
    need = jnp.any(sel, axis=0)
    holder = home // 16
    rank = jnp.sum(
        jnp.where(
            need[None, :] & (holder[None, :] == holder[:, None]) & (home[None, :] < home[:, None]),
            1,
            0,
        ),
        axis=1,
    )
    kb = jnp.array([0, 2, 1, 3], i32)[:, None, None, None]
    from_core = core ^ jnp.array([0, 1], i32)[None, :, None, None]
    ka = jnp.arange(4, dtype=i32)[None, None, :, None]
    place = jnp.array([0, 1], i32)[None, None, None, :]
    kx = jnp.where(from_core == 0, ka, kb)
    kz = jnp.where(from_core == 0, kb, ka)
    dev = (((px - kx) % 4) * 4 + (pz - kz) % 4) * 8 + (lane - core + from_core)
    want_key = (dev * 2 + place).reshape(64)
    key = jnp.where(need, holder * 2 + rank, -1)
    hit = key[:, None] == want_key[None, :]
    use = jnp.dot(sel.astype(bf16), hit.astype(bf16), preferred_element_type=f32).astype(bf16)
    token = jnp.arange(4096, dtype=i32)
    slot_of = (token // 1024) * 16 + (token // 32) % 16
    spread = (jnp.arange(64, dtype=i32)[:, None] == slot_of[None, :]).astype(bf16)
    bias = (jnp.dot(use, spread, preferred_element_type=f32) - 1.0) * -NEG

    y = lane // 2
    parts = []
    for k in (2, 1, 3, 0):
        (o,) = attend((y ^ k).reshape(1), q_all, bias, pieces)
        parts.append(send_y(o, k) if k else o)
    per_head = merge(parts, q, own, value_up)

    near = [per_head] + [send_dp(per_head, 0, 4 - k) for k in (1, 2, 3)]
    near = jnp.concatenate(near, axis=0)
    far = [near] + [send_dp(near, 1, 4 - k) for k in (1, 2, 3)]
    keep, give = call(
        project_kernel,
        "project",
        [shape(2, 4, 16, 448, dtype=f32), shape(2, 4, 16, 448)],
        [where, *far, out_weight.T],
        scalars=1,
    )
    pair = (keep + swap_core(give).astype(f32)).astype(bf16)
    terms = [send_y(pair, k) for k in (1, 2, 3)]
    (half,) = call(
        join_kernel,
        "join",
        [shape(2, 4, 16, 448)],
        [where, pair, *terms, residual.reshape(16, 16, 448)],
        scalars=1,
    )
    other = swap_core(half)
    stream, *sums = call(
        ffn_kernel,
        "ffn",
        [shape(16, 16, 448)] + [shape(4, 16, 2 * FF + 128)] * 4,
        [where, half, other, norm_gain.reshape(1, 448), gate_weight, up_weight],
        scalars=1,
        limit=30,
    )
    got = [sums[0]] + [send_dp(sums[k], 0, k) for k in (2, 1, 3)]
    sums = call(fold_kernel, "fold", [shape(16, 2 * FF + 128)] * 4, got)
    got = [sums[0]] + [send_dp(sums[k], 1, k) for k in (2, 1, 3)]
    (hidden,) = call(finish_kernel, "finish", [shape(16, FF)], got)
    return (stream.reshape(256, 448), hidden)


def solution(mesh):
    placed = (
        P("dp", "tp"),
        P("dp", None),
        P(("dp", "tp"), None),
        P(),
        P(),
        P(),
        P("tp", None, None),
        P("tp", "dp"),
        P(None, "dp"),
        P("dp"),
        P("dp", "tp"),
        P("dp", "tp"),
    )
    return jax.shard_map(
        local, mesh=mesh, in_specs=placed, out_specs=(P(None, "dp"), P("dp", "tp")), check_vma=False
    )
```

time: 178 us -> 167 us (0.938)
  starting transfers between devices: 66.8 us -> 41.1 us
  waiting for transfers between devices: 54.5 us -> 69 us
  between operations: 1.91 us -> 15.2 us
  local copies, waits for them, and re-layouts: 18.9 us -> 9.21 us
  other arithmetic: 8.67 us -> 3.27 us
    ppermute x49 -> x12, starting transfers between devices: 66.8 us -> 10.3 us  [send(): return lax.ppermute(x, axis, [(i, to(i)) for i in range(n)])]
    ppermute x0 -> x18, waiting for transfers between devices: none -> 52.8 us  [send_dp(): return lax.ppermute(x, ('dp', 'tp'), pairs)]
    ppermute x49 -> x12, waiting for transfers between devices: 54.5 us -> 16.2 us  [send(): return lax.ppermute(x, axis, [(i, to(i)) for i in range(n)])]
    ppermute x0 -> x18, starting transfers between devices: none -> 30.7 us  [send_dp(): return lax.ppermute(x, ('dp', 'tp'), pairs)]
    unnamed x55 -> x34, local copies, waits for them, and re-layouts: 8.07 us -> 4.86 us
    convert_element_type x4 -> x1, other arithmetic: 3.04 us -> 0.03 us  [local(): pair = (keep + swap_core(give).astype(f32)).astype(bf16)]
    reshape x3 -> x2, local copies, waits for them, and re-layouts: 4.47 us -> 1.73 us  [the longest x1 1.64 us: local(): prefix_cache.reshape(16, BS, KV)]
    squeeze x4 -> x0, local copies, waits for them, and re-layouts: 2.45 us -> none  [the longest x1 0.94 us: local(): b_in[k] = send_x(b_next[k], k)]
  transfers between devices with their start and end apart: 49 -> 31, of which waited for: 23 -> 22; matrix products, arithmetic and copies ran while one was open for 10% -> 5% of each run, Pallas kernels for 13% -> 10%
where the time goes in v3:
time: 167 us
  waiting for transfers between devices  69 us (41%)
  starting transfers between devices  41.1 us (25%)
  Pallas kernels  27.6 us (17%)
  between operations  15.2 us (9%)
  local copies, waits for them, and re-layouts  9.21 us (6%)
  other arithmetic  3.27 us (2%)
    ppermute x18, waiting for transfers between devices, send_dp(): return lax.ppermute(x, ('dp', 'tp'), pairs)  52.8 us
    ppermute x18, starting transfers between devices, send_dp(): return lax.ppermute(x, ('dp', 'tp'), pairs)  30.7 us
    pallas_call x11, Pallas kernels, call(): pl.pallas_call(kernel, out_shape=outs, in_specs=[SMEM] * scalars + [VMEM]...  26.9 us
    ppermute x12, waiting for transfers between devices, send(): return lax.ppermute(x, axis, [(i, to(i)) for i in range(n)])  16.2 us
    ppermute x12, starting transfers between devices, send(): return lax.ppermute(x, axis, [(i, to(i)) for i in range(n)])  10.3 us
    unnamed x34, local copies, waits for them, and re-layouts  4.86 us
  transfers between devices with their start and end apart: 31, of which 22 were waited for; matrix products, arithmetic and copies ran while one was open for 5% of the time, Pallas kernels for 10%

profile of v3, /device:TPU:0, one launch (start us, length us, event | category | flops | bytes accessed | tf_op | source)
XLA Modules:
  0.0 166.5 jit_solution(10001394149365663543)
XLA Ops:
  7.2 1.3 reshape.189
  8.7 0.8 pad_maximum_fusion.q_ref
  10.0 0.4 compare_reduce_fusion
  11.1 1.6 reshape.192.tokens
  12.9 2.0 %fetch.1 = (bf16[8,288,128]{2,1,0:T(8,128)(2,1)S(1)}, bf16[8,288,128]{2,1,0:T(8,128)(2,1)}, bf16[8,288,128]{2,1,0:T(8,128)(2,1)}, bf16[8,288,128]{2,1,0:T(8,128)(2,1)S(1)}) custom-call(s32[3]{0:T(128)S(1)} %pad_add_fusion.where, s32[32]{0:T(128)S(1)} %reshape.191.picks, bf16[16,64,576]{2,1,0:T(8,128)(2,1)S(1)} %reshape.192.tokens), custom_call_target="tpu_custom_call" | custom-call | tf_op jit(solution)/shard_map/fetch/pallas_call | solution.py:57
  14.9 1.6 collective-permute-start
  16.5 2.7 %collective-permute-start.1 = (bf16[8,288,128]{2,1,0:T(8,128)(2,1)}, bf16[8,288,128]{2,1,0:T(8,128)(2,1)S(1)}, u32[]{:S(2)}, u32[]{:S(2)}) collective-permute-start(bf16[8,288,128]{2,1,0:T(8,128)(2,1)} %get-tuple-element.23), channel_id=1, source_target_pairs={{0,64},{1,17},{2,66},{3,19},{4,68},{5,21},{6,70},{7,23},{8,72},{9,... | collective-permute-start | bytes 1769480 | tf_op jit(solution)/shard_map/ppermute | solution.py:49
  19.2 1.4 collective-permute-start.2
  20.6 0.7 dynamic_slice.10
  22.3 0.4 fusion.1
  22.6 3.6 %collective-permute-done.refs_1_ = bf16[8,288,128]{2,1,0:T(8,128)(2,1)S(1)} collective-permute-done((bf16[8,288,128]{2,1,0:T(8,128)(2,1)}, bf16[8,288,128]{2,1,0:T(8,128)(2,1)S(1)}, u32[]{:S(2)}, u32[]{:S(2)}) %collective-permute-start) | collective-permute-done | bytes 589856 | tf_op jit(solution)/shard_map/ppermute | solution.py:49
  26.2 7.4 %collective-permute-done.1.refs_2_ = bf16[8,288,128]{2,1,0:T(8,128)(2,1)S(1)} collective-permute-done((bf16[8,288,128]{2,1,0:T(8,128)(2,1)}, bf16[8,288,128]{2,1,0:T(8,128)(2,1)S(1)}, u32[]{:S(2)}, u32[]{:S(2)}) %collective-permute-start.1) | collective-permute-done | bytes 589856 | tf_op jit(solution)/shard_map/ppermute | solution.py:49
  33.8 4.0 %collective-permute-start.4 = (bf16[8,288,128]{2,1,0:T(8,128)(2,1)S(1)}, bf16[8,288,128]{2,1,0:T(8,128)(2,1)S(1)}, u32[]{:S(2)}, u32[]{:S(2)}) collective-permute-start(bf16[8,288,128]{2,1,0:T(8,128)(2,1)S(1)} %get-tuple-element.26), channel_id=1, source_target_pairs={{0,16},{1,65},{2,18},{3,67},{4,20},{5,69},{6,22},{7,71},{8,24},{9,... | collective-permute-start | bytes 1769480 | tf_op jit(solution)/shard_map/ppermute | solution.py:49
  37.7 1.0 collective-permute-start.6
  38.7 2.2 %collective-permute-start.8 = (bf16[8,288,128]{2,1,0:T(8,128)(2,1)S(1)}, bf16[8,288,128]{2,1,0:T(8,128)(2,1)S(1)}, u32[]{:S(2)}, u32[]{:S(2)}) collective-permute-start(bf16[8,288,128]{2,1,0:T(8,128)(2,1)S(1)} %get-tuple-element.28), channel_id=1, source_target_pairs={{0,24},{1,97},{2,26},{3,99},{4,28},{5,101},{6,30},{7,103},{8,0},{9... | collective-permute-start | bytes 1769480 | tf_op jit(solution)/shard_map/ppermute | solution.py:49
  40.9 0.5 select_reduce_fusion
  41.7 4.0 %collective-permute-done.4.refs_5_ = bf16[8,288,128]{2,1,0:T(8,128)(2,1)S(1)} collective-permute-done((bf16[8,288,128]{2,1,0:T(8,128)(2,1)S(1)}, bf16[8,288,128]{2,1,0:T(8,128)(2,1)S(1)}, u32[]{:S(2)}, u32[]{:S(2)}) %collective-permute-start.4) | collective-permute-done | bytes 589856 | tf_op jit(solution)/shard_map/ppermute | solution.py:49
  45.7 6.2 %collective-permute-done.6.refs_7_ = bf16[8,288,128]{2,1,0:T(8,128)(2,1)S(1)} collective-permute-done((bf16[8,288,128]{2,1,0:T(8,128)(2,1)S(1)}, bf16[8,288,128]{2,1,0:T(8,128)(2,1)S(1)}, u32[]{:S(2)}, u32[]{:S(2)}) %collective-permute-start.6) | collective-permute-done | bytes 589856 | tf_op jit(solution)/shard_map/ppermute | solution.py:49
  51.9 1.1 collective-permute-done.8.refs_9_
  53.2 1.2 fusion.refs_2_
  54.4 0.7 collective-permute-done.9.refs_10_
  55.1 1.3 copy-done.5
  56.4 0.9 copy-done.7
  57.4 4.8 %attend.6 = bf16[256,640]{1,0:T(8,128)(2,1)S(1)} custom-call(s32[1]{0:T(128)} %bitcast.10.refs_0_, bf16[4,256,640]{2,1,0:T(8,128)(2,1)S(1)} %bitcast.19, f32[16,4096]{1,0:T(8,128)S(1)} %copy-done.7, bf16[8,288,128]{2,1,0:T(8,128)(2,1)S(1)} %get-tuple-element.25.refs_3_, bf16[8,288,128]{2,1,0:T(8,128)(2,1)S(1)} %collective-permute-done.3.refs_4_, ...), custom_call_target="tpu_custom_call" | custom-call | flops 5368709120 | bytes 4718592 | tf_op jit(solution)/shard_map/attend/pallas_call | solution.py:57
  62.2 3.3 %collective-permute-start.12 = (bf16[256,640]{1,0:T(8,128)(2,1)S(1)}, bf16[256,640]{1,0:T(8,128)(2,1)S(1)}, u32[]{:S(2)}, u32[]{:S(2)}) collective-permute-start(bf16[256,640]{1,0:T(8,128)(2,1)S(1)} %attend.6), channel_id=1, source_target_pairs={{0,6},{1,7},{2,4},{3,5},{4,2},{5,3},{6,0},{7,1},{8,14},{9,15},{10,... | collective-permute-start | bytes 983048 | tf_op jit(solution)/shard_map/ppermute | solution.py:29
  65.4 4.9 %attend.5 = bf16[256,640]{1,0:T(8,128)(2,1)S(1)} custom-call(s32[1]{0:T(128)} %bitcast.9.refs_0_, bf16[4,256,640]{2,1,0:T(8,128)(2,1)S(1)} %bitcast.20, f32[16,4096]{1,0:T(8,128)S(1)} %copy-done.7, bf16[8,288,128]{2,1,0:T(8,128)(2,1)S(1)} %get-tuple-element.25.refs_3_, bf16[8,288,128]{2,1,0:T(8,128)(2,1)S(1)} %collective-permute-done.3.refs_4_, ...), custom_call_target="tpu_custom_call" | custom-call | flops 5368709120 | bytes 4718592 | tf_op jit(solution)/shard_map/attend/pallas_call | solution.py:57
  70.6 4.8 %attend.4 = bf16[256,640]{1,0:T(8,128)(2,1)S(1)} custom-call(s32[1]{0:T(128)} %bitcast.3.refs_0_, bf16[4,256,640]{2,1,0:T(8,128)(2,1)S(1)} %bitcast.21, f32[16,4096]{1,0:T(8,128)S(1)} %copy-done.7, bf16[8,288,128]{2,1,0:T(8,128)(2,1)S(1)} %get-tuple-element.25.refs_3_, bf16[8,288,128]{2,1,0:T(8,128)(2,1)S(1)} %collective-permute-done.3.refs_4_, ...), custom_call_target="tpu_custom_call" | custom-call | flops 5368709120 | bytes 4718592 | tf_op jit(solution)/shard_map/attend/pallas_call | solution.py:57
  75.4 1.6 collective-permute-start.10
  77.1 5.0 %attend.7.o3 = bf16[256,640]{1,0:T(8,128)(2,1)S(1)} custom-call(s32[1]{0:T(128)} %bitcast.11.refs_0_, bf16[4,256,640]{2,1,0:T(8,128)(2,1)S(1)} %bitcast.22, f32[16,4096]{1,0:T(8,128)S(1)} %copy-done.7, bf16[8,288,128]{2,1,0:T(8,128)(2,1)S(1)} %get-tuple-element.25.refs_3_, bf16[8,288,128]{2,1,0:T(8,128)(2,1)S(1)} %collective-permute-done.3.refs_4_, ...), custom_call_target="tpu_custom_call" | custom-call | flops 5368709120 | bytes 4718592 | tf_op jit(solution)/shard_map/attend/pallas_call | solution.py:57
  82.1 4.6 %collective-permute-done.10.o0 = bf16[256,640]{1,0:T(8,128)(2,1)S(1)} collective-permute-done((bf16[256,640]{1,0:T(8,128)(2,1)S(1)}, bf16[256,640]{1,0:T(8,128)(2,1)S(1)}, u32[]{:S(2)}, u32[]{:S(2)}) %collective-permute-start.10) | collective-permute-done | bytes 327712 | tf_op jit(solution)/shard_map/ppermute | solution.py:29
  86.7 0.7 merge.1
  87.3 2.6 %collective-permute-start.13 = (bf16[16,2048]{1,0:T(8,128)(2,1)S(1)}, bf16[16,2048]{1,0:T(8,128)(2,1)S(1)}, u32[]{:S(2)}, u32[]{:S(2)}) collective-permute-start(bf16[16,2048]{1,0:T(8,128)(2,1)S(1)} %merge.1), channel_id=1, source_target_pairs={{0,96},{1,25},{2,98},{3,27},{4,100},{5,29},{6,102},{7,31},{8,104},... | collective-permute-start | bytes 196616 | tf_op jit(solution)/shard_map/ppermute | solution.py:49
  90.0 1.2 collective-permute-start.14
  91.2 0.6 collective-permute-start.15
  91.9 3.9 %collective-permute-done.14 = bf16[16,2048]{1,0:T(8,128)(2,1)S(1)} collective-permute-done((bf16[16,2048]{1,0:T(8,128)(2,1)S(1)}, bf16[16,2048]{1,0:T(8,128)(2,1)S(1)}, u32[]{:S(2)}, u32[]{:S(2)}) %collective-permute-start.14) | collective-permute-done | bytes 65568 | tf_op jit(solution)/shard_map/ppermute | solution.py:49
  95.7 0.9 collective-permute-done.15
  96.7 2.7 %collective-permute-start.16 = (bf16[64,2048]{1,0:T(8,128)(2,1)S(1)}, bf16[64,2048]{1,0:T(8,128)(2,1)S(1)}, u32[]{:S(2)}, u32[]{:S(2)}) collective-permute-start(bf16[64,2048]{1,0:T(8,128)(2,1)S(1)} %pad_maximum_fusion.1.p0), channel_id=1, source_target_pairs={{0,24},{1,97},{2,26},{3,99},{4,28},{5,101},{6,30},{7,103},{8,0},{9... | collective-permute-start | bytes 786440 | tf_op jit(solution)/shard_map/ppermute | solution.py:49
  99.4 1.3 collective-permute-start.17
  100.7 0.4 collective-permute-start.18
  101.0 5.1 %collective-permute-done.16.p1 = bf16[64,2048]{1,0:T(8,128)(2,1)S(1)} collective-permute-done((bf16[64,2048]{1,0:T(8,128)(2,1)S(1)}, bf16[64,2048]{1,0:T(8,128)(2,1)S(1)}, u32[]{:S(2)}, u32[]{:S(2)}) %collective-permute-start.16) | collective-permute-done | bytes 262176 | tf_op jit(solution)/shard_map/ppermute | solution.py:49
  106.1 1.2 collective-permute-done.17.p2
  107.4 2.7 %collective-permute-done.18.p3 = bf16[64,2048]{1,0:T(8,128)(2,1)S(1)} collective-permute-done((bf16[64,2048]{1,0:T(8,128)(2,1)S(1)}, bf16[64,2048]{1,0:T(8,128)(2,1)S(1)}, u32[]{:S(2)}, u32[]{:S(2)}) %collective-permute-start.18) | collective-permute-done | bytes 262176 | tf_op jit(solution)/shard_map/ppermute | solution.py:49
  110.1 1.3 project.1
  111.7 1.3 collective-permute-done.19
  113.1 1.5 collective-permute-start.20
  114.5 3.0 %collective-permute-start.21 = (bf16[2,4,16,448]{3,2,1,0:T(8,128)(2,1)S(1)}, bf16[2,4,16,448]{3,2,1,0:T(8,128)(2,1)S(1)}, u32[]{:S(2)}, u32[]{:S(2)}) collective-permute-start(bf16[2,4,16,448]{3,2,1,0:T(8,128)(2,1)S(1)} %add_convert_fusion.pair), channel_id=1, source_target_pairs={{0,4},{1,5},{2,6},{3,7},{4,0},{5,1},{6,2},{7,3},{8,12},{9,13},{10,... | collective-permute-start | bytes 344072 | tf_op jit(solution)/shard_map/ppermute | solution.py:29
  118.0 1.5 collective-permute-done.20.t1
  119.5 4.5 %collective-permute-done.21.t2 = bf16[2,4,16,448]{3,2,1,0:T(8,128)(2,1)S(1)} collective-permute-done((bf16[2,4,16,448]{3,2,1,0:T(8,128)(2,1)S(1)}, bf16[2,4,16,448]{3,2,1,0:T(8,128)(2,1)S(1)}, u32[]{:S(2)}, u32[]{:S(2)}) %collective-permute-start.21) | collective-permute-done | bytes 114720 | tf_op jit(solution)/shard_map/ppermute | solution.py:29
  124.0 2.2 %collective-permute-done.22.t3 = bf16[2,4,16,448]{3,2,1,0:T(8,128)(2,1)S(1)} collective-permute-done((bf16[2,4,16,448]{3,2,1,0:T(8,128)(2,1)S(1)}, bf16[2,4,16,448]{3,2,1,0:T(8,128)(2,1)S(1)}, u32[]{:S(2)}, u32[]{:S(2)}) %collective-permute-start.22) | collective-permute-done | bytes 114720 | tf_op jit(solution)/shard_map/ppermute | solution.py:29
  126.2 0.6 join.1.half_ref
  127.0 1.3 collective-permute-done.23.other_ref
  128.3 1.6 copy-done.3
  129.9 2.0 %ffn.1 = (bf16[16,16,448]{2,1,0:T(8,128)(2,1)S(1)}, bf16[4,16,4736]{2,1,0:T(8,128)(2,1)S(1)}, bf16[4,16,4736]{2,1,0:T(8,128)(2,1)S(1)}, bf16[4,16,4736]{2,1,0:T(8,128)(2,1)S(1)}, bf16[4,16,4736]{2,1,0:T(8,128)(2,1)S(1)}) custom-call(s32[3]{0:T(128)S(1)} %pad_add_fusion.where, bf16[2,4,16,448]{3,2,1,0:T(8,128)(2,1)S(1)} %join.1.half_ref, ...), custom_call_target="tpu_custom_call" | custom-call | tf_op jit(solution)/shard_map/ffn/pallas_call | solution.py:57
  131.8 1.2 collective-permute-start.24
  133.1 3.1 %collective-permute-start.26 = (bf16[4,16,4736]{2,1,0:T(8,128)(2,1)S(1)}, bf16[4,16,4736]{2,1,0:T(8,128)(2,1)S(1)}, u32[]{:S(2)}, u32[]{:S(2)}) collective-permute-start(bf16[4,16,4736]{2,1,0:T(8,128)(2,1)S(1)} %get-tuple-element.35), channel_id=1, source_target_pairs={{0,96},{1,25},{2,98},{3,27},{4,100},{5,29},{6,102},{7,31},{8,104},... | collective-permute-start | bytes 1818632 | tf_op jit(solution)/shard_map/ppermute | solution.py:49
  136.2 7.3 %collective-permute-done.24.refs_1_ = bf16[4,16,4736]{2,1,0:T(8,128)(2,1)S(1)} collective-permute-done((bf16[4,16,4736]{2,1,0:T(8,128)(2,1)S(1)}, bf16[4,16,4736]{2,1,0:T(8,128)(2,1)S(1)}, u32[]{:S(2)}, u32[]{:S(2)}) %collective-permute-start.24) | collective-permute-done | bytes 606240 | tf_op jit(solution)/shard_map/ppermute | solution.py:49
  143.6 6.4 %collective-permute-done.25.refs_2_ = bf16[4,16,4736]{2,1,0:T(8,128)(2,1)S(1)} collective-permute-done((bf16[4,16,4736]{2,1,0:T(8,128)(2,1)S(1)}, bf16[4,16,4736]{2,1,0:T(8,128)(2,1)S(1)}, u32[]{:S(2)}, u32[]{:S(2)}) %collective-permute-start.25) | collective-permute-done | bytes 606240 | tf_op jit(solution)/shard_map/ppermute | solution.py:49
  150.0 0.5 fold.1
  150.5 1.4 collective-permute-start.27
  152.0 3.1 %collective-permute-start.29 = (bf16[16,4736]{1,0:T(8,128)(2,1)S(1)}, bf16[16,4736]{1,0:T(8,128)(2,1)S(1)}, u32[]{:S(2)}, u32[]{:S(2)}) collective-permute-start(bf16[16,4736]{1,0:T(8,128)(2,1)S(1)} %get-tuple-element.39), channel_id=1, source_target_pairs={{0,24},{1,97},{2,26},{3,99},{4,28},{5,101},{6,30},{7,103},{8,0},{9... | collective-permute-start | bytes 454664 | tf_op jit(solution)/shard_map/ppermute | solution.py:49
  155.1 0.8 copy.31
  155.9 1.4 collective-permute-done.27.r1
  157.3 1.6 collective-permute-done.28.r2
  158.9 0.8 finish.1
  (83 shorter events, 3.6 us)
Async XLA Ops:
  7.2 2.4 %copy-start.14 = (s32[256]{0:T(256)S(1)}, s32[256]{0:T(256)}, u32[]{:S(2)}) copy-start(s32[256]{0:T(256)} %param.19) | copy-start | bytes 3076
  7.2 2.4 %copy-start.10 = (s32[256,32]{0,1:T(8,128)S(1)}, s32[256,32]{0,1:T(8,128)}, u32[]{:S(2)}) copy-start(s32[256,32]{0,1:T(8,128)} %param.20) | copy-start | bytes 98308
  7.2 2.6 %copy-start.12 = (s32[2048]{0:T(1024)S(1)}, s32[2048]{0:T(1024)}, u32[]{:S(2)}) copy-start(s32[2048]{0:T(1024)} %param.18) | copy-start | bytes 24580
  7.2 3.9 %copy-start.8 = (bf16[16,36864]{1,0:T(8,128)(2,1)S(1)}, bf16[16,36864]{1,0:T(8,128)(2,1)}, u32[]{:S(2)}) copy-start(bf16[16,36864]{1,0:T(8,128)(2,1)} %param.17) | copy-start | bytes 3538948
  7.2 47.9 %all-gather.3.cloned.1.call-start = ((), (), s32[]{:S(2)}) async-start(), calls=%async_computation | async-start | bytes 1638400 | tf_op jit(solution)/shard_map/all_gather | solution.py:344
  12.9 28.6 %copy-start.15 = (s32[4]{0:T(128)S(1)}, s32[4]{0:T(128)}, u32[]{:S(2)}) copy-start(s32[4]{0:T(128)} %constant.148.clone) | copy-start | bytes 52
  12.9 40.2 %copy-start.11 = (bf16[16,576]{1,0:T(8,128)(2,1)S(1)}, bf16[16,576]{1,0:T(8,128)(2,1)}, u32[]{:S(2)}) copy-start(bf16[16,576]{1,0:T(8,128)(2,1)} %param.16) | copy-start | bytes 55300
  12.9 40.2 %slice-start = ((bf16[16,576]{1,0:T(8,128)(2,1)}), bf16[16,64]{1,0:T(8,128)(2,1)S(1)}, s32[]{:S(2)}) async-start(bf16[16,576]{1,0:T(8,128)(2,1)} %param.16), calls=%async_computation.1 | async-start | bytes 8192 | tf_op jit(solution)/shard_map/slice | solution.py:342
  14.9 11.3 %collective-permute-start = (bf16[8,288,128]{2,1,0:T(8,128)(2,1)}, bf16[8,288,128]{2,1,0:T(8,128)(2,1)S(1)}, u32[]{:S(2)}, u32[]{:S(2)}) collective-permute-start(bf16[8,288,128]{2,1,0:T(8,128)(2,1)} %get-tuple-element.22), channel_id=1, source_target_pairs={{0,32},{1,9},{2,34},{3,11},{4,36},{5,13},{6,38},{7,15},{8,40},{9,1... | collective-permute-start | bytes 1769480 | tf_op jit(solution)/shard_map/ppermute | solution.py:49
  16.5 17.1 %collective-permute-start.1 = (bf16[8,288,128]{2,1,0:T(8,128)(2,1)}, bf16[8,288,128]{2,1,0:T(8,128)(2,1)S(1)}, u32[]{:S(2)}, u32[]{:S(2)}) collective-permute-start(bf16[8,288,128]{2,1,0:T(8,128)(2,1)} %get-tuple-element.23), channel_id=1, source_target_pairs={{0,64},{1,17},{2,66},{3,19},{4,68},{5,21},{6,70},{7,23},{8,72},{9,... | collective-permute-start | bytes 1769480 | tf_op jit(solution)/shard_map/ppermute | solution.py:49
  19.2 14.4 %collective-permute-start.2 = (bf16[8,288,128]{2,1,0:T(8,128)(2,1)S(1)}, bf16[8,288,128]{2,1,0:T(8,128)(2,1)S(1)}, u32[]{:S(2)}, u32[]{:S(2)}) collective-permute-start(bf16[8,288,128]{2,1,0:T(8,128)(2,1)S(1)} %get-tuple-element.24), channel_id=1, source_target_pairs={{0,96},{1,25},{2,98},{3,27},{4,100},{5,29},{6,102},{7,31},{8,104},... | collective-permute-start | bytes 1769480 | tf_op jit(solution)/shard_map/ppermute | solution.py:49
  33.8 11.9 %collective-permute-start.4 = (bf16[8,288,128]{2,1,0:T(8,128)(2,1)S(1)}, bf16[8,288,128]{2,1,0:T(8,128)(2,1)S(1)}, u32[]{:S(2)}, u32[]{:S(2)}) collective-permute-start(bf16[8,288,128]{2,1,0:T(8,128)(2,1)S(1)} %get-tuple-element.26), channel_id=1, source_target_pairs={{0,16},{1,65},{2,18},{3,67},{4,20},{5,69},{6,22},{7,71},{8,24},{9,... | collective-permute-start | bytes 1769480 | tf_op jit(solution)/shard_map/ppermute | solution.py:49
  37.7 14.2 %collective-permute-start.6 = (bf16[8,288,128]{2,1,0:T(8,128)(2,1)S(1)}, bf16[8,288,128]{2,1,0:T(8,128)(2,1)S(1)}, u32[]{:S(2)}, u32[]{:S(2)}) collective-permute-start(bf16[8,288,128]{2,1,0:T(8,128)(2,1)S(1)} %get-tuple-element.27), channel_id=1, source_target_pairs={{0,8},{1,33},{2,10},{3,35},{4,12},{5,37},{6,14},{7,39},{8,16},{9,4... | collective-permute-start | bytes 1769480 | tf_op jit(solution)/shard_map/ppermute | solution.py:49
  38.7 14.2 %collective-permute-start.8 = (bf16[8,288,128]{2,1,0:T(8,128)(2,1)S(1)}, bf16[8,288,128]{2,1,0:T(8,128)(2,1)S(1)}, u32[]{:S(2)}, u32[]{:S(2)}) collective-permute-start(bf16[8,288,128]{2,1,0:T(8,128)(2,1)S(1)} %get-tuple-element.28), channel_id=1, source_target_pairs={{0,24},{1,97},{2,26},{3,99},{4,28},{5,101},{6,30},{7,103},{8,0},{9... | collective-permute-start | bytes 1769480 | tf_op jit(solution)/shard_map/ppermute | solution.py:49
  41.6 12.7 %collective-permute-start.3 = (bf16[8,288,128]{2,1,0:T(8,128)(2,1)S(1)}, bf16[8,288,128]{2,1,0:T(8,128)(2,1)S(1)}, u32[]{:S(2)}, u32[]{:S(2)}) collective-permute-start(bf16[8,288,128]{2,1,0:T(8,128)(2,1)S(1)} %get-tuple-element.25.refs_3_), channel_id=1, source_target_pairs={{0,1},{1,0},{2,3},{3,2},{4,5},{5,4},{6,7},{7,6},{8,9},{9,8},{10,11... | collective-permute-start | bytes 1769480 | tf_op jit(solution)/shard_map/ppermute | solution.py:29
  45.7 8.7 %collective-permute-start.5 = (bf16[8,288,128]{2,1,0:T(8,128)(2,1)S(1)}, bf16[8,288,128]{2,1,0:T(8,128)(2,1)}, u32[]{:S(2)}, u32[]{:S(2)}) collective-permute-start(bf16[8,288,128]{2,1,0:T(8,128)(2,1)S(1)} %collective-permute-done.4.refs_5_), channel_id=1, source_target_pairs={{0,1},{1,0},{2,3},{3,2},{4,5},{5,4},{6,7},{7,6},{8,9},{9,8},{10,11... | collective-permute-start | bytes 1769480 | tf_op jit(solution)/shard_map/ppermute | solution.py:29
  51.9 2.5 %collective-permute-start.7 = (bf16[8,288,128]{2,1,0:T(8,128)(2,1)S(1)}, bf16[8,288,128]{2,1,0:T(8,128)(2,1)}, u32[]{:S(2)}, u32[]{:S(2)}) collective-permute-start(bf16[8,288,128]{2,1,0:T(8,128)(2,1)S(1)} %collective-permute-done.6.refs_7_), channel_id=1, source_target_pairs={{0,1},{1,0},{2,3},{3,2},{4,5},{5,4},{6,7},{7,6},{8,9},{9,8},{10,11... | collective-permute-start | bytes 1769480 | tf_op jit(solution)/shard_map/ppermute | solution.py:29
  52.9 2.1 %collective-permute-start.9 = (bf16[8,288,128]{2,1,0:T(8,128)(2,1)S(1)}, bf16[8,288,128]{2,1,0:T(8,128)(2,1)}, u32[]{:S(2)}, u32[]{:S(2)}) collective-permute-start(bf16[8,288,128]{2,1,0:T(8,128)(2,1)S(1)} %collective-permute-done.8.refs_9_), channel_id=1, source_target_pairs={{0,1},{1,0},{2,3},{3,2},{4,5},{5,4},{6,7},{7,6},{8,9},{9,8},{10,11... | collective-permute-start | bytes 1769480 | tf_op jit(solution)/shard_map/ppermute | solution.py:29
  55.1 1.3 copy-start.5
  56.4 0.9 copy-start.7
  62.2 19.9 %collective-permute-start.12 = (bf16[256,640]{1,0:T(8,128)(2,1)S(1)}, bf16[256,640]{1,0:T(8,128)(2,1)S(1)}, u32[]{:S(2)}, u32[]{:S(2)}) collective-permute-start(bf16[256,640]{1,0:T(8,128)(2,1)S(1)} %attend.6), channel_id=1, source_target_pairs={{0,6},{1,7},{2,4},{3,5},{4,2},{5,3},{6,0},{7,1},{8,14},{9,15},{10,... | collective-permute-start | bytes 983048 | tf_op jit(solution)/shard_map/ppermute | solution.py:29
  65.4 5.1 %copy-start.6 = (bf16[1024,640]{1,0:T(8,128)(2,1)S(1)}, bf16[1024,640]{1,0:T(8,128)(2,1)}, u32[]{:S(2)}) copy-start(bf16[1024,640]{1,0:T(8,128)(2,1)} %all-gather.3.cloned.1.call-done) | copy-start | bytes 3932164
  70.4 11.7 %collective-permute-start.11 = (bf16[256,640]{1,0:T(8,128)(2,1)S(1)}, bf16[256,640]{1,0:T(8,128)(2,1)S(1)}, u32[]{:S(2)}, u32[]{:S(2)}) collective-permute-start(bf16[256,640]{1,0:T(8,128)(2,1)S(1)} %attend.5), channel_id=1, source_target_pairs={{0,2},{1,3},{2,0},{3,1},{4,6},{5,7},{6,4},{7,5},{8,10},{9,11},{10,... | collective-permute-start | bytes 983048 | tf_op jit(solution)/shard_map/ppermute | solution.py:29
  75.4 11.2 %collective-permute-start.10 = (bf16[256,640]{1,0:T(8,128)(2,1)S(1)}, bf16[256,640]{1,0:T(8,128)(2,1)S(1)}, u32[]{:S(2)}, u32[]{:S(2)}) collective-permute-start(bf16[256,640]{1,0:T(8,128)(2,1)S(1)} %attend.4), channel_id=1, source_target_pairs={{0,4},{1,5},{2,6},{3,7},{4,0},{5,1},{6,2},{7,3},{8,12},{9,13},{10,... | collective-permute-start | bytes 983048 | tf_op jit(solution)/shard_map/ppermute | solution.py:29
  77.1 9.6 %copy-start = (bf16[256,640]{1,0:T(8,128)(2,1)S(1)}, bf16[256,640]{1,0:T(8,128)(2,1)}, u32[]{:S(2)}) copy-start(bf16[256,640]{1,0:T(8,128)(2,1)} %pad_maximum_fusion.q_ref) | copy-start | bytes 983044
  77.1 9.6 %copy-start.1 = (bf16[16,512,128]{2,1,0:T(8,128)(2,1)S(1)}, bf16[16,512,128]{2,1,0:T(8,128)(2,1)}, u32[]{:S(2)}) copy-start(bf16[16,512,128]{2,1,0:T(8,128)(2,1)} %up_ref.1) | copy-start | bytes 6291460
  82.1 28.0 %copy-start.4 = (bf16[2048,448]{0,1:T(8,128)(2,1)S(1)}, bf16[2048,448]{0,1:T(8,128)(2,1)}, u32[]{:S(2)}) copy-start(bf16[2048,448]{0,1:T(8,128)(2,1)} %param.22) | copy-start | bytes 5505028
  87.3 4.5 %collective-permute-start.13 = (bf16[16,2048]{1,0:T(8,128)(2,1)S(1)}, bf16[16,2048]{1,0:T(8,128)(2,1)S(1)}, u32[]{:S(2)}, u32[]{:S(2)}) collective-permute-start(bf16[16,2048]{1,0:T(8,128)(2,1)S(1)} %merge.1), channel_id=1, source_target_pairs={{0,96},{1,25},{2,98},{3,27},{4,100},{5,29},{6,102},{7,31},{8,104},... | collective-permute-start | bytes 196616 | tf_op jit(solution)/shard_map/ppermute | solution.py:49
  90.0 5.8 %collective-permute-start.14 = (bf16[16,2048]{1,0:T(8,128)(2,1)S(1)}, bf16[16,2048]{1,0:T(8,128)(2,1)S(1)}, u32[]{:S(2)}, u32[]{:S(2)}) collective-permute-start(bf16[16,2048]{1,0:T(8,128)(2,1)S(1)} %merge.1), channel_id=1, source_target_pairs={{0,64},{1,17},{2,66},{3,19},{4,68},{5,21},{6,70},{7,23},{8,72},{9,... | collective-permute-start | bytes 196616 | tf_op jit(solution)/shard_map/ppermute | solution.py:49
  91.2 5.5 %collective-permute-start.15 = (bf16[16,2048]{1,0:T(8,128)(2,1)S(1)}, bf16[16,2048]{1,0:T(8,128)(2,1)S(1)}, u32[]{:S(2)}, u32[]{:S(2)}) collective-permute-start(bf16[16,2048]{1,0:T(8,128)(2,1)S(1)} %merge.1), channel_id=1, source_target_pairs={{0,32},{1,9},{2,34},{3,11},{4,36},{5,13},{6,38},{7,15},{8,40},{9,1... | collective-permute-start | bytes 196616 | tf_op jit(solution)/shard_map/ppermute | solution.py:49
  96.7 21.2 %copy-start.9 = (bf16[256,448]{0,1:T(8,128)(2,1)S(1)}, bf16[256,448]{0,1:T(8,128)(2,1)}, u32[]{:S(2)}) copy-start(bf16[256,448]{0,1:T(8,128)(2,1)} %param.23) | copy-start | bytes 688132
  96.7 9.4 %collective-permute-start.16 = (bf16[64,2048]{1,0:T(8,128)(2,1)S(1)}, bf16[64,2048]{1,0:T(8,128)(2,1)S(1)}, u32[]{:S(2)}, u32[]{:S(2)}) collective-permute-start(bf16[64,2048]{1,0:T(8,128)(2,1)S(1)} %pad_maximum_fusion.1.p0), channel_id=1, source_target_pairs={{0,24},{1,97},{2,26},{3,99},{4,28},{5,101},{6,30},{7,103},{8,0},{9... | collective-permute-start | bytes 786440 | tf_op jit(solution)/shard_map/ppermute | solution.py:49
  99.4 8.0 %collective-permute-start.17 = (bf16[64,2048]{1,0:T(8,128)(2,1)S(1)}, bf16[64,2048]{1,0:T(8,128)(2,1)S(1)}, u32[]{:S(2)}, u32[]{:S(2)}) collective-permute-start(bf16[64,2048]{1,0:T(8,128)(2,1)S(1)} %pad_maximum_fusion.1.p0), channel_id=1, source_target_pairs={{0,16},{1,65},{2,18},{3,67},{4,20},{5,69},{6,22},{7,71},{8,24},{9,... | collective-permute-start | bytes 786440 | tf_op jit(solution)/shard_map/ppermute | solution.py:49
  100.7 9.4 %collective-permute-start.18 = (bf16[64,2048]{1,0:T(8,128)(2,1)S(1)}, bf16[64,2048]{1,0:T(8,128)(2,1)S(1)}, u32[]{:S(2)}, u32[]{:S(2)}) collective-permute-start(bf16[64,2048]{1,0:T(8,128)(2,1)S(1)} %pad_maximum_fusion.1.p0), channel_id=1, source_target_pairs={{0,8},{1,33},{2,10},{3,35},{4,12},{5,37},{6,14},{7,39},{8,16},{9,4... | collective-permute-start | bytes 786440 | tf_op jit(solution)/shard_map/ppermute | solution.py:49
  110.1 16.9 %copy-start.13 = (bf16[448]{0:T(512)(128)(2,1)S(1)}, bf16[448]{0:T(512)(128)(2,1)}, u32[]{:S(2)}) copy-start(bf16[448]{0:T(512)(128)(2,1)} %param.24) | copy-start | bytes 2692
  110.1 18.2 %copy-start.2 = (bf16[448,2304]{1,0:T(8,128)(2,1)S(1)}, bf16[448,2304]{1,0:T(8,128)(2,1)}, u32[]{:S(2)}) copy-start(bf16[448,2304]{1,0:T(8,128)(2,1)} %wg_ref.1) | copy-start | bytes 6193156
  111.4 1.6 collective-permute-start.19
  113.1 6.4 %collective-permute-start.20 = (bf16[2,4,16,448]{3,2,1,0:T(8,128)(2,1)S(1)}, bf16[2,4,16,448]{3,2,1,0:T(8,128)(2,1)S(1)}, u32[]{:S(2)}, u32[]{:S(2)}) collective-permute-start(bf16[2,4,16,448]{3,2,1,0:T(8,128)(2,1)S(1)} %add_convert_fusion.pair), channel_id=1, source_target_pairs={{0,2},{1,3},{2,0},{3,1},{4,6},{5,7},{6,4},{7,5},{8,10},{9,11},{10,... | collective-permute-start | bytes 344072 | tf_op jit(solution)/shard_map/ppermute | solution.py:29
  114.5 9.4 %collective-permute-start.21 = (bf16[2,4,16,448]{3,2,1,0:T(8,128)(2,1)S(1)}, bf16[2,4,16,448]{3,2,1,0:T(8,128)(2,1)S(1)}, u32[]{:S(2)}, u32[]{:S(2)}) collective-permute-start(bf16[2,4,16,448]{3,2,1,0:T(8,128)(2,1)S(1)} %add_convert_fusion.pair), channel_id=1, source_target_pairs={{0,4},{1,5},{2,6},{3,7},{4,0},{5,1},{6,2},{7,3},{8,12},{9,13},{10,... | collective-permute-start | bytes 344072 | tf_op jit(solution)/shard_map/ppermute | solution.py:29
  117.5 8.7 %collective-permute-start.22 = (bf16[2,4,16,448]{3,2,1,0:T(8,128)(2,1)S(1)}, bf16[2,4,16,448]{3,2,1,0:T(8,128)(2,1)S(1)}, u32[]{:S(2)}, u32[]{:S(2)}) collective-permute-start(bf16[2,4,16,448]{3,2,1,0:T(8,128)(2,1)S(1)} %add_convert_fusion.pair), channel_id=1, source_target_pairs={{0,6},{1,7},{2,4},{3,5},{4,2},{5,3},{6,0},{7,1},{8,14},{9,15},{10,... | collective-permute-start | bytes 344072 | tf_op jit(solution)/shard_map/ppermute | solution.py:29
  126.8 1.4 collective-permute-start.23
  128.3 1.6 copy-start.3
  131.8 11.7 %collective-permute-start.24 = (bf16[4,16,4736]{2,1,0:T(8,128)(2,1)S(1)}, bf16[4,16,4736]{2,1,0:T(8,128)(2,1)S(1)}, u32[]{:S(2)}, u32[]{:S(2)}) collective-permute-start(bf16[4,16,4736]{2,1,0:T(8,128)(2,1)S(1)} %get-tuple-element.33), channel_id=1, source_target_pairs={{0,64},{1,17},{2,66},{3,19},{4,68},{5,21},{6,70},{7,23},{8,72},{9,... | collective-permute-start | bytes 1818632 | tf_op jit(solution)/shard_map/ppermute | solution.py:49
  133.0 17.0 %collective-permute-start.25 = (bf16[4,16,4736]{2,1,0:T(8,128)(2,1)S(1)}, bf16[4,16,4736]{2,1,0:T(8,128)(2,1)S(1)}, u32[]{:S(2)}, u32[]{:S(2)}) collective-permute-start(bf16[4,16,4736]{2,1,0:T(8,128)(2,1)S(1)} %get-tuple-element.34), channel_id=1, source_target_pairs={{0,32},{1,9},{2,34},{3,11},{4,36},{5,13},{6,38},{7,15},{8,40},{9,1... | collective-permute-start | bytes 1818632 | tf_op jit(solution)/shard_map/ppermute | solution.py:49
  133.1 16.9 %collective-permute-start.26 = (bf16[4,16,4736]{2,1,0:T(8,128)(2,1)S(1)}, bf16[4,16,4736]{2,1,0:T(8,128)(2,1)S(1)}, u32[]{:S(2)}, u32[]{:S(2)}) collective-permute-start(bf16[4,16,4736]{2,1,0:T(8,128)(2,1)S(1)} %get-tuple-element.35), channel_id=1, source_target_pairs={{0,96},{1,25},{2,98},{3,27},{4,100},{5,29},{6,102},{7,31},{8,104},... | collective-permute-start | bytes 1818632 | tf_op jit(solution)/shard_map/ppermute | solution.py:49
  150.5 6.8 %collective-permute-start.27 = (bf16[16,4736]{1,0:T(8,128)(2,1)S(1)}, bf16[16,4736]{1,0:T(8,128)(2,1)S(1)}, u32[]{:S(2)}, u32[]{:S(2)}) collective-permute-start(bf16[16,4736]{1,0:T(8,128)(2,1)S(1)} %get-tuple-element.37), channel_id=1, source_target_pairs={{0,16},{1,65},{2,18},{3,67},{4,20},{5,69},{6,22},{7,71},{8,24},{9,... | collective-permute-start | bytes 454664 | tf_op jit(solution)/shard_map/ppermute | solution.py:49
  151.9 7.0 %collective-permute-start.28 = (bf16[16,4736]{1,0:T(8,128)(2,1)S(1)}, bf16[16,4736]{1,0:T(8,128)(2,1)S(1)}, u32[]{:S(2)}, u32[]{:S(2)}) collective-permute-start(bf16[16,4736]{1,0:T(8,128)(2,1)S(1)} %get-tuple-element.38), channel_id=1, source_target_pairs={{0,8},{1,33},{2,10},{3,35},{4,12},{5,37},{6,14},{7,39},{8,16},{9,4... | collective-permute-start | bytes 454664 | tf_op jit(solution)/shard_map/ppermute | solution.py:49
  152.0 6.9 %collective-permute-start.29 = (bf16[16,4736]{1,0:T(8,128)(2,1)S(1)}, bf16[16,4736]{1,0:T(8,128)(2,1)S(1)}, u32[]{:S(2)}, u32[]{:S(2)}) collective-permute-start(bf16[16,4736]{1,0:T(8,128)(2,1)S(1)} %get-tuple-element.39), channel_id=1, source_target_pairs={{0,24},{1,97},{2,26},{3,99},{4,28},{5,101},{6,30},{7,103},{8,0},{9... | collective-permute-start | bytes 454664 | tf_op jit(solution)/shard_map/ppermute | solution.py:49
Sparse Core Ops, SparseCore 0:
  9.7 27.3 all-gather.2

commit v4 on v3

--- a/solution.py
+++ b/solution.py
@@ -51,13 +51,14 @@
 
 VMEM = pl.BlockSpec(memory_space=pltpu.VMEM)
 SMEM = pl.BlockSpec(memory_space=pltpu.SMEM)
-
-
-def call(kernel, name, outs, ins, scalars=0, limit=20, **kw):
+ANY = pl.BlockSpec(memory_space=pl.ANY)
+
+
+def call(kernel, name, outs, ins, scalars=0, anys=0, limit=20, **kw):
     return pl.pallas_call(
         kernel,
         out_shape=outs,
-        in_specs=[SMEM] * scalars + [VMEM] * (len(ins) - scalars),
+        in_specs=[SMEM] * scalars + [VMEM] * (len(ins) - scalars - anys) + [ANY] * anys,
         out_specs=[VMEM] * len(outs),
         compiler_params=pltpu.CompilerParams(vmem_limit_bytes=limit * 1024 * 1024),
         name=name,
@@ -117,34 +118,45 @@
 
 
 def attend_kernel(groups, resume, last, *refs):
-    index, q_ref, bias_ref = refs[:3]
+    index, q_ref, use_ref = refs[:3]
     pieces = refs[3 : 3 + 2 * groups]
     refs = refs[3 + 2 * groups :]
     if resume:
         acc_in, stat_in = refs[0], refs[1]
         refs = refs[2:]
-    q = q_ref[index[0]]
-    m_rows = q.shape[0]
+    m_rows = q_ref.shape[1]
+    chips = [index[0]] if last else list(range(4))
+    slot = lax.broadcasted_iota(jnp.int32, (16, 1024), 0)
+    token = lax.broadcasted_iota(jnp.int32, (16, 1024), 1)
+    spread = ((token // 32) % 16 == slot).astype(f32).astype(bf16)
+    biases = [
+        (jnp.dot(use_ref[g], spread, preferred_element_type=f32) - 1.0) * -NEG
+        for g in range(groups)
+    ]
 
     def values(g):
         mine = pieces[2 * g : 2 * g + 2]
         return jnp.concatenate([half_latent(mine, 0), half_latent(mine, 1)], axis=0)
 
-    def scores(g):
+    def scores(chip, g):
         mine = pieces[2 * g : 2 * g + 2]
         ropes = jnp.concatenate([half_rope(mine, 0), half_rope(mine, 1)], axis=0)
         keys = jnp.concatenate([values(g), ropes], axis=1)
-        s = lax.dot_general(q, keys, (((1,), (1,)), ((), ())), preferred_element_type=f32)
+        s = lax.dot_general(
+            q_ref[chip], keys, (((1,), (1,)), ((), ())), preferred_element_type=f32
+        )
         n = s.shape[1]
-        s = s.reshape(m_rows // 16, 16, n) + bias_ref[:, g * n : (g + 1) * n][None]
-        return s.reshape(m_rows, n)
-
-    top = total = acc = None
-    if resume:
-        top, total, acc = stat_in[:, 0:1], stat_in[:, 64:65], acc_in[...]
-    s = scores(0)
-    for g in range(groups):
-        ahead = scores(g + 1) if g + 1 < groups else None
+        return (s.reshape(m_rows // 16, 16, n) + biases[g][None]).reshape(m_rows, n)
+
+    steps = [(chip, g) for chip in chips for g in range(groups)]
+    s = scores(*steps[0])
+    for i, (chip, g) in enumerate(steps):
+        ahead = scores(*steps[i + 1]) if i + 1 < len(steps) else None
+        if g == 0:
+            top = total = acc = None
+            if resume:
+                top, total = stat_in[chip, :, 0:1], stat_in[chip, :, 64:65]
+                acc = acc_in[chip]
         high = jnp.max(s, axis=1, keepdims=True)
         new = high if top is None else jnp.maximum(top, high)
         p = jnp.exp2((s - new) * SCALE2)
@@ -156,39 +168,44 @@
             fade = jnp.exp2((top - new) * SCALE2)
             acc, total = acc * fade + o, total * fade + part
         top, s = new, ahead
-    lane = lax.broadcasted_iota(jnp.int32, (m_rows, 128), 1)
+        if g == groups - 1 and not last:
+            lane = lax.broadcasted_iota(jnp.int32, (m_rows, 128), 1)
+            refs[0][chip] = acc
+            refs[1][chip] = jnp.where(lane < 64, top, total)
     if not last:
-        refs[0][...] = acc
-        refs[1][...] = jnp.where(lane < 64, top, total)
         return
     out_ref = refs[0]
-    out_ref[:, :LAT] = (acc / total).astype(bf16)
+    out_ref[:m_rows] = (acc / total).astype(bf16)
     lse = top * SCALE + jnp.log(total)
     hi = lse.astype(bf16).astype(f32)
     mid = (lse - hi).astype(bf16).astype(f32)
     low = lse - hi - mid
+    lane = lax.broadcasted_iota(jnp.int32, (m_rows, 128), 1)
     stats = jnp.where(lane == 0, hi, jnp.where(lane == 1, mid, jnp.where(lane == 2, low, 0.0)))
-    out_ref[:, LAT:] = stats.astype(bf16)
-
-
-def attend(index, q, bias, pieces, carry=(), last=True):
+    stats = stats.T[:16]
+    out_ref[m_rows:] = jnp.concatenate([stats, jnp.zeros_like(stats)], axis=1).astype(bf16)
+
+
+def attend(index, q, use, pieces, carry=(), last=True):
     m_rows = q.shape[1]
     groups = len(pieces) // 2
     if last:
-        outs = [shape(m_rows, LAT + 128)]
+        outs = [shape(m_rows + 16, LAT)]
     else:
-        outs = [shape(m_rows, LAT, dtype=f32), shape(m_rows, 128, dtype=f32)]
+        outs = [shape(4, m_rows, LAT, dtype=f32), shape(4, m_rows, 128, dtype=f32)]
+    chips = 1 if last else 4
     cost = pl.CostEstimate(
-        flops=2 * m_rows * groups * 1024 * (768 + 512) * 2,
+        flops=2 * chips * m_rows * groups * 1024 * (768 + 512) * 2,
         bytes_accessed=groups * 16 * 288 * 128 * 2,
-        transcendentals=m_rows * groups * 1024,
+        transcendentals=chips * m_rows * groups * 1024,
     )
     return call(
         functools.partial(attend_kernel, groups, bool(carry), last),
         "attend",
         outs,
-        [index, q, bias, *pieces, *carry],
+        [index, q, use, *pieces, *carry],
         scalars=1,
+        limit=28,
         cost_estimate=cost,
     )
 
@@ -202,7 +219,8 @@
     s_own = jnp.sum(q * key[None], axis=2, keepdims=True).reshape(heads * rows, 1) * SCALE
     lses = []
     for o in (o0, o1, o2, o3):
-        lses.append(jnp.sum(o[:, LAT:].astype(f32), axis=1, keepdims=True))
+        row = jnp.sum(o[256:, :256].astype(f32), axis=0, keepdims=True)
+        lses.append(jnp.broadcast_to(row, (128, 256)).T[:, :1])
     top = s_own
     for v in lses:
         top = jnp.maximum(top, v)
@@ -212,7 +230,7 @@
     mix = (e_own / den).reshape(heads, rows, 1) * own[None, :, :LAT]
     mix = mix.reshape(heads * rows, LAT)
     for o, e in zip((o0, o1, o2, o3), es):
-        mix = mix + (e / den) * o[:, :LAT].astype(f32)
+        mix = mix + (e / den) * o[:256].astype(f32)
     mix = mix.astype(bf16)
     for h in range(heads):
         out_ref[:, h * 128 : (h + 1) * 128] = jnp.dot(
@@ -262,7 +280,10 @@
             out[i, kx] = (residual[dp].astype(f32) + attn).astype(bf16)
 
 
-def ffn_kernel(where, half_ref, other_ref, gain_ref, wg_ref, wu_ref, stream_ref, *outs):
+def ffn_kernel(where, half_ref, other_ref, gain_ref, wg_ref, wu_any, stream_ref, *outs):
+    *outs, wu_ref, sem = outs
+    bring = pltpu.make_async_copy(wu_any, wu_ref, sem)
+    bring.start()
     px, pz, core = where[0], where[1], where[2]
     half, other = half_ref[...].astype(f32), other_ref[...].astype(f32)
     rows = jnp.concatenate(
@@ -284,6 +305,7 @@
     for k in range(4):
         outs[k][:, :, :FF] = gate[:, k]
         outs[k][:, :, 2 * FF :] = tail[:, k]
+    bring.wait()
     up = jnp.dot(scaled, wu_ref[...], preferred_element_type=f32).astype(bf16)
     up = up.reshape(4, 4, 16, FF)
     for k in range(4):
@@ -365,13 +387,6 @@
         scalars=2,
     )
     got = [sent[0]] + [send_dp(sent[k], 0, k) for k in (1, 2, 3)]
-    groups = call(regroup_kernel, "regroup", [shape(8, 288, 128)] * 4, got)
-    arrived = {0: groups[0]}
-    for k in (2, 1, 3):
-        arrived[k] = send_dp(groups[k], 1, k)
-    pieces = []
-    for k in (0, 2, 1, 3):
-        pieces += [arrived[k], swap_core(arrived[k])]
 
     prompt = lax.dynamic_slice_in_dim(row_prompt, replica * 16, 1, 0)[0]
     home = lax.dynamic_slice_in_dim(block_home, prompt * PB, PB, 0)
@@ -398,15 +413,21 @@
     key = jnp.where(need, holder * 2 + rank, -1)
     hit = key[:, None] == want_key[None, :]
     use = jnp.dot(sel.astype(bf16), hit.astype(bf16), preferred_element_type=f32).astype(bf16)
-    token = jnp.arange(4096, dtype=i32)
-    slot_of = (token // 1024) * 16 + (token // 32) % 16
-    spread = (jnp.arange(64, dtype=i32)[:, None] == slot_of[None, :]).astype(bf16)
-    bias = (jnp.dot(use, spread, preferred_element_type=f32) - 1.0) * -NEG
-
+    use = use.reshape(16, 4, 16).transpose(1, 0, 2)
+
+    got[0], use = lax.optimization_barrier((got[0], use))
+    groups = call(regroup_kernel, "regroup", [shape(8, 288, 128)] * 4, got)
+    arrived = {0: groups[0]}
+    for k in (2, 1, 3):
+        arrived[k] = send_dp(groups[k], 1, k)
+    pieces = {k: [arrived[k], swap_core(arrived[k])] for k in (0, 2, 1, 3)}
     y = lane // 2
+    carry = attend(y.reshape(1), q_all, use[0:1], pieces[0], last=False)
+    carry = attend(y.reshape(1), q_all, use[1:2], pieces[2], carry, last=False)
     parts = []
     for k in (2, 1, 3, 0):
-        (o,) = attend((y ^ k).reshape(1), q_all, bias, pieces)
+        index = (y ^ k).reshape(1)
+        (o,) = attend(index, q_all, use[2:4], pieces[1] + pieces[3], carry)
         parts.append(send_y(o, k) if k else o)
     per_head = merge(parts, q, own, value_up)
 
@@ -436,7 +457,9 @@
         [shape(16, 16, 448)] + [shape(4, 16, 2 * FF + 128)] * 4,
         [where, half, other, norm_gain.reshape(1, 448), gate_weight, up_weight],
         scalars=1,
+        anys=1,
         limit=30,
+        scratch_shapes=[pltpu.VMEM((448, FF), bf16), pltpu.SemaphoreType.DMA(())],
     )
     got = [sums[0]] + [send_dp(sums[k], 0, k) for k in (2, 1, 3)]
     sums = call(fold_kernel, "fold", [shape(16, 2 * FF + 128)] * 4, got)

time: 167 us -> 172 us (1.030)
  Pallas kernels: 27.6 us -> 31.6 us
  other arithmetic: 3.27 us -> 6.14 us
  local copies, waits for them, and re-layouts: 9.21 us -> 11.1 us
    pallas_call x11 -> x13, Pallas kernels: 26.9 us -> 30.7 us  [call(): pl.pallas_call(kernel, out_shape=outs, in_specs=[SMEM] * scalars + [VMEM]...]
    ppermute x18, waiting for transfers between devices: 52.8 us -> 51 us  [send_dp(): return lax.ppermute(x, ('dp', 'tp'), pairs)]
    unnamed x34 -> x32, local copies, waits for them, and re-layouts: 4.86 us -> 5.79 us
  transfers between devices with their start and end apart: 31 -> 31, of which waited for: 22 -> 21; matrix products, arithmetic and copies ran while one was open for 5% -> 4% of each run, Pallas kernels for 10% -> 11%
where the time goes in v4:
time: 172 us; the launch traced here: 171 us
  waiting for transfers between devices  67.9 us (39%)
  starting transfers between devices  39.4 us (23%)
  Pallas kernels  31.6 us (18%)
  between operations  15.1 us (9%)
  local copies, waits for them, and re-layouts  11.1 us (6%)
  other arithmetic  6.14 us (4%)
    ppermute x18, waiting for transfers between devices, send_dp(): return lax.ppermute(x, ('dp', 'tp'), pairs)  51 us
    pallas_call x13, Pallas kernels, call(): pl.pallas_call(kernel, out_shape=outs, in_specs=[SMEM] * scalars + [VMEM]...  30.7 us
    ppermute x18, starting transfers between devices, send_dp(): return lax.ppermute(x, ('dp', 'tp'), pairs)  29.2 us
    ppermute x12, waiting for transfers between devices, send(): return lax.ppermute(x, axis, [(i, to(i)) for i in range(n)])  16.9 us
    ppermute x12, starting transfers between devices, send(): return lax.ppermute(x, axis, [(i, to(i)) for i in range(n)])  10.1 us
    unnamed x32, local copies, waits for them, and re-layouts  5.79 us
  transfers between devices with their start and end apart: 31, of which 21 were waited for; matrix products, arithmetic and copies ran while one was open for 4% of the time, Pallas kernels for 11%

profile of v4, /device:TPU:0, one launch (start us, length us, event | category | flops | bytes accessed | tf_op | source)
XLA Modules:
  0.0 171.5 jit_solution(15802198800003574773)
XLA Ops:
  7.3 0.7 broadcast_multiply_fusion
  8.0 0.8 broadcast_add_fusion
  8.9 0.9 select_reduce_fusion.2
  10.9 2.7 %reshape.163.tokens = bf16[16,64,576]{2,1,0:T(8,128)(2,1)S(1)} reshape(bf16[16,36864]{1,0:T(8,128)(2,1)} %param.17) | data formatting | bytes 2359296 | tf_op jit(solution)/shard_map/reshape | solution.py:386
  13.7 2.0 %fetch.1 = (bf16[8,288,128]{2,1,0:T(8,128)(2,1)S(1)}, bf16[8,288,128]{2,1,0:T(8,128)(2,1)}, bf16[8,288,128]{2,1,0:T(8,128)(2,1)}, bf16[8,288,128]{2,1,0:T(8,128)(2,1)S(1)}) custom-call(s32[3]{0:T(128)S(1)} %pad_add_fusion.where, s32[32]{0:T(128)S(1)} %reshape.162.picks, bf16[16,64,576]{2,1,0:T(8,128)(2,1)S(1)} %reshape.163.tokens), custom_call_target="tpu_custom_call" | custom-call | tf_op jit(solution)/shard_map/fetch/pallas_call | solution.py:58
  15.7 1.6 collective-permute-start
  17.3 2.7 %collective-permute-start.1 = (bf16[8,288,128]{2,1,0:T(8,128)(2,1)}, bf16[8,288,128]{2,1,0:T(8,128)(2,1)S(1)}, u32[]{:S(2)}, u32[]{:S(2)}) collective-permute-start(bf16[8,288,128]{2,1,0:T(8,128)(2,1)} %get-tuple-element.31), channel_id=1, source_target_pairs={{0,64},{1,17},{2,66},{3,19},{4,68},{5,21},{6,70},{7,23},{8,72},{9,... | collective-permute-start | bytes 1769480 | tf_op jit(solution)/shard_map/ppermute | solution.py:49
  20.0 1.4 collective-permute-start.2
  21.5 1.2 reshape.160
  22.8 0.8 pad_maximum_fusion.q_ref
  23.7 0.6 dynamic_slice.10
  25.4 0.8 add_select_fusion
  27.4 7.0 %collective-permute-done.1.refs_2_ = bf16[8,288,128]{2,1,0:T(8,128)(2,1)S(1)} collective-permute-done((bf16[8,288,128]{2,1,0:T(8,128)(2,1)}, bf16[8,288,128]{2,1,0:T(8,128)(2,1)S(1)}, u32[]{:S(2)}, u32[]{:S(2)}) %collective-permute-start.1) | collective-permute-done | bytes 589856 | tf_op jit(solution)/shard_map/ppermute | solution.py:49
  34.4 1.3 regroup.1
  35.7 3.9 %collective-permute-start.7 = (bf16[8,288,128]{2,1,0:T(8,128)(2,1)S(1)}, bf16[8,288,128]{2,1,0:T(8,128)(2,1)S(1)}, u32[]{:S(2)}, u32[]{:S(2)}) collective-permute-start(bf16[8,288,128]{2,1,0:T(8,128)(2,1)S(1)} %get-tuple-element.35), channel_id=1, source_target_pairs={{0,16},{1,65},{2,18},{3,67},{4,20},{5,69},{6,22},{7,71},{8,24},{9,... | collective-permute-start | bytes 1769480 | tf_op jit(solution)/shard_map/ppermute | solution.py:49
  39.6 1.0 collective-permute-start.3
  40.6 2.2 %collective-permute-start.5 = (bf16[8,288,128]{2,1,0:T(8,128)(2,1)}, bf16[8,288,128]{2,1,0:T(8,128)(2,1)S(1)}, u32[]{:S(2)}, u32[]{:S(2)}) collective-permute-start(bf16[8,288,128]{2,1,0:T(8,128)(2,1)} %get-tuple-element.34), channel_id=1, source_target_pairs={{0,24},{1,97},{2,26},{3,99},{4,28},{5,101},{6,30},{7,103},{8,0},{9... | collective-permute-start | bytes 1769480 | tf_op jit(solution)/shard_map/ppermute | solution.py:49
  42.8 4.7 %collective-permute-done.7.refs_3_ = bf16[8,288,128]{2,1,0:T(8,128)(2,1)S(1)} collective-permute-done((bf16[8,288,128]{2,1,0:T(8,128)(2,1)S(1)}, bf16[8,288,128]{2,1,0:T(8,128)(2,1)S(1)}, u32[]{:S(2)}, u32[]{:S(2)}) %collective-permute-start.7) | collective-permute-done | bytes 589856 | tf_op jit(solution)/shard_map/ppermute | solution.py:49
  47.6 6.2 %collective-permute-done.3.refs_3_ = bf16[8,288,128]{2,1,0:T(8,128)(2,1)S(1)} collective-permute-done((bf16[8,288,128]{2,1,0:T(8,128)(2,1)}, bf16[8,288,128]{2,1,0:T(8,128)(2,1)S(1)}, u32[]{:S(2)}, u32[]{:S(2)}) %collective-permute-start.3) | collective-permute-done | bytes 589856 | tf_op jit(solution)/shard_map/ppermute | solution.py:49
  53.8 1.1 collective-permute-done.5.refs_5_
  54.8 0.8 copy-done.7
  55.7 1.3 copy-done.5
  57.0 1.1 copy-done.8
  58.0 4.4 %attend.6 = (f32[4,256,512]{2,1,0:T(8,128)S(1)}, f32[4,256,128]{2,1,0:T(8,128)S(1)}) custom-call(s32[1]{0:T(128)} %bitcast.10.refs_0_, bf16[4,256,640]{2,1,0:T(8,128)(2,1)S(1)} %bitcast.22, bf16[1,16,16]{2,1,0:T(8,128)(2,1)S(1)} %get-tuple-element.62.refs_2_, bf16[8,288,128]{2,1,0:T(8,128)(2,1)} %get-tuple-element.36.refs_3_, bf16[8,288,128]{2,1,0:T(8,128)(2,1)S(1)} %copy-done.8), custom_call_target="tpu_custom_call" | custom-call | flops 5368709120 | bytes 1179648 | tf_op jit(solution)/shard_map/attend/pallas_call | solution.py:58
  62.5 4.5 %attend.7 = (f32[4,256,512]{2,1,0:T(8,128)S(1)}, f32[4,256,128]{2,1,0:T(8,128)S(1)}) custom-call(s32[1]{0:T(128)} %bitcast.10.refs_0_, bf16[4,256,640]{2,1,0:T(8,128)(2,1)S(1)} %bitcast.23, bf16[1,16,16]{2,1,0:T(8,128)(2,1)S(1)} %get-tuple-element.63.refs_2_, bf16[8,288,128]{2,1,0:T(8,128)(2,1)S(1)} %collective-permute-done.7.refs_3_, ...), custom_call_target="tpu_custom_call" | custom-call | flops 5368709120 | bytes 1179648 | tf_op jit(solution)/shard_map/attend/pallas_call | solution.py:58
  67.0 3.1 %attend.10 = bf16[272,512]{1,0:T(8,128)(2,1)S(1)} custom-call(s32[1]{0:T(128)} %bitcast.12.refs_0_, bf16[4,256,640]{2,1,0:T(8,128)(2,1)S(1)} %bitcast.24, bf16[2,16,16]{2,1,0:T(8,128)(2,1)S(1)} %slice.19.refs_2_, bf16[8,288,128]{2,1,0:T(8,128)(2,1)S(1)} %collective-permute-done.3.refs_3_, bf16[8,288,128]{2,1,0:T(8,128)(2,1)} %collective-permute-done.4.refs_4_, ...), custom_call_target="tpu_custom_call" | custom-call | flops 2684354560 | bytes 2359296 | tf_op jit(solution)/shard_map/attend/pallas_call | solution.py:58
  70.1 3.1 %collective-permute-start.12 = (bf16[272,512]{1,0:T(8,128)(2,1)S(1)}, bf16[272,512]{1,0:T(8,128)(2,1)S(1)}, u32[]{:S(2)}, u32[]{:S(2)}) collective-permute-start(bf16[272,512]{1,0:T(8,128)(2,1)S(1)} %attend.10), channel_id=1, source_target_pairs={{0,6},{1,7},{2,4},{3,5},{4,2},{5,3},{6,0},{7,1},{8,14},{9,15},{10,... | collective-permute-start | bytes 835592 | tf_op jit(solution)/shard_map/ppermute | solution.py:29
  73.2 3.1 %attend.9 = bf16[272,512]{1,0:T(8,128)(2,1)S(1)} custom-call(s32[1]{0:T(128)} %bitcast.11.refs_0_, bf16[4,256,640]{2,1,0:T(8,128)(2,1)S(1)} %bitcast.25, bf16[2,16,16]{2,1,0:T(8,128)(2,1)S(1)} %slice.19.refs_2_, bf16[8,288,128]{2,1,0:T(8,128)(2,1)S(1)} %collective-permute-done.3.refs_3_, bf16[8,288,128]{2,1,0:T(8,128)(2,1)} %collective-permute-done.4.refs_4_, ...), custom_call_target="tpu_custom_call" | custom-call | flops 2684354560 | bytes 2359296 | tf_op jit(solution)/shard_map/attend/pallas_call | solution.py:58
  76.6 3.1 %attend.8 = bf16[272,512]{1,0:T(8,128)(2,1)S(1)} custom-call(s32[1]{0:T(128)} %bitcast.3.refs_0_, bf16[4,256,640]{2,1,0:T(8,128)(2,1)S(1)} %bitcast.26, bf16[2,16,16]{2,1,0:T(8,128)(2,1)S(1)} %slice.19.refs_2_, bf16[8,288,128]{2,1,0:T(8,128)(2,1)S(1)} %collective-permute-done.3.refs_3_, bf16[8,288,128]{2,1,0:T(8,128)(2,1)} %collective-permute-done.4.refs_4_, ...), custom_call_target="tpu_custom_call" | custom-call | flops 2684354560 | bytes 2359296 | tf_op jit(solution)/shard_map/attend/pallas_call | solution.py:58
  79.7 1.9 %collective-permute-start.10 = (bf16[272,512]{1,0:T(8,128)(2,1)S(1)}, bf16[272,512]{1,0:T(8,128)(2,1)S(1)}, u32[]{:S(2)}, u32[]{:S(2)}) collective-permute-start(bf16[272,512]{1,0:T(8,128)(2,1)S(1)} %attend.8), channel_id=1, source_target_pairs={{0,4},{1,5},{2,6},{3,7},{4,0},{5,1},{6,2},{7,3},{8,12},{9,13},{10,... | collective-permute-start | bytes 835592 | tf_op jit(solution)/shard_map/ppermute | solution.py:29
  81.6 3.3 %attend.11.o3 = bf16[272,512]{1,0:T(8,128)(2,1)S(1)} custom-call(s32[1]{0:T(128)} %bitcast.10.refs_0_, bf16[4,256,640]{2,1,0:T(8,128)(2,1)S(1)} %bitcast.27, bf16[2,16,16]{2,1,0:T(8,128)(2,1)S(1)} %slice.19.refs_2_, bf16[8,288,128]{2,1,0:T(8,128)(2,1)S(1)} %collective-permute-done.3.refs_3_, bf16[8,288,128]{2,1,0:T(8,128)(2,1)} %collective-permute-done.4.refs_4_, ...), custom_call_target="tpu_custom_call" | custom-call | flops 2684354560 | bytes 2359296 | tf_op jit(solution)/shard_map/attend/pallas_call | solution.py:58
  84.9 1.0 collective-permute-done.11.o1
  85.9 5.0 %collective-permute-done.10.o0 = bf16[272,512]{1,0:T(8,128)(2,1)S(1)} collective-permute-done((bf16[272,512]{1,0:T(8,128)(2,1)S(1)}, bf16[272,512]{1,0:T(8,128)(2,1)S(1)}, u32[]{:S(2)}, u32[]{:S(2)}) %collective-permute-start.10) | collective-permute-done | bytes 278560 | tf_op jit(solution)/shard_map/ppermute | solution.py:29
  90.9 0.9 merge.1
  91.8 2.6 %collective-permute-start.13 = (bf16[16,2048]{1,0:T(8,128)(2,1)S(1)}, bf16[16,2048]{1,0:T(8,128)(2,1)S(1)}, u32[]{:S(2)}, u32[]{:S(2)}) collective-permute-start(bf16[16,2048]{1,0:T(8,128)(2,1)S(1)} %merge.1), channel_id=1, source_target_pairs={{0,96},{1,25},{2,98},{3,27},{4,100},{5,29},{6,102},{7,31},{8,104},... | collective-permute-start | bytes 196616 | tf_op jit(solution)/shard_map/ppermute | solution.py:49
  94.4 1.2 collective-permute-start.14
  95.6 0.6 collective-permute-start.15
  96.3 3.9 %collective-permute-done.14 = bf16[16,2048]{1,0:T(8,128)(2,1)S(1)} collective-permute-done((bf16[16,2048]{1,0:T(8,128)(2,1)S(1)}, bf16[16,2048]{1,0:T(8,128)(2,1)S(1)}, u32[]{:S(2)}, u32[]{:S(2)}) %collective-permute-start.14) | collective-permute-done | bytes 65568 | tf_op jit(solution)/shard_map/ppermute | solution.py:49
  100.2 0.9 collective-permute-done.15
  101.1 2.7 %collective-permute-start.16 = (bf16[64,2048]{1,0:T(8,128)(2,1)S(1)}, bf16[64,2048]{1,0:T(8,128)(2,1)S(1)}, u32[]{:S(2)}, u32[]{:S(2)}) collective-permute-start(bf16[64,2048]{1,0:T(8,128)(2,1)S(1)} %pad_maximum_fusion.1.p0), channel_id=1, source_target_pairs={{0,24},{1,97},{2,26},{3,99},{4,28},{5,101},{6,30},{7,103},{8,0},{9... | collective-permute-start | bytes 786440 | tf_op jit(solution)/shard_map/ppermute | solution.py:49
  104.8 5.7 %collective-permute-done.16.p1 = bf16[64,2048]{1,0:T(8,128)(2,1)S(1)} collective-permute-done((bf16[64,2048]{1,0:T(8,128)(2,1)S(1)}, bf16[64,2048]{1,0:T(8,128)(2,1)S(1)}, u32[]{:S(2)}, u32[]{:S(2)}) %collective-permute-start.16) | collective-permute-done | bytes 262176 | tf_op jit(solution)/shard_map/ppermute | solution.py:49
  110.5 1.2 collective-permute-done.17.p2
  111.8 2.7 %collective-permute-done.18.p3 = bf16[64,2048]{1,0:T(8,128)(2,1)S(1)} collective-permute-done((bf16[64,2048]{1,0:T(8,128)(2,1)S(1)}, bf16[64,2048]{1,0:T(8,128)(2,1)S(1)}, u32[]{:S(2)}, u32[]{:S(2)}) %collective-permute-start.18) | collective-permute-done | bytes 262176 | tf_op jit(solution)/shard_map/ppermute | solution.py:49
  114.5 1.3 project.1
  115.9 1.3 collective-permute-done.19
  117.2 1.1 collective-permute-start.20
  118.3 3.4 %collective-permute-start.21 = (bf16[2,4,16,448]{3,2,1,0:T(8,128)(2,1)S(1)}, bf16[2,4,16,448]{3,2,1,0:T(8,128)(2,1)S(1)}, u32[]{:S(2)}, u32[]{:S(2)}) collective-permute-start(bf16[2,4,16,448]{3,2,1,0:T(8,128)(2,1)S(1)} %add_convert_fusion.pair), channel_id=1, source_target_pairs={{0,4},{1,5},{2,6},{3,7},{4,0},{5,1},{6,2},{7,3},{8,12},{9,13},{10,... | collective-permute-start | bytes 344072 | tf_op jit(solution)/shard_map/ppermute | solution.py:29
  122.2 1.5 collective-permute-done.20.t1
  123.7 4.5 %collective-permute-done.21.t2 = bf16[2,4,16,448]{3,2,1,0:T(8,128)(2,1)S(1)} collective-permute-done((bf16[2,4,16,448]{3,2,1,0:T(8,128)(2,1)S(1)}, bf16[2,4,16,448]{3,2,1,0:T(8,128)(2,1)S(1)}, u32[]{:S(2)}, u32[]{:S(2)}) %collective-permute-start.21) | collective-permute-done | bytes 114720 | tf_op jit(solution)/shard_map/ppermute | solution.py:29
  128.2 2.2 %collective-permute-done.22.t3 = bf16[2,4,16,448]{3,2,1,0:T(8,128)(2,1)S(1)} collective-permute-done((bf16[2,4,16,448]{3,2,1,0:T(8,128)(2,1)S(1)}, bf16[2,4,16,448]{3,2,1,0:T(8,128)(2,1)S(1)}, u32[]{:S(2)}, u32[]{:S(2)}) %collective-permute-start.22) | collective-permute-done | bytes 114720 | tf_op jit(solution)/shard_map/ppermute | solution.py:29
  130.4 0.6 join.1.half_ref
  131.2 1.3 collective-permute-done.23.other_ref
  132.5 1.6 copy-done.3
  134.1 2.7 %ffn.1 = (bf16[16,16,448]{2,1,0:T(8,128)(2,1)S(1)}, bf16[4,16,4736]{2,1,0:T(8,128)(2,1)S(1)}, bf16[4,16,4736]{2,1,0:T(8,128)(2,1)S(1)}, bf16[4,16,4736]{2,1,0:T(8,128)(2,1)S(1)}, bf16[4,16,4736]{2,1,0:T(8,128)(2,1)S(1)}) custom-call(s32[3]{0:T(128)S(1)} %pad_add_fusion.where, bf16[2,4,16,448]{3,2,1,0:T(8,128)(2,1)S(1)} %join.1.half_ref, ...), custom_call_target="tpu_custom_call" | custom-call | tf_op jit(solution)/shard_map/ffn/pallas_call | solution.py:58
  136.8 1.2 collective-permute-start.24
  138.0 3.1 %collective-permute-start.26 = (bf16[4,16,4736]{2,1,0:T(8,128)(2,1)S(1)}, bf16[4,16,4736]{2,1,0:T(8,128)(2,1)S(1)}, u32[]{:S(2)}, u32[]{:S(2)}) collective-permute-start(bf16[4,16,4736]{2,1,0:T(8,128)(2,1)S(1)} %get-tuple-element.47), channel_id=1, source_target_pairs={{0,96},{1,25},{2,98},{3,27},{4,100},{5,29},{6,102},{7,31},{8,104},... | collective-permute-start | bytes 1818632 | tf_op jit(solution)/shard_map/ppermute | solution.py:49
  141.2 7.3 %collective-permute-done.24.refs_1_ = bf16[4,16,4736]{2,1,0:T(8,128)(2,1)S(1)} collective-permute-done((bf16[4,16,4736]{2,1,0:T(8,128)(2,1)S(1)}, bf16[4,16,4736]{2,1,0:T(8,128)(2,1)S(1)}, u32[]{:S(2)}, u32[]{:S(2)}) %collective-permute-start.24) | collective-permute-done | bytes 606240 | tf_op jit(solution)/shard_map/ppermute | solution.py:49
  148.5 6.4 %collective-permute-done.25.refs_2_ = bf16[4,16,4736]{2,1,0:T(8,128)(2,1)S(1)} collective-permute-done((bf16[4,16,4736]{2,1,0:T(8,128)(2,1)S(1)}, bf16[4,16,4736]{2,1,0:T(8,128)(2,1)S(1)}, u32[]{:S(2)}, u32[]{:S(2)}) %collective-permute-start.25) | collective-permute-done | bytes 606240 | tf_op jit(solution)/shard_map/ppermute | solution.py:49
  156.0 1.0 collective-permute-start.28
  157.0 2.2 %collective-permute-start.29 = (bf16[16,4736]{1,0:T(8,128)(2,1)S(1)}, bf16[16,4736]{1,0:T(8,128)(2,1)S(1)}, u32[]{:S(2)}, u32[]{:S(2)}) collective-permute-start(bf16[16,4736]{1,0:T(8,128)(2,1)S(1)} %get-tuple-element.51), channel_id=1, source_target_pairs={{0,24},{1,97},{2,26},{3,99},{4,28},{5,101},{6,30},{7,103},{8,0},{9... | collective-permute-start | bytes 454664 | tf_op jit(solution)/shard_map/ppermute | solution.py:49
  159.2 0.8 copy.33
  160.0 2.3 %collective-permute-done.27.r1 = bf16[16,4736]{1,0:T(8,128)(2,1)S(1)} collective-permute-done((bf16[16,4736]{1,0:T(8,128)(2,1)S(1)}, bf16[16,4736]{1,0:T(8,128)(2,1)S(1)}, u32[]{:S(2)}, u32[]{:S(2)}) %collective-permute-start.27) | collective-permute-done | bytes 151584 | tf_op jit(solution)/shard_map/ppermute | solution.py:49
  162.3 1.5 collective-permute-done.28.r2
  163.8 0.8 finish.1
  (86 shorter events, 6.5 us)
Async XLA Ops:
  7.2 48.5 %all-gather.3.cloned.1.call-start = ((), (), s32[]{:S(2)}) async-start(), calls=%async_computation | async-start | bytes 1638400 | tf_op jit(solution)/shard_map/all_gather | solution.py:366
  13.6 10.1 %copy-start.13 = (s32[256]{0:T(256)S(1)}, s32[256]{0:T(256)}, u32[]{:S(2)}) copy-start(s32[256]{0:T(256)} %param.19) | copy-start | bytes 3076
  13.6 11.3 %copy-start.14 = (s32[4]{0:T(128)S(1)}, s32[4]{0:T(128)}, u32[]{:S(2)}) copy-start(s32[4]{0:T(128)} %constant.103.clone) | copy-start | bytes 52
  13.6 11.4 %copy-start.10 = (s32[256,32]{0,1:T(8,128)S(1)}, s32[256,32]{0,1:T(8,128)}, u32[]{:S(2)}) copy-start(s32[256,32]{0,1:T(8,128)} %param.20) | copy-start | bytes 98308
  15.7 11.7 %collective-permute-start = (bf16[8,288,128]{2,1,0:T(8,128)(2,1)}, bf16[8,288,128]{2,1,0:T(8,128)(2,1)S(1)}, u32[]{:S(2)}, u32[]{:S(2)}) collective-permute-start(bf16[8,288,128]{2,1,0:T(8,128)(2,1)} %get-tuple-element.30), channel_id=1, source_target_pairs={{0,32},{1,9},{2,34},{3,11},{4,36},{5,13},{6,38},{7,15},{8,40},{9,1... | collective-permute-start | bytes 1769480 | tf_op jit(solution)/shard_map/ppermute | solution.py:49
  17.3 17.1 %collective-permute-start.1 = (bf16[8,288,128]{2,1,0:T(8,128)(2,1)}, bf16[8,288,128]{2,1,0:T(8,128)(2,1)S(1)}, u32[]{:S(2)}, u32[]{:S(2)}) collective-permute-start(bf16[8,288,128]{2,1,0:T(8,128)(2,1)} %get-tuple-element.31), channel_id=1, source_target_pairs={{0,64},{1,17},{2,66},{3,19},{4,68},{5,21},{6,70},{7,23},{8,72},{9,... | collective-permute-start | bytes 1769480 | tf_op jit(solution)/shard_map/ppermute | solution.py:49
  20.0 14.4 %collective-permute-start.2 = (bf16[8,288,128]{2,1,0:T(8,128)(2,1)S(1)}, bf16[8,288,128]{2,1,0:T(8,128)(2,1)S(1)}, u32[]{:S(2)}, u32[]{:S(2)}) collective-permute-start(bf16[8,288,128]{2,1,0:T(8,128)(2,1)S(1)} %get-tuple-element.32), channel_id=1, source_target_pairs={{0,96},{1,25},{2,98},{3,27},{4,100},{5,29},{6,102},{7,31},{8,104},... | collective-permute-start | bytes 1769480 | tf_op jit(solution)/shard_map/ppermute | solution.py:49
  35.7 11.8 %collective-permute-start.7 = (bf16[8,288,128]{2,1,0:T(8,128)(2,1)S(1)}, bf16[8,288,128]{2,1,0:T(8,128)(2,1)S(1)}, u32[]{:S(2)}, u32[]{:S(2)}) collective-permute-start(bf16[8,288,128]{2,1,0:T(8,128)(2,1)S(1)} %get-tuple-element.35), channel_id=1, source_target_pairs={{0,16},{1,65},{2,18},{3,67},{4,20},{5,69},{6,22},{7,71},{8,24},{9,... | collective-permute-start | bytes 1769480 | tf_op jit(solution)/shard_map/ppermute | solution.py:49
  39.6 14.2 %collective-permute-start.3 = (bf16[8,288,128]{2,1,0:T(8,128)(2,1)}, bf16[8,288,128]{2,1,0:T(8,128)(2,1)S(1)}, u32[]{:S(2)}, u32[]{:S(2)}) collective-permute-start(bf16[8,288,128]{2,1,0:T(8,128)(2,1)} %get-tuple-element.33), channel_id=1, source_target_pairs={{0,8},{1,33},{2,10},{3,35},{4,12},{5,37},{6,14},{7,39},{8,16},{9,4... | collective-permute-start | bytes 1769480 | tf_op jit(solution)/shard_map/ppermute | solution.py:49
  40.6 14.2 %collective-permute-start.5 = (bf16[8,288,128]{2,1,0:T(8,128)(2,1)}, bf16[8,288,128]{2,1,0:T(8,128)(2,1)S(1)}, u32[]{:S(2)}, u32[]{:S(2)}) collective-permute-start(bf16[8,288,128]{2,1,0:T(8,128)(2,1)} %get-tuple-element.34), channel_id=1, source_target_pairs={{0,24},{1,97},{2,26},{3,99},{4,28},{5,101},{6,30},{7,103},{8,0},{9... | collective-permute-start | bytes 1769480 | tf_op jit(solution)/shard_map/ppermute | solution.py:49
  42.8 12.0 %collective-permute-start.9 = (bf16[8,288,128]{2,1,0:T(8,128)(2,1)}, bf16[8,288,128]{2,1,0:T(8,128)(2,1)S(1)}, u32[]{:S(2)}, u32[]{:S(2)}) collective-permute-start(bf16[8,288,128]{2,1,0:T(8,128)(2,1)} %get-tuple-element.36.refs_3_), channel_id=1, source_target_pairs={{0,1},{1,0},{2,3},{3,2},{4,5},{5,4},{6,7},{7,6},{8,9},{9,8},{10,11... | collective-permute-start | bytes 1769480 | tf_op jit(solution)/shard_map/ppermute | solution.py:29
  47.6 14.9 %collective-permute-start.8 = (bf16[8,288,128]{2,1,0:T(8,128)(2,1)S(1)}, bf16[8,288,128]{2,1,0:T(8,128)(2,1)}, u32[]{:S(2)}, u32[]{:S(2)}) collective-permute-start(bf16[8,288,128]{2,1,0:T(8,128)(2,1)S(1)} %collective-permute-done.7.refs_3_), channel_id=1, source_target_pairs={{0,1},{1,0},{2,3},{3,2},{4,5},{5,4},{6,7},{7,6},{8,9},{9,8},{10,11... | collective-permute-start | bytes 1769480 | tf_op jit(solution)/shard_map/ppermute | solution.py:29
  53.8 13.2 %collective-permute-start.4 = (bf16[8,288,128]{2,1,0:T(8,128)(2,1)S(1)}, bf16[8,288,128]{2,1,0:T(8,128)(2,1)}, u32[]{:S(2)}, u32[]{:S(2)}) collective-permute-start(bf16[8,288,128]{2,1,0:T(8,128)(2,1)S(1)} %collective-permute-done.3.refs_3_), channel_id=1, source_target_pairs={{0,1},{1,0},{2,3},{3,2},{4,5},{5,4},{6,7},{7,6},{8,9},{9,8},{10,11... | collective-permute-start | bytes 1769480 | tf_op jit(solution)/shard_map/ppermute | solution.py:29
  54.8 12.2 %collective-permute-start.6 = (bf16[8,288,128]{2,1,0:T(8,128)(2,1)S(1)}, bf16[8,288,128]{2,1,0:T(8,128)(2,1)}, u32[]{:S(2)}, u32[]{:S(2)}) collective-permute-start(bf16[8,288,128]{2,1,0:T(8,128)(2,1)S(1)} %collective-permute-done.5.refs_5_), channel_id=1, source_target_pairs={{0,1},{1,0},{2,3},{3,2},{4,5},{5,4},{6,7},{7,6},{8,9},{9,8},{10,11... | collective-permute-start | bytes 1769480 | tf_op jit(solution)/shard_map/ppermute | solution.py:29
  54.8 0.8 copy-start.7
  55.7 1.3 copy-start.5
  57.0 1.1 copy-start.8
  58.0 4.5 %copy-start.6 = (bf16[1024,640]{1,0:T(8,128)(2,1)S(1)}, bf16[1024,640]{1,0:T(8,128)(2,1)}, u32[]{:S(2)}) copy-start(bf16[1024,640]{1,0:T(8,128)(2,1)} %all-gather.3.cloned.1.call-done) | copy-start | bytes 3932164
  70.1 14.8 %collective-permute-start.12 = (bf16[272,512]{1,0:T(8,128)(2,1)S(1)}, bf16[272,512]{1,0:T(8,128)(2,1)S(1)}, u32[]{:S(2)}, u32[]{:S(2)}) collective-permute-start(bf16[272,512]{1,0:T(8,128)(2,1)S(1)} %attend.10), channel_id=1, source_target_pairs={{0,6},{1,7},{2,4},{3,5},{4,2},{5,3},{6,0},{7,1},{8,14},{9,15},{10,... | collective-permute-start | bytes 835592 | tf_op jit(solution)/shard_map/ppermute | solution.py:29
  76.3 9.6 %collective-permute-start.11 = (bf16[272,512]{1,0:T(8,128)(2,1)S(1)}, bf16[272,512]{1,0:T(8,128)(2,1)S(1)}, u32[]{:S(2)}, u32[]{:S(2)}) collective-permute-start(bf16[272,512]{1,0:T(8,128)(2,1)S(1)} %attend.9), channel_id=1, source_target_pairs={{0,2},{1,3},{2,0},{3,1},{4,6},{5,7},{6,4},{7,5},{8,10},{9,11},{10,... | collective-permute-start | bytes 835592 | tf_op jit(solution)/shard_map/ppermute | solution.py:29
  76.5 5.0 %copy-start.11 = (bf16[16,576]{1,0:T(8,128)(2,1)S(1)}, bf16[16,576]{1,0:T(8,128)(2,1)}, u32[]{:S(2)}) copy-start(bf16[16,576]{1,0:T(8,128)(2,1)} %param.16) | copy-start | bytes 55300
  76.6 5.0 %slice-start = ((bf16[16,576]{1,0:T(8,128)(2,1)}), bf16[16,64]{1,0:T(8,128)(2,1)S(1)}, s32[]{:S(2)}) async-start(bf16[16,576]{1,0:T(8,128)(2,1)} %param.16), calls=%async_computation.1 | async-start | bytes 8192 | tf_op jit(solution)/shard_map/slice | solution.py:364
  79.7 11.2 %collective-permute-start.10 = (bf16[272,512]{1,0:T(8,128)(2,1)S(1)}, bf16[272,512]{1,0:T(8,128)(2,1)S(1)}, u32[]{:S(2)}, u32[]{:S(2)}) collective-permute-start(bf16[272,512]{1,0:T(8,128)(2,1)S(1)} %attend.8), channel_id=1, source_target_pairs={{0,4},{1,5},{2,6},{3,7},{4,0},{5,1},{6,2},{7,3},{8,12},{9,13},{10,... | collective-permute-start | bytes 835592 | tf_op jit(solution)/shard_map/ppermute | solution.py:29
  81.6 9.3 %copy-start = (bf16[256,640]{1,0:T(8,128)(2,1)S(1)}, bf16[256,640]{1,0:T(8,128)(2,1)}, u32[]{:S(2)}) copy-start(bf16[256,640]{1,0:T(8,128)(2,1)} %pad_maximum_fusion.q_ref) | copy-start | bytes 983044
  81.6 9.3 %copy-start.1 = (bf16[16,512,128]{2,1,0:T(8,128)(2,1)S(1)}, bf16[16,512,128]{2,1,0:T(8,128)(2,1)}, u32[]{:S(2)}) copy-start(bf16[16,512,128]{2,1,0:T(8,128)(2,1)} %up_ref.1) | copy-start | bytes 6291460
  84.9 29.6 %copy-start.4 = (bf16[2048,448]{0,1:T(8,128)(2,1)S(1)}, bf16[2048,448]{0,1:T(8,128)(2,1)}, u32[]{:S(2)}) copy-start(bf16[2048,448]{0,1:T(8,128)(2,1)} %param.22) | copy-start | bytes 5505028
  91.8 30.3 %copy-start.9 = (bf16[256,448]{0,1:T(8,128)(2,1)S(1)}, bf16[256,448]{0,1:T(8,128)(2,1)}, u32[]{:S(2)}) copy-start(bf16[256,448]{0,1:T(8,128)(2,1)} %param.23) | copy-start | bytes 688132
  91.8 4.5 %collective-permute-start.13 = (bf16[16,2048]{1,0:T(8,128)(2,1)S(1)}, bf16[16,2048]{1,0:T(8,128)(2,1)S(1)}, u32[]{:S(2)}, u32[]{:S(2)}) collective-permute-start(bf16[16,2048]{1,0:T(8,128)(2,1)S(1)} %merge.1), channel_id=1, source_target_pairs={{0,96},{1,25},{2,98},{3,27},{4,100},{5,29},{6,102},{7,31},{8,104},... | collective-permute-start | bytes 196616 | tf_op jit(solution)/shard_map/ppermute | solution.py:49
  94.4 5.8 %collective-permute-start.14 = (bf16[16,2048]{1,0:T(8,128)(2,1)S(1)}, bf16[16,2048]{1,0:T(8,128)(2,1)S(1)}, u32[]{:S(2)}, u32[]{:S(2)}) collective-permute-start(bf16[16,2048]{1,0:T(8,128)(2,1)S(1)} %merge.1), channel_id=1, source_target_pairs={{0,64},{1,17},{2,66},{3,19},{4,68},{5,21},{6,70},{7,23},{8,72},{9,... | collective-permute-start | bytes 196616 | tf_op jit(solution)/shard_map/ppermute | solution.py:49
  95.6 5.5 %collective-permute-start.15 = (bf16[16,2048]{1,0:T(8,128)(2,1)S(1)}, bf16[16,2048]{1,0:T(8,128)(2,1)S(1)}, u32[]{:S(2)}, u32[]{:S(2)}) collective-permute-start(bf16[16,2048]{1,0:T(8,128)(2,1)S(1)} %merge.1), channel_id=1, source_target_pairs={{0,32},{1,9},{2,34},{3,11},{4,36},{5,13},{6,38},{7,15},{8,40},{9,1... | collective-permute-start | bytes 196616 | tf_op jit(solution)/shard_map/ppermute | solution.py:49
  101.1 9.4 %collective-permute-start.16 = (bf16[64,2048]{1,0:T(8,128)(2,1)S(1)}, bf16[64,2048]{1,0:T(8,128)(2,1)S(1)}, u32[]{:S(2)}, u32[]{:S(2)}) collective-permute-start(bf16[64,2048]{1,0:T(8,128)(2,1)S(1)} %pad_maximum_fusion.1.p0), channel_id=1, source_target_pairs={{0,24},{1,97},{2,26},{3,99},{4,28},{5,101},{6,30},{7,103},{8,0},{9... | collective-permute-start | bytes 786440 | tf_op jit(solution)/shard_map/ppermute | solution.py:49
  103.8 8.0 %collective-permute-start.17 = (bf16[64,2048]{1,0:T(8,128)(2,1)S(1)}, bf16[64,2048]{1,0:T(8,128)(2,1)S(1)}, u32[]{:S(2)}, u32[]{:S(2)}) collective-permute-start(bf16[64,2048]{1,0:T(8,128)(2,1)S(1)} %pad_maximum_fusion.1.p0), channel_id=1, source_target_pairs={{0,16},{1,65},{2,18},{3,67},{4,20},{5,69},{6,22},{7,71},{8,24},{9,... | collective-permute-start | bytes 786440 | tf_op jit(solution)/shard_map/ppermute | solution.py:49
  104.3 10.2 %collective-permute-start.18 = (bf16[64,2048]{1,0:T(8,128)(2,1)S(1)}, bf16[64,2048]{1,0:T(8,128)(2,1)S(1)}, u32[]{:S(2)}, u32[]{:S(2)}) collective-permute-start(bf16[64,2048]{1,0:T(8,128)(2,1)S(1)} %pad_maximum_fusion.1.p0), channel_id=1, source_target_pairs={{0,8},{1,33},{2,10},{3,35},{4,12},{5,37},{6,14},{7,39},{8,16},{9,4... | collective-permute-start | bytes 786440 | tf_op jit(solution)/shard_map/ppermute | solution.py:49
  114.5 16.7 %copy-start.12 = (bf16[448]{0:T(512)(128)(2,1)S(1)}, bf16[448]{0:T(512)(128)(2,1)}, u32[]{:S(2)}) copy-start(bf16[448]{0:T(512)(128)(2,1)} %param.24) | copy-start | bytes 2692
  114.5 18.0 %copy-start.2 = (bf16[448,2304]{1,0:T(8,128)(2,1)S(1)}, bf16[448,2304]{1,0:T(8,128)(2,1)}, u32[]{:S(2)}) copy-start(bf16[448,2304]{1,0:T(8,128)(2,1)} %wg_ref.1) | copy-start | bytes 6193156
  115.8 1.4 collective-permute-start.19
  117.2 6.4 %collective-permute-start.20 = (bf16[2,4,16,448]{3,2,1,0:T(8,128)(2,1)S(1)}, bf16[2,4,16,448]{3,2,1,0:T(8,128)(2,1)S(1)}, u32[]{:S(2)}, u32[]{:S(2)}) collective-permute-start(bf16[2,4,16,448]{3,2,1,0:T(8,128)(2,1)S(1)} %add_convert_fusion.pair), channel_id=1, source_target_pairs={{0,2},{1,3},{2,0},{3,1},{4,6},{5,7},{6,4},{7,5},{8,10},{9,11},{10,... | collective-permute-start | bytes 344072 | tf_op jit(solution)/shard_map/ppermute | solution.py:29
  118.3 9.9 %collective-permute-start.21 = (bf16[2,4,16,448]{3,2,1,0:T(8,128)(2,1)S(1)}, bf16[2,4,16,448]{3,2,1,0:T(8,128)(2,1)S(1)}, u32[]{:S(2)}, u32[]{:S(2)}) collective-permute-start(bf16[2,4,16,448]{3,2,1,0:T(8,128)(2,1)S(1)} %add_convert_fusion.pair), channel_id=1, source_target_pairs={{0,4},{1,5},{2,6},{3,7},{4,0},{5,1},{6,2},{7,3},{8,12},{9,13},{10,... | collective-permute-start | bytes 344072 | tf_op jit(solution)/shard_map/ppermute | solution.py:29
  121.7 8.7 %collective-permute-start.22 = (bf16[2,4,16,448]{3,2,1,0:T(8,128)(2,1)S(1)}, bf16[2,4,16,448]{3,2,1,0:T(8,128)(2,1)S(1)}, u32[]{:S(2)}, u32[]{:S(2)}) collective-permute-start(bf16[2,4,16,448]{3,2,1,0:T(8,128)(2,1)S(1)} %add_convert_fusion.pair), channel_id=1, source_target_pairs={{0,6},{1,7},{2,4},{3,5},{4,2},{5,3},{6,0},{7,1},{8,14},{9,15},{10,... | collective-permute-start | bytes 344072 | tf_op jit(solution)/shard_map/ppermute | solution.py:29
  131.0 1.4 collective-permute-start.23
  132.5 1.6 copy-start.3
  136.8 11.7 %collective-permute-start.24 = (bf16[4,16,4736]{2,1,0:T(8,128)(2,1)S(1)}, bf16[4,16,4736]{2,1,0:T(8,128)(2,1)S(1)}, u32[]{:S(2)}, u32[]{:S(2)}) collective-permute-start(bf16[4,16,4736]{2,1,0:T(8,128)(2,1)S(1)} %get-tuple-element.45), channel_id=1, source_target_pairs={{0,64},{1,17},{2,66},{3,19},{4,68},{5,21},{6,70},{7,23},{8,72},{9,... | collective-permute-start | bytes 1818632 | tf_op jit(solution)/shard_map/ppermute | solution.py:49
  138.0 16.9 %collective-permute-start.25 = (bf16[4,16,4736]{2,1,0:T(8,128)(2,1)S(1)}, bf16[4,16,4736]{2,1,0:T(8,128)(2,1)S(1)}, u32[]{:S(2)}, u32[]{:S(2)}) collective-permute-start(bf16[4,16,4736]{2,1,0:T(8,128)(2,1)S(1)} %get-tuple-element.46), channel_id=1, source_target_pairs={{0,32},{1,9},{2,34},{3,11},{4,36},{5,13},{6,38},{7,15},{8,40},{9,1... | collective-permute-start | bytes 1818632 | tf_op jit(solution)/shard_map/ppermute | solution.py:49
  138.0 16.9 %collective-permute-start.26 = (bf16[4,16,4736]{2,1,0:T(8,128)(2,1)S(1)}, bf16[4,16,4736]{2,1,0:T(8,128)(2,1)S(1)}, u32[]{:S(2)}, u32[]{:S(2)}) collective-permute-start(bf16[4,16,4736]{2,1,0:T(8,128)(2,1)S(1)} %get-tuple-element.47), channel_id=1, source_target_pairs={{0,96},{1,25},{2,98},{3,27},{4,100},{5,29},{6,102},{7,31},{8,104},... | collective-permute-start | bytes 1818632 | tf_op jit(solution)/shard_map/ppermute | solution.py:49
  155.4 6.9 %collective-permute-start.27 = (bf16[16,4736]{1,0:T(8,128)(2,1)S(1)}, bf16[16,4736]{1,0:T(8,128)(2,1)S(1)}, u32[]{:S(2)}, u32[]{:S(2)}) collective-permute-start(bf16[16,4736]{1,0:T(8,128)(2,1)S(1)} %get-tuple-element.49), channel_id=1, source_target_pairs={{0,16},{1,65},{2,18},{3,67},{4,20},{5,69},{6,22},{7,71},{8,24},{9,... | collective-permute-start | bytes 454664 | tf_op jit(solution)/shard_map/ppermute | solution.py:49
  156.0 7.9 %collective-permute-start.28 = (bf16[16,4736]{1,0:T(8,128)(2,1)S(1)}, bf16[16,4736]{1,0:T(8,128)(2,1)S(1)}, u32[]{:S(2)}, u32[]{:S(2)}) collective-permute-start(bf16[16,4736]{1,0:T(8,128)(2,1)S(1)} %get-tuple-element.50), channel_id=1, source_target_pairs={{0,8},{1,33},{2,10},{3,35},{4,12},{5,37},{6,14},{7,39},{8,16},{9,4... | collective-permute-start | bytes 454664 | tf_op jit(solution)/shard_map/ppermute | solution.py:49
  157.0 6.9 %collective-permute-start.29 = (bf16[16,4736]{1,0:T(8,128)(2,1)S(1)}, bf16[16,4736]{1,0:T(8,128)(2,1)S(1)}, u32[]{:S(2)}, u32[]{:S(2)}) collective-permute-start(bf16[16,4736]{1,0:T(8,128)(2,1)S(1)} %get-tuple-element.51), channel_id=1, source_target_pairs={{0,24},{1,97},{2,26},{3,99},{4,28},{5,101},{6,30},{7,103},{8,0},{9... | collective-permute-start | bytes 454664 | tf_op jit(solution)/shard_map/ppermute | solution.py:49
Sparse Core Ops, SparseCore 0:
  23.8 24.8 all-gather.2

commit v5 on v4

--- a/solution.py
+++ b/solution.py
@@ -77,12 +77,69 @@
     return ((px + kx) % 4) * 4 + (pz + kz) % 4
 
 
+def plan_kernel(where, prompts, home_ref, prompt_ref, chosen_ref, picks_ref, use_ref):
+    px, pz, core, lane = where[0], where[1], where[2], where[3]
+    replica = px * 4 + pz
+    i32 = jnp.int32
+    home = home_ref[...].reshape(16, 128)
+    ids = lax.broadcasted_iota(i32, (16, 128), 0) * 128 + lax.broadcasted_iota(i32, (16, 128), 1)
+    chosen = chosen_ref[...]
+    wanted = chosen + prompt_ref[...] * PB
+    asked = []
+    for slot in range(16):
+        found = home == (replica * 8 + lane) * 16 + slot
+        block = jnp.sum(jnp.where(found, ids, 0), axis=(0, 1), keepdims=True)
+        asked.append(jnp.max(jnp.where(wanted == block, 1.0, 0.0), axis=0, keepdims=True))
+    asked = jnp.concatenate(asked, axis=0).astype(bf16)
+    row = lax.broadcasted_iota(i32, (256, 128), 0)
+    owner = lax.broadcasted_iota(i32, (256, 128), 1)
+    owns = jnp.where(row // 16 == owner, 1.0, 0.0).astype(bf16)
+    needed = jnp.dot(asked, owns, preferred_element_type=f32) > 0.5
+    flag = jnp.where(needed, 1.0, 0.0)
+    slot = lax.broadcasted_iota(i32, (16, 128), 0)
+    low = lax.broadcasted_iota(i32, (16, 16), 0) > lax.broadcasted_iota(i32, (16, 16), 1)
+    low = jnp.where(low, 1.0, 0.0).astype(bf16)
+    before = jnp.dot(low, flag.astype(bf16), preferred_element_type=f32)
+    for rank in range(CAP):
+        pick = needed & (before > rank - 0.5) & (before < rank + 0.5)
+        picks_ref[rank : rank + 1] = jnp.sum(jnp.where(pick, slot, 0), axis=0, keepdims=True)
+
+    mine = pltpu.roll(chosen, (256 - replica * 16) % 256, 1)[:, :128]
+    mine = jnp.concatenate([mine.astype(f32), jnp.zeros((96, 128), f32)], axis=0).T[:16]
+    block = lax.broadcasted_iota(i32, (16, PB), 1).astype(f32)
+    uses = jnp.zeros((16, PB), f32)
+    for t in range(32):
+        uses = jnp.where(mine[:, t : t + 1] == block, 1.0, uses)
+    need = jnp.max(uses, axis=0, keepdims=True) > 0.5
+    here = home_ref[prompts[replica * 16]]
+    here = jnp.concatenate([here[i : i + 1] for i in range(4)], axis=1)
+    holder = here // 16
+    live = jnp.where(need, here, -1).astype(f32)
+    column = jnp.broadcast_to(live, (128, PB)).T[:, :1].astype(i32)
+    fewer = (column // 16 == holder) & (column < here) & (column >= 0)
+    rank = jnp.sum(jnp.where(fewer, 1, 0), axis=0, keepdims=True)
+    key = jnp.where(need, holder * CAP + rank, -1)
+    at = lax.broadcasted_iota(i32, (64, PB), 0)
+    kb = at // 16
+    kb = jnp.where(kb == 2, 3, jnp.where(kb == 3, 2, kb))
+    sib, ka, place = (at // 8) % 2, (at // 2) % 4, at % 2
+    from_core = core ^ sib
+    kx = jnp.where(from_core == 0, ka, kb)
+    kz = jnp.where(from_core == 0, kb, ka)
+    dev = (((px + 4 - kx) % 4) * 4 + (pz + 4 - kz) % 4) * 8 + lane - core + from_core
+    hit = jnp.where(dev * CAP + place == key, 1.0, 0.0).astype(bf16)
+    use = lax.dot_general(
+        uses.astype(bf16), hit, (((1,), (1,)), ((), ())), preferred_element_type=f32
+    )
+    use_ref[...] = use.astype(bf16)
+
+
 def fetch_kernel(where, picks, tokens, *outs):
     for ka in range(4):
         for kb in range(4):
             dest = place_of(where, ka, kb)
             for rank in range(CAP):
-                pick = picks[dest * CAP + rank]
+                pick = picks[rank, dest]
                 out = outs[ka]
                 at = kb * CAP + rank
                 for c in range(4):
@@ -92,9 +149,20 @@
 
 
 def regroup_kernel(*refs):
+    refs = refs[:4] + refs[8:]
     for ka in range(4):
         for kb in range(4):
             refs[4 + kb][ka * CAP : (ka + 1) * CAP] = refs[ka][kb * CAP : (kb + 1) * CAP]
+
+
+def after_kernel(_, *refs):
+    count = len(refs) // 2
+    for i in range(count):
+        refs[count + i][...] = refs[i][...]
+
+
+def after(first, *blocks):
+    return call(after_kernel, "after", [shape(8, 288, 128)] * len(blocks), [first, *blocks])
 
 
 def half_latent(refs, half):
@@ -117,22 +185,20 @@
     return jnp.where(keep, rope, jnp.zeros_like(rope))
 
 
-def attend_kernel(groups, resume, last, *refs):
-    index, q_ref, use_ref = refs[:3]
-    pieces = refs[3 : 3 + 2 * groups]
-    refs = refs[3 + 2 * groups :]
+def attend_kernel(first, groups, chips, resume, last, *refs):
+    use_ref, refs = refs[0], refs[1:]
+    qs, refs = dict(zip(chips, refs)), refs[len(chips) :]
+    pieces, refs = refs[: 2 * groups], refs[2 * groups :]
     if resume:
-        acc_in, stat_in = refs[0], refs[1]
-        refs = refs[2:]
-    m_rows = q_ref.shape[1]
-    chips = [index[0]] if last else list(range(4))
-    slot = lax.broadcasted_iota(jnp.int32, (16, 1024), 0)
-    token = lax.broadcasted_iota(jnp.int32, (16, 1024), 1)
-    spread = ((token // 32) % 16 == slot).astype(f32).astype(bf16)
-    biases = [
-        (jnp.dot(use_ref[g], spread, preferred_element_type=f32) - 1.0) * -NEG
-        for g in range(groups)
-    ]
+        (acc_in, stat_in), refs = refs[:2], refs[2:]
+    m_rows = 256
+    slot = lax.broadcasted_iota(jnp.int32, (64, 1024), 0)
+    token = lax.broadcasted_iota(jnp.int32, (64, 1024), 1)
+    biases = []
+    for g in range(groups):
+        spread = ((token // 32) % 16 + 16 * (first + g) == slot).astype(f32).astype(bf16)
+        used = jnp.dot(use_ref[...], spread, preferred_element_type=f32)
+        biases.append((used - 1.0) * -NEG)
 
     def values(g):
         mine = pieces[2 * g : 2 * g + 2]
@@ -143,7 +209,7 @@
         ropes = jnp.concatenate([half_rope(mine, 0), half_rope(mine, 1)], axis=0)
         keys = jnp.concatenate([values(g), ropes], axis=1)
         s = lax.dot_general(
-            q_ref[chip], keys, (((1,), (1,)), ((), ())), preferred_element_type=f32
+            qs[chip][...], keys, (((1,), (1,)), ((), ())), preferred_element_type=f32
         )
         n = s.shape[1]
         return (s.reshape(m_rows // 16, 16, n) + biases[g][None]).reshape(m_rows, n)
@@ -173,6 +239,7 @@
             refs[0][chip] = acc
             refs[1][chip] = jnp.where(lane < 64, top, total)
     if not last:
+        refs[2][...] = jnp.zeros((8, 128), f32)
         return
     out_ref = refs[0]
     out_ref[:m_rows] = (acc / total).astype(bf16)
@@ -186,27 +253,19 @@
     out_ref[m_rows:] = jnp.concatenate([stats, jnp.zeros_like(stats)], axis=1).astype(bf16)
 
 
-def attend(index, q, use, pieces, carry=(), last=True):
-    m_rows = q.shape[1]
+def attend(use, qs, first, pieces, carry=(), last=True):
     groups = len(pieces) // 2
     if last:
-        outs = [shape(m_rows + 16, LAT)]
+        outs = [shape(256 + 16, LAT)]
     else:
-        outs = [shape(4, m_rows, LAT, dtype=f32), shape(4, m_rows, 128, dtype=f32)]
-    chips = 1 if last else 4
-    cost = pl.CostEstimate(
-        flops=2 * chips * m_rows * groups * 1024 * (768 + 512) * 2,
-        bytes_accessed=groups * 16 * 288 * 128 * 2,
-        transcendentals=chips * m_rows * groups * 1024,
-    )
+        outs = [shape(4, 256, LAT, dtype=f32), shape(4, 256, 128, dtype=f32)]
+        outs.append(shape(8, 128, dtype=f32))
     return call(
-        functools.partial(attend_kernel, groups, bool(carry), last),
+        functools.partial(attend_kernel, first, groups, list(qs), bool(carry), last),
         "attend",
         outs,
-        [index, q, use, *pieces, *carry],
-        scalars=1,
-        limit=28,
-        cost_estimate=cost,
+        [use, *qs.values(), *pieces, *carry],
+        limit=16,
     )
 
 
@@ -280,10 +339,12 @@
             out[i, kx] = (residual[dp].astype(f32) + attn).astype(bf16)
 
 
-def ffn_kernel(where, half_ref, other_ref, gain_ref, wg_ref, wu_any, stream_ref, *outs):
-    *outs, wu_ref, sem = outs
-    bring = pltpu.make_async_copy(wu_any, wu_ref, sem)
-    bring.start()
+def ffn_kernel(where, half_ref, other_ref, gain_ref, wg_any, wu_any, stream_ref, *outs):
+    *outs, wg_ref, wu_ref, sem_g, sem_u = outs
+    bring_g = pltpu.make_async_copy(wg_any, wg_ref, sem_g)
+    bring_u = pltpu.make_async_copy(wu_any, wu_ref, sem_u)
+    bring_g.start()
+    bring_u.start()
     px, pz, core = where[0], where[1], where[2]
     half, other = half_ref[...].astype(f32), other_ref[...].astype(f32)
     rows = jnp.concatenate(
@@ -299,17 +360,26 @@
     lane = lax.broadcasted_iota(jnp.int32, (256, 128), 1)
     tail = jnp.where(lane == 0, hi, jnp.where(lane == 1, squares - hi, 0.0)).astype(bf16)
     scaled = (wide * gain_ref[...].astype(f32)).astype(bf16)
+    bring_g.wait()
     gate = jnp.dot(scaled, wg_ref[...], preferred_element_type=f32).astype(bf16)
     gate = gate.reshape(4, 4, 16, FF)
     tail = tail.reshape(4, 4, 16, 128)
     for k in range(4):
         outs[k][:, :, :FF] = gate[:, k]
         outs[k][:, :, 2 * FF :] = tail[:, k]
-    bring.wait()
+    bring_u.wait()
     up = jnp.dot(scaled, wu_ref[...], preferred_element_type=f32).astype(bf16)
     up = up.reshape(4, 4, 16, FF)
     for k in range(4):
         outs[k][:, :, FF : 2 * FF] = up[:, k]
+
+
+def turn_kernel(x, out):
+    out[...] = x[...].astype(f32).T.astype(bf16)
+
+
+def turn(x):
+    return call(turn_kernel, "turn", [shape(x.shape[1], x.shape[0])], [x])[0]
 
 
 def sum4(refs, at):
@@ -355,79 +425,45 @@
     lane = lax.axis_index("tp")
     px, pz = replica // 4, replica % 4
     core = lane % 2
-    me = replica * 8 + lane
     i32 = jnp.int32
-    where = jnp.stack([px, pz, core]).astype(i32)
+    where = jnp.stack([px, pz, core, lane]).astype(i32)
 
     q = queries.reshape(16, 16, KV).transpose(1, 0, 2).reshape(256, KV)
     q = jnp.concatenate([q, q[:, LAT:]], axis=1)
     own = jnp.concatenate([own_latent, own_latent[:, LAT:]], axis=1)
-    chips = [[c + 2 * y for y in range(4)] for c in range(2)]
-    q_all = lax.all_gather(q, "tp", axis_index_groups=chips)
-
-    slots = me * 16 + jnp.arange(16, dtype=i32)
-    ids = jnp.arange(2048, dtype=i32)
-    held = jnp.sum(jnp.where(block_home[None, :] == slots[:, None], ids[None, :], 0), axis=1)
-    wanted = (row_prompt[:, None] * PB + chosen).reshape(16, 512)
-    needed = jnp.any(wanted[:, None, :] == held[None, :, None], axis=2)
-    offs = jnp.arange(16, dtype=i32)
-    before = jnp.sum(
-        jnp.where(needed[:, None, :] & (offs[None, :] < offs[:, None])[None], 1, 0), axis=2
-    )
-    places = jnp.arange(CAP, dtype=i32)
-    picks = jnp.sum(
-        jnp.where(needed[:, None, :] & (before[:, None, :] == places[None, :, None]), offs, 0),
-        axis=2,
-    )
+    qs = {0: q, **{k: send_y(q, k) for k in (1, 2, 3)}}
+
+    picks, use = call(
+        plan_kernel,
+        "plan",
+        [shape(CAP, 128, dtype=i32), shape(16, 64)],
+        [where, row_prompt, block_home.reshape(4, 4, 128), row_prompt.reshape(1, 256), chosen.T],
+        scalars=2,
+    )
+
     sent = call(
         fetch_kernel,
         "fetch",
         [shape(8, 288, 128)] * 4,
-        [where, picks.reshape(-1), prefix_cache.reshape(16, BS, KV)],
+        [where, picks, prefix_cache.reshape(16, BS, KV)],
         scalars=2,
     )
     got = [sent[0]] + [send_dp(sent[k], 0, k) for k in (1, 2, 3)]
 
-    prompt = lax.dynamic_slice_in_dim(row_prompt, replica * 16, 1, 0)[0]
-    home = lax.dynamic_slice_in_dim(block_home, prompt * PB, PB, 0)
-    my_chosen = lax.dynamic_slice_in_dim(chosen, replica * 16, 16, 0)
-    sel = jnp.any(my_chosen[:, :, None] == jnp.arange(PB, dtype=i32)[None, None, :], axis=1)
-    need = jnp.any(sel, axis=0)
-    holder = home // 16
-    rank = jnp.sum(
-        jnp.where(
-            need[None, :] & (holder[None, :] == holder[:, None]) & (home[None, :] < home[:, None]),
-            1,
-            0,
-        ),
-        axis=1,
-    )
-    kb = jnp.array([0, 2, 1, 3], i32)[:, None, None, None]
-    from_core = core ^ jnp.array([0, 1], i32)[None, :, None, None]
-    ka = jnp.arange(4, dtype=i32)[None, None, :, None]
-    place = jnp.array([0, 1], i32)[None, None, None, :]
-    kx = jnp.where(from_core == 0, ka, kb)
-    kz = jnp.where(from_core == 0, kb, ka)
-    dev = (((px - kx) % 4) * 4 + (pz - kz) % 4) * 8 + (lane - core + from_core)
-    want_key = (dev * 2 + place).reshape(64)
-    key = jnp.where(need, holder * 2 + rank, -1)
-    hit = key[:, None] == want_key[None, :]
-    use = jnp.dot(sel.astype(bf16), hit.astype(bf16), preferred_element_type=f32).astype(bf16)
-    use = use.reshape(16, 4, 16).transpose(1, 0, 2)
-
-    got[0], use = lax.optimization_barrier((got[0], use))
-    groups = call(regroup_kernel, "regroup", [shape(8, 288, 128)] * 4, got)
+    groups = call(regroup_kernel, "regroup", [shape(8, 288, 128)] * 4, [*got, use, *list(qs.values())[1:]], anys=4)
     arrived = {0: groups[0]}
-    for k in (2, 1, 3):
+    for k in (1, 3, 2):
         arrived[k] = send_dp(groups[k], 1, k)
-    pieces = {k: [arrived[k], swap_core(arrived[k])] for k in (0, 2, 1, 3)}
-    y = lane // 2
-    carry = attend(y.reshape(1), q_all, use[0:1], pieces[0], last=False)
-    carry = attend(y.reshape(1), q_all, use[1:2], pieces[2], carry, last=False)
+    pieces = [groups[0], swap_core(groups[0])]
+    *carry, done = attend(use, qs, 0, pieces, last=False)
+    second, third = after(done, arrived[1], arrived[3])
+    pieces = [second, swap_core(second), third, swap_core(third)]
+    *carry, done = attend(use, qs, 1, pieces, carry, last=False)
+    (fourth,) = after(done, arrived[2])
+    pieces = [fourth, swap_core(fourth)]
     parts = []
     for k in (2, 1, 3, 0):
-        index = (y ^ k).reshape(1)
-        (o,) = attend(index, q_all, use[2:4], pieces[1] + pieces[3], carry)
+        (o,) = attend(use, {k: qs[k]}, 3, pieces, carry)
         parts.append(send_y(o, k) if k else o)
     per_head = merge(parts, q, own, value_up)
 
@@ -447,7 +483,7 @@
         join_kernel,
         "join",
         [shape(2, 4, 16, 448)],
-        [where, pair, *terms, residual.reshape(16, 16, 448)],
+        [where, pair, *terms, turn(residual.T).reshape(16, 16, 448)],
         scalars=1,
     )
     other = swap_core(half)
@@ -457,15 +493,15 @@
         [shape(16, 16, 448)] + [shape(4, 16, 2 * FF + 128)] * 4,
         [where, half, other, norm_gain.reshape(1, 448), gate_weight, up_weight],
         scalars=1,
-        anys=1,
+        anys=2,
         limit=30,
-        scratch_shapes=[pltpu.VMEM((448, FF), bf16), pltpu.SemaphoreType.DMA(())],
+        scratch_shapes=[pltpu.VMEM((448, FF), bf16)] * 2 + [pltpu.SemaphoreType.DMA(())] * 2,
     )
     got = [sums[0]] + [send_dp(sums[k], 0, k) for k in (2, 1, 3)]
     sums = call(fold_kernel, "fold", [shape(16, 2 * FF + 128)] * 4, got)
     got = [sums[0]] + [send_dp(sums[k], 1, k) for k in (2, 1, 3)]
     (hidden,) = call(finish_kernel, "finish", [shape(16, FF)], got)
-    return (stream.reshape(256, 448), hidden)
+    return (turn(stream.reshape(256, 448)).T, hidden)
 
 
 def solution(mesh):

time: 172 us -> 147 us (0.85)
  between operations: 15.1 us -> 0.92 us
  local copies, waits for them, and re-layouts: 11.1 us -> 3.1 us
  starting transfers between devices: 39.4 us -> 46 us
  other arithmetic: 6.14 us -> 0.3 us
  Pallas kernels: 31.6 us -> 26.9 us
    ppermute x12 -> x15, waiting for transfers between devices: 16.9 us -> 30.4 us  [send(): return lax.ppermute(x, axis, [(i, to(i)) for i in range(n)])]
    ppermute x18, waiting for transfers between devices: 51 us -> 39.1 us  [send_dp(): return lax.ppermute(x, ('dp', 'tp'), pairs)]
    unnamed x32 -> x22, local copies, waits for them, and re-layouts: 5.79 us -> 0.05 us
    ppermute x12 -> x15, starting transfers between devices: 10.1 us -> 15 us  [send(): return lax.ppermute(x, axis, [(i, to(i)) for i in range(n)])]
    pallas_call x13 -> x18, Pallas kernels: 30.7 us -> 26.1 us  [call(): pl.pallas_call(kernel, out_shape=outs, in_specs=[SMEM] * scalars + [VMEM]...]
    reduce_sum x4 -> x0, other arithmetic: 1.89 us -> none  [the longest x1 0.9 us: local(): jnp.sum(jnp.where(block_home[None, :] == slots[:, None], ids[None, :], 0)...]
    ppermute x18, starting transfers between devices: 29.2 us -> 31 us  [send_dp(): return lax.ppermute(x, ('dp', 'tp'), pairs)]
  transfers between devices with their start and end apart: 31 -> 33, of which waited for: 21 -> 24; matrix products, arithmetic and copies ran while one was open for 4% -> 1% of each run, Pallas kernels for 11% -> 12%
where the time goes in v5:
time: 147 us
  waiting for transfers between devices  69.4 us (47%)
  starting transfers between devices  46 us (31%)
  Pallas kernels  26.9 us (18%)
  local copies, waits for them, and re-layouts  3.1 us (2%)
    ppermute x18, waiting for transfers between devices, send_dp(): return lax.ppermute(x, ('dp', 'tp'), pairs)  39.1 us
    ppermute x18, starting transfers between devices, send_dp(): return lax.ppermute(x, ('dp', 'tp'), pairs)  31 us
    ppermute x15, waiting for transfers between devices, send(): return lax.ppermute(x, axis, [(i, to(i)) for i in range(n)])  30.4 us
    pallas_call x18, Pallas kernels, call(): pl.pallas_call(kernel, out_shape=outs, in_specs=[SMEM] * scalars + [VMEM]...  26.1 us
    ppermute x15, starting transfers between devices, send(): return lax.ppermute(x, axis, [(i, to(i)) for i in range(n)])  15 us
  transfers between devices with their start and end apart: 33, of which 24 were waited for; matrix products, arithmetic and copies ran while one was open for 1% of the time, Pallas kernels for 12%

profile of v5, /device:TPU:0, one launch (start us, length us, event | category | flops | bytes accessed | tf_op | source)
XLA Modules:
  0.0 146.6 jit_solution(5956155840959344502)
XLA Ops:
  0.6 1.3 reshape.30
  2.2 3.4 %collective-permute-start = (bf16[256,640]{1,0:T(8,128)(2,1)S(1)}, bf16[256,640]{1,0:T(8,128)(2,1)S(1)}, u32[]{:S(2)}, u32[]{:S(2)}) collective-permute-start(bf16[256,640]{1,0:T(8,128)(2,1)S(1)} %pad_maximum_fusion.refs_1_.q_ref), channel_id=1, source_target_pairs={{0,4},{1,5},{2,6},{3,7},{4,0},{5,1},{6,2},{7,3},{8,12},{9,13},{10,... | collective-permute-start | bytes 983048 | tf_op jit(solution)/shard_map/ppermute | solution.py:29
  5.6 1.6 %reshape.32.tokens = bf16[16,64,576]{2,1,0:T(8,128)(2,1)S(1)} reshape(bf16[16,36864]{1,0:T(8,128)(2,1)S(1)} %copy-done.8) | data formatting | bytes 2359296 | tf_op jit(solution)/shard_map/reshape | solution.py:448
  7.3 1.7 %plan.1 = (s32[2,128]{1,0:T(2,128)S(1)}, bf16[16,64]{1,0:T(8,128)(2,1)S(1)}) custom-call(s32[4]{0:T(128)S(1)} %pad_add_fusion.where, s32[256]{0:T(256)S(1)} %copy-done.7, s32[4,4,128]{2,1,0:T(4,128)S(1)} %bitcast.20, s32[1,256]{1,0:T(1,128)S(1)} %bitcast.21, s32[32,256]{1,0:T(8,128)S(1)} %bitcast.19), custom_call_target="tpu_custom_call" | custom-call | tf_op jit(solution)/shard_map/plan/pallas_call | solution.py:58
  9.0 1.2 fetch.1
  10.1 1.5 %collective-permute-start.3 = (bf16[8,288,128]{2,1,0:T(8,128)(2,1)S(1)}, bf16[8,288,128]{2,1,0:T(8,128)(2,1)S(1)}, u32[]{:S(2)}, u32[]{:S(2)}) collective-permute-start(bf16[8,288,128]{2,1,0:T(8,128)(2,1)S(1)} %get-tuple-element.34), channel_id=1, source_target_pairs={{0,32},{1,9},{2,34},{3,11},{4,36},{5,13},{6,38},{7,15},{8,40},{9,1... | collective-permute-start | bytes 1769480 | tf_op jit(solution)/shard_map/ppermute | solution.py:49
  11.7 2.7 %collective-permute-start.4 = (bf16[8,288,128]{2,1,0:T(8,128)(2,1)S(1)}, bf16[8,288,128]{2,1,0:T(8,128)(2,1)S(1)}, u32[]{:S(2)}, u32[]{:S(2)}) collective-permute-start(bf16[8,288,128]{2,1,0:T(8,128)(2,1)S(1)} %get-tuple-element.35), channel_id=1, source_target_pairs={{0,64},{1,17},{2,66},{3,19},{4,68},{5,21},{6,70},{7,23},{8,72},{9,... | collective-permute-start | bytes 1769480 | tf_op jit(solution)/shard_map/ppermute | solution.py:49
  14.4 1.4 collective-permute-start.5
  15.9 0.7 collective-permute-start.1
  16.9 8.1 %collective-permute-done.1.refs_5_.refs_2_.refs_1_ = bf16[256,640]{1,0:T(8,128)(2,1)S(1)} collective-permute-done((bf16[256,640]{1,0:T(8,128)(2,1)S(1)}, bf16[256,640]{1,0:T(8,128)(2,1)S(1)}, u32[]{:S(2)}, u32[]{:S(2)}) %collective-permute-start.1) | collective-permute-done | bytes 327712 | tf_op jit(solution)/shard_map/ppermute | solution.py:29
  25.0 1.6 %collective-permute-done.2.refs_7_.refs_4_.refs_1_ = bf16[256,640]{1,0:T(8,128)(2,1)S(1)} collective-permute-done((bf16[256,640]{1,0:T(8,128)(2,1)S(1)}, bf16[256,640]{1,0:T(8,128)(2,1)S(1)}, u32[]{:S(2)}, u32[]{:S(2)}) %collective-permute-start.2) | collective-permute-done | bytes 327712 | tf_op jit(solution)/shard_map/ppermute | solution.py:29
  26.7 1.9 %collective-permute-done.4.refs_2_ = bf16[8,288,128]{2,1,0:T(8,128)(2,1)S(1)} collective-permute-done((bf16[8,288,128]{2,1,0:T(8,128)(2,1)S(1)}, bf16[8,288,128]{2,1,0:T(8,128)(2,1)S(1)}, u32[]{:S(2)}, u32[]{:S(2)}) %collective-permute-start.4) | collective-permute-done | bytes 589856 | tf_op jit(solution)/shard_map/ppermute | solution.py:49
  28.8 2.0 %collective-permute-start.7 = (bf16[8,288,128]{2,1,0:T(8,128)(2,1)S(1)}, bf16[8,288,128]{2,1,0:T(8,128)(2,1)S(1)}, u32[]{:S(2)}, u32[]{:S(2)}) collective-permute-start(bf16[8,288,128]{2,1,0:T(8,128)(2,1)S(1)} %get-tuple-element.39), channel_id=1, source_target_pairs={{0,8},{1,33},{2,10},{3,35},{4,12},{5,37},{6,14},{7,39},{8,16},{9,4... | collective-permute-start | bytes 1769480 | tf_op jit(solution)/shard_map/ppermute | solution.py:49
  30.8 2.2 %collective-permute-start.8 = (bf16[8,288,128]{2,1,0:T(8,128)(2,1)S(1)}, bf16[8,288,128]{2,1,0:T(8,128)(2,1)S(1)}, u32[]{:S(2)}, u32[]{:S(2)}) collective-permute-start(bf16[8,288,128]{2,1,0:T(8,128)(2,1)S(1)} %get-tuple-element.40), channel_id=1, source_target_pairs={{0,24},{1,97},{2,26},{3,99},{4,28},{5,101},{6,30},{7,103},{8,0},{9... | collective-permute-start | bytes 1769480 | tf_op jit(solution)/shard_map/ppermute | solution.py:49
  33.0 3.3 %attend.6 = (f32[4,256,512]{2,1,0:T(8,128)S(1)}, f32[4,256,128]{2,1,0:T(8,128)S(1)}, f32[8,128]{1,0:T(8,128)S(1)}) custom-call(bf16[16,64]{1,0:T(8,128)(2,1)S(1)} %get-tuple-element.31.refs_4_.refs_0_, bf16[256,640]{1,0:T(8,128)(2,1)S(1)} %pad_maximum_fusion.refs_1_.q_ref, bf16[256,640]{1,0:T(8,128)(2,1)S(1)} %collective-permute-done.1.refs_5_.refs_2_.refs_1_, ...), custom_call_target="tpu_custom_call" | custom-call | tf_op jit(solution)/shard_map/attend/pallas_call | solution.py:58
  36.4 4.5 %collective-permute-done.7.refs_0_ = bf16[8,288,128]{2,1,0:T(8,128)(2,1)S(1)} collective-permute-done((bf16[8,288,128]{2,1,0:T(8,128)(2,1)S(1)}, bf16[8,288,128]{2,1,0:T(8,128)(2,1)S(1)}, u32[]{:S(2)}, u32[]{:S(2)}) %collective-permute-start.7) | collective-permute-done | bytes 589856 | tf_op jit(solution)/shard_map/ppermute | solution.py:49
  41.0 0.5 collective-permute-start.9
  41.5 3.5 %collective-permute-start.11 = (bf16[8,288,128]{2,1,0:T(8,128)(2,1)S(1)}, bf16[8,288,128]{2,1,0:T(8,128)(2,1)S(1)}, u32[]{:S(2)}, u32[]{:S(2)}) collective-permute-start(bf16[8,288,128]{2,1,0:T(8,128)(2,1)S(1)} %get-tuple-element.46), channel_id=1, source_target_pairs={{0,16},{1,65},{2,18},{3,67},{4,20},{5,69},{6,22},{7,71},{8,24},{9,... | collective-permute-start | bytes 1769480 | tf_op jit(solution)/shard_map/ppermute | solution.py:49
  45.0 6.9 %attend.7 = (f32[4,256,512]{2,1,0:T(8,128)S(1)}, f32[4,256,128]{2,1,0:T(8,128)S(1)}, f32[8,128]{1,0:T(8,128)S(1)}) custom-call(bf16[16,64]{1,0:T(8,128)(2,1)S(1)} %get-tuple-element.31.refs_4_.refs_0_, bf16[256,640]{1,0:T(8,128)(2,1)S(1)} %pad_maximum_fusion.refs_1_.q_ref, bf16[256,640]{1,0:T(8,128)(2,1)S(1)} %collective-permute-done.1.refs_5_.refs_2_.refs_1_, ...), custom_call_target="tpu_custom_call" | custom-call | tf_op jit(solution)/shard_map/attend/pallas_call | solution.py:58
  51.9 1.0 collective-permute-done.11.refs_0_
  53.0 2.0 %collective-permute-done.12.refs_3_ = bf16[8,288,128]{2,1,0:T(8,128)(2,1)S(1)} collective-permute-done((bf16[8,288,128]{2,1,0:T(8,128)(2,1)S(1)}, bf16[8,288,128]{2,1,0:T(8,128)(2,1)S(1)}, u32[]{:S(2)}, u32[]{:S(2)}) %collective-permute-start.12) | collective-permute-done | bytes 589856 | tf_op jit(solution)/shard_map/ppermute | solution.py:29
  55.0 1.3 attend.10
  56.3 1.1 collective-permute-start.15
  57.4 1.3 attend.9
  58.8 1.3 attend.8
  60.2 3.7 %collective-permute-start.13 = (bf16[272,512]{1,0:T(8,128)(2,1)S(1)}, bf16[272,512]{1,0:T(8,128)(2,1)S(1)}, u32[]{:S(2)}, u32[]{:S(2)}) collective-permute-start(bf16[272,512]{1,0:T(8,128)(2,1)S(1)} %attend.8), channel_id=1, source_target_pairs={{0,4},{1,5},{2,6},{3,7},{4,0},{5,1},{6,2},{7,3},{8,12},{9,13},{10,... | collective-permute-start | bytes 835592 | tf_op jit(solution)/shard_map/ppermute | solution.py:29
  63.9 1.3 attend.11.o3
  65.2 1.1 collective-permute-done.15.o2
  66.3 2.1 %collective-permute-done.14.o1 = bf16[272,512]{1,0:T(8,128)(2,1)S(1)} collective-permute-done((bf16[272,512]{1,0:T(8,128)(2,1)S(1)}, bf16[272,512]{1,0:T(8,128)(2,1)S(1)}, u32[]{:S(2)}, u32[]{:S(2)}) %collective-permute-start.14) | collective-permute-done | bytes 278560 | tf_op jit(solution)/shard_map/ppermute | solution.py:29
  68.4 6.5 %collective-permute-done.13.o0 = bf16[272,512]{1,0:T(8,128)(2,1)S(1)} collective-permute-done((bf16[272,512]{1,0:T(8,128)(2,1)S(1)}, bf16[272,512]{1,0:T(8,128)(2,1)S(1)}, u32[]{:S(2)}, u32[]{:S(2)}) %collective-permute-start.13) | collective-permute-done | bytes 278560 | tf_op jit(solution)/shard_map/ppermute | solution.py:29
  74.8 0.8 merge.1
  75.7 2.6 %collective-permute-start.16 = (bf16[16,2048]{1,0:T(8,128)(2,1)S(1)}, bf16[16,2048]{1,0:T(8,128)(2,1)S(1)}, u32[]{:S(2)}, u32[]{:S(2)}) collective-permute-start(bf16[16,2048]{1,0:T(8,128)(2,1)S(1)} %merge.1), channel_id=1, source_target_pairs={{0,96},{1,25},{2,98},{3,27},{4,100},{5,29},{6,102},{7,31},{8,104},... | collective-permute-start | bytes 196616 | tf_op jit(solution)/shard_map/ppermute | solution.py:49
  78.3 1.4 collective-permute-start.17
  79.7 0.4 collective-permute-start.18
  80.2 3.9 %collective-permute-done.17 = bf16[16,2048]{1,0:T(8,128)(2,1)S(1)} collective-permute-done((bf16[16,2048]{1,0:T(8,128)(2,1)S(1)}, bf16[16,2048]{1,0:T(8,128)(2,1)S(1)}, u32[]{:S(2)}, u32[]{:S(2)}) %collective-permute-start.17) | collective-permute-done | bytes 65568 | tf_op jit(solution)/shard_map/ppermute | solution.py:49
  84.1 1.1 collective-permute-done.18
  85.2 3.4 %collective-permute-start.19 = (bf16[64,2048]{1,0:T(8,128)(2,1)S(1)}, bf16[64,2048]{1,0:T(8,128)(2,1)S(1)}, u32[]{:S(2)}, u32[]{:S(2)}) collective-permute-start(bf16[64,2048]{1,0:T(8,128)(2,1)S(1)} %pad_maximum_fusion.1.p0), channel_id=1, source_target_pairs={{0,24},{1,97},{2,26},{3,99},{4,28},{5,101},{6,30},{7,103},{8,0},{9... | collective-permute-start | bytes 786440 | tf_op jit(solution)/shard_map/ppermute | solution.py:49
  88.6 0.6 collective-permute-start.20
  89.2 1.0 collective-permute-start.21
  90.2 5.1 %collective-permute-done.19.p1 = bf16[64,2048]{1,0:T(8,128)(2,1)S(1)} collective-permute-done((bf16[64,2048]{1,0:T(8,128)(2,1)S(1)}, bf16[64,2048]{1,0:T(8,128)(2,1)S(1)}, u32[]{:S(2)}, u32[]{:S(2)}) %collective-permute-start.19) | collective-permute-done | bytes 262176 | tf_op jit(solution)/shard_map/ppermute | solution.py:49
  95.3 1.3 collective-permute-done.20.p2
  96.6 2.7 %collective-permute-done.21.p3 = bf16[64,2048]{1,0:T(8,128)(2,1)S(1)} collective-permute-done((bf16[64,2048]{1,0:T(8,128)(2,1)S(1)}, bf16[64,2048]{1,0:T(8,128)(2,1)S(1)}, u32[]{:S(2)}, u32[]{:S(2)}) %collective-permute-start.21) | collective-permute-done | bytes 262176 | tf_op jit(solution)/shard_map/ppermute | solution.py:49
  99.3 1.3 project.1
  100.7 1.3 collective-permute-done.22
  102.2 2.5 %collective-permute-start.24 = (bf16[2,4,16,448]{3,2,1,0:T(8,128)(2,1)S(1)}, bf16[2,4,16,448]{3,2,1,0:T(8,128)(2,1)S(1)}, u32[]{:S(2)}, u32[]{:S(2)}) collective-permute-start(bf16[2,4,16,448]{3,2,1,0:T(8,128)(2,1)S(1)} %add_convert_fusion.pair), channel_id=1, source_target_pairs={{0,4},{1,5},{2,6},{3,7},{4,0},{5,1},{6,2},{7,3},{8,12},{9,13},{10,... | collective-permute-start | bytes 344072 | tf_op jit(solution)/shard_map/ppermute | solution.py:29
  104.7 2.2 %collective-permute-start.25 = (bf16[2,4,16,448]{3,2,1,0:T(8,128)(2,1)S(1)}, bf16[2,4,16,448]{3,2,1,0:T(8,128)(2,1)S(1)}, u32[]{:S(2)}, u32[]{:S(2)}) collective-permute-start(bf16[2,4,16,448]{3,2,1,0:T(8,128)(2,1)S(1)} %add_convert_fusion.pair), channel_id=1, source_target_pairs={{0,6},{1,7},{2,4},{3,5},{4,2},{5,3},{6,0},{7,1},{8,14},{9,15},{10,... | collective-permute-start | bytes 344072 | tf_op jit(solution)/shard_map/ppermute | solution.py:29
  107.0 1.5 %collective-permute-done.23.t1 = bf16[2,4,16,448]{3,2,1,0:T(8,128)(2,1)S(1)} collective-permute-done((bf16[2,4,16,448]{3,2,1,0:T(8,128)(2,1)S(1)}, bf16[2,4,16,448]{3,2,1,0:T(8,128)(2,1)S(1)}, u32[]{:S(2)}, u32[]{:S(2)}) %collective-permute-start.23) | collective-permute-done | bytes 114720 | tf_op jit(solution)/shard_map/ppermute | solution.py:29
  108.5 2.6 %collective-permute-done.24.t2 = bf16[2,4,16,448]{3,2,1,0:T(8,128)(2,1)S(1)} collective-permute-done((bf16[2,4,16,448]{3,2,1,0:T(8,128)(2,1)S(1)}, bf16[2,4,16,448]{3,2,1,0:T(8,128)(2,1)S(1)}, u32[]{:S(2)}, u32[]{:S(2)}) %collective-permute-start.24) | collective-permute-done | bytes 114720 | tf_op jit(solution)/shard_map/ppermute | solution.py:29
  111.1 2.2 %collective-permute-done.25.t3 = bf16[2,4,16,448]{3,2,1,0:T(8,128)(2,1)S(1)} collective-permute-done((bf16[2,4,16,448]{3,2,1,0:T(8,128)(2,1)S(1)}, bf16[2,4,16,448]{3,2,1,0:T(8,128)(2,1)S(1)}, u32[]{:S(2)}, u32[]{:S(2)}) %collective-permute-start.25) | collective-permute-done | bytes 114720 | tf_op jit(solution)/shard_map/ppermute | solution.py:29
  113.3 0.6 join.1.half_ref
  114.1 1.3 collective-permute-done.26.other_ref
  115.4 3.4 %ffn.1 = (bf16[16,16,448]{2,1,0:T(8,128)(2,1)S(1)}, bf16[4,16,4736]{2,1,0:T(8,128)(2,1)S(1)}, bf16[4,16,4736]{2,1,0:T(8,128)(2,1)S(1)}, bf16[4,16,4736]{2,1,0:T(8,128)(2,1)S(1)}, bf16[4,16,4736]{2,1,0:T(8,128)(2,1)S(1)}) custom-call(s32[4]{0:T(128)S(1)} %pad_add_fusion.where, bf16[2,4,16,448]{3,2,1,0:T(8,128)(2,1)S(1)} %join.1.half_ref, ...), custom_call_target="tpu_custom_call" | custom-call | tf_op jit(solution)/shard_map/ffn/pallas_call | solution.py:58
  118.8 1.1 collective-permute-start.27
  119.8 3.2 %collective-permute-start.29 = (bf16[4,16,4736]{2,1,0:T(8,128)(2,1)S(1)}, bf16[4,16,4736]{2,1,0:T(8,128)(2,1)S(1)}, u32[]{:S(2)}, u32[]{:S(2)}) collective-permute-start(bf16[4,16,4736]{2,1,0:T(8,128)(2,1)S(1)} %get-tuple-element.55), channel_id=1, source_target_pairs={{0,96},{1,25},{2,98},{3,27},{4,100},{5,29},{6,102},{7,31},{8,104},... | collective-permute-start | bytes 1818632 | tf_op jit(solution)/shard_map/ppermute | solution.py:49
  123.1 7.4 %collective-permute-done.27.refs_1_ = bf16[4,16,4736]{2,1,0:T(8,128)(2,1)S(1)} collective-permute-done((bf16[4,16,4736]{2,1,0:T(8,128)(2,1)S(1)}, bf16[4,16,4736]{2,1,0:T(8,128)(2,1)S(1)}, u32[]{:S(2)}, u32[]{:S(2)}) %collective-permute-start.27) | collective-permute-done | bytes 606240 | tf_op jit(solution)/shard_map/ppermute | solution.py:49
  130.5 6.4 %collective-permute-done.28.refs_2_ = bf16[4,16,4736]{2,1,0:T(8,128)(2,1)S(1)} collective-permute-done((bf16[4,16,4736]{2,1,0:T(8,128)(2,1)S(1)}, bf16[4,16,4736]{2,1,0:T(8,128)(2,1)S(1)}, u32[]{:S(2)}, u32[]{:S(2)}) %collective-permute-start.28) | collective-permute-done | bytes 606240 | tf_op jit(solution)/shard_map/ppermute | solution.py:49
  136.9 0.5 fold.1
  137.4 0.7 collective-permute-start.30
  138.1 0.9 collective-permute-start.31
  139.0 2.3 %collective-permute-start.32 = (bf16[16,4736]{1,0:T(8,128)(2,1)S(1)}, bf16[16,4736]{1,0:T(8,128)(2,1)S(1)}, u32[]{:S(2)}, u32[]{:S(2)}) collective-permute-start(bf16[16,4736]{1,0:T(8,128)(2,1)S(1)} %get-tuple-element.59), channel_id=1, source_target_pairs={{0,24},{1,97},{2,26},{3,99},{4,28},{5,101},{6,30},{7,103},{8,0},{9... | collective-permute-start | bytes 454664 | tf_op jit(solution)/shard_map/ppermute | solution.py:49
  141.3 0.8 turn.3
  142.2 2.2 %collective-permute-done.30.r1 = bf16[16,4736]{1,0:T(8,128)(2,1)S(1)} collective-permute-done((bf16[16,4736]{1,0:T(8,128)(2,1)S(1)}, bf16[16,4736]{1,0:T(8,128)(2,1)S(1)}, u32[]{:S(2)}, u32[]{:S(2)}) %collective-permute-start.30) | collective-permute-done | bytes 151584 | tf_op jit(solution)/shard_map/ppermute | solution.py:49
  144.3 1.5 %collective-permute-done.31.r2 = bf16[16,4736]{1,0:T(8,128)(2,1)S(1)} collective-permute-done((bf16[16,4736]{1,0:T(8,128)(2,1)S(1)}, bf16[16,4736]{1,0:T(8,128)(2,1)S(1)}, u32[]{:S(2)}, u32[]{:S(2)}) %collective-permute-start.31) | collective-permute-done | bytes 151584 | tf_op jit(solution)/shard_map/ppermute | solution.py:49
  145.8 0.8 finish.1
  (55 shorter events, 1.9 us)
Async XLA Ops:
  0.6 4.9 %copy-start.8 = (bf16[16,36864]{1,0:T(8,128)(2,1)S(1)}, bf16[16,36864]{1,0:T(8,128)(2,1)}, u32[]{:S(2)}) copy-start(bf16[16,36864]{1,0:T(8,128)(2,1)} %param.14) | copy-start | bytes 3538948
  2.0 5.3 %copy-start.5 = (s32[256,32]{0,1:T(8,128)S(1)}, s32[256,32]{0,1:T(8,128)}, u32[]{:S(2)}) copy-start(s32[256,32]{0,1:T(8,128)} %param.17) | copy-start | bytes 98308
  2.0 5.3 %copy-start.6 = (s32[2048]{0:T(1024)S(1)}, s32[2048]{0:T(1024)}, u32[]{:S(2)}) copy-start(s32[2048]{0:T(1024)} %param.15) | copy-start | bytes 24580
  2.0 5.3 %copy-start.7 = (s32[256]{0:T(256)S(1)}, s32[256]{0:T(256)}, u32[]{:S(2)}) copy-start(s32[256]{0:T(256)} %prompts.1) | copy-start | bytes 3076
  2.2 14.3 %collective-permute-start = (bf16[256,640]{1,0:T(8,128)(2,1)S(1)}, bf16[256,640]{1,0:T(8,128)(2,1)S(1)}, u32[]{:S(2)}, u32[]{:S(2)}) collective-permute-start(bf16[256,640]{1,0:T(8,128)(2,1)S(1)} %pad_maximum_fusion.refs_1_.q_ref), channel_id=1, source_target_pairs={{0,4},{1,5},{2,6},{3,7},{4,0},{5,1},{6,2},{7,3},{8,12},{9,13},{10,... | collective-permute-start | bytes 983048 | tf_op jit(solution)/shard_map/ppermute | solution.py:29
  10.1 16.5 %collective-permute-start.3 = (bf16[8,288,128]{2,1,0:T(8,128)(2,1)S(1)}, bf16[8,288,128]{2,1,0:T(8,128)(2,1)S(1)}, u32[]{:S(2)}, u32[]{:S(2)}) collective-permute-start(bf16[8,288,128]{2,1,0:T(8,128)(2,1)S(1)} %get-tuple-element.34), channel_id=1, source_target_pairs={{0,32},{1,9},{2,34},{3,11},{4,36},{5,13},{6,38},{7,15},{8,40},{9,1... | collective-permute-start | bytes 1769480 | tf_op jit(solution)/shard_map/ppermute | solution.py:49
  11.7 16.9 %collective-permute-start.4 = (bf16[8,288,128]{2,1,0:T(8,128)(2,1)S(1)}, bf16[8,288,128]{2,1,0:T(8,128)(2,1)S(1)}, u32[]{:S(2)}, u32[]{:S(2)}) collective-permute-start(bf16[8,288,128]{2,1,0:T(8,128)(2,1)S(1)} %get-tuple-element.35), channel_id=1, source_target_pairs={{0,64},{1,17},{2,66},{3,19},{4,68},{5,21},{6,70},{7,23},{8,72},{9,... | collective-permute-start | bytes 1769480 | tf_op jit(solution)/shard_map/ppermute | solution.py:49
  14.4 14.2 %collective-permute-start.5 = (bf16[8,288,128]{2,1,0:T(8,128)(2,1)S(1)}, bf16[8,288,128]{2,1,0:T(8,128)(2,1)S(1)}, u32[]{:S(2)}, u32[]{:S(2)}) collective-permute-start(bf16[8,288,128]{2,1,0:T(8,128)(2,1)S(1)} %get-tuple-element.36), channel_id=1, source_target_pairs={{0,96},{1,25},{2,98},{3,27},{4,100},{5,29},{6,102},{7,31},{8,104},... | collective-permute-start | bytes 1769480 | tf_op jit(solution)/shard_map/ppermute | solution.py:49
  15.9 9.2 %collective-permute-start.1 = (bf16[256,640]{1,0:T(8,128)(2,1)S(1)}, bf16[256,640]{1,0:T(8,128)(2,1)S(1)}, u32[]{:S(2)}, u32[]{:S(2)}) collective-permute-start(bf16[256,640]{1,0:T(8,128)(2,1)S(1)} %pad_maximum_fusion.refs_1_.q_ref), channel_id=1, source_target_pairs={{0,2},{1,3},{2,0},{3,1},{4,6},{5,7},{6,4},{7,5},{8,10},{9,11},{10,... | collective-permute-start | bytes 983048 | tf_op jit(solution)/shard_map/ppermute | solution.py:29
  16.5 10.1 %collective-permute-start.2 = (bf16[256,640]{1,0:T(8,128)(2,1)S(1)}, bf16[256,640]{1,0:T(8,128)(2,1)S(1)}, u32[]{:S(2)}, u32[]{:S(2)}) collective-permute-start(bf16[256,640]{1,0:T(8,128)(2,1)S(1)} %pad_maximum_fusion.refs_1_.q_ref), channel_id=1, source_target_pairs={{0,6},{1,7},{2,4},{3,5},{4,2},{5,3},{6,0},{7,1},{8,14},{9,15},{10,... | collective-permute-start | bytes 983048 | tf_op jit(solution)/shard_map/ppermute | solution.py:29
  28.8 4.3 %collective-permute-start.6 = (bf16[8,288,128]{2,1,0:T(8,128)(2,1)S(1)}, bf16[8,288,128]{2,1,0:T(8,128)(2,1)S(1)}, u32[]{:S(2)}, u32[]{:S(2)}) collective-permute-start(bf16[8,288,128]{2,1,0:T(8,128)(2,1)S(1)} %get-tuple-element.37.refs_5_), channel_id=1, source_target_pairs={{0,1},{1,0},{2,3},{3,2},{4,5},{5,4},{6,7},{7,6},{8,9},{9,8},{10,11... | collective-permute-start | bytes 1769480 | tf_op jit(solution)/shard_map/ppermute | solution.py:29
  28.8 12.0 %collective-permute-start.7 = (bf16[8,288,128]{2,1,0:T(8,128)(2,1)S(1)}, bf16[8,288,128]{2,1,0:T(8,128)(2,1)S(1)}, u32[]{:S(2)}, u32[]{:S(2)}) collective-permute-start(bf16[8,288,128]{2,1,0:T(8,128)(2,1)S(1)} %get-tuple-element.39), channel_id=1, source_target_pairs={{0,8},{1,33},{2,10},{3,35},{4,12},{5,37},{6,14},{7,39},{8,16},{9,4... | collective-permute-start | bytes 1769480 | tf_op jit(solution)/shard_map/ppermute | solution.py:49
  30.8 10.0 %collective-permute-start.8 = (bf16[8,288,128]{2,1,0:T(8,128)(2,1)S(1)}, bf16[8,288,128]{2,1,0:T(8,128)(2,1)S(1)}, u32[]{:S(2)}, u32[]{:S(2)}) collective-permute-start(bf16[8,288,128]{2,1,0:T(8,128)(2,1)S(1)} %get-tuple-element.40), channel_id=1, source_target_pairs={{0,24},{1,97},{2,26},{3,99},{4,28},{5,101},{6,30},{7,103},{8,0},{9... | collective-permute-start | bytes 1769480 | tf_op jit(solution)/shard_map/ppermute | solution.py:49
  40.9 4.1 %collective-permute-start.10 = (bf16[8,288,128]{2,1,0:T(8,128)(2,1)S(1)}, bf16[8,288,128]{2,1,0:T(8,128)(2,1)S(1)}, u32[]{:S(2)}, u32[]{:S(2)}) collective-permute-start(bf16[8,288,128]{2,1,0:T(8,128)(2,1)S(1)} %get-tuple-element.42.refs_7_), channel_id=1, source_target_pairs={{0,1},{1,0},{2,3},{3,2},{4,5},{5,4},{6,7},{7,6},{8,9},{9,8},{10,11... | collective-permute-start | bytes 1769480 | tf_op jit(solution)/shard_map/ppermute | solution.py:29
  41.0 4.0 %collective-permute-start.9 = (bf16[8,288,128]{2,1,0:T(8,128)(2,1)S(1)}, bf16[8,288,128]{2,1,0:T(8,128)(2,1)S(1)}, u32[]{:S(2)}, u32[]{:S(2)}) collective-permute-start(bf16[8,288,128]{2,1,0:T(8,128)(2,1)S(1)} %get-tuple-element.41.refs_5_), channel_id=1, source_target_pairs={{0,1},{1,0},{2,3},{3,2},{4,5},{5,4},{6,7},{7,6},{8,9},{9,8},{10,11... | collective-permute-start | bytes 1769480 | tf_op jit(solution)/shard_map/ppermute | solution.py:29
  41.5 11.4 %collective-permute-start.11 = (bf16[8,288,128]{2,1,0:T(8,128)(2,1)S(1)}, bf16[8,288,128]{2,1,0:T(8,128)(2,1)S(1)}, u32[]{:S(2)}, u32[]{:S(2)}) collective-permute-start(bf16[8,288,128]{2,1,0:T(8,128)(2,1)S(1)} %get-tuple-element.46), channel_id=1, source_target_pairs={{0,16},{1,65},{2,18},{3,67},{4,20},{5,69},{6,22},{7,71},{8,24},{9,... | collective-permute-start | bytes 1769480 | tf_op jit(solution)/shard_map/ppermute | solution.py:49
  52.9 2.1 %collective-permute-start.12 = (bf16[8,288,128]{2,1,0:T(8,128)(2,1)S(1)}, bf16[8,288,128]{2,1,0:T(8,128)(2,1)S(1)}, u32[]{:S(2)}, u32[]{:S(2)}) collective-permute-start(bf16[8,288,128]{2,1,0:T(8,128)(2,1)S(1)} %after.3.refs_2_), channel_id=1, source_target_pairs={{0,1},{1,0},{2,3},{3,2},{4,5},{5,4},{6,7},{7,6},{8,9},{9,8},{10,11... | collective-permute-start | bytes 1769480 | tf_op jit(solution)/shard_map/ppermute | solution.py:29
  56.3 10.0 %collective-permute-start.15 = (bf16[272,512]{1,0:T(8,128)(2,1)S(1)}, bf16[272,512]{1,0:T(8,128)(2,1)S(1)}, u32[]{:S(2)}, u32[]{:S(2)}) collective-permute-start(bf16[272,512]{1,0:T(8,128)(2,1)S(1)} %attend.10), channel_id=1, source_target_pairs={{0,6},{1,7},{2,4},{3,5},{4,2},{5,3},{6,0},{7,1},{8,14},{9,15},{10,... | collective-permute-start | bytes 835592 | tf_op jit(solution)/shard_map/ppermute | solution.py:29
  58.8 5.1 %copy-start.9 = (bf16[16,576]{1,0:T(8,128)(2,1)S(1)}, bf16[16,576]{1,0:T(8,128)(2,1)}, u32[]{:S(2)}) copy-start(bf16[16,576]{1,0:T(8,128)(2,1)} %param.13) | copy-start | bytes 55300
  58.8 5.1 %slice-start = ((bf16[16,576]{1,0:T(8,128)(2,1)}), bf16[16,64]{1,0:T(8,128)(2,1)S(1)}, s32[]{:S(2)}) async-start(bf16[16,576]{1,0:T(8,128)(2,1)} %param.13), calls=%async_computation | async-start | bytes 8192 | tf_op jit(solution)/shard_map/slice | solution.py:433
  58.8 9.6 %collective-permute-start.14 = (bf16[272,512]{1,0:T(8,128)(2,1)S(1)}, bf16[272,512]{1,0:T(8,128)(2,1)S(1)}, u32[]{:S(2)}, u32[]{:S(2)}) collective-permute-start(bf16[272,512]{1,0:T(8,128)(2,1)S(1)} %attend.9), channel_id=1, source_target_pairs={{0,2},{1,3},{2,0},{3,1},{4,6},{5,7},{6,4},{7,5},{8,10},{9,11},{10,... | collective-permute-start | bytes 835592 | tf_op jit(solution)/shard_map/ppermute | solution.py:29
  60.2 14.7 %collective-permute-start.13 = (bf16[272,512]{1,0:T(8,128)(2,1)S(1)}, bf16[272,512]{1,0:T(8,128)(2,1)S(1)}, u32[]{:S(2)}, u32[]{:S(2)}) collective-permute-start(bf16[272,512]{1,0:T(8,128)(2,1)S(1)} %attend.8), channel_id=1, source_target_pairs={{0,4},{1,5},{2,6},{3,7},{4,0},{5,1},{6,2},{7,3},{8,12},{9,13},{10,... | collective-permute-start | bytes 835592 | tf_op jit(solution)/shard_map/ppermute | solution.py:29
  63.9 10.9 %copy-start = (bf16[16,512,128]{2,1,0:T(8,128)(2,1)S(1)}, bf16[16,512,128]{2,1,0:T(8,128)(2,1)}, u32[]{:S(2)}) copy-start(bf16[16,512,128]{2,1,0:T(8,128)(2,1)} %up_ref.1) | copy-start | bytes 6291460
  65.2 34.1 %copy-start.3 = (bf16[2048,448]{0,1:T(8,128)(2,1)S(1)}, bf16[2048,448]{0,1:T(8,128)(2,1)}, u32[]{:S(2)}) copy-start(bf16[2048,448]{0,1:T(8,128)(2,1)} %param.19) | copy-start | bytes 5505028
  75.7 31.2 %copy-start.4 = (bf16[256,448]{0,1:T(8,128)(2,1)S(1)}, bf16[256,448]{0,1:T(8,128)(2,1)}, u32[]{:S(2)}) copy-start(bf16[256,448]{0,1:T(8,128)(2,1)} %param.20) | copy-start | bytes 688132
  75.7 4.5 %collective-permute-start.16 = (bf16[16,2048]{1,0:T(8,128)(2,1)S(1)}, bf16[16,2048]{1,0:T(8,128)(2,1)S(1)}, u32[]{:S(2)}, u32[]{:S(2)}) collective-permute-start(bf16[16,2048]{1,0:T(8,128)(2,1)S(1)} %merge.1), channel_id=1, source_target_pairs={{0,96},{1,25},{2,98},{3,27},{4,100},{5,29},{6,102},{7,31},{8,104},... | collective-permute-start | bytes 196616 | tf_op jit(solution)/shard_map/ppermute | solution.py:49
  78.3 5.8 %collective-permute-start.17 = (bf16[16,2048]{1,0:T(8,128)(2,1)S(1)}, bf16[16,2048]{1,0:T(8,128)(2,1)S(1)}, u32[]{:S(2)}, u32[]{:S(2)}) collective-permute-start(bf16[16,2048]{1,0:T(8,128)(2,1)S(1)} %merge.1), channel_id=1, source_target_pairs={{0,64},{1,17},{2,66},{3,19},{4,68},{5,21},{6,70},{7,23},{8,72},{9,... | collective-permute-start | bytes 196616 | tf_op jit(solution)/shard_map/ppermute | solution.py:49
  79.7 5.5 %collective-permute-start.18 = (bf16[16,2048]{1,0:T(8,128)(2,1)S(1)}, bf16[16,2048]{1,0:T(8,128)(2,1)S(1)}, u32[]{:S(2)}, u32[]{:S(2)}) collective-permute-start(bf16[16,2048]{1,0:T(8,128)(2,1)S(1)} %merge.1), channel_id=1, source_target_pairs={{0,32},{1,9},{2,34},{3,11},{4,36},{5,13},{6,38},{7,15},{8,40},{9,1... | collective-permute-start | bytes 196616 | tf_op jit(solution)/shard_map/ppermute | solution.py:49
  85.2 10.1 %collective-permute-start.19 = (bf16[64,2048]{1,0:T(8,128)(2,1)S(1)}, bf16[64,2048]{1,0:T(8,128)(2,1)S(1)}, u32[]{:S(2)}, u32[]{:S(2)}) collective-permute-start(bf16[64,2048]{1,0:T(8,128)(2,1)S(1)} %pad_maximum_fusion.1.p0), channel_id=1, source_target_pairs={{0,24},{1,97},{2,26},{3,99},{4,28},{5,101},{6,30},{7,103},{8,0},{9... | collective-permute-start | bytes 786440 | tf_op jit(solution)/shard_map/ppermute | solution.py:49
  88.6 8.0 %collective-permute-start.20 = (bf16[64,2048]{1,0:T(8,128)(2,1)S(1)}, bf16[64,2048]{1,0:T(8,128)(2,1)S(1)}, u32[]{:S(2)}, u32[]{:S(2)}) collective-permute-start(bf16[64,2048]{1,0:T(8,128)(2,1)S(1)} %pad_maximum_fusion.1.p0), channel_id=1, source_target_pairs={{0,16},{1,65},{2,18},{3,67},{4,20},{5,69},{6,22},{7,71},{8,24},{9,... | collective-permute-start | bytes 786440 | tf_op jit(solution)/shard_map/ppermute | solution.py:49
  89.2 10.1 %collective-permute-start.21 = (bf16[64,2048]{1,0:T(8,128)(2,1)S(1)}, bf16[64,2048]{1,0:T(8,128)(2,1)S(1)}, u32[]{:S(2)}, u32[]{:S(2)}) collective-permute-start(bf16[64,2048]{1,0:T(8,128)(2,1)S(1)} %pad_maximum_fusion.1.p0), channel_id=1, source_target_pairs={{0,8},{1,33},{2,10},{3,35},{4,12},{5,37},{6,14},{7,39},{8,16},{9,4... | collective-permute-start | bytes 786440 | tf_op jit(solution)/shard_map/ppermute | solution.py:49
  99.3 14.8 %copy-start.10 = (bf16[448]{0:T(512)(128)(2,1)S(1)}, bf16[448]{0:T(512)(128)(2,1)}, u32[]{:S(2)}) copy-start(bf16[448]{0:T(512)(128)(2,1)} %param.21) | copy-start | bytes 2692
  99.3 16.1 %copy-start.1 = (bf16[448,2304]{1,0:T(8,128)(2,1)S(1)}, bf16[448,2304]{1,0:T(8,128)(2,1)}, u32[]{:S(2)}) copy-start(bf16[448,2304]{1,0:T(8,128)(2,1)} %wg_any.1) | copy-start | bytes 6193156
  99.3 16.1 %copy-start.2 = (bf16[448,2304]{1,0:T(8,128)(2,1)S(1)}, bf16[448,2304]{1,0:T(8,128)(2,1)}, u32[]{:S(2)}) copy-start(bf16[448,2304]{1,0:T(8,128)(2,1)} %wu_any.1) | copy-start | bytes 6193156
  100.6 1.4 collective-permute-start.22
  102.1 6.4 %collective-permute-start.23 = (bf16[2,4,16,448]{3,2,1,0:T(8,128)(2,1)S(1)}, bf16[2,4,16,448]{3,2,1,0:T(8,128)(2,1)S(1)}, u32[]{:S(2)}, u32[]{:S(2)}) collective-permute-start(bf16[2,4,16,448]{3,2,1,0:T(8,128)(2,1)S(1)} %add_convert_fusion.pair), channel_id=1, source_target_pairs={{0,2},{1,3},{2,0},{3,1},{4,6},{5,7},{6,4},{7,5},{8,10},{9,11},{10,... | collective-permute-start | bytes 344072 | tf_op jit(solution)/shard_map/ppermute | solution.py:29
  102.2 8.9 %collective-permute-start.24 = (bf16[2,4,16,448]{3,2,1,0:T(8,128)(2,1)S(1)}, bf16[2,4,16,448]{3,2,1,0:T(8,128)(2,1)S(1)}, u32[]{:S(2)}, u32[]{:S(2)}) collective-permute-start(bf16[2,4,16,448]{3,2,1,0:T(8,128)(2,1)S(1)} %add_convert_fusion.pair), channel_id=1, source_target_pairs={{0,4},{1,5},{2,6},{3,7},{4,0},{5,1},{6,2},{7,3},{8,12},{9,13},{10,... | collective-permute-start | bytes 344072 | tf_op jit(solution)/shard_map/ppermute | solution.py:29
  104.7 8.7 %collective-permute-start.25 = (bf16[2,4,16,448]{3,2,1,0:T(8,128)(2,1)S(1)}, bf16[2,4,16,448]{3,2,1,0:T(8,128)(2,1)S(1)}, u32[]{:S(2)}, u32[]{:S(2)}) collective-permute-start(bf16[2,4,16,448]{3,2,1,0:T(8,128)(2,1)S(1)} %add_convert_fusion.pair), channel_id=1, source_target_pairs={{0,6},{1,7},{2,4},{3,5},{4,2},{5,3},{6,0},{7,1},{8,14},{9,15},{10,... | collective-permute-start | bytes 344072 | tf_op jit(solution)/shard_map/ppermute | solution.py:29
  114.0 1.4 collective-permute-start.26
  118.8 11.7 %collective-permute-start.27 = (bf16[4,16,4736]{2,1,0:T(8,128)(2,1)S(1)}, bf16[4,16,4736]{2,1,0:T(8,128)(2,1)S(1)}, u32[]{:S(2)}, u32[]{:S(2)}) collective-permute-start(bf16[4,16,4736]{2,1,0:T(8,128)(2,1)S(1)} %get-tuple-element.53), channel_id=1, source_target_pairs={{0,64},{1,17},{2,66},{3,19},{4,68},{5,21},{6,70},{7,23},{8,72},{9,... | collective-permute-start | bytes 1818632 | tf_op jit(solution)/shard_map/ppermute | solution.py:49
  119.8 17.1 %collective-permute-start.28 = (bf16[4,16,4736]{2,1,0:T(8,128)(2,1)S(1)}, bf16[4,16,4736]{2,1,0:T(8,128)(2,1)S(1)}, u32[]{:S(2)}, u32[]{:S(2)}) collective-permute-start(bf16[4,16,4736]{2,1,0:T(8,128)(2,1)S(1)} %get-tuple-element.54), channel_id=1, source_target_pairs={{0,32},{1,9},{2,34},{3,11},{4,36},{5,13},{6,38},{7,15},{8,40},{9,1... | collective-permute-start | bytes 1818632 | tf_op jit(solution)/shard_map/ppermute | solution.py:49
  119.8 17.1 %collective-permute-start.29 = (bf16[4,16,4736]{2,1,0:T(8,128)(2,1)S(1)}, bf16[4,16,4736]{2,1,0:T(8,128)(2,1)S(1)}, u32[]{:S(2)}, u32[]{:S(2)}) collective-permute-start(bf16[4,16,4736]{2,1,0:T(8,128)(2,1)S(1)} %get-tuple-element.55), channel_id=1, source_target_pairs={{0,96},{1,25},{2,98},{3,27},{4,100},{5,29},{6,102},{7,31},{8,104},... | collective-permute-start | bytes 1818632 | tf_op jit(solution)/shard_map/ppermute | solution.py:49
  137.4 6.9 %collective-permute-start.30 = (bf16[16,4736]{1,0:T(8,128)(2,1)S(1)}, bf16[16,4736]{1,0:T(8,128)(2,1)S(1)}, u32[]{:S(2)}, u32[]{:S(2)}) collective-permute-start(bf16[16,4736]{1,0:T(8,128)(2,1)S(1)} %get-tuple-element.57), channel_id=1, source_target_pairs={{0,16},{1,65},{2,18},{3,67},{4,20},{5,69},{6,22},{7,71},{8,24},{9,... | collective-permute-start | bytes 454664 | tf_op jit(solution)/shard_map/ppermute | solution.py:49
  138.1 7.7 %collective-permute-start.31 = (bf16[16,4736]{1,0:T(8,128)(2,1)S(1)}, bf16[16,4736]{1,0:T(8,128)(2,1)S(1)}, u32[]{:S(2)}, u32[]{:S(2)}) collective-permute-start(bf16[16,4736]{1,0:T(8,128)(2,1)S(1)} %get-tuple-element.58), channel_id=1, source_target_pairs={{0,8},{1,33},{2,10},{3,35},{4,12},{5,37},{6,14},{7,39},{8,16},{9,4... | collective-permute-start | bytes 454664 | tf_op jit(solution)/shard_map/ppermute | solution.py:49
  139.0 6.9 %collective-permute-start.32 = (bf16[16,4736]{1,0:T(8,128)(2,1)S(1)}, bf16[16,4736]{1,0:T(8,128)(2,1)S(1)}, u32[]{:S(2)}, u32[]{:S(2)}) collective-permute-start(bf16[16,4736]{1,0:T(8,128)(2,1)S(1)} %get-tuple-element.59), channel_id=1, source_target_pairs={{0,24},{1,97},{2,26},{3,99},{4,28},{5,101},{6,30},{7,103},{8,0},{9... | collective-permute-start | bytes 454664 | tf_op jit(solution)/shard_map/ppermute | solution.py:49

commit v6 on v5

--- a/solution.py
+++ b/solution.py
@@ -77,8 +77,8 @@
     return ((px + kx) % 4) * 4 + (pz + kz) % 4
 
 
-def plan_kernel(where, prompts, home_ref, prompt_ref, chosen_ref, picks_ref, use_ref):
-    px, pz, core, lane = where[0], where[1], where[2], where[3]
+def plan_kernel(where, home_ref, prompt_ref, chosen_ref, picks_ref):
+    px, pz, lane = where[0], where[1], where[3]
     replica = px * 4 + pz
     i32 = jnp.int32
     home = home_ref[...].reshape(16, 128)
@@ -104,6 +104,12 @@
         pick = needed & (before > rank - 0.5) & (before < rank + 0.5)
         picks_ref[rank : rank + 1] = jnp.sum(jnp.where(pick, slot, 0), axis=0, keepdims=True)
 
+
+def use_kernel(where, prompts, home_ref, chosen_ref, _, use_ref):
+    px, pz, core, lane = where[0], where[1], where[2], where[3]
+    replica = px * 4 + pz
+    i32 = jnp.int32
+    chosen = chosen_ref[...]
     mine = pltpu.roll(chosen, (256 - replica * 16) % 256, 1)[:, :128]
     mine = jnp.concatenate([mine.astype(f32), jnp.zeros((96, 128), f32)], axis=0).T[:16]
     block = lax.broadcasted_iota(i32, (16, PB), 1).astype(f32)
@@ -120,9 +126,9 @@
     rank = jnp.sum(jnp.where(fewer, 1, 0), axis=0, keepdims=True)
     key = jnp.where(need, holder * CAP + rank, -1)
     at = lax.broadcasted_iota(i32, (64, PB), 0)
-    kb = at // 16
-    kb = jnp.where(kb == 2, 3, jnp.where(kb == 3, 2, kb))
-    sib, ka, place = (at // 8) % 2, (at // 2) % 4, at % 2
+    piece, ka, place = at // 8, (at // 2) % 4, at % 2
+    sib = jnp.where((piece == 1) | (piece >= 5), 1, 0)
+    kb = jnp.where(piece < 2, 0, (piece + 1) % 3 + 1)
     from_core = core ^ sib
     kx = jnp.where(from_core == 0, ka, kb)
     kz = jnp.where(from_core == 0, kb, ka)
@@ -148,6 +154,17 @@
                 out[at, 4 * BS :, :] = jnp.concatenate([rope[:32], rope[32:]], axis=1)
 
 
+def ask_kernel(queries, own, _, q_ref, own_ref):
+    for head in range(16):
+        x = queries[:, head * KV : (head + 1) * KV]
+        rows = slice(head * 16, (head + 1) * 16)
+        q_ref[rows, :LAT] = x[:, :LAT]
+        q_ref[rows, LAT:] = jnp.concatenate([x[:, LAT:], x[:, LAT:]], axis=1)
+    x = own[...]
+    own_ref[:, :LAT] = x[:, :LAT]
+    own_ref[:, LAT:] = jnp.concatenate([x[:, LAT:], x[:, LAT:]], axis=1)
+
+
 def regroup_kernel(*refs):
     refs = refs[:4] + refs[8:]
     for ka in range(4):
@@ -185,28 +202,30 @@
     return jnp.where(keep, rope, jnp.zeros_like(rope))
 
 
-def attend_kernel(first, groups, chips, resume, last, *refs):
+def attend_kernel(first, sizes, chips, resume, last, *refs):
+    groups, count = len(sizes), sum(sizes)
     use_ref, refs = refs[0], refs[1:]
     qs, refs = dict(zip(chips, refs)), refs[len(chips) :]
-    pieces, refs = refs[: 2 * groups], refs[2 * groups :]
+    pieces, refs = refs[:count], refs[count:]
     if resume:
         (acc_in, stat_in), refs = refs[:2], refs[2:]
     m_rows = 256
-    slot = lax.broadcasted_iota(jnp.int32, (64, 1024), 0)
-    token = lax.broadcasted_iota(jnp.int32, (64, 1024), 1)
-    biases = []
-    for g in range(groups):
-        spread = ((token // 32) % 16 + 16 * (first + g) == slot).astype(f32).astype(bf16)
+    members, biases = [], []
+    for g, size in enumerate(sizes):
+        at = sum(sizes[:g])
+        members.append(pieces[at : at + size])
+        slot = lax.broadcasted_iota(jnp.int32, (64, size * 512), 0)
+        token = lax.broadcasted_iota(jnp.int32, (64, size * 512), 1)
+        spread = (token // 32) % (8 * size) + 8 * (first + at) == slot
+        spread = spread.astype(f32).astype(bf16)
         used = jnp.dot(use_ref[...], spread, preferred_element_type=f32)
         biases.append((used - 1.0) * -NEG)
 
     def values(g):
-        mine = pieces[2 * g : 2 * g + 2]
-        return jnp.concatenate([half_latent(mine, 0), half_latent(mine, 1)], axis=0)
+        return jnp.concatenate([half_latent(members[g], h) for h in range(2)], axis=0)
 
     def scores(chip, g):
-        mine = pieces[2 * g : 2 * g + 2]
-        ropes = jnp.concatenate([half_rope(mine, 0), half_rope(mine, 1)], axis=0)
+        ropes = jnp.concatenate([half_rope(members[g], h) for h in range(2)], axis=0)
         keys = jnp.concatenate([values(g), ropes], axis=1)
         s = lax.dot_general(
             qs[chip][...], keys, (((1,), (1,)), ((), ())), preferred_element_type=f32
@@ -234,14 +253,18 @@
             fade = jnp.exp2((top - new) * SCALE2)
             acc, total = acc * fade + o, total * fade + part
         top, s = new, ahead
-        if g == groups - 1 and not last:
+        if g == groups - 1 and last:
+            finish_heads(acc, top, total, refs[chips.index(chip)])
+        elif g == groups - 1:
             lane = lax.broadcasted_iota(jnp.int32, (m_rows, 128), 1)
             refs[0][chip] = acc
             refs[1][chip] = jnp.where(lane < 64, top, total)
     if not last:
         refs[2][...] = jnp.zeros((8, 128), f32)
-        return
-    out_ref = refs[0]
+
+
+def finish_heads(acc, top, total, out_ref):
+    m_rows = 256
     out_ref[:m_rows] = (acc / total).astype(bf16)
     lse = top * SCALE + jnp.log(total)
     hi = lse.astype(bf16).astype(f32)
@@ -253,15 +276,14 @@
     out_ref[m_rows:] = jnp.concatenate([stats, jnp.zeros_like(stats)], axis=1).astype(bf16)
 
 
-def attend(use, qs, first, pieces, carry=(), last=True):
-    groups = len(pieces) // 2
+def attend(use, qs, first, sizes, pieces, carry=(), last=True):
     if last:
-        outs = [shape(256 + 16, LAT)]
+        outs = [shape(256 + 16, LAT)] * len(qs)
     else:
         outs = [shape(4, 256, LAT, dtype=f32), shape(4, 256, 128, dtype=f32)]
         outs.append(shape(8, 128, dtype=f32))
     return call(
-        functools.partial(attend_kernel, first, groups, list(qs), bool(carry), last),
+        functools.partial(attend_kernel, first, sizes, list(qs), bool(carry), last),
         "attend",
         outs,
         [use, *qs.values(), *pieces, *carry],
@@ -339,12 +361,7 @@
             out[i, kx] = (residual[dp].astype(f32) + attn).astype(bf16)
 
 
-def ffn_kernel(where, half_ref, other_ref, gain_ref, wg_any, wu_any, stream_ref, *outs):
-    *outs, wg_ref, wu_ref, sem_g, sem_u = outs
-    bring_g = pltpu.make_async_copy(wg_any, wg_ref, sem_g)
-    bring_u = pltpu.make_async_copy(wu_any, wu_ref, sem_u)
-    bring_g.start()
-    bring_u.start()
+def ffn_kernel(where, half_ref, other_ref, gain_ref, wg_ref, wu_ref, stream_ref, *outs):
     px, pz, core = where[0], where[1], where[2]
     half, other = half_ref[...].astype(f32), other_ref[...].astype(f32)
     rows = jnp.concatenate(
@@ -360,14 +377,12 @@
     lane = lax.broadcasted_iota(jnp.int32, (256, 128), 1)
     tail = jnp.where(lane == 0, hi, jnp.where(lane == 1, squares - hi, 0.0)).astype(bf16)
     scaled = (wide * gain_ref[...].astype(f32)).astype(bf16)
-    bring_g.wait()
     gate = jnp.dot(scaled, wg_ref[...], preferred_element_type=f32).astype(bf16)
     gate = gate.reshape(4, 4, 16, FF)
     tail = tail.reshape(4, 4, 16, 128)
     for k in range(4):
         outs[k][:, :, :FF] = gate[:, k]
         outs[k][:, :, 2 * FF :] = tail[:, k]
-    bring_u.wait()
     up = jnp.dot(scaled, wu_ref[...], preferred_element_type=f32).astype(bf16)
     up = up.reshape(4, 4, 16, FF)
     for k in range(4):
@@ -428,17 +443,13 @@
     i32 = jnp.int32
     where = jnp.stack([px, pz, core, lane]).astype(i32)
 
-    q = queries.reshape(16, 16, KV).transpose(1, 0, 2).reshape(256, KV)
-    q = jnp.concatenate([q, q[:, LAT:]], axis=1)
-    own = jnp.concatenate([own_latent, own_latent[:, LAT:]], axis=1)
-    qs = {0: q, **{k: send_y(q, k) for k in (1, 2, 3)}}
-
-    picks, use = call(
+    homes = block_home.reshape(4, 4, 128)
+    (picks,) = call(
         plan_kernel,
         "plan",
-        [shape(CAP, 128, dtype=i32), shape(16, 64)],
-        [where, row_prompt, block_home.reshape(4, 4, 128), row_prompt.reshape(1, 256), chosen.T],
-        scalars=2,
+        [shape(CAP, 128, dtype=i32)],
+        [where, homes, row_prompt.reshape(1, 256), chosen.T],
+        scalars=1,
     )
 
     sent = call(
@@ -450,21 +461,39 @@
     )
     got = [sent[0]] + [send_dp(sent[k], 0, k) for k in (1, 2, 3)]
 
+    (use,) = call(
+        use_kernel,
+        "use",
+        [shape(16, 64)],
+        [where, row_prompt, homes, chosen.T, sent[0]],
+        scalars=2,
+        anys=1,
+    )
+
+    q, own = call(
+        ask_kernel,
+        "ask",
+        [shape(256, LAT + 128), shape(16, LAT + 128)],
+        [queries, own_latent, sent[0]],
+        anys=1,
+    )
+    qs = {0: q, **{k: send_y(q, k) for k in (1, 2, 3)}}
+
     groups = call(regroup_kernel, "regroup", [shape(8, 288, 128)] * 4, [*got, use, *list(qs.values())[1:]], anys=4)
     arrived = {0: groups[0]}
     for k in (1, 3, 2):
         arrived[k] = send_dp(groups[k], 1, k)
     pieces = [groups[0], swap_core(groups[0])]
-    *carry, done = attend(use, qs, 0, pieces, last=False)
-    second, third = after(done, arrived[1], arrived[3])
-    pieces = [second, swap_core(second), third, swap_core(third)]
-    *carry, done = attend(use, qs, 1, pieces, carry, last=False)
-    (fourth,) = after(done, arrived[2])
-    pieces = [fourth, swap_core(fourth)]
+    *carry, done = attend(use, qs, 0, (2,), pieces, last=False)
+    far = after(done, arrived[1], arrived[2], arrived[3])
+    far_other = [swap_core(v) for v in far]
+    others = {k: qs[k] for k in (2, 1, 3)}
+    *rest, done = attend(use, others, 2, (2, 1), far, carry, last=False)
     parts = []
-    for k in (2, 1, 3, 0):
-        (o,) = attend(use, {k: qs[k]}, 3, pieces, carry)
-        parts.append(send_y(o, k) if k else o)
+    for k in others:
+        (o,) = attend(use, {k: qs[k]}, 5, (2, 1), far_other, rest)
+        parts.append(send_y(o, k))
+    parts += attend(use, {0: q}, 2, (2, 2, 2), list(far) + far_other, carry)
     per_head = merge(parts, q, own, value_up)
 
     near = [per_head] + [send_dp(per_head, 0, 4 - k) for k in (1, 2, 3)]
@@ -493,9 +522,7 @@
         [shape(16, 16, 448)] + [shape(4, 16, 2 * FF + 128)] * 4,
         [where, half, other, norm_gain.reshape(1, 448), gate_weight, up_weight],
         scalars=1,
-        anys=2,
         limit=30,
-        scratch_shapes=[pltpu.VMEM((448, FF), bf16)] * 2 + [pltpu.SemaphoreType.DMA(())] * 2,
     )
     got = [sums[0]] + [send_dp(sums[k], 0, k) for k in (2, 1, 3)]
     sums = call(fold_kernel, "fold", [shape(16, 2 * FF + 128)] * 4, got)

time: 147 us -> 141 us (0.959)
  waiting for transfers between devices: 69.4 us -> 61.3 us
  starting transfers between devices: 46 us -> 49 us
    ppermute x15, waiting for transfers between devices: 30.4 us -> 23.1 us  [send(): return lax.ppermute(x, axis, [(i, to(i)) for i in range(n)])]
    ppermute x15, starting transfers between devices: 15 us -> 17.1 us  [send(): return lax.ppermute(x, axis, [(i, to(i)) for i in range(n)])]
    pallas_call x18 -> x19, Pallas kernels: 26.1 us -> 25.7 us  [call(): pl.pallas_call(kernel, out_shape=outs, in_specs=[SMEM] * scalars + [VMEM]...]
  transfers between devices with their start and end apart: 33 -> 33, of which waited for: 24 -> 23; matrix products, arithmetic and copies ran while one was open for 1% -> 0% of each run, Pallas kernels for 12% -> 12%
where the time goes in v6:
time: 141 us
  waiting for transfers between devices  61.3 us (43%)
  starting transfers between devices  49 us (35%)
  Pallas kernels  26.6 us (19%)
  local copies, waits for them, and re-layouts  2.75 us (2%)
    ppermute x18, waiting for transfers between devices, send_dp(): return lax.ppermute(x, ('dp', 'tp'), pairs)  38.2 us
    ppermute x18, starting transfers between devices, send_dp(): return lax.ppermute(x, ('dp', 'tp'), pairs)  31.8 us
    pallas_call x19, Pallas kernels, call(): pl.pallas_call(kernel, out_shape=outs, in_specs=[SMEM] * scalars + [VMEM]...  25.7 us
    ppermute x15, waiting for transfers between devices, send(): return lax.ppermute(x, axis, [(i, to(i)) for i in range(n)])  23.1 us
    ppermute x15, starting transfers between devices, send(): return lax.ppermute(x, axis, [(i, to(i)) for i in range(n)])  17.1 us
  transfers between devices with their start and end apart: 33, of which 23 were waited for; matrix products, arithmetic and copies ran while one was open for 0% of the time, Pallas kernels for 12%

profile of v6, /device:TPU:0, one launch (start us, length us, event | category | flops | bytes accessed | tf_op | source)
XLA Modules:
  0.0 140.6 jit_solution(1021998053848776088)
XLA Ops:
  0.7 2.7 %reshape.24.tokens = bf16[16,64,576]{2,1,0:T(8,128)(2,1)S(1)} reshape(bf16[16,36864]{1,0:T(8,128)(2,1)} %param.14) | data formatting | bytes 2359296 | tf_op jit(solution)/shard_map/reshape | solution.py:459
  3.5 1.0 plan.1.picks
  4.5 1.2 fetch.1
  5.8 3.4 %collective-permute-start = (bf16[256,640]{1,0:T(8,128)(2,1)S(1)}, bf16[256,640]{1,0:T(8,128)(2,1)S(1)}, u32[]{:S(2)}, u32[]{:S(2)}) collective-permute-start(bf16[256,640]{1,0:T(8,128)(2,1)S(1)} %get-tuple-element.32.refs_1_.q_ref), channel_id=1, source_target_pairs={{0,4},{1,5},{2,6},{3,7},{4,0},{5,1},{6,2},{7,3},{8,12},{9,13},{10,... | collective-permute-start | bytes 983048 | tf_op jit(solution)/shard_map/ppermute | solution.py:29
  9.2 1.5 %collective-permute-start.3 = (bf16[8,288,128]{2,1,0:T(8,128)(2,1)S(1)}, bf16[8,288,128]{2,1,0:T(8,128)(2,1)S(1)}, u32[]{:S(2)}, u32[]{:S(2)}) collective-permute-start(bf16[8,288,128]{2,1,0:T(8,128)(2,1)S(1)} %get-tuple-element.33), channel_id=1, source_target_pairs={{0,32},{1,9},{2,34},{3,11},{4,36},{5,13},{6,38},{7,15},{8,40},{9,1... | collective-permute-start | bytes 1769480 | tf_op jit(solution)/shard_map/ppermute | solution.py:49
  10.7 2.7 %collective-permute-start.4 = (bf16[8,288,128]{2,1,0:T(8,128)(2,1)S(1)}, bf16[8,288,128]{2,1,0:T(8,128)(2,1)S(1)}, u32[]{:S(2)}, u32[]{:S(2)}) collective-permute-start(bf16[8,288,128]{2,1,0:T(8,128)(2,1)S(1)} %get-tuple-element.34), channel_id=1, source_target_pairs={{0,64},{1,17},{2,66},{3,19},{4,68},{5,21},{6,70},{7,23},{8,72},{9,... | collective-permute-start | bytes 1769480 | tf_op jit(solution)/shard_map/ppermute | solution.py:49
  13.4 1.4 %collective-permute-start.5 = (bf16[8,288,128]{2,1,0:T(8,128)(2,1)S(1)}, bf16[8,288,128]{2,1,0:T(8,128)(2,1)S(1)}, u32[]{:S(2)}, u32[]{:S(2)}) collective-permute-start(bf16[8,288,128]{2,1,0:T(8,128)(2,1)S(1)} %get-tuple-element.35), channel_id=1, source_target_pairs={{0,96},{1,25},{2,98},{3,27},{4,100},{5,29},{6,102},{7,31},{8,104},... | collective-permute-start | bytes 1769480 | tf_op jit(solution)/shard_map/ppermute | solution.py:49
  14.9 0.7 collective-permute-start.1
  15.5 1.5 %collective-permute-done.refs_6_.refs_3_.refs_1_ = bf16[256,640]{1,0:T(8,128)(2,1)S(1)} collective-permute-done((bf16[256,640]{1,0:T(8,128)(2,1)S(1)}, bf16[256,640]{1,0:T(8,128)(2,1)S(1)}, u32[]{:S(2)}, u32[]{:S(2)}) %collective-permute-start) | collective-permute-done | bytes 327712 | tf_op jit(solution)/shard_map/ppermute | solution.py:29
  17.1 3.1 %collective-permute-start.2 = (bf16[256,640]{1,0:T(8,128)(2,1)S(1)}, bf16[256,640]{1,0:T(8,128)(2,1)S(1)}, u32[]{:S(2)}, u32[]{:S(2)}) collective-permute-start(bf16[256,640]{1,0:T(8,128)(2,1)S(1)} %get-tuple-element.32.refs_1_.q_ref), channel_id=1, source_target_pairs={{0,6},{1,7},{2,4},{3,5},{4,2},{5,3},{6,0},{7,1},{8,14},{9,15},{10,... | collective-permute-start | bytes 983048 | tf_op jit(solution)/shard_map/ppermute | solution.py:29
  20.2 1.6 %use.1.refs_4_.refs_0_ = bf16[16,64]{1,0:T(8,128)(2,1)S(1)} custom-call(s32[4]{0:T(128)S(1)} %pad_add_fusion.where, s32[256]{0:T(256)S(1)} %copy-done.9, s32[4,4,128]{2,1,0:T(4,128)S(1)} %bitcast.19, s32[32,256]{1,0:T(8,128)S(1)} %bitcast.17, bf16[8,288,128]{2,1,0:T(8,128)(2,1)S(1)} %get-tuple-element.31._.refs_0_), custom_call_target="tpu_custom_call" | custom-call | tf_op jit(solution)/shard_map/use/pallas_call | solution.py:58
  21.8 2.6 %collective-permute-done.1.refs_5_.refs_2_.refs_1_ = bf16[256,640]{1,0:T(8,128)(2,1)S(1)} collective-permute-done((bf16[256,640]{1,0:T(8,128)(2,1)S(1)}, bf16[256,640]{1,0:T(8,128)(2,1)S(1)}, u32[]{:S(2)}, u32[]{:S(2)}) %collective-permute-start.1) | collective-permute-done | bytes 327712 | tf_op jit(solution)/shard_map/ppermute | solution.py:29
  24.3 2.5 %collective-permute-done.2.refs_7_.refs_4_.refs_3_.refs_1_ = bf16[256,640]{1,0:T(8,128)(2,1)S(1)} collective-permute-done((bf16[256,640]{1,0:T(8,128)(2,1)S(1)}, bf16[256,640]{1,0:T(8,128)(2,1)S(1)}, u32[]{:S(2)}, u32[]{:S(2)}) %collective-permute-start.2) | collective-permute-done | bytes 327712 | tf_op jit(solution)/shard_map/ppermute | solution.py:29
  26.8 0.8 collective-permute-done.4.refs_2_
  27.9 2.0 %collective-permute-start.7 = (bf16[8,288,128]{2,1,0:T(8,128)(2,1)S(1)}, bf16[8,288,128]{2,1,0:T(8,128)(2,1)S(1)}, u32[]{:S(2)}, u32[]{:S(2)}) collective-permute-start(bf16[8,288,128]{2,1,0:T(8,128)(2,1)S(1)} %get-tuple-element.38), channel_id=1, source_target_pairs={{0,8},{1,33},{2,10},{3,35},{4,12},{5,37},{6,14},{7,39},{8,16},{9,4... | collective-permute-start | bytes 1769480 | tf_op jit(solution)/shard_map/ppermute | solution.py:49
  29.8 3.6 %collective-permute-start.8 = (bf16[8,288,128]{2,1,0:T(8,128)(2,1)S(1)}, bf16[8,288,128]{2,1,0:T(8,128)(2,1)S(1)}, u32[]{:S(2)}, u32[]{:S(2)}) collective-permute-start(bf16[8,288,128]{2,1,0:T(8,128)(2,1)S(1)} %get-tuple-element.39), channel_id=1, source_target_pairs={{0,16},{1,65},{2,18},{3,67},{4,20},{5,69},{6,22},{7,71},{8,24},{9,... | collective-permute-start | bytes 1769480 | tf_op jit(solution)/shard_map/ppermute | solution.py:49
  33.4 1.0 collective-permute-start.9
  34.4 3.2 %attend.6 = (f32[4,256,512]{2,1,0:T(8,128)S(1)}, f32[4,256,128]{2,1,0:T(8,128)S(1)}, f32[8,128]{1,0:T(8,128)S(1)}) custom-call(bf16[16,64]{1,0:T(8,128)(2,1)S(1)} %use.1.refs_4_.refs_0_, bf16[256,640]{1,0:T(8,128)(2,1)S(1)} %get-tuple-element.32.refs_1_.q_ref, bf16[256,640]{1,0:T(8,128)(2,1)S(1)} %collective-permute-done.1.refs_5_.refs_2_.refs_1_, ...), custom_call_target="tpu_custom_call" | custom-call | tf_op jit(solution)/shard_map/attend/pallas_call | solution.py:58
  37.7 2.2 %collective-permute-done.7.refs_0_ = bf16[8,288,128]{2,1,0:T(8,128)(2,1)S(1)} collective-permute-done((bf16[8,288,128]{2,1,0:T(8,128)(2,1)S(1)}, bf16[8,288,128]{2,1,0:T(8,128)(2,1)S(1)}, u32[]{:S(2)}, u32[]{:S(2)}) %collective-permute-start.7) | collective-permute-done | bytes 589856 | tf_op jit(solution)/shard_map/ppermute | solution.py:49
  39.8 7.8 %collective-permute-done.8.refs_1_ = bf16[8,288,128]{2,1,0:T(8,128)(2,1)S(1)} collective-permute-done((bf16[8,288,128]{2,1,0:T(8,128)(2,1)S(1)}, bf16[8,288,128]{2,1,0:T(8,128)(2,1)S(1)}, u32[]{:S(2)}, u32[]{:S(2)}) %collective-permute-start.8) | collective-permute-done | bytes 589856 | tf_op jit(solution)/shard_map/ppermute | solution.py:49
  48.4 4.6 %attend.7 = (f32[4,256,512]{2,1,0:T(8,128)S(1)}, f32[4,256,128]{2,1,0:T(8,128)S(1)}, f32[8,128]{1,0:T(8,128)}) custom-call(bf16[16,64]{1,0:T(8,128)(2,1)S(1)} %use.1.refs_4_.refs_0_, bf16[256,640]{1,0:T(8,128)(2,1)S(1)} %collective-permute-done.refs_6_.refs_3_.refs_1_, bf16[256,640]{1,0:T(8,128)(2,1)S(1)} %collective-permute-done.1.refs_5_.refs_2_.refs_1_, ...), custom_call_target="tpu_custom_call" | custom-call | tf_op jit(solution)/shard_map/attend/pallas_call | solution.py:58
  53.0 1.6 %attend.8 = bf16[272,512]{1,0:T(8,128)(2,1)S(1)} custom-call(bf16[16,64]{1,0:T(8,128)(2,1)S(1)} %use.1.refs_4_.refs_0_, bf16[256,640]{1,0:T(8,128)(2,1)S(1)} %collective-permute-done.refs_6_.refs_3_.refs_1_, bf16[8,288,128]{2,1,0:T(8,128)(2,1)S(1)} %collective-permute-done.10.refs_2_.refs_5_, ...), custom_call_target="tpu_custom_call" | custom-call | tf_op jit(solution)/shard_map/attend/pallas_call | solution.py:58
  54.6 1.2 collective-permute-start.13
  55.8 1.6 %attend.9 = bf16[272,512]{1,0:T(8,128)(2,1)S(1)} custom-call(bf16[16,64]{1,0:T(8,128)(2,1)S(1)} %use.1.refs_4_.refs_0_, bf16[256,640]{1,0:T(8,128)(2,1)S(1)} %collective-permute-done.1.refs_5_.refs_2_.refs_1_, bf16[8,288,128]{2,1,0:T(8,128)(2,1)S(1)} %collective-permute-done.10.refs_2_.refs_5_, ...), custom_call_target="tpu_custom_call" | custom-call | tf_op jit(solution)/shard_map/attend/pallas_call | solution.py:58
  57.4 1.9 %collective-permute-start.14 = (bf16[272,512]{1,0:T(8,128)(2,1)S(1)}, bf16[272,512]{1,0:T(8,128)(2,1)S(1)}, u32[]{:S(2)}, u32[]{:S(2)}) collective-permute-start(bf16[272,512]{1,0:T(8,128)(2,1)S(1)} %attend.9), channel_id=1, source_target_pairs={{0,2},{1,3},{2,0},{3,1},{4,6},{5,7},{6,4},{7,5},{8,10},{9,11},{10,... | collective-permute-start | bytes 835592 | tf_op jit(solution)/shard_map/ppermute | solution.py:29
  59.4 1.6 %attend.10 = bf16[272,512]{1,0:T(8,128)(2,1)S(1)} custom-call(bf16[16,64]{1,0:T(8,128)(2,1)S(1)} %use.1.refs_4_.refs_0_, bf16[256,640]{1,0:T(8,128)(2,1)S(1)} %collective-permute-done.2.refs_7_.refs_4_.refs_3_.refs_1_, bf16[8,288,128]{2,1,0:T(8,128)(2,1)S(1)} %collective-permute-done.10.refs_2_.refs_5_, ...), custom_call_target="tpu_custom_call" | custom-call | tf_op jit(solution)/shard_map/attend/pallas_call | solution.py:58
  61.0 1.1 collective-permute-start.15
  62.1 2.8 %attend.11.o3 = bf16[272,512]{1,0:T(8,128)(2,1)S(1)} custom-call(bf16[16,64]{1,0:T(8,128)(2,1)S(1)} %use.1.refs_4_.refs_0_, bf16[256,640]{1,0:T(8,128)(2,1)S(1)} %get-tuple-element.32.refs_1_.q_ref, bf16[8,288,128]{2,1,0:T(8,128)(2,1)S(1)} %get-tuple-element.41.refs_4_.refs_2_, bf16[8,288,128]{2,1,0:T(8,128)(2,1)S(1)} %get-tuple-element.42.refs_5_.refs_3_, ...), custom_call_target="tpu_custom_call" | custom-call | tf_op jit(solution)/shard_map/attend/pallas_call | solution.py:58
  64.9 0.8 collective-permute-done.13.o0
  65.6 5.0 %collective-permute-done.14.o1 = bf16[272,512]{1,0:T(8,128)(2,1)S(1)} collective-permute-done((bf16[272,512]{1,0:T(8,128)(2,1)S(1)}, bf16[272,512]{1,0:T(8,128)(2,1)S(1)}, u32[]{:S(2)}, u32[]{:S(2)}) %collective-permute-start.14) | collective-permute-done | bytes 278560 | tf_op jit(solution)/shard_map/ppermute | solution.py:29
  71.2 0.8 merge.1
  72.0 1.9 %collective-permute-start.18 = (bf16[16,2048]{1,0:T(8,128)(2,1)S(1)}, bf16[16,2048]{1,0:T(8,128)(2,1)S(1)}, u32[]{:S(2)}, u32[]{:S(2)}) collective-permute-start(bf16[16,2048]{1,0:T(8,128)(2,1)S(1)} %merge.1), channel_id=1, source_target_pairs={{0,32},{1,9},{2,34},{3,11},{4,36},{5,13},{6,38},{7,15},{8,40},{9,1... | collective-permute-start | bytes 196616 | tf_op jit(solution)/shard_map/ppermute | solution.py:49
  74.0 2.2 %collective-permute-start.17 = (bf16[16,2048]{1,0:T(8,128)(2,1)S(1)}, bf16[16,2048]{1,0:T(8,128)(2,1)S(1)}, u32[]{:S(2)}, u32[]{:S(2)}) collective-permute-start(bf16[16,2048]{1,0:T(8,128)(2,1)S(1)} %merge.1), channel_id=1, source_target_pairs={{0,64},{1,17},{2,66},{3,19},{4,68},{5,21},{6,70},{7,23},{8,72},{9,... | collective-permute-start | bytes 196616 | tf_op jit(solution)/shard_map/ppermute | solution.py:49
  76.2 1.5 %collective-permute-start.16 = (bf16[16,2048]{1,0:T(8,128)(2,1)S(1)}, bf16[16,2048]{1,0:T(8,128)(2,1)S(1)}, u32[]{:S(2)}, u32[]{:S(2)}) collective-permute-start(bf16[16,2048]{1,0:T(8,128)(2,1)S(1)} %merge.1), channel_id=1, source_target_pairs={{0,96},{1,25},{2,98},{3,27},{4,100},{5,29},{6,102},{7,31},{8,104},... | collective-permute-start | bytes 196616 | tf_op jit(solution)/shard_map/ppermute | solution.py:49
  77.7 2.0 %collective-permute-done.17 = bf16[16,2048]{1,0:T(8,128)(2,1)S(1)} collective-permute-done((bf16[16,2048]{1,0:T(8,128)(2,1)S(1)}, bf16[16,2048]{1,0:T(8,128)(2,1)S(1)}, u32[]{:S(2)}, u32[]{:S(2)}) %collective-permute-start.17) | collective-permute-done | bytes 65568 | tf_op jit(solution)/shard_map/ppermute | solution.py:49
  79.7 0.7 collective-permute-done.16
  80.5 2.2 %collective-permute-start.19 = (bf16[64,2048]{1,0:T(8,128)(2,1)S(1)}, bf16[64,2048]{1,0:T(8,128)(2,1)S(1)}, u32[]{:S(2)}, u32[]{:S(2)}) collective-permute-start(bf16[64,2048]{1,0:T(8,128)(2,1)S(1)} %pad_maximum_fusion.p0), channel_id=1, source_target_pairs={{0,24},{1,97},{2,26},{3,99},{4,28},{5,101},{6,30},{7,103},{8,0},{9... | collective-permute-start | bytes 786440 | tf_op jit(solution)/shard_map/ppermute | solution.py:49
  82.7 1.4 %collective-permute-start.20 = (bf16[64,2048]{1,0:T(8,128)(2,1)S(1)}, bf16[64,2048]{1,0:T(8,128)(2,1)S(1)}, u32[]{:S(2)}, u32[]{:S(2)}) collective-permute-start(bf16[64,2048]{1,0:T(8,128)(2,1)S(1)} %pad_maximum_fusion.p0), channel_id=1, source_target_pairs={{0,16},{1,65},{2,18},{3,67},{4,20},{5,69},{6,22},{7,71},{8,24},{9,... | collective-permute-start | bytes 786440 | tf_op jit(solution)/shard_map/ppermute | solution.py:49
  84.1 0.7 collective-permute-start.21
  84.8 4.7 %collective-permute-done.19.p1 = bf16[64,2048]{1,0:T(8,128)(2,1)S(1)} collective-permute-done((bf16[64,2048]{1,0:T(8,128)(2,1)S(1)}, bf16[64,2048]{1,0:T(8,128)(2,1)S(1)}, u32[]{:S(2)}, u32[]{:S(2)}) %collective-permute-start.19) | collective-permute-done | bytes 262176 | tf_op jit(solution)/shard_map/ppermute | solution.py:49
  89.4 1.2 collective-permute-done.20.p2
  90.7 2.7 %collective-permute-done.21.p3 = bf16[64,2048]{1,0:T(8,128)(2,1)S(1)} collective-permute-done((bf16[64,2048]{1,0:T(8,128)(2,1)S(1)}, bf16[64,2048]{1,0:T(8,128)(2,1)S(1)}, u32[]{:S(2)}, u32[]{:S(2)}) %collective-permute-start.21) | collective-permute-done | bytes 262176 | tf_op jit(solution)/shard_map/ppermute | solution.py:49
  93.4 1.3 project.1
  94.8 1.3 collective-permute-done.22
  96.2 0.6 collective-permute-start.23
  96.8 3.2 %collective-permute-start.24 = (bf16[2,4,16,448]{3,2,1,0:T(8,128)(2,1)S(1)}, bf16[2,4,16,448]{3,2,1,0:T(8,128)(2,1)S(1)}, u32[]{:S(2)}, u32[]{:S(2)}) collective-permute-start(bf16[2,4,16,448]{3,2,1,0:T(8,128)(2,1)S(1)} %add_convert_fusion.pair), channel_id=1, source_target_pairs={{0,4},{1,5},{2,6},{3,7},{4,0},{5,1},{6,2},{7,3},{8,12},{9,13},{10,... | collective-permute-start | bytes 344072 | tf_op jit(solution)/shard_map/ppermute | solution.py:29
  100.0 1.0 collective-permute-start.25
  101.1 1.5 %collective-permute-done.23.t1 = bf16[2,4,16,448]{3,2,1,0:T(8,128)(2,1)S(1)} collective-permute-done((bf16[2,4,16,448]{3,2,1,0:T(8,128)(2,1)S(1)}, bf16[2,4,16,448]{3,2,1,0:T(8,128)(2,1)S(1)}, u32[]{:S(2)}, u32[]{:S(2)}) %collective-permute-start.23) | collective-permute-done | bytes 114720 | tf_op jit(solution)/shard_map/ppermute | solution.py:29
  102.6 3.8 %collective-permute-done.24.t2 = bf16[2,4,16,448]{3,2,1,0:T(8,128)(2,1)S(1)} collective-permute-done((bf16[2,4,16,448]{3,2,1,0:T(8,128)(2,1)S(1)}, bf16[2,4,16,448]{3,2,1,0:T(8,128)(2,1)S(1)}, u32[]{:S(2)}, u32[]{:S(2)}) %collective-permute-start.24) | collective-permute-done | bytes 114720 | tf_op jit(solution)/shard_map/ppermute | solution.py:29
  106.4 2.2 %collective-permute-done.25.t3 = bf16[2,4,16,448]{3,2,1,0:T(8,128)(2,1)S(1)} collective-permute-done((bf16[2,4,16,448]{3,2,1,0:T(8,128)(2,1)S(1)}, bf16[2,4,16,448]{3,2,1,0:T(8,128)(2,1)S(1)}, u32[]{:S(2)}, u32[]{:S(2)}) %collective-permute-start.25) | collective-permute-done | bytes 114720 | tf_op jit(solution)/shard_map/ppermute | solution.py:29
  108.7 0.6 join.1.half_ref
  109.4 1.3 collective-permute-done.26.other_ref
  110.7 2.0 %ffn.1 = (bf16[16,16,448]{2,1,0:T(8,128)(2,1)S(1)}, bf16[4,16,4736]{2,1,0:T(8,128)(2,1)S(1)}, bf16[4,16,4736]{2,1,0:T(8,128)(2,1)S(1)}, bf16[4,16,4736]{2,1,0:T(8,128)(2,1)S(1)}, bf16[4,16,4736]{2,1,0:T(8,128)(2,1)S(1)}) custom-call(s32[4]{0:T(128)S(1)} %pad_add_fusion.where, bf16[2,4,16,448]{3,2,1,0:T(8,128)(2,1)S(1)} %join.1.half_ref, ...), custom_call_target="tpu_custom_call" | custom-call | tf_op jit(solution)/shard_map/ffn/pallas_call | solution.py:58
  112.7 1.7 %collective-permute-start.27 = (bf16[4,16,4736]{2,1,0:T(8,128)(2,1)S(1)}, bf16[4,16,4736]{2,1,0:T(8,128)(2,1)S(1)}, u32[]{:S(2)}, u32[]{:S(2)}) collective-permute-start(bf16[4,16,4736]{2,1,0:T(8,128)(2,1)S(1)} %get-tuple-element.53), channel_id=1, source_target_pairs={{0,64},{1,17},{2,66},{3,19},{4,68},{5,21},{6,70},{7,23},{8,72},{9,... | collective-permute-start | bytes 1818632 | tf_op jit(solution)/shard_map/ppermute | solution.py:49
  114.4 1.9 %collective-permute-start.28 = (bf16[4,16,4736]{2,1,0:T(8,128)(2,1)S(1)}, bf16[4,16,4736]{2,1,0:T(8,128)(2,1)S(1)}, u32[]{:S(2)}, u32[]{:S(2)}) collective-permute-start(bf16[4,16,4736]{2,1,0:T(8,128)(2,1)S(1)} %get-tuple-element.54), channel_id=1, source_target_pairs={{0,32},{1,9},{2,34},{3,11},{4,36},{5,13},{6,38},{7,15},{8,40},{9,1... | collective-permute-start | bytes 1818632 | tf_op jit(solution)/shard_map/ppermute | solution.py:49
  116.3 1.3 collective-permute-start.29
  117.6 6.8 %collective-permute-done.27.refs_1_ = bf16[4,16,4736]{2,1,0:T(8,128)(2,1)S(1)} collective-permute-done((bf16[4,16,4736]{2,1,0:T(8,128)(2,1)S(1)}, bf16[4,16,4736]{2,1,0:T(8,128)(2,1)S(1)}, u32[]{:S(2)}, u32[]{:S(2)}) %collective-permute-start.27) | collective-permute-done | bytes 606240 | tf_op jit(solution)/shard_map/ppermute | solution.py:49
  124.4 6.4 %collective-permute-done.28.refs_2_ = bf16[4,16,4736]{2,1,0:T(8,128)(2,1)S(1)} collective-permute-done((bf16[4,16,4736]{2,1,0:T(8,128)(2,1)S(1)}, bf16[4,16,4736]{2,1,0:T(8,128)(2,1)S(1)}, u32[]{:S(2)}, u32[]{:S(2)}) %collective-permute-start.28) | collective-permute-done | bytes 606240 | tf_op jit(solution)/shard_map/ppermute | solution.py:49
  131.4 1.5 %collective-permute-start.30 = (bf16[16,4736]{1,0:T(8,128)(2,1)S(1)}, bf16[16,4736]{1,0:T(8,128)(2,1)S(1)}, u32[]{:S(2)}, u32[]{:S(2)}) collective-permute-start(bf16[16,4736]{1,0:T(8,128)(2,1)S(1)} %get-tuple-element.57), channel_id=1, source_target_pairs={{0,16},{1,65},{2,18},{3,67},{4,20},{5,69},{6,22},{7,71},{8,24},{9,... | collective-permute-start | bytes 454664 | tf_op jit(solution)/shard_map/ppermute | solution.py:49
  132.9 3.2 %collective-permute-start.32 = (bf16[16,4736]{1,0:T(8,128)(2,1)S(1)}, bf16[16,4736]{1,0:T(8,128)(2,1)S(1)}, u32[]{:S(2)}, u32[]{:S(2)}) collective-permute-start(bf16[16,4736]{1,0:T(8,128)(2,1)S(1)} %get-tuple-element.59), channel_id=1, source_target_pairs={{0,24},{1,97},{2,26},{3,99},{4,28},{5,101},{6,30},{7,103},{8,0},{9... | collective-permute-start | bytes 454664 | tf_op jit(solution)/shard_map/ppermute | solution.py:49
  136.1 0.8 turn.3
  136.9 1.3 collective-permute-done.30.r1
  138.2 1.6 %collective-permute-done.31.r2 = bf16[16,4736]{1,0:T(8,128)(2,1)S(1)} collective-permute-done((bf16[16,4736]{1,0:T(8,128)(2,1)S(1)}, bf16[16,4736]{1,0:T(8,128)(2,1)S(1)}, u32[]{:S(2)}, u32[]{:S(2)}) %collective-permute-start.31) | collective-permute-done | bytes 151584 | tf_op jit(solution)/shard_map/ppermute | solution.py:49
  139.8 0.8 finish.1
  (49 shorter events, 2.8 us)
Async XLA Ops:
  0.6 2.9 %copy-start.7 = (s32[2048]{0:T(1024)S(1)}, s32[2048]{0:T(1024)}, u32[]{:S(2)}) copy-start(s32[2048]{0:T(1024)} %param.15) | copy-start | bytes 24580
  0.6 2.9 %copy-start.6 = (s32[256,32]{0,1:T(8,128)S(1)}, s32[256,32]{0,1:T(8,128)}, u32[]{:S(2)}) copy-start(s32[256,32]{0,1:T(8,128)} %param.17) | copy-start | bytes 98308
  0.7 2.9 %copy-start.9 = (s32[256]{0:T(256)S(1)}, s32[256]{0:T(256)}, u32[]{:S(2)}) copy-start(s32[256]{0:T(256)} %prompts.1) | copy-start | bytes 3076
  0.7 5.0 %copy-start.4 = (bf16[16,9216]{1,0:T(8,128)(2,1)S(1)}, bf16[16,9216]{1,0:T(8,128)(2,1)}, u32[]{:S(2)}) copy-start(bf16[16,9216]{1,0:T(8,128)(2,1)} %queries.1) | copy-start | bytes 884740
  0.7 5.0 %copy-start.8 = (bf16[16,576]{1,0:T(8,128)(2,1)S(1)}, bf16[16,576]{1,0:T(8,128)(2,1)}, u32[]{:S(2)}) copy-start(bf16[16,576]{1,0:T(8,128)(2,1)} %own.1) | copy-start | bytes 55300
  5.8 11.2 %collective-permute-start = (bf16[256,640]{1,0:T(8,128)(2,1)S(1)}, bf16[256,640]{1,0:T(8,128)(2,1)S(1)}, u32[]{:S(2)}, u32[]{:S(2)}) collective-permute-start(bf16[256,640]{1,0:T(8,128)(2,1)S(1)} %get-tuple-element.32.refs_1_.q_ref), channel_id=1, source_target_pairs={{0,4},{1,5},{2,6},{3,7},{4,0},{5,1},{6,2},{7,3},{8,12},{9,13},{10,... | collective-permute-start | bytes 983048 | tf_op jit(solution)/shard_map/ppermute | solution.py:29
  9.2 17.6 %collective-permute-start.3 = (bf16[8,288,128]{2,1,0:T(8,128)(2,1)S(1)}, bf16[8,288,128]{2,1,0:T(8,128)(2,1)S(1)}, u32[]{:S(2)}, u32[]{:S(2)}) collective-permute-start(bf16[8,288,128]{2,1,0:T(8,128)(2,1)S(1)} %get-tuple-element.33), channel_id=1, source_target_pairs={{0,32},{1,9},{2,34},{3,11},{4,36},{5,13},{6,38},{7,15},{8,40},{9,1... | collective-permute-start | bytes 1769480 | tf_op jit(solution)/shard_map/ppermute | solution.py:49
  10.7 16.9 %collective-permute-start.4 = (bf16[8,288,128]{2,1,0:T(8,128)(2,1)S(1)}, bf16[8,288,128]{2,1,0:T(8,128)(2,1)S(1)}, u32[]{:S(2)}, u32[]{:S(2)}) collective-permute-start(bf16[8,288,128]{2,1,0:T(8,128)(2,1)S(1)} %get-tuple-element.34), channel_id=1, source_target_pairs={{0,64},{1,17},{2,66},{3,19},{4,68},{5,21},{6,70},{7,23},{8,72},{9,... | collective-permute-start | bytes 1769480 | tf_op jit(solution)/shard_map/ppermute | solution.py:49
  13.4 14.2 %collective-permute-start.5 = (bf16[8,288,128]{2,1,0:T(8,128)(2,1)S(1)}, bf16[8,288,128]{2,1,0:T(8,128)(2,1)S(1)}, u32[]{:S(2)}, u32[]{:S(2)}) collective-permute-start(bf16[8,288,128]{2,1,0:T(8,128)(2,1)S(1)} %get-tuple-element.35), channel_id=1, source_target_pairs={{0,96},{1,25},{2,98},{3,27},{4,100},{5,29},{6,102},{7,31},{8,104},... | collective-permute-start | bytes 1769480 | tf_op jit(solution)/shard_map/ppermute | solution.py:49
  14.9 9.5 %collective-permute-start.1 = (bf16[256,640]{1,0:T(8,128)(2,1)S(1)}, bf16[256,640]{1,0:T(8,128)(2,1)S(1)}, u32[]{:S(2)}, u32[]{:S(2)}) collective-permute-start(bf16[256,640]{1,0:T(8,128)(2,1)S(1)} %get-tuple-element.32.refs_1_.q_ref), channel_id=1, source_target_pairs={{0,2},{1,3},{2,0},{3,1},{4,6},{5,7},{6,4},{7,5},{8,10},{9,11},{10,... | collective-permute-start | bytes 983048 | tf_op jit(solution)/shard_map/ppermute | solution.py:29
  17.1 9.8 %collective-permute-start.2 = (bf16[256,640]{1,0:T(8,128)(2,1)S(1)}, bf16[256,640]{1,0:T(8,128)(2,1)S(1)}, u32[]{:S(2)}, u32[]{:S(2)}) collective-permute-start(bf16[256,640]{1,0:T(8,128)(2,1)S(1)} %get-tuple-element.32.refs_1_.q_ref), channel_id=1, source_target_pairs={{0,6},{1,7},{2,4},{3,5},{4,2},{5,3},{6,0},{7,1},{8,14},{9,15},{10,... | collective-permute-start | bytes 983048 | tf_op jit(solution)/shard_map/ppermute | solution.py:29
  27.8 6.7 %collective-permute-start.6 = (bf16[8,288,128]{2,1,0:T(8,128)(2,1)S(1)}, bf16[8,288,128]{2,1,0:T(8,128)(2,1)S(1)}, u32[]{:S(2)}, u32[]{:S(2)}) collective-permute-start(bf16[8,288,128]{2,1,0:T(8,128)(2,1)S(1)} %get-tuple-element.36.refs_5_), channel_id=1, source_target_pairs={{0,1},{1,0},{2,3},{3,2},{4,5},{5,4},{6,7},{7,6},{8,9},{9,8},{10,11... | collective-permute-start | bytes 1769480 | tf_op jit(solution)/shard_map/ppermute | solution.py:29
  27.9 12.0 %collective-permute-start.7 = (bf16[8,288,128]{2,1,0:T(8,128)(2,1)S(1)}, bf16[8,288,128]{2,1,0:T(8,128)(2,1)S(1)}, u32[]{:S(2)}, u32[]{:S(2)}) collective-permute-start(bf16[8,288,128]{2,1,0:T(8,128)(2,1)S(1)} %get-tuple-element.38), channel_id=1, source_target_pairs={{0,8},{1,33},{2,10},{3,35},{4,12},{5,37},{6,14},{7,39},{8,16},{9,4... | collective-permute-start | bytes 1769480 | tf_op jit(solution)/shard_map/ppermute | solution.py:49
  29.8 17.8 %collective-permute-start.8 = (bf16[8,288,128]{2,1,0:T(8,128)(2,1)S(1)}, bf16[8,288,128]{2,1,0:T(8,128)(2,1)S(1)}, u32[]{:S(2)}, u32[]{:S(2)}) collective-permute-start(bf16[8,288,128]{2,1,0:T(8,128)(2,1)S(1)} %get-tuple-element.39), channel_id=1, source_target_pairs={{0,16},{1,65},{2,18},{3,67},{4,20},{5,69},{6,22},{7,71},{8,24},{9,... | collective-permute-start | bytes 1769480 | tf_op jit(solution)/shard_map/ppermute | solution.py:49
  33.4 14.2 %collective-permute-start.9 = (bf16[8,288,128]{2,1,0:T(8,128)(2,1)S(1)}, bf16[8,288,128]{2,1,0:T(8,128)(2,1)S(1)}, u32[]{:S(2)}, u32[]{:S(2)}) collective-permute-start(bf16[8,288,128]{2,1,0:T(8,128)(2,1)S(1)} %get-tuple-element.40), channel_id=1, source_target_pairs={{0,24},{1,97},{2,26},{3,99},{4,28},{5,101},{6,30},{7,103},{8,0},{9... | collective-permute-start | bytes 1769480 | tf_op jit(solution)/shard_map/ppermute | solution.py:49
  47.7 5.3 %collective-permute-start.10 = (bf16[8,288,128]{2,1,0:T(8,128)(2,1)S(1)}, bf16[8,288,128]{2,1,0:T(8,128)(2,1)S(1)}, u32[]{:S(2)}, u32[]{:S(2)}) collective-permute-start(bf16[8,288,128]{2,1,0:T(8,128)(2,1)S(1)} %get-tuple-element.41.refs_4_.refs_2_), channel_id=1, source_target_pairs={{0,1},{1,0},{2,3},{3,2},{4,5},{5,4},{6,7},{7,6},{8,9},{9,8},{10,11... | collective-permute-start | bytes 1769480 | tf_op jit(solution)/shard_map/ppermute | solution.py:29
  47.8 5.2 %collective-permute-start.11 = (bf16[8,288,128]{2,1,0:T(8,128)(2,1)S(1)}, bf16[8,288,128]{2,1,0:T(8,128)(2,1)S(1)}, u32[]{:S(2)}, u32[]{:S(2)}) collective-permute-start(bf16[8,288,128]{2,1,0:T(8,128)(2,1)S(1)} %get-tuple-element.42.refs_5_.refs_3_), channel_id=1, source_target_pairs={{0,1},{1,0},{2,3},{3,2},{4,5},{5,4},{6,7},{7,6},{8,9},{9,8},{10,11... | collective-permute-start | bytes 1769480 | tf_op jit(solution)/shard_map/ppermute | solution.py:29
  48.3 4.7 %collective-permute-start.12 = (bf16[8,288,128]{2,1,0:T(8,128)(2,1)S(1)}, bf16[8,288,128]{2,1,0:T(8,128)(2,1)S(1)}, u32[]{:S(2)}, u32[]{:S(2)}) collective-permute-start(bf16[8,288,128]{2,1,0:T(8,128)(2,1)S(1)} %get-tuple-element.43.refs_6_.refs_4_), channel_id=1, source_target_pairs={{0,1},{1,0},{2,3},{3,2},{4,5},{5,4},{6,7},{7,6},{8,9},{9,8},{10,11... | collective-permute-start | bytes 1769480 | tf_op jit(solution)/shard_map/ppermute | solution.py:29
  54.6 11.0 %collective-permute-start.13 = (bf16[272,512]{1,0:T(8,128)(2,1)S(1)}, bf16[272,512]{1,0:T(8,128)(2,1)S(1)}, u32[]{:S(2)}, u32[]{:S(2)}) collective-permute-start(bf16[272,512]{1,0:T(8,128)(2,1)S(1)} %attend.8), channel_id=1, source_target_pairs={{0,4},{1,5},{2,6},{3,7},{4,0},{5,1},{6,2},{7,3},{8,12},{9,13},{10,... | collective-permute-start | bytes 835592 | tf_op jit(solution)/shard_map/ppermute | solution.py:29
  57.4 13.2 %collective-permute-start.14 = (bf16[272,512]{1,0:T(8,128)(2,1)S(1)}, bf16[272,512]{1,0:T(8,128)(2,1)S(1)}, u32[]{:S(2)}, u32[]{:S(2)}) collective-permute-start(bf16[272,512]{1,0:T(8,128)(2,1)S(1)} %attend.9), channel_id=1, source_target_pairs={{0,2},{1,3},{2,0},{3,1},{4,6},{5,7},{6,4},{7,5},{8,10},{9,11},{10,... | collective-permute-start | bytes 835592 | tf_op jit(solution)/shard_map/ppermute | solution.py:29
  61.0 10.2 %copy-start = (bf16[16,512,128]{2,1,0:T(8,128)(2,1)S(1)}, bf16[16,512,128]{2,1,0:T(8,128)(2,1)}, u32[]{:S(2)}) copy-start(bf16[16,512,128]{2,1,0:T(8,128)(2,1)} %up_ref.1) | copy-start | bytes 6291460
  61.0 10.2 %collective-permute-start.15 = (bf16[272,512]{1,0:T(8,128)(2,1)S(1)}, bf16[272,512]{1,0:T(8,128)(2,1)S(1)}, u32[]{:S(2)}, u32[]{:S(2)}) collective-permute-start(bf16[272,512]{1,0:T(8,128)(2,1)S(1)} %attend.10), channel_id=1, source_target_pairs={{0,6},{1,7},{2,4},{3,5},{4,2},{5,3},{6,0},{7,1},{8,14},{9,15},{10,... | collective-permute-start | bytes 835592 | tf_op jit(solution)/shard_map/ppermute | solution.py:29
  71.2 22.2 %copy-start.3 = (bf16[2048,448]{0,1:T(8,128)(2,1)S(1)}, bf16[2048,448]{0,1:T(8,128)(2,1)}, u32[]{:S(2)}) copy-start(bf16[2048,448]{0,1:T(8,128)(2,1)} %param.19) | copy-start | bytes 5505028
  72.0 28.9 %copy-start.5 = (bf16[256,448]{0,1:T(8,128)(2,1)S(1)}, bf16[256,448]{0,1:T(8,128)(2,1)}, u32[]{:S(2)}) copy-start(bf16[256,448]{0,1:T(8,128)(2,1)} %param.20) | copy-start | bytes 688132
  72.0 5.7 %collective-permute-start.18 = (bf16[16,2048]{1,0:T(8,128)(2,1)S(1)}, bf16[16,2048]{1,0:T(8,128)(2,1)S(1)}, u32[]{:S(2)}, u32[]{:S(2)}) collective-permute-start(bf16[16,2048]{1,0:T(8,128)(2,1)S(1)} %merge.1), channel_id=1, source_target_pairs={{0,32},{1,9},{2,34},{3,11},{4,36},{5,13},{6,38},{7,15},{8,40},{9,1... | collective-permute-start | bytes 196616 | tf_op jit(solution)/shard_map/ppermute | solution.py:49
  74.0 5.8 %collective-permute-start.17 = (bf16[16,2048]{1,0:T(8,128)(2,1)S(1)}, bf16[16,2048]{1,0:T(8,128)(2,1)S(1)}, u32[]{:S(2)}, u32[]{:S(2)}) collective-permute-start(bf16[16,2048]{1,0:T(8,128)(2,1)S(1)} %merge.1), channel_id=1, source_target_pairs={{0,64},{1,17},{2,66},{3,19},{4,68},{5,21},{6,70},{7,23},{8,72},{9,... | collective-permute-start | bytes 196616 | tf_op jit(solution)/shard_map/ppermute | solution.py:49
  76.2 4.3 %collective-permute-start.16 = (bf16[16,2048]{1,0:T(8,128)(2,1)S(1)}, bf16[16,2048]{1,0:T(8,128)(2,1)S(1)}, u32[]{:S(2)}, u32[]{:S(2)}) collective-permute-start(bf16[16,2048]{1,0:T(8,128)(2,1)S(1)} %merge.1), channel_id=1, source_target_pairs={{0,96},{1,25},{2,98},{3,27},{4,100},{5,29},{6,102},{7,31},{8,104},... | collective-permute-start | bytes 196616 | tf_op jit(solution)/shard_map/ppermute | solution.py:49
  80.5 9.0 %collective-permute-start.19 = (bf16[64,2048]{1,0:T(8,128)(2,1)S(1)}, bf16[64,2048]{1,0:T(8,128)(2,1)S(1)}, u32[]{:S(2)}, u32[]{:S(2)}) collective-permute-start(bf16[64,2048]{1,0:T(8,128)(2,1)S(1)} %pad_maximum_fusion.p0), channel_id=1, source_target_pairs={{0,24},{1,97},{2,26},{3,99},{4,28},{5,101},{6,30},{7,103},{8,0},{9... | collective-permute-start | bytes 786440 | tf_op jit(solution)/shard_map/ppermute | solution.py:49
  82.7 8.0 %collective-permute-start.20 = (bf16[64,2048]{1,0:T(8,128)(2,1)S(1)}, bf16[64,2048]{1,0:T(8,128)(2,1)S(1)}, u32[]{:S(2)}, u32[]{:S(2)}) collective-permute-start(bf16[64,2048]{1,0:T(8,128)(2,1)S(1)} %pad_maximum_fusion.p0), channel_id=1, source_target_pairs={{0,16},{1,65},{2,18},{3,67},{4,20},{5,69},{6,22},{7,71},{8,24},{9,... | collective-permute-start | bytes 786440 | tf_op jit(solution)/shard_map/ppermute | solution.py:49
  84.1 9.3 %collective-permute-start.21 = (bf16[64,2048]{1,0:T(8,128)(2,1)S(1)}, bf16[64,2048]{1,0:T(8,128)(2,1)S(1)}, u32[]{:S(2)}, u32[]{:S(2)}) collective-permute-start(bf16[64,2048]{1,0:T(8,128)(2,1)S(1)} %pad_maximum_fusion.p0), channel_id=1, source_target_pairs={{0,8},{1,33},{2,10},{3,35},{4,12},{5,37},{6,14},{7,39},{8,16},{9,4... | collective-permute-start | bytes 786440 | tf_op jit(solution)/shard_map/ppermute | solution.py:49
  93.4 16.0 %copy-start.10 = (bf16[448]{0:T(512)(128)(2,1)S(1)}, bf16[448]{0:T(512)(128)(2,1)}, u32[]{:S(2)}) copy-start(bf16[448]{0:T(512)(128)(2,1)} %param.21) | copy-start | bytes 2692
  93.4 17.3 %copy-start.1 = (bf16[448,2304]{1,0:T(8,128)(2,1)S(1)}, bf16[448,2304]{1,0:T(8,128)(2,1)}, u32[]{:S(2)}) copy-start(bf16[448,2304]{1,0:T(8,128)(2,1)} %wg_ref.1) | copy-start | bytes 6193156
  93.4 17.3 %copy-start.2 = (bf16[448,2304]{1,0:T(8,128)(2,1)S(1)}, bf16[448,2304]{1,0:T(8,128)(2,1)}, u32[]{:S(2)}) copy-start(bf16[448,2304]{1,0:T(8,128)(2,1)} %wu_ref.1) | copy-start | bytes 6193156
  94.7 1.4 %collective-permute-start.22 = (bf16[2,4,16,448]{3,2,1,0:T(8,128)(2,1)S(1)}, bf16[2,4,16,448]{3,2,1,0:T(8,128)(2,1)S(1)}, u32[]{:S(2)}, u32[]{:S(2)}) collective-permute-start(bf16[2,4,16,448]{3,2,1,0:T(8,128)(2,1)S(1)} %get-tuple-element.50), channel_id=1, source_target_pairs={{0,1},{1,0},{2,3},{3,2},{4,5},{5,4},{6,7},{7,6},{8,9},{9,8},{10,11... | collective-permute-start | bytes 344072 | tf_op jit(solution)/shard_map/ppermute | solution.py:29
  96.2 6.4 %collective-permute-start.23 = (bf16[2,4,16,448]{3,2,1,0:T(8,128)(2,1)S(1)}, bf16[2,4,16,448]{3,2,1,0:T(8,128)(2,1)S(1)}, u32[]{:S(2)}, u32[]{:S(2)}) collective-permute-start(bf16[2,4,16,448]{3,2,1,0:T(8,128)(2,1)S(1)} %add_convert_fusion.pair), channel_id=1, source_target_pairs={{0,2},{1,3},{2,0},{3,1},{4,6},{5,7},{6,4},{7,5},{8,10},{9,11},{10,... | collective-permute-start | bytes 344072 | tf_op jit(solution)/shard_map/ppermute | solution.py:29
  96.8 9.6 %collective-permute-start.24 = (bf16[2,4,16,448]{3,2,1,0:T(8,128)(2,1)S(1)}, bf16[2,4,16,448]{3,2,1,0:T(8,128)(2,1)S(1)}, u32[]{:S(2)}, u32[]{:S(2)}) collective-permute-start(bf16[2,4,16,448]{3,2,1,0:T(8,128)(2,1)S(1)} %add_convert_fusion.pair), channel_id=1, source_target_pairs={{0,4},{1,5},{2,6},{3,7},{4,0},{5,1},{6,2},{7,3},{8,12},{9,13},{10,... | collective-permute-start | bytes 344072 | tf_op jit(solution)/shard_map/ppermute | solution.py:29
  100.0 8.7 %collective-permute-start.25 = (bf16[2,4,16,448]{3,2,1,0:T(8,128)(2,1)S(1)}, bf16[2,4,16,448]{3,2,1,0:T(8,128)(2,1)S(1)}, u32[]{:S(2)}, u32[]{:S(2)}) collective-permute-start(bf16[2,4,16,448]{3,2,1,0:T(8,128)(2,1)S(1)} %add_convert_fusion.pair), channel_id=1, source_target_pairs={{0,6},{1,7},{2,4},{3,5},{4,2},{5,3},{6,0},{7,1},{8,14},{9,15},{10,... | collective-permute-start | bytes 344072 | tf_op jit(solution)/shard_map/ppermute | solution.py:29
  109.3 1.4 %collective-permute-start.26 = (bf16[2,4,16,448]{3,2,1,0:T(8,128)(2,1)S(1)}, bf16[2,4,16,448]{3,2,1,0:T(8,128)(2,1)S(1)}, u32[]{:S(2)}, u32[]{:S(2)}) collective-permute-start(bf16[2,4,16,448]{3,2,1,0:T(8,128)(2,1)S(1)} %join.1.half_ref), channel_id=1, source_target_pairs={{0,1},{1,0},{2,3},{3,2},{4,5},{5,4},{6,7},{7,6},{8,9},{9,8},{10,11... | collective-permute-start | bytes 344072 | tf_op jit(solution)/shard_map/ppermute | solution.py:29
  112.7 11.7 %collective-permute-start.27 = (bf16[4,16,4736]{2,1,0:T(8,128)(2,1)S(1)}, bf16[4,16,4736]{2,1,0:T(8,128)(2,1)S(1)}, u32[]{:S(2)}, u32[]{:S(2)}) collective-permute-start(bf16[4,16,4736]{2,1,0:T(8,128)(2,1)S(1)} %get-tuple-element.53), channel_id=1, source_target_pairs={{0,64},{1,17},{2,66},{3,19},{4,68},{5,21},{6,70},{7,23},{8,72},{9,... | collective-permute-start | bytes 1818632 | tf_op jit(solution)/shard_map/ppermute | solution.py:49
  114.4 16.5 %collective-permute-start.28 = (bf16[4,16,4736]{2,1,0:T(8,128)(2,1)S(1)}, bf16[4,16,4736]{2,1,0:T(8,128)(2,1)S(1)}, u32[]{:S(2)}, u32[]{:S(2)}) collective-permute-start(bf16[4,16,4736]{2,1,0:T(8,128)(2,1)S(1)} %get-tuple-element.54), channel_id=1, source_target_pairs={{0,32},{1,9},{2,34},{3,11},{4,36},{5,13},{6,38},{7,15},{8,40},{9,1... | collective-permute-start | bytes 1818632 | tf_op jit(solution)/shard_map/ppermute | solution.py:49
  116.3 14.6 %collective-permute-start.29 = (bf16[4,16,4736]{2,1,0:T(8,128)(2,1)S(1)}, bf16[4,16,4736]{2,1,0:T(8,128)(2,1)S(1)}, u32[]{:S(2)}, u32[]{:S(2)}) collective-permute-start(bf16[4,16,4736]{2,1,0:T(8,128)(2,1)S(1)} %get-tuple-element.55), channel_id=1, source_target_pairs={{0,96},{1,25},{2,98},{3,27},{4,100},{5,29},{6,102},{7,31},{8,104},... | collective-permute-start | bytes 1818632 | tf_op jit(solution)/shard_map/ppermute | solution.py:49
  131.4 6.8 %collective-permute-start.30 = (bf16[16,4736]{1,0:T(8,128)(2,1)S(1)}, bf16[16,4736]{1,0:T(8,128)(2,1)S(1)}, u32[]{:S(2)}, u32[]{:S(2)}) collective-permute-start(bf16[16,4736]{1,0:T(8,128)(2,1)S(1)} %get-tuple-element.57), channel_id=1, source_target_pairs={{0,16},{1,65},{2,18},{3,67},{4,20},{5,69},{6,22},{7,71},{8,24},{9,... | collective-permute-start | bytes 454664 | tf_op jit(solution)/shard_map/ppermute | solution.py:49
  132.9 6.9 %collective-permute-start.31 = (bf16[16,4736]{1,0:T(8,128)(2,1)S(1)}, bf16[16,4736]{1,0:T(8,128)(2,1)S(1)}, u32[]{:S(2)}, u32[]{:S(2)}) collective-permute-start(bf16[16,4736]{1,0:T(8,128)(2,1)S(1)} %get-tuple-element.58), channel_id=1, source_target_pairs={{0,8},{1,33},{2,10},{3,35},{4,12},{5,37},{6,14},{7,39},{8,16},{9,4... | collective-permute-start | bytes 454664 | tf_op jit(solution)/shard_map/ppermute | solution.py:49
  132.9 6.9 %collective-permute-start.32 = (bf16[16,4736]{1,0:T(8,128)(2,1)S(1)}, bf16[16,4736]{1,0:T(8,128)(2,1)S(1)}, u32[]{:S(2)}, u32[]{:S(2)}) collective-permute-start(bf16[16,4736]{1,0:T(8,128)(2,1)S(1)} %get-tuple-element.59), channel_id=1, source_target_pairs={{0,24},{1,97},{2,26},{3,99},{4,28},{5,101},{6,30},{7,103},{8,0},{9... | collective-permute-start | bytes 454664 | tf_op jit(solution)/shard_map/ppermute | solution.py:49

commit v7 on v6

--- a/solution.py
+++ b/solution.py
@@ -166,7 +166,7 @@
 
 
 def regroup_kernel(*refs):
-    refs = refs[:4] + refs[8:]
+    refs = refs[:4] + refs[6:]
     for ka in range(4):
         for kb in range(4):
             refs[4 + kb][ka * CAP : (ka + 1) * CAP] = refs[ka][kb * CAP : (kb + 1) * CAP]
@@ -479,7 +479,7 @@
     )
     qs = {0: q, **{k: send_y(q, k) for k in (1, 2, 3)}}
 
-    groups = call(regroup_kernel, "regroup", [shape(8, 288, 128)] * 4, [*got, use, *list(qs.values())[1:]], anys=4)
+    groups = call(regroup_kernel, "regroup", [shape(8, 288, 128)] * 4, [*got, use, qs[2]], anys=2)
     arrived = {0: groups[0]}
     for k in (1, 3, 2):
         arrived[k] = send_dp(groups[k], 1, k)

time: 141 us -> 138 us (0.979)
  waiting for transfers between devices: 61.3 us -> 58.6 us
    ppermute x18, waiting for transfers between devices: 38.2 us -> 28.3 us  [send_dp(): return lax.ppermute(x, ('dp', 'tp'), pairs)]
    ppermute x15, waiting for transfers between devices: 23.1 us -> 30.2 us  [send(): return lax.ppermute(x, axis, [(i, to(i)) for i in range(n)])]
  transfers between devices with their start and end apart: 33 -> 33, of which waited for: 23 -> 22; matrix products, arithmetic and copies ran while one was open for 0% -> 0% of each run, Pallas kernels for 12% -> 12%
where the time goes in v7:
time: 138 us
  waiting for transfers between devices  58.6 us (42%)
  starting transfers between devices  49 us (36%)
  Pallas kernels  26.6 us (19%)
  local copies, waits for them, and re-layouts  2.75 us (2%)
    ppermute x18, starting transfers between devices, send_dp(): return lax.ppermute(x, ('dp', 'tp'), pairs)  31.8 us
    ppermute x15, waiting for transfers between devices, send(): return lax.ppermute(x, axis, [(i, to(i)) for i in range(n)])  30.2 us
    ppermute x18, waiting for transfers between devices, send_dp(): return lax.ppermute(x, ('dp', 'tp'), pairs)  28.3 us
    pallas_call x19, Pallas kernels, call(): pl.pallas_call(kernel, out_shape=outs, in_specs=[SMEM] * scalars + [VMEM]...  25.7 us
    ppermute x15, starting transfers between devices, send(): return lax.ppermute(x, axis, [(i, to(i)) for i in range(n)])  17.2 us
  transfers between devices with their start and end apart: 33, of which 22 were waited for; matrix products, arithmetic and copies ran while one was open for 0% of the time, Pallas kernels for 12%

profile of v7, /device:TPU:0, one launch (start us, length us, event | category | flops | bytes accessed | tf_op | source)
XLA Modules:
  0.0 138.0 jit_solution(1390420617111924204)
XLA Ops:
  0.7 2.7 %reshape.24.tokens = bf16[16,64,576]{2,1,0:T(8,128)(2,1)S(1)} reshape(bf16[16,36864]{1,0:T(8,128)(2,1)} %param.14) | data formatting | bytes 2359296 | tf_op jit(solution)/shard_map/reshape | solution.py:459
  3.5 1.0 plan.1.picks
  4.5 1.2 fetch.1
  5.7 1.6 %collective-permute-start.3 = (bf16[8,288,128]{2,1,0:T(8,128)(2,1)S(1)}, bf16[8,288,128]{2,1,0:T(8,128)(2,1)S(1)}, u32[]{:S(2)}, u32[]{:S(2)}) collective-permute-start(bf16[8,288,128]{2,1,0:T(8,128)(2,1)S(1)} %get-tuple-element.33), channel_id=1, source_target_pairs={{0,32},{1,9},{2,34},{3,11},{4,36},{5,13},{6,38},{7,15},{8,40},{9,1... | collective-permute-start | bytes 1769480 | tf_op jit(solution)/shard_map/ppermute | solution.py:49
  7.3 2.7 %collective-permute-start.4 = (bf16[8,288,128]{2,1,0:T(8,128)(2,1)S(1)}, bf16[8,288,128]{2,1,0:T(8,128)(2,1)S(1)}, u32[]{:S(2)}, u32[]{:S(2)}) collective-permute-start(bf16[8,288,128]{2,1,0:T(8,128)(2,1)S(1)} %get-tuple-element.34), channel_id=1, source_target_pairs={{0,64},{1,17},{2,66},{3,19},{4,68},{5,21},{6,70},{7,23},{8,72},{9,... | collective-permute-start | bytes 1769480 | tf_op jit(solution)/shard_map/ppermute | solution.py:49
  10.0 1.4 %collective-permute-start.5 = (bf16[8,288,128]{2,1,0:T(8,128)(2,1)S(1)}, bf16[8,288,128]{2,1,0:T(8,128)(2,1)S(1)}, u32[]{:S(2)}, u32[]{:S(2)}) collective-permute-start(bf16[8,288,128]{2,1,0:T(8,128)(2,1)S(1)} %get-tuple-element.35), channel_id=1, source_target_pairs={{0,96},{1,25},{2,98},{3,27},{4,100},{5,29},{6,102},{7,31},{8,104},... | collective-permute-start | bytes 1769480 | tf_op jit(solution)/shard_map/ppermute | solution.py:49
  11.6 3.3 %collective-permute-start = (bf16[256,640]{1,0:T(8,128)(2,1)S(1)}, bf16[256,640]{1,0:T(8,128)(2,1)S(1)}, u32[]{:S(2)}, u32[]{:S(2)}) collective-permute-start(bf16[256,640]{1,0:T(8,128)(2,1)S(1)} %get-tuple-element.32.refs_1_.q_ref), channel_id=1, source_target_pairs={{0,4},{1,5},{2,6},{3,7},{4,0},{5,1},{6,2},{7,3},{8,12},{9,13},{10,... | collective-permute-start | bytes 983048 | tf_op jit(solution)/shard_map/ppermute | solution.py:29
  14.9 0.7 collective-permute-start.1
  15.6 1.6 %use.1.refs_4_.refs_0_ = bf16[16,64]{1,0:T(8,128)(2,1)S(1)} custom-call(s32[4]{0:T(128)S(1)} %pad_add_fusion.where, s32[256]{0:T(256)S(1)} %copy-done.9, s32[4,4,128]{2,1,0:T(4,128)S(1)} %bitcast.19, s32[32,256]{1,0:T(8,128)S(1)} %bitcast.17, bf16[8,288,128]{2,1,0:T(8,128)(2,1)S(1)} %get-tuple-element.31._.refs_0_), custom_call_target="tpu_custom_call" | custom-call | tf_op jit(solution)/shard_map/use/pallas_call | solution.py:58
  17.2 6.6 %collective-permute-done.refs_5_.refs_3_.refs_1_ = bf16[256,640]{1,0:T(8,128)(2,1)S(1)} collective-permute-done((bf16[256,640]{1,0:T(8,128)(2,1)S(1)}, bf16[256,640]{1,0:T(8,128)(2,1)S(1)}, u32[]{:S(2)}, u32[]{:S(2)}) %collective-permute-start) | collective-permute-done | bytes 327712 | tf_op jit(solution)/shard_map/ppermute | solution.py:29
  23.8 0.4 collective-permute-done.4.refs_2_
  24.6 1.9 %collective-permute-start.7 = (bf16[8,288,128]{2,1,0:T(8,128)(2,1)S(1)}, bf16[8,288,128]{2,1,0:T(8,128)(2,1)S(1)}, u32[]{:S(2)}, u32[]{:S(2)}) collective-permute-start(bf16[8,288,128]{2,1,0:T(8,128)(2,1)S(1)} %get-tuple-element.38), channel_id=1, source_target_pairs={{0,8},{1,33},{2,10},{3,35},{4,12},{5,37},{6,14},{7,39},{8,16},{9,4... | collective-permute-start | bytes 1769480 | tf_op jit(solution)/shard_map/ppermute | solution.py:49
  26.5 3.6 %collective-permute-start.8 = (bf16[8,288,128]{2,1,0:T(8,128)(2,1)S(1)}, bf16[8,288,128]{2,1,0:T(8,128)(2,1)S(1)}, u32[]{:S(2)}, u32[]{:S(2)}) collective-permute-start(bf16[8,288,128]{2,1,0:T(8,128)(2,1)S(1)} %get-tuple-element.39), channel_id=1, source_target_pairs={{0,16},{1,65},{2,18},{3,67},{4,20},{5,69},{6,22},{7,71},{8,24},{9,... | collective-permute-start | bytes 1769480 | tf_op jit(solution)/shard_map/ppermute | solution.py:49
  30.0 1.0 collective-permute-start.9
  31.1 3.0 %collective-permute-start.2 = (bf16[256,640]{1,0:T(8,128)(2,1)S(1)}, bf16[256,640]{1,0:T(8,128)(2,1)S(1)}, u32[]{:S(2)}, u32[]{:S(2)}) collective-permute-start(bf16[256,640]{1,0:T(8,128)(2,1)S(1)} %get-tuple-element.32.refs_1_.q_ref), channel_id=1, source_target_pairs={{0,6},{1,7},{2,4},{3,5},{4,2},{5,3},{6,0},{7,1},{8,14},{9,15},{10,... | collective-permute-start | bytes 983048 | tf_op jit(solution)/shard_map/ppermute | solution.py:29
  34.1 6.5 %collective-permute-done.2.refs_4_.refs_3_.refs_1_ = bf16[256,640]{1,0:T(8,128)(2,1)S(1)} collective-permute-done((bf16[256,640]{1,0:T(8,128)(2,1)S(1)}, bf16[256,640]{1,0:T(8,128)(2,1)S(1)}, u32[]{:S(2)}, u32[]{:S(2)}) %collective-permute-start.2) | collective-permute-done | bytes 327712 | tf_op jit(solution)/shard_map/ppermute | solution.py:29
  40.6 3.2 %attend.6 = (f32[4,256,512]{2,1,0:T(8,128)S(1)}, f32[4,256,128]{2,1,0:T(8,128)S(1)}, f32[8,128]{1,0:T(8,128)S(1)}) custom-call(bf16[16,64]{1,0:T(8,128)(2,1)S(1)} %use.1.refs_4_.refs_0_, bf16[256,640]{1,0:T(8,128)(2,1)S(1)} %get-tuple-element.32.refs_1_.q_ref, bf16[256,640]{1,0:T(8,128)(2,1)S(1)} %collective-permute-done.1.refs_2_.refs_1_, ...), custom_call_target="tpu_custom_call" | custom-call | tf_op jit(solution)/shard_map/attend/pallas_call | solution.py:58
  43.8 0.4 collective-permute-done.8.refs_1_
  44.4 0.5 collective-permute-start.11
  45.0 4.6 %attend.7 = (f32[4,256,512]{2,1,0:T(8,128)S(1)}, f32[4,256,128]{2,1,0:T(8,128)S(1)}, f32[8,128]{1,0:T(8,128)}) custom-call(bf16[16,64]{1,0:T(8,128)(2,1)S(1)} %use.1.refs_4_.refs_0_, bf16[256,640]{1,0:T(8,128)(2,1)S(1)} %collective-permute-done.refs_5_.refs_3_.refs_1_, bf16[256,640]{1,0:T(8,128)(2,1)S(1)} %collective-permute-done.1.refs_2_.refs_1_, ...), custom_call_target="tpu_custom_call" | custom-call | tf_op jit(solution)/shard_map/attend/pallas_call | solution.py:58
  49.6 1.6 %attend.8 = bf16[272,512]{1,0:T(8,128)(2,1)S(1)} custom-call(bf16[16,64]{1,0:T(8,128)(2,1)S(1)} %use.1.refs_4_.refs_0_, bf16[256,640]{1,0:T(8,128)(2,1)S(1)} %collective-permute-done.refs_5_.refs_3_.refs_1_, bf16[8,288,128]{2,1,0:T(8,128)(2,1)S(1)} %collective-permute-done.10.refs_2_.refs_5_, ...), custom_call_target="tpu_custom_call" | custom-call | tf_op jit(solution)/shard_map/attend/pallas_call | solution.py:58
  51.2 3.2 %collective-permute-start.13 = (bf16[272,512]{1,0:T(8,128)(2,1)S(1)}, bf16[272,512]{1,0:T(8,128)(2,1)S(1)}, u32[]{:S(2)}, u32[]{:S(2)}) collective-permute-start(bf16[272,512]{1,0:T(8,128)(2,1)S(1)} %attend.8), channel_id=1, source_target_pairs={{0,4},{1,5},{2,6},{3,7},{4,0},{5,1},{6,2},{7,3},{8,12},{9,13},{10,... | collective-permute-start | bytes 835592 | tf_op jit(solution)/shard_map/ppermute | solution.py:29
  54.5 1.6 %attend.9 = bf16[272,512]{1,0:T(8,128)(2,1)S(1)} custom-call(bf16[16,64]{1,0:T(8,128)(2,1)S(1)} %use.1.refs_4_.refs_0_, bf16[256,640]{1,0:T(8,128)(2,1)S(1)} %collective-permute-done.1.refs_2_.refs_1_, bf16[8,288,128]{2,1,0:T(8,128)(2,1)S(1)} %collective-permute-done.10.refs_2_.refs_5_, bf16[8,288,128]{2,1,0:T(8,128)(2,1)S(1)} %collective-permute-done.11.refs_3_.refs_6_, ...), custom_call_target="tpu_custom_call" | custom-call | tf_op jit(solution)/shard_map/attend/pallas_call | solution.py:58
  56.1 0.7 collective-permute-start.14
  56.8 1.6 %attend.10 = bf16[272,512]{1,0:T(8,128)(2,1)S(1)} custom-call(bf16[16,64]{1,0:T(8,128)(2,1)S(1)} %use.1.refs_4_.refs_0_, bf16[256,640]{1,0:T(8,128)(2,1)S(1)} %collective-permute-done.2.refs_4_.refs_3_.refs_1_, bf16[8,288,128]{2,1,0:T(8,128)(2,1)S(1)} %collective-permute-done.10.refs_2_.refs_5_, ...), custom_call_target="tpu_custom_call" | custom-call | tf_op jit(solution)/shard_map/attend/pallas_call | solution.py:58
  58.5 0.5 collective-permute-start.15
  58.9 2.8 %attend.11.o3 = bf16[272,512]{1,0:T(8,128)(2,1)S(1)} custom-call(bf16[16,64]{1,0:T(8,128)(2,1)S(1)} %use.1.refs_4_.refs_0_, bf16[256,640]{1,0:T(8,128)(2,1)S(1)} %get-tuple-element.32.refs_1_.q_ref, bf16[8,288,128]{2,1,0:T(8,128)(2,1)S(1)} %get-tuple-element.41.refs_4_.refs_2_, bf16[8,288,128]{2,1,0:T(8,128)(2,1)S(1)} %get-tuple-element.42.refs_5_.refs_3_, ...), custom_call_target="tpu_custom_call" | custom-call | tf_op jit(solution)/shard_map/attend/pallas_call | solution.py:58
  61.7 0.6 collective-permute-done.13.o0
  62.3 5.8 %collective-permute-done.14.o1 = bf16[272,512]{1,0:T(8,128)(2,1)S(1)} collective-permute-done((bf16[272,512]{1,0:T(8,128)(2,1)S(1)}, bf16[272,512]{1,0:T(8,128)(2,1)S(1)}, u32[]{:S(2)}, u32[]{:S(2)}) %collective-permute-start.14) | collective-permute-done | bytes 278560 | tf_op jit(solution)/shard_map/ppermute | solution.py:29
  68.2 0.8 merge.1
  69.1 1.9 %collective-permute-start.18 = (bf16[16,2048]{1,0:T(8,128)(2,1)S(1)}, bf16[16,2048]{1,0:T(8,128)(2,1)S(1)}, u32[]{:S(2)}, u32[]{:S(2)}) collective-permute-start(bf16[16,2048]{1,0:T(8,128)(2,1)S(1)} %merge.1), channel_id=1, source_target_pairs={{0,32},{1,9},{2,34},{3,11},{4,36},{5,13},{6,38},{7,15},{8,40},{9,1... | collective-permute-start | bytes 196616 | tf_op jit(solution)/shard_map/ppermute | solution.py:49
  71.0 2.1 %collective-permute-start.17 = (bf16[16,2048]{1,0:T(8,128)(2,1)S(1)}, bf16[16,2048]{1,0:T(8,128)(2,1)S(1)}, u32[]{:S(2)}, u32[]{:S(2)}) collective-permute-start(bf16[16,2048]{1,0:T(8,128)(2,1)S(1)} %merge.1), channel_id=1, source_target_pairs={{0,64},{1,17},{2,66},{3,19},{4,68},{5,21},{6,70},{7,23},{8,72},{9,... | collective-permute-start | bytes 196616 | tf_op jit(solution)/shard_map/ppermute | solution.py:49
  73.1 1.6 %collective-permute-start.16 = (bf16[16,2048]{1,0:T(8,128)(2,1)S(1)}, bf16[16,2048]{1,0:T(8,128)(2,1)S(1)}, u32[]{:S(2)}, u32[]{:S(2)}) collective-permute-start(bf16[16,2048]{1,0:T(8,128)(2,1)S(1)} %merge.1), channel_id=1, source_target_pairs={{0,96},{1,25},{2,98},{3,27},{4,100},{5,29},{6,102},{7,31},{8,104},... | collective-permute-start | bytes 196616 | tf_op jit(solution)/shard_map/ppermute | solution.py:49
  74.7 2.1 %collective-permute-done.17 = bf16[16,2048]{1,0:T(8,128)(2,1)S(1)} collective-permute-done((bf16[16,2048]{1,0:T(8,128)(2,1)S(1)}, bf16[16,2048]{1,0:T(8,128)(2,1)S(1)}, u32[]{:S(2)}, u32[]{:S(2)}) %collective-permute-start.17) | collective-permute-done | bytes 65568 | tf_op jit(solution)/shard_map/ppermute | solution.py:49
  76.8 0.6 collective-permute-done.16
  77.4 2.2 %collective-permute-start.19 = (bf16[64,2048]{1,0:T(8,128)(2,1)S(1)}, bf16[64,2048]{1,0:T(8,128)(2,1)S(1)}, u32[]{:S(2)}, u32[]{:S(2)}) collective-permute-start(bf16[64,2048]{1,0:T(8,128)(2,1)S(1)} %pad_maximum_fusion.p0), channel_id=1, source_target_pairs={{0,24},{1,97},{2,26},{3,99},{4,28},{5,101},{6,30},{7,103},{8,0},{9... | collective-permute-start | bytes 786440 | tf_op jit(solution)/shard_map/ppermute | solution.py:49
  79.7 1.4 %collective-permute-start.20 = (bf16[64,2048]{1,0:T(8,128)(2,1)S(1)}, bf16[64,2048]{1,0:T(8,128)(2,1)S(1)}, u32[]{:S(2)}, u32[]{:S(2)}) collective-permute-start(bf16[64,2048]{1,0:T(8,128)(2,1)S(1)} %pad_maximum_fusion.p0), channel_id=1, source_target_pairs={{0,16},{1,65},{2,18},{3,67},{4,20},{5,69},{6,22},{7,71},{8,24},{9,... | collective-permute-start | bytes 786440 | tf_op jit(solution)/shard_map/ppermute | solution.py:49
  81.1 0.6 collective-permute-start.21
  81.6 4.8 %collective-permute-done.19.p1 = bf16[64,2048]{1,0:T(8,128)(2,1)S(1)} collective-permute-done((bf16[64,2048]{1,0:T(8,128)(2,1)S(1)}, bf16[64,2048]{1,0:T(8,128)(2,1)S(1)}, u32[]{:S(2)}, u32[]{:S(2)}) %collective-permute-start.19) | collective-permute-done | bytes 262176 | tf_op jit(solution)/shard_map/ppermute | solution.py:49
  86.4 1.2 collective-permute-done.20.p2
  87.6 2.7 %collective-permute-done.21.p3 = bf16[64,2048]{1,0:T(8,128)(2,1)S(1)} collective-permute-done((bf16[64,2048]{1,0:T(8,128)(2,1)S(1)}, bf16[64,2048]{1,0:T(8,128)(2,1)S(1)}, u32[]{:S(2)}, u32[]{:S(2)}) %collective-permute-start.21) | collective-permute-done | bytes 262176 | tf_op jit(solution)/shard_map/ppermute | solution.py:49
  90.4 1.3 project.1
  91.7 1.3 collective-permute-done.22
  93.1 1.4 collective-permute-start.23
  94.5 2.8 %collective-permute-start.24 = (bf16[2,4,16,448]{3,2,1,0:T(8,128)(2,1)S(1)}, bf16[2,4,16,448]{3,2,1,0:T(8,128)(2,1)S(1)}, u32[]{:S(2)}, u32[]{:S(2)}) collective-permute-start(bf16[2,4,16,448]{3,2,1,0:T(8,128)(2,1)S(1)} %add_convert_fusion.pair), channel_id=1, source_target_pairs={{0,4},{1,5},{2,6},{3,7},{4,0},{5,1},{6,2},{7,3},{8,12},{9,13},{10,... | collective-permute-start | bytes 344072 | tf_op jit(solution)/shard_map/ppermute | solution.py:29
  97.2 0.7 collective-permute-start.25
  98.0 1.5 %collective-permute-done.23.t1 = bf16[2,4,16,448]{3,2,1,0:T(8,128)(2,1)S(1)} collective-permute-done((bf16[2,4,16,448]{3,2,1,0:T(8,128)(2,1)S(1)}, bf16[2,4,16,448]{3,2,1,0:T(8,128)(2,1)S(1)}, u32[]{:S(2)}, u32[]{:S(2)}) %collective-permute-start.23) | collective-permute-done | bytes 114720 | tf_op jit(solution)/shard_map/ppermute | solution.py:29
  99.5 4.1 %collective-permute-done.24.t2 = bf16[2,4,16,448]{3,2,1,0:T(8,128)(2,1)S(1)} collective-permute-done((bf16[2,4,16,448]{3,2,1,0:T(8,128)(2,1)S(1)}, bf16[2,4,16,448]{3,2,1,0:T(8,128)(2,1)S(1)}, u32[]{:S(2)}, u32[]{:S(2)}) %collective-permute-start.24) | collective-permute-done | bytes 114720 | tf_op jit(solution)/shard_map/ppermute | solution.py:29
  103.7 2.2 %collective-permute-done.25.t3 = bf16[2,4,16,448]{3,2,1,0:T(8,128)(2,1)S(1)} collective-permute-done((bf16[2,4,16,448]{3,2,1,0:T(8,128)(2,1)S(1)}, bf16[2,4,16,448]{3,2,1,0:T(8,128)(2,1)S(1)}, u32[]{:S(2)}, u32[]{:S(2)}) %collective-permute-start.25) | collective-permute-done | bytes 114720 | tf_op jit(solution)/shard_map/ppermute | solution.py:29
  105.9 0.6 join.1.half_ref
  106.7 1.3 collective-permute-done.26.other_ref
  108.0 2.0 %ffn.1 = (bf16[16,16,448]{2,1,0:T(8,128)(2,1)S(1)}, bf16[4,16,4736]{2,1,0:T(8,128)(2,1)S(1)}, bf16[4,16,4736]{2,1,0:T(8,128)(2,1)S(1)}, bf16[4,16,4736]{2,1,0:T(8,128)(2,1)S(1)}, bf16[4,16,4736]{2,1,0:T(8,128)(2,1)S(1)}) custom-call(s32[4]{0:T(128)S(1)} %pad_add_fusion.where, bf16[2,4,16,448]{3,2,1,0:T(8,128)(2,1)S(1)} %join.1.half_ref, ...), custom_call_target="tpu_custom_call" | custom-call | tf_op jit(solution)/shard_map/ffn/pallas_call | solution.py:58
  109.9 1.8 %collective-permute-start.27 = (bf16[4,16,4736]{2,1,0:T(8,128)(2,1)S(1)}, bf16[4,16,4736]{2,1,0:T(8,128)(2,1)S(1)}, u32[]{:S(2)}, u32[]{:S(2)}) collective-permute-start(bf16[4,16,4736]{2,1,0:T(8,128)(2,1)S(1)} %get-tuple-element.53), channel_id=1, source_target_pairs={{0,64},{1,17},{2,66},{3,19},{4,68},{5,21},{6,70},{7,23},{8,72},{9,... | collective-permute-start | bytes 1818632 | tf_op jit(solution)/shard_map/ppermute | solution.py:49
  111.7 1.9 %collective-permute-start.28 = (bf16[4,16,4736]{2,1,0:T(8,128)(2,1)S(1)}, bf16[4,16,4736]{2,1,0:T(8,128)(2,1)S(1)}, u32[]{:S(2)}, u32[]{:S(2)}) collective-permute-start(bf16[4,16,4736]{2,1,0:T(8,128)(2,1)S(1)} %get-tuple-element.54), channel_id=1, source_target_pairs={{0,32},{1,9},{2,34},{3,11},{4,36},{5,13},{6,38},{7,15},{8,40},{9,1... | collective-permute-start | bytes 1818632 | tf_op jit(solution)/shard_map/ppermute | solution.py:49
  113.7 1.3 collective-permute-start.29
  115.0 6.7 %collective-permute-done.27.refs_1_ = bf16[4,16,4736]{2,1,0:T(8,128)(2,1)S(1)} collective-permute-done((bf16[4,16,4736]{2,1,0:T(8,128)(2,1)S(1)}, bf16[4,16,4736]{2,1,0:T(8,128)(2,1)S(1)}, u32[]{:S(2)}, u32[]{:S(2)}) %collective-permute-start.27) | collective-permute-done | bytes 606240 | tf_op jit(solution)/shard_map/ppermute | solution.py:49
  121.7 6.4 %collective-permute-done.28.refs_2_ = bf16[4,16,4736]{2,1,0:T(8,128)(2,1)S(1)} collective-permute-done((bf16[4,16,4736]{2,1,0:T(8,128)(2,1)S(1)}, bf16[4,16,4736]{2,1,0:T(8,128)(2,1)S(1)}, u32[]{:S(2)}, u32[]{:S(2)}) %collective-permute-start.28) | collective-permute-done | bytes 606240 | tf_op jit(solution)/shard_map/ppermute | solution.py:49
  128.2 0.5 fold.1
  128.8 1.5 %collective-permute-start.30 = (bf16[16,4736]{1,0:T(8,128)(2,1)S(1)}, bf16[16,4736]{1,0:T(8,128)(2,1)S(1)}, u32[]{:S(2)}, u32[]{:S(2)}) collective-permute-start(bf16[16,4736]{1,0:T(8,128)(2,1)S(1)} %get-tuple-element.57), channel_id=1, source_target_pairs={{0,16},{1,65},{2,18},{3,67},{4,20},{5,69},{6,22},{7,71},{8,24},{9,... | collective-permute-start | bytes 454664 | tf_op jit(solution)/shard_map/ppermute | solution.py:49
  130.3 3.2 %collective-permute-start.32 = (bf16[16,4736]{1,0:T(8,128)(2,1)S(1)}, bf16[16,4736]{1,0:T(8,128)(2,1)S(1)}, u32[]{:S(2)}, u32[]{:S(2)}) collective-permute-start(bf16[16,4736]{1,0:T(8,128)(2,1)S(1)} %get-tuple-element.59), channel_id=1, source_target_pairs={{0,24},{1,97},{2,26},{3,99},{4,28},{5,101},{6,30},{7,103},{8,0},{9... | collective-permute-start | bytes 454664 | tf_op jit(solution)/shard_map/ppermute | solution.py:49
  133.5 0.8 turn.3
  134.3 1.3 collective-permute-done.30.r1
  135.6 1.6 %collective-permute-done.31.r2 = bf16[16,4736]{1,0:T(8,128)(2,1)S(1)} collective-permute-done((bf16[16,4736]{1,0:T(8,128)(2,1)S(1)}, bf16[16,4736]{1,0:T(8,128)(2,1)S(1)}, u32[]{:S(2)}, u32[]{:S(2)}) %collective-permute-start.31) | collective-permute-done | bytes 151584 | tf_op jit(solution)/shard_map/ppermute | solution.py:49
  137.2 0.8 finish.1
  (49 shorter events, 1.6 us)
Async XLA Ops:
  0.6 2.9 %copy-start.7 = (s32[2048]{0:T(1024)S(1)}, s32[2048]{0:T(1024)}, u32[]{:S(2)}) copy-start(s32[2048]{0:T(1024)} %param.15) | copy-start | bytes 24580
  0.6 2.9 %copy-start.6 = (s32[256,32]{0,1:T(8,128)S(1)}, s32[256,32]{0,1:T(8,128)}, u32[]{:S(2)}) copy-start(s32[256,32]{0,1:T(8,128)} %param.17) | copy-start | bytes 98308
  0.7 2.9 %copy-start.9 = (s32[256]{0:T(256)S(1)}, s32[256]{0:T(256)}, u32[]{:S(2)}) copy-start(s32[256]{0:T(256)} %prompts.1) | copy-start | bytes 3076
  0.7 10.8 %copy-start.4 = (bf16[16,9216]{1,0:T(8,128)(2,1)S(1)}, bf16[16,9216]{1,0:T(8,128)(2,1)}, u32[]{:S(2)}) copy-start(bf16[16,9216]{1,0:T(8,128)(2,1)} %queries.1) | copy-start | bytes 884740
  0.7 10.8 %copy-start.8 = (bf16[16,576]{1,0:T(8,128)(2,1)S(1)}, bf16[16,576]{1,0:T(8,128)(2,1)}, u32[]{:S(2)}) copy-start(bf16[16,576]{1,0:T(8,128)(2,1)} %own.1) | copy-start | bytes 55300
  5.7 18.1 %collective-permute-start.3 = (bf16[8,288,128]{2,1,0:T(8,128)(2,1)S(1)}, bf16[8,288,128]{2,1,0:T(8,128)(2,1)S(1)}, u32[]{:S(2)}, u32[]{:S(2)}) collective-permute-start(bf16[8,288,128]{2,1,0:T(8,128)(2,1)S(1)} %get-tuple-element.33), channel_id=1, source_target_pairs={{0,32},{1,9},{2,34},{3,11},{4,36},{5,13},{6,38},{7,15},{8,40},{9,1... | collective-permute-start | bytes 1769480 | tf_op jit(solution)/shard_map/ppermute | solution.py:49
  7.3 16.9 %collective-permute-start.4 = (bf16[8,288,128]{2,1,0:T(8,128)(2,1)S(1)}, bf16[8,288,128]{2,1,0:T(8,128)(2,1)S(1)}, u32[]{:S(2)}, u32[]{:S(2)}) collective-permute-start(bf16[8,288,128]{2,1,0:T(8,128)(2,1)S(1)} %get-tuple-element.34), channel_id=1, source_target_pairs={{0,64},{1,17},{2,66},{3,19},{4,68},{5,21},{6,70},{7,23},{8,72},{9,... | collective-permute-start | bytes 1769480 | tf_op jit(solution)/shard_map/ppermute | solution.py:49
  10.0 14.2 %collective-permute-start.5 = (bf16[8,288,128]{2,1,0:T(8,128)(2,1)S(1)}, bf16[8,288,128]{2,1,0:T(8,128)(2,1)S(1)}, u32[]{:S(2)}, u32[]{:S(2)}) collective-permute-start(bf16[8,288,128]{2,1,0:T(8,128)(2,1)S(1)} %get-tuple-element.35), channel_id=1, source_target_pairs={{0,96},{1,25},{2,98},{3,27},{4,100},{5,29},{6,102},{7,31},{8,104},... | collective-permute-start | bytes 1769480 | tf_op jit(solution)/shard_map/ppermute | solution.py:49
  11.6 12.2 %collective-permute-start = (bf16[256,640]{1,0:T(8,128)(2,1)S(1)}, bf16[256,640]{1,0:T(8,128)(2,1)S(1)}, u32[]{:S(2)}, u32[]{:S(2)}) collective-permute-start(bf16[256,640]{1,0:T(8,128)(2,1)S(1)} %get-tuple-element.32.refs_1_.q_ref), channel_id=1, source_target_pairs={{0,4},{1,5},{2,6},{3,7},{4,0},{5,1},{6,2},{7,3},{8,12},{9,13},{10,... | collective-permute-start | bytes 983048 | tf_op jit(solution)/shard_map/ppermute | solution.py:29
  14.9 16.2 %collective-permute-start.1 = (bf16[256,640]{1,0:T(8,128)(2,1)S(1)}, bf16[256,640]{1,0:T(8,128)(2,1)S(1)}, u32[]{:S(2)}, u32[]{:S(2)}) collective-permute-start(bf16[256,640]{1,0:T(8,128)(2,1)S(1)} %get-tuple-element.32.refs_1_.q_ref), channel_id=1, source_target_pairs={{0,2},{1,3},{2,0},{3,1},{4,6},{5,7},{6,4},{7,5},{8,10},{9,11},{10,... | collective-permute-start | bytes 983048 | tf_op jit(solution)/shard_map/ppermute | solution.py:29
  24.4 16.2 %collective-permute-start.6 = (bf16[8,288,128]{2,1,0:T(8,128)(2,1)S(1)}, bf16[8,288,128]{2,1,0:T(8,128)(2,1)S(1)}, u32[]{:S(2)}, u32[]{:S(2)}) collective-permute-start(bf16[8,288,128]{2,1,0:T(8,128)(2,1)S(1)} %get-tuple-element.36.refs_5_), channel_id=1, source_target_pairs={{0,1},{1,0},{2,3},{3,2},{4,5},{5,4},{6,7},{7,6},{8,9},{9,8},{10,11... | collective-permute-start | bytes 1769480 | tf_op jit(solution)/shard_map/ppermute | solution.py:29
  24.6 19.3 %collective-permute-start.7 = (bf16[8,288,128]{2,1,0:T(8,128)(2,1)S(1)}, bf16[8,288,128]{2,1,0:T(8,128)(2,1)S(1)}, u32[]{:S(2)}, u32[]{:S(2)}) collective-permute-start(bf16[8,288,128]{2,1,0:T(8,128)(2,1)S(1)} %get-tuple-element.38), channel_id=1, source_target_pairs={{0,8},{1,33},{2,10},{3,35},{4,12},{5,37},{6,14},{7,39},{8,16},{9,4... | collective-permute-start | bytes 1769480 | tf_op jit(solution)/shard_map/ppermute | solution.py:49
  26.5 17.8 %collective-permute-start.8 = (bf16[8,288,128]{2,1,0:T(8,128)(2,1)S(1)}, bf16[8,288,128]{2,1,0:T(8,128)(2,1)S(1)}, u32[]{:S(2)}, u32[]{:S(2)}) collective-permute-start(bf16[8,288,128]{2,1,0:T(8,128)(2,1)S(1)} %get-tuple-element.39), channel_id=1, source_target_pairs={{0,16},{1,65},{2,18},{3,67},{4,20},{5,69},{6,22},{7,71},{8,24},{9,... | collective-permute-start | bytes 1769480 | tf_op jit(solution)/shard_map/ppermute | solution.py:49
  30.0 14.2 %collective-permute-start.9 = (bf16[8,288,128]{2,1,0:T(8,128)(2,1)S(1)}, bf16[8,288,128]{2,1,0:T(8,128)(2,1)S(1)}, u32[]{:S(2)}, u32[]{:S(2)}) collective-permute-start(bf16[8,288,128]{2,1,0:T(8,128)(2,1)S(1)} %get-tuple-element.40), channel_id=1, source_target_pairs={{0,24},{1,97},{2,26},{3,99},{4,28},{5,101},{6,30},{7,103},{8,0},{9... | collective-permute-start | bytes 1769480 | tf_op jit(solution)/shard_map/ppermute | solution.py:49
  31.1 9.5 %collective-permute-start.2 = (bf16[256,640]{1,0:T(8,128)(2,1)S(1)}, bf16[256,640]{1,0:T(8,128)(2,1)S(1)}, u32[]{:S(2)}, u32[]{:S(2)}) collective-permute-start(bf16[256,640]{1,0:T(8,128)(2,1)S(1)} %get-tuple-element.32.refs_1_.q_ref), channel_id=1, source_target_pairs={{0,6},{1,7},{2,4},{3,5},{4,2},{5,3},{6,0},{7,1},{8,14},{9,15},{10,... | collective-permute-start | bytes 983048 | tf_op jit(solution)/shard_map/ppermute | solution.py:29
  44.3 5.3 %collective-permute-start.10 = (bf16[8,288,128]{2,1,0:T(8,128)(2,1)S(1)}, bf16[8,288,128]{2,1,0:T(8,128)(2,1)S(1)}, u32[]{:S(2)}, u32[]{:S(2)}) collective-permute-start(bf16[8,288,128]{2,1,0:T(8,128)(2,1)S(1)} %get-tuple-element.41.refs_4_.refs_2_), channel_id=1, source_target_pairs={{0,1},{1,0},{2,3},{3,2},{4,5},{5,4},{6,7},{7,6},{8,9},{9,8},{10,11... | collective-permute-start | bytes 1769480 | tf_op jit(solution)/shard_map/ppermute | solution.py:29
  44.4 5.2 %collective-permute-start.11 = (bf16[8,288,128]{2,1,0:T(8,128)(2,1)S(1)}, bf16[8,288,128]{2,1,0:T(8,128)(2,1)S(1)}, u32[]{:S(2)}, u32[]{:S(2)}) collective-permute-start(bf16[8,288,128]{2,1,0:T(8,128)(2,1)S(1)} %get-tuple-element.42.refs_5_.refs_3_), channel_id=1, source_target_pairs={{0,1},{1,0},{2,3},{3,2},{4,5},{5,4},{6,7},{7,6},{8,9},{9,8},{10,11... | collective-permute-start | bytes 1769480 | tf_op jit(solution)/shard_map/ppermute | solution.py:29
  44.9 4.7 %collective-permute-start.12 = (bf16[8,288,128]{2,1,0:T(8,128)(2,1)S(1)}, bf16[8,288,128]{2,1,0:T(8,128)(2,1)S(1)}, u32[]{:S(2)}, u32[]{:S(2)}) collective-permute-start(bf16[8,288,128]{2,1,0:T(8,128)(2,1)S(1)} %get-tuple-element.43.refs_6_.refs_4_), channel_id=1, source_target_pairs={{0,1},{1,0},{2,3},{3,2},{4,5},{5,4},{6,7},{7,6},{8,9},{9,8},{10,11... | collective-permute-start | bytes 1769480 | tf_op jit(solution)/shard_map/ppermute | solution.py:29
  51.2 11.0 %collective-permute-start.13 = (bf16[272,512]{1,0:T(8,128)(2,1)S(1)}, bf16[272,512]{1,0:T(8,128)(2,1)S(1)}, u32[]{:S(2)}, u32[]{:S(2)}) collective-permute-start(bf16[272,512]{1,0:T(8,128)(2,1)S(1)} %attend.8), channel_id=1, source_target_pairs={{0,4},{1,5},{2,6},{3,7},{4,0},{5,1},{6,2},{7,3},{8,12},{9,13},{10,... | collective-permute-start | bytes 835592 | tf_op jit(solution)/shard_map/ppermute | solution.py:29
  56.1 12.0 %collective-permute-start.14 = (bf16[272,512]{1,0:T(8,128)(2,1)S(1)}, bf16[272,512]{1,0:T(8,128)(2,1)S(1)}, u32[]{:S(2)}, u32[]{:S(2)}) collective-permute-start(bf16[272,512]{1,0:T(8,128)(2,1)S(1)} %attend.9), channel_id=1, source_target_pairs={{0,2},{1,3},{2,0},{3,1},{4,6},{5,7},{6,4},{7,5},{8,10},{9,11},{10,... | collective-permute-start | bytes 835592 | tf_op jit(solution)/shard_map/ppermute | solution.py:29
  58.5 9.7 %copy-start = (bf16[16,512,128]{2,1,0:T(8,128)(2,1)S(1)}, bf16[16,512,128]{2,1,0:T(8,128)(2,1)}, u32[]{:S(2)}) copy-start(bf16[16,512,128]{2,1,0:T(8,128)(2,1)} %up_ref.1) | copy-start | bytes 6291460
  58.5 9.7 %collective-permute-start.15 = (bf16[272,512]{1,0:T(8,128)(2,1)S(1)}, bf16[272,512]{1,0:T(8,128)(2,1)S(1)}, u32[]{:S(2)}, u32[]{:S(2)}) collective-permute-start(bf16[272,512]{1,0:T(8,128)(2,1)S(1)} %attend.10), channel_id=1, source_target_pairs={{0,6},{1,7},{2,4},{3,5},{4,2},{5,3},{6,0},{7,1},{8,14},{9,15},{10,... | collective-permute-start | bytes 835592 | tf_op jit(solution)/shard_map/ppermute | solution.py:29
  68.2 22.1 %copy-start.3 = (bf16[2048,448]{0,1:T(8,128)(2,1)S(1)}, bf16[2048,448]{0,1:T(8,128)(2,1)}, u32[]{:S(2)}) copy-start(bf16[2048,448]{0,1:T(8,128)(2,1)} %param.19) | copy-start | bytes 5505028
  69.1 28.8 %copy-start.5 = (bf16[256,448]{0,1:T(8,128)(2,1)S(1)}, bf16[256,448]{0,1:T(8,128)(2,1)}, u32[]{:S(2)}) copy-start(bf16[256,448]{0,1:T(8,128)(2,1)} %param.20) | copy-start | bytes 688132
  69.1 5.6 %collective-permute-start.18 = (bf16[16,2048]{1,0:T(8,128)(2,1)S(1)}, bf16[16,2048]{1,0:T(8,128)(2,1)S(1)}, u32[]{:S(2)}, u32[]{:S(2)}) collective-permute-start(bf16[16,2048]{1,0:T(8,128)(2,1)S(1)} %merge.1), channel_id=1, source_target_pairs={{0,32},{1,9},{2,34},{3,11},{4,36},{5,13},{6,38},{7,15},{8,40},{9,1... | collective-permute-start | bytes 196616 | tf_op jit(solution)/shard_map/ppermute | solution.py:49
  71.0 5.8 %collective-permute-start.17 = (bf16[16,2048]{1,0:T(8,128)(2,1)S(1)}, bf16[16,2048]{1,0:T(8,128)(2,1)S(1)}, u32[]{:S(2)}, u32[]{:S(2)}) collective-permute-start(bf16[16,2048]{1,0:T(8,128)(2,1)S(1)} %merge.1), channel_id=1, source_target_pairs={{0,64},{1,17},{2,66},{3,19},{4,68},{5,21},{6,70},{7,23},{8,72},{9,... | collective-permute-start | bytes 196616 | tf_op jit(solution)/shard_map/ppermute | solution.py:49
  73.1 4.3 %collective-permute-start.16 = (bf16[16,2048]{1,0:T(8,128)(2,1)S(1)}, bf16[16,2048]{1,0:T(8,128)(2,1)S(1)}, u32[]{:S(2)}, u32[]{:S(2)}) collective-permute-start(bf16[16,2048]{1,0:T(8,128)(2,1)S(1)} %merge.1), channel_id=1, source_target_pairs={{0,96},{1,25},{2,98},{3,27},{4,100},{5,29},{6,102},{7,31},{8,104},... | collective-permute-start | bytes 196616 | tf_op jit(solution)/shard_map/ppermute | solution.py:49
  77.4 9.0 %collective-permute-start.19 = (bf16[64,2048]{1,0:T(8,128)(2,1)S(1)}, bf16[64,2048]{1,0:T(8,128)(2,1)S(1)}, u32[]{:S(2)}, u32[]{:S(2)}) collective-permute-start(bf16[64,2048]{1,0:T(8,128)(2,1)S(1)} %pad_maximum_fusion.p0), channel_id=1, source_target_pairs={{0,24},{1,97},{2,26},{3,99},{4,28},{5,101},{6,30},{7,103},{8,0},{9... | collective-permute-start | bytes 786440 | tf_op jit(solution)/shard_map/ppermute | solution.py:49
  79.7 8.0 %collective-permute-start.20 = (bf16[64,2048]{1,0:T(8,128)(2,1)S(1)}, bf16[64,2048]{1,0:T(8,128)(2,1)S(1)}, u32[]{:S(2)}, u32[]{:S(2)}) collective-permute-start(bf16[64,2048]{1,0:T(8,128)(2,1)S(1)} %pad_maximum_fusion.p0), channel_id=1, source_target_pairs={{0,16},{1,65},{2,18},{3,67},{4,20},{5,69},{6,22},{7,71},{8,24},{9,... | collective-permute-start | bytes 786440 | tf_op jit(solution)/shard_map/ppermute | solution.py:49
  81.1 9.3 %collective-permute-start.21 = (bf16[64,2048]{1,0:T(8,128)(2,1)S(1)}, bf16[64,2048]{1,0:T(8,128)(2,1)S(1)}, u32[]{:S(2)}, u32[]{:S(2)}) collective-permute-start(bf16[64,2048]{1,0:T(8,128)(2,1)S(1)} %pad_maximum_fusion.p0), channel_id=1, source_target_pairs={{0,8},{1,33},{2,10},{3,35},{4,12},{5,37},{6,14},{7,39},{8,16},{9,4... | collective-permute-start | bytes 786440 | tf_op jit(solution)/shard_map/ppermute | solution.py:49
  90.3 16.3 %copy-start.10 = (bf16[448]{0:T(512)(128)(2,1)S(1)}, bf16[448]{0:T(512)(128)(2,1)}, u32[]{:S(2)}) copy-start(bf16[448]{0:T(512)(128)(2,1)} %param.21) | copy-start | bytes 2692
  90.3 17.6 %copy-start.1 = (bf16[448,2304]{1,0:T(8,128)(2,1)S(1)}, bf16[448,2304]{1,0:T(8,128)(2,1)}, u32[]{:S(2)}) copy-start(bf16[448,2304]{1,0:T(8,128)(2,1)} %wg_ref.1) | copy-start | bytes 6193156
  90.3 17.6 %copy-start.2 = (bf16[448,2304]{1,0:T(8,128)(2,1)S(1)}, bf16[448,2304]{1,0:T(8,128)(2,1)}, u32[]{:S(2)}) copy-start(bf16[448,2304]{1,0:T(8,128)(2,1)} %wu_ref.1) | copy-start | bytes 6193156
  91.7 1.4 %collective-permute-start.22 = (bf16[2,4,16,448]{3,2,1,0:T(8,128)(2,1)S(1)}, bf16[2,4,16,448]{3,2,1,0:T(8,128)(2,1)S(1)}, u32[]{:S(2)}, u32[]{:S(2)}) collective-permute-start(bf16[2,4,16,448]{3,2,1,0:T(8,128)(2,1)S(1)} %get-tuple-element.50), channel_id=1, source_target_pairs={{0,1},{1,0},{2,3},{3,2},{4,5},{5,4},{6,7},{7,6},{8,9},{9,8},{10,11... | collective-permute-start | bytes 344072 | tf_op jit(solution)/shard_map/ppermute | solution.py:29
  93.1 6.4 %collective-permute-start.23 = (bf16[2,4,16,448]{3,2,1,0:T(8,128)(2,1)S(1)}, bf16[2,4,16,448]{3,2,1,0:T(8,128)(2,1)S(1)}, u32[]{:S(2)}, u32[]{:S(2)}) collective-permute-start(bf16[2,4,16,448]{3,2,1,0:T(8,128)(2,1)S(1)} %add_convert_fusion.pair), channel_id=1, source_target_pairs={{0,2},{1,3},{2,0},{3,1},{4,6},{5,7},{6,4},{7,5},{8,10},{9,11},{10,... | collective-permute-start | bytes 344072 | tf_op jit(solution)/shard_map/ppermute | solution.py:29
  94.5 9.2 %collective-permute-start.24 = (bf16[2,4,16,448]{3,2,1,0:T(8,128)(2,1)S(1)}, bf16[2,4,16,448]{3,2,1,0:T(8,128)(2,1)S(1)}, u32[]{:S(2)}, u32[]{:S(2)}) collective-permute-start(bf16[2,4,16,448]{3,2,1,0:T(8,128)(2,1)S(1)} %add_convert_fusion.pair), channel_id=1, source_target_pairs={{0,4},{1,5},{2,6},{3,7},{4,0},{5,1},{6,2},{7,3},{8,12},{9,13},{10,... | collective-permute-start | bytes 344072 | tf_op jit(solution)/shard_map/ppermute | solution.py:29
  97.2 8.7 %collective-permute-start.25 = (bf16[2,4,16,448]{3,2,1,0:T(8,128)(2,1)S(1)}, bf16[2,4,16,448]{3,2,1,0:T(8,128)(2,1)S(1)}, u32[]{:S(2)}, u32[]{:S(2)}) collective-permute-start(bf16[2,4,16,448]{3,2,1,0:T(8,128)(2,1)S(1)} %add_convert_fusion.pair), channel_id=1, source_target_pairs={{0,6},{1,7},{2,4},{3,5},{4,2},{5,3},{6,0},{7,1},{8,14},{9,15},{10,... | collective-permute-start | bytes 344072 | tf_op jit(solution)/shard_map/ppermute | solution.py:29
  106.5 1.4 %collective-permute-start.26 = (bf16[2,4,16,448]{3,2,1,0:T(8,128)(2,1)S(1)}, bf16[2,4,16,448]{3,2,1,0:T(8,128)(2,1)S(1)}, u32[]{:S(2)}, u32[]{:S(2)}) collective-permute-start(bf16[2,4,16,448]{3,2,1,0:T(8,128)(2,1)S(1)} %join.1.half_ref), channel_id=1, source_target_pairs={{0,1},{1,0},{2,3},{3,2},{4,5},{5,4},{6,7},{7,6},{8,9},{9,8},{10,11... | collective-permute-start | bytes 344072 | tf_op jit(solution)/shard_map/ppermute | solution.py:29
  109.9 11.7 %collective-permute-start.27 = (bf16[4,16,4736]{2,1,0:T(8,128)(2,1)S(1)}, bf16[4,16,4736]{2,1,0:T(8,128)(2,1)S(1)}, u32[]{:S(2)}, u32[]{:S(2)}) collective-permute-start(bf16[4,16,4736]{2,1,0:T(8,128)(2,1)S(1)} %get-tuple-element.53), channel_id=1, source_target_pairs={{0,64},{1,17},{2,66},{3,19},{4,68},{5,21},{6,70},{7,23},{8,72},{9,... | collective-permute-start | bytes 1818632 | tf_op jit(solution)/shard_map/ppermute | solution.py:49
  111.7 16.4 %collective-permute-start.28 = (bf16[4,16,4736]{2,1,0:T(8,128)(2,1)S(1)}, bf16[4,16,4736]{2,1,0:T(8,128)(2,1)S(1)}, u32[]{:S(2)}, u32[]{:S(2)}) collective-permute-start(bf16[4,16,4736]{2,1,0:T(8,128)(2,1)S(1)} %get-tuple-element.54), channel_id=1, source_target_pairs={{0,32},{1,9},{2,34},{3,11},{4,36},{5,13},{6,38},{7,15},{8,40},{9,1... | collective-permute-start | bytes 1818632 | tf_op jit(solution)/shard_map/ppermute | solution.py:49
  113.7 14.6 %collective-permute-start.29 = (bf16[4,16,4736]{2,1,0:T(8,128)(2,1)S(1)}, bf16[4,16,4736]{2,1,0:T(8,128)(2,1)S(1)}, u32[]{:S(2)}, u32[]{:S(2)}) collective-permute-start(bf16[4,16,4736]{2,1,0:T(8,128)(2,1)S(1)} %get-tuple-element.55), channel_id=1, source_target_pairs={{0,96},{1,25},{2,98},{3,27},{4,100},{5,29},{6,102},{7,31},{8,104},... | collective-permute-start | bytes 1818632 | tf_op jit(solution)/shard_map/ppermute | solution.py:49
  128.8 6.8 %collective-permute-start.30 = (bf16[16,4736]{1,0:T(8,128)(2,1)S(1)}, bf16[16,4736]{1,0:T(8,128)(2,1)S(1)}, u32[]{:S(2)}, u32[]{:S(2)}) collective-permute-start(bf16[16,4736]{1,0:T(8,128)(2,1)S(1)} %get-tuple-element.57), channel_id=1, source_target_pairs={{0,16},{1,65},{2,18},{3,67},{4,20},{5,69},{6,22},{7,71},{8,24},{9,... | collective-permute-start | bytes 454664 | tf_op jit(solution)/shard_map/ppermute | solution.py:49
  130.2 6.9 %collective-permute-start.31 = (bf16[16,4736]{1,0:T(8,128)(2,1)S(1)}, bf16[16,4736]{1,0:T(8,128)(2,1)S(1)}, u32[]{:S(2)}, u32[]{:S(2)}) collective-permute-start(bf16[16,4736]{1,0:T(8,128)(2,1)S(1)} %get-tuple-element.58), channel_id=1, source_target_pairs={{0,8},{1,33},{2,10},{3,35},{4,12},{5,37},{6,14},{7,39},{8,16},{9,4... | collective-permute-start | bytes 454664 | tf_op jit(solution)/shard_map/ppermute | solution.py:49
  130.3 6.9 %collective-permute-start.32 = (bf16[16,4736]{1,0:T(8,128)(2,1)S(1)}, bf16[16,4736]{1,0:T(8,128)(2,1)S(1)}, u32[]{:S(2)}, u32[]{:S(2)}) collective-permute-start(bf16[16,4736]{1,0:T(8,128)(2,1)S(1)} %get-tuple-element.59), channel_id=1, source_target_pairs={{0,24},{1,97},{2,26},{3,99},{4,28},{5,101},{6,30},{7,103},{8,0},{9... | collective-permute-start | bytes 454664 | tf_op jit(solution)/shard_map/ppermute | solution.py:49

commit v8 on v7

--- a/solution.py
+++ b/solution.py
@@ -488,12 +488,12 @@
     far = after(done, arrived[1], arrived[2], arrived[3])
     far_other = [swap_core(v) for v in far]
     others = {k: qs[k] for k in (2, 1, 3)}
-    *rest, done = attend(use, others, 2, (2, 1), far, carry, last=False)
+    *rest, done = attend(use, others, 2, (3,), far, carry, last=False)
     parts = []
     for k in others:
-        (o,) = attend(use, {k: qs[k]}, 5, (2, 1), far_other, rest)
+        (o,) = attend(use, {k: qs[k]}, 5, (3,), far_other, rest)
         parts.append(send_y(o, k))
-    parts += attend(use, {0: q}, 2, (2, 2, 2), list(far) + far_other, carry)
+    parts += attend(use, {0: q}, 2, (3, 3), list(far) + far_other, carry)
     per_head = merge(parts, q, own, value_up)
 
     near = [per_head] + [send_dp(per_head, 0, 4 - k) for k in (1, 2, 3)]

time: 138 us -> 138 us (level)
  no operation moved by 1% of the time
where the time goes in v8:
time: 138 us
  waiting for transfers between devices  58 us (42%)
  starting transfers between devices  49.4 us (36%)
  Pallas kernels  26.7 us (19%)
  local copies, waits for them, and re-layouts  2.75 us (2%)
    ppermute x18, starting transfers between devices, send_dp(): return lax.ppermute(x, ('dp', 'tp'), pairs)  32.1 us
    ppermute x15, waiting for transfers between devices, send(): return lax.ppermute(x, axis, [(i, to(i)) for i in range(n)])  29.9 us
    ppermute x18, waiting for transfers between devices, send_dp(): return lax.ppermute(x, ('dp', 'tp'), pairs)  28.1 us
    pallas_call x19, Pallas kernels, call(): pl.pallas_call(kernel, out_shape=outs, in_specs=[SMEM] * scalars + [VMEM]...  25.8 us
    ppermute x15, starting transfers between devices, send(): return lax.ppermute(x, axis, [(i, to(i)) for i in range(n)])  17.3 us
  transfers between devices with their start and end apart: 33, of which 22 were waited for; matrix products, arithmetic and copies ran while one was open for 0% of the time, Pallas kernels for 12%

profile of v8, /device:TPU:0, one launch (start us, length us, event | category | flops | bytes accessed | tf_op | source)
XLA Modules:
  0.0 137.9 jit_solution(6774731434164450242)
XLA Ops:
  0.7 2.7 %reshape.24.tokens = bf16[16,64,576]{2,1,0:T(8,128)(2,1)S(1)} reshape(bf16[16,36864]{1,0:T(8,128)(2,1)} %param.14) | data formatting | bytes 2359296 | tf_op jit(solution)/shard_map/reshape | solution.py:459
  3.5 1.0 plan.1.picks
  4.5 1.2 fetch.1
  5.7 1.6 %collective-permute-start.3 = (bf16[8,288,128]{2,1,0:T(8,128)(2,1)S(1)}, bf16[8,288,128]{2,1,0:T(8,128)(2,1)S(1)}, u32[]{:S(2)}, u32[]{:S(2)}) collective-permute-start(bf16[8,288,128]{2,1,0:T(8,128)(2,1)S(1)} %get-tuple-element.33), channel_id=1, source_target_pairs={{0,32},{1,9},{2,34},{3,11},{4,36},{5,13},{6,38},{7,15},{8,40},{9,1... | collective-permute-start | bytes 1769480 | tf_op jit(solution)/shard_map/ppermute | solution.py:49
  7.3 2.7 %collective-permute-start.4 = (bf16[8,288,128]{2,1,0:T(8,128)(2,1)S(1)}, bf16[8,288,128]{2,1,0:T(8,128)(2,1)S(1)}, u32[]{:S(2)}, u32[]{:S(2)}) collective-permute-start(bf16[8,288,128]{2,1,0:T(8,128)(2,1)S(1)} %get-tuple-element.34), channel_id=1, source_target_pairs={{0,64},{1,17},{2,66},{3,19},{4,68},{5,21},{6,70},{7,23},{8,72},{9,... | collective-permute-start | bytes 1769480 | tf_op jit(solution)/shard_map/ppermute | solution.py:49
  10.0 1.4 %collective-permute-start.5 = (bf16[8,288,128]{2,1,0:T(8,128)(2,1)S(1)}, bf16[8,288,128]{2,1,0:T(8,128)(2,1)S(1)}, u32[]{:S(2)}, u32[]{:S(2)}) collective-permute-start(bf16[8,288,128]{2,1,0:T(8,128)(2,1)S(1)} %get-tuple-element.35), channel_id=1, source_target_pairs={{0,96},{1,25},{2,98},{3,27},{4,100},{5,29},{6,102},{7,31},{8,104},... | collective-permute-start | bytes 1769480 | tf_op jit(solution)/shard_map/ppermute | solution.py:49
  11.6 3.3 %collective-permute-start = (bf16[256,640]{1,0:T(8,128)(2,1)S(1)}, bf16[256,640]{1,0:T(8,128)(2,1)S(1)}, u32[]{:S(2)}, u32[]{:S(2)}) collective-permute-start(bf16[256,640]{1,0:T(8,128)(2,1)S(1)} %get-tuple-element.32.refs_1_.q_ref), channel_id=1, source_target_pairs={{0,4},{1,5},{2,6},{3,7},{4,0},{5,1},{6,2},{7,3},{8,12},{9,13},{10,... | collective-permute-start | bytes 983048 | tf_op jit(solution)/shard_map/ppermute | solution.py:29
  14.9 0.7 collective-permute-start.1
  15.6 1.6 %use.1.refs_4_.refs_0_ = bf16[16,64]{1,0:T(8,128)(2,1)S(1)} custom-call(s32[4]{0:T(128)S(1)} %pad_add_fusion.where, s32[256]{0:T(256)S(1)} %copy-done.9, s32[4,4,128]{2,1,0:T(4,128)S(1)} %bitcast.19, s32[32,256]{1,0:T(8,128)S(1)} %bitcast.17, bf16[8,288,128]{2,1,0:T(8,128)(2,1)S(1)} %get-tuple-element.31._.refs_0_), custom_call_target="tpu_custom_call" | custom-call | tf_op jit(solution)/shard_map/use/pallas_call | solution.py:58
  17.2 6.6 %collective-permute-done.refs_5_.refs_3_.refs_1_ = bf16[256,640]{1,0:T(8,128)(2,1)S(1)} collective-permute-done((bf16[256,640]{1,0:T(8,128)(2,1)S(1)}, bf16[256,640]{1,0:T(8,128)(2,1)S(1)}, u32[]{:S(2)}, u32[]{:S(2)}) %collective-permute-start) | collective-permute-done | bytes 327712 | tf_op jit(solution)/shard_map/ppermute | solution.py:29
  23.8 0.4 collective-permute-done.4.refs_2_
  24.6 1.9 %collective-permute-start.7 = (bf16[8,288,128]{2,1,0:T(8,128)(2,1)S(1)}, bf16[8,288,128]{2,1,0:T(8,128)(2,1)S(1)}, u32[]{:S(2)}, u32[]{:S(2)}) collective-permute-start(bf16[8,288,128]{2,1,0:T(8,128)(2,1)S(1)} %get-tuple-element.38), channel_id=1, source_target_pairs={{0,8},{1,33},{2,10},{3,35},{4,12},{5,37},{6,14},{7,39},{8,16},{9,4... | collective-permute-start | bytes 1769480 | tf_op jit(solution)/shard_map/ppermute | solution.py:49
  26.5 3.6 %collective-permute-start.8 = (bf16[8,288,128]{2,1,0:T(8,128)(2,1)S(1)}, bf16[8,288,128]{2,1,0:T(8,128)(2,1)S(1)}, u32[]{:S(2)}, u32[]{:S(2)}) collective-permute-start(bf16[8,288,128]{2,1,0:T(8,128)(2,1)S(1)} %get-tuple-element.39), channel_id=1, source_target_pairs={{0,16},{1,65},{2,18},{3,67},{4,20},{5,69},{6,22},{7,71},{8,24},{9,... | collective-permute-start | bytes 1769480 | tf_op jit(solution)/shard_map/ppermute | solution.py:49
  30.0 1.0 collective-permute-start.9
  31.1 3.0 %collective-permute-start.2 = (bf16[256,640]{1,0:T(8,128)(2,1)S(1)}, bf16[256,640]{1,0:T(8,128)(2,1)S(1)}, u32[]{:S(2)}, u32[]{:S(2)}) collective-permute-start(bf16[256,640]{1,0:T(8,128)(2,1)S(1)} %get-tuple-element.32.refs_1_.q_ref), channel_id=1, source_target_pairs={{0,6},{1,7},{2,4},{3,5},{4,2},{5,3},{6,0},{7,1},{8,14},{9,15},{10,... | collective-permute-start | bytes 983048 | tf_op jit(solution)/shard_map/ppermute | solution.py:29
  34.1 6.5 %collective-permute-done.2.refs_4_.refs_3_.refs_1_ = bf16[256,640]{1,0:T(8,128)(2,1)S(1)} collective-permute-done((bf16[256,640]{1,0:T(8,128)(2,1)S(1)}, bf16[256,640]{1,0:T(8,128)(2,1)S(1)}, u32[]{:S(2)}, u32[]{:S(2)}) %collective-permute-start.2) | collective-permute-done | bytes 327712 | tf_op jit(solution)/shard_map/ppermute | solution.py:29
  40.6 3.2 %attend.6 = (f32[4,256,512]{2,1,0:T(8,128)S(1)}, f32[4,256,128]{2,1,0:T(8,128)S(1)}, f32[8,128]{1,0:T(8,128)S(1)}) custom-call(bf16[16,64]{1,0:T(8,128)(2,1)S(1)} %use.1.refs_4_.refs_0_, bf16[256,640]{1,0:T(8,128)(2,1)S(1)} %get-tuple-element.32.refs_1_.q_ref, bf16[256,640]{1,0:T(8,128)(2,1)S(1)} %collective-permute-done.1.refs_2_.refs_1_, ...), custom_call_target="tpu_custom_call" | custom-call | tf_op jit(solution)/shard_map/attend/pallas_call | solution.py:58
  43.8 0.4 collective-permute-done.8.refs_1_
  44.4 0.5 collective-permute-start.11
  45.0 4.4 %attend.7 = (f32[4,256,512]{2,1,0:T(8,128)S(1)}, f32[4,256,128]{2,1,0:T(8,128)S(1)}, f32[8,128]{1,0:T(8,128)}) custom-call(bf16[16,64]{1,0:T(8,128)(2,1)S(1)} %use.1.refs_4_.refs_0_, bf16[256,640]{1,0:T(8,128)(2,1)S(1)} %collective-permute-done.refs_5_.refs_3_.refs_1_, bf16[256,640]{1,0:T(8,128)(2,1)S(1)} %collective-permute-done.1.refs_2_.refs_1_, ...), custom_call_target="tpu_custom_call" | custom-call | tf_op jit(solution)/shard_map/attend/pallas_call | solution.py:58
  49.5 1.7 %attend.8 = bf16[272,512]{1,0:T(8,128)(2,1)S(1)} custom-call(bf16[16,64]{1,0:T(8,128)(2,1)S(1)} %use.1.refs_4_.refs_0_, bf16[256,640]{1,0:T(8,128)(2,1)S(1)} %collective-permute-done.refs_5_.refs_3_.refs_1_, bf16[8,288,128]{2,1,0:T(8,128)(2,1)S(1)} %collective-permute-done.10.refs_2_.refs_5_, ...), custom_call_target="tpu_custom_call" | custom-call | tf_op jit(solution)/shard_map/attend/pallas_call | solution.py:58
  51.2 3.3 %collective-permute-start.13 = (bf16[272,512]{1,0:T(8,128)(2,1)S(1)}, bf16[272,512]{1,0:T(8,128)(2,1)S(1)}, u32[]{:S(2)}, u32[]{:S(2)}) collective-permute-start(bf16[272,512]{1,0:T(8,128)(2,1)S(1)} %attend.8), channel_id=1, source_target_pairs={{0,4},{1,5},{2,6},{3,7},{4,0},{5,1},{6,2},{7,3},{8,12},{9,13},{10,... | collective-permute-start | bytes 835592 | tf_op jit(solution)/shard_map/ppermute | solution.py:29
  54.4 1.7 %attend.9 = bf16[272,512]{1,0:T(8,128)(2,1)S(1)} custom-call(bf16[16,64]{1,0:T(8,128)(2,1)S(1)} %use.1.refs_4_.refs_0_, bf16[256,640]{1,0:T(8,128)(2,1)S(1)} %collective-permute-done.1.refs_2_.refs_1_, bf16[8,288,128]{2,1,0:T(8,128)(2,1)S(1)} %collective-permute-done.10.refs_2_.refs_5_, bf16[8,288,128]{2,1,0:T(8,128)(2,1)S(1)} %collective-permute-done.11.refs_3_.refs_6_, ...), custom_call_target="tpu_custom_call" | custom-call | tf_op jit(solution)/shard_map/attend/pallas_call | solution.py:58
  56.1 0.8 collective-permute-start.14
  56.9 1.7 %attend.10 = bf16[272,512]{1,0:T(8,128)(2,1)S(1)} custom-call(bf16[16,64]{1,0:T(8,128)(2,1)S(1)} %use.1.refs_4_.refs_0_, bf16[256,640]{1,0:T(8,128)(2,1)S(1)} %collective-permute-done.2.refs_4_.refs_3_.refs_1_, bf16[8,288,128]{2,1,0:T(8,128)(2,1)S(1)} %collective-permute-done.10.refs_2_.refs_5_, ...), custom_call_target="tpu_custom_call" | custom-call | tf_op jit(solution)/shard_map/attend/pallas_call | solution.py:58
  58.6 0.5 collective-permute-start.15
  59.1 2.8 %attend.11.o3 = bf16[272,512]{1,0:T(8,128)(2,1)S(1)} custom-call(bf16[16,64]{1,0:T(8,128)(2,1)S(1)} %use.1.refs_4_.refs_0_, bf16[256,640]{1,0:T(8,128)(2,1)S(1)} %get-tuple-element.32.refs_1_.q_ref, bf16[8,288,128]{2,1,0:T(8,128)(2,1)S(1)} %get-tuple-element.41.refs_4_.refs_2_, bf16[8,288,128]{2,1,0:T(8,128)(2,1)S(1)} %get-tuple-element.42.refs_5_.refs_3_, ...), custom_call_target="tpu_custom_call" | custom-call | tf_op jit(solution)/shard_map/attend/pallas_call | solution.py:58
  61.9 0.3 collective-permute-done.13.o0
  62.2 5.8 %collective-permute-done.14.o1 = bf16[272,512]{1,0:T(8,128)(2,1)S(1)} collective-permute-done((bf16[272,512]{1,0:T(8,128)(2,1)S(1)}, bf16[272,512]{1,0:T(8,128)(2,1)S(1)}, u32[]{:S(2)}, u32[]{:S(2)}) %collective-permute-start.14) | collective-permute-done | bytes 278560 | tf_op jit(solution)/shard_map/ppermute | solution.py:29
  68.3 0.8 merge.1
  69.1 2.0 %collective-permute-start.18 = (bf16[16,2048]{1,0:T(8,128)(2,1)S(1)}, bf16[16,2048]{1,0:T(8,128)(2,1)S(1)}, u32[]{:S(2)}, u32[]{:S(2)}) collective-permute-start(bf16[16,2048]{1,0:T(8,128)(2,1)S(1)} %merge.1), channel_id=1, source_target_pairs={{0,32},{1,9},{2,34},{3,11},{4,36},{5,13},{6,38},{7,15},{8,40},{9,1... | collective-permute-start | bytes 196616 | tf_op jit(solution)/shard_map/ppermute | solution.py:49
  71.1 2.1 %collective-permute-start.17 = (bf16[16,2048]{1,0:T(8,128)(2,1)S(1)}, bf16[16,2048]{1,0:T(8,128)(2,1)S(1)}, u32[]{:S(2)}, u32[]{:S(2)}) collective-permute-start(bf16[16,2048]{1,0:T(8,128)(2,1)S(1)} %merge.1), channel_id=1, source_target_pairs={{0,64},{1,17},{2,66},{3,19},{4,68},{5,21},{6,70},{7,23},{8,72},{9,... | collective-permute-start | bytes 196616 | tf_op jit(solution)/shard_map/ppermute | solution.py:49
  73.2 1.6 %collective-permute-start.16 = (bf16[16,2048]{1,0:T(8,128)(2,1)S(1)}, bf16[16,2048]{1,0:T(8,128)(2,1)S(1)}, u32[]{:S(2)}, u32[]{:S(2)}) collective-permute-start(bf16[16,2048]{1,0:T(8,128)(2,1)S(1)} %merge.1), channel_id=1, source_target_pairs={{0,96},{1,25},{2,98},{3,27},{4,100},{5,29},{6,102},{7,31},{8,104},... | collective-permute-start | bytes 196616 | tf_op jit(solution)/shard_map/ppermute | solution.py:49
  74.8 2.1 %collective-permute-done.17 = bf16[16,2048]{1,0:T(8,128)(2,1)S(1)} collective-permute-done((bf16[16,2048]{1,0:T(8,128)(2,1)S(1)}, bf16[16,2048]{1,0:T(8,128)(2,1)S(1)}, u32[]{:S(2)}, u32[]{:S(2)}) %collective-permute-start.17) | collective-permute-done | bytes 65568 | tf_op jit(solution)/shard_map/ppermute | solution.py:49
  76.9 0.6 collective-permute-done.16
  77.5 2.2 %collective-permute-start.19 = (bf16[64,2048]{1,0:T(8,128)(2,1)S(1)}, bf16[64,2048]{1,0:T(8,128)(2,1)S(1)}, u32[]{:S(2)}, u32[]{:S(2)}) collective-permute-start(bf16[64,2048]{1,0:T(8,128)(2,1)S(1)} %pad_maximum_fusion.p0), channel_id=1, source_target_pairs={{0,24},{1,97},{2,26},{3,99},{4,28},{5,101},{6,30},{7,103},{8,0},{9... | collective-permute-start | bytes 786440 | tf_op jit(solution)/shard_map/ppermute | solution.py:49
  79.7 1.5 %collective-permute-start.20 = (bf16[64,2048]{1,0:T(8,128)(2,1)S(1)}, bf16[64,2048]{1,0:T(8,128)(2,1)S(1)}, u32[]{:S(2)}, u32[]{:S(2)}) collective-permute-start(bf16[64,2048]{1,0:T(8,128)(2,1)S(1)} %pad_maximum_fusion.p0), channel_id=1, source_target_pairs={{0,16},{1,65},{2,18},{3,67},{4,20},{5,69},{6,22},{7,71},{8,24},{9,... | collective-permute-start | bytes 786440 | tf_op jit(solution)/shard_map/ppermute | solution.py:49
  81.2 0.7 collective-permute-start.21
  81.9 4.5 %collective-permute-done.19.p1 = bf16[64,2048]{1,0:T(8,128)(2,1)S(1)} collective-permute-done((bf16[64,2048]{1,0:T(8,128)(2,1)S(1)}, bf16[64,2048]{1,0:T(8,128)(2,1)S(1)}, u32[]{:S(2)}, u32[]{:S(2)}) %collective-permute-start.19) | collective-permute-done | bytes 262176 | tf_op jit(solution)/shard_map/ppermute | solution.py:49
  86.5 1.2 collective-permute-done.20.p2
  87.7 2.7 %collective-permute-done.21.p3 = bf16[64,2048]{1,0:T(8,128)(2,1)S(1)} collective-permute-done((bf16[64,2048]{1,0:T(8,128)(2,1)S(1)}, bf16[64,2048]{1,0:T(8,128)(2,1)S(1)}, u32[]{:S(2)}, u32[]{:S(2)}) %collective-permute-start.21) | collective-permute-done | bytes 262176 | tf_op jit(solution)/shard_map/ppermute | solution.py:49
  90.4 1.3 project.1
  91.8 1.3 collective-permute-done.22
  93.2 1.2 collective-permute-start.23
  94.4 2.8 %collective-permute-start.24 = (bf16[2,4,16,448]{3,2,1,0:T(8,128)(2,1)S(1)}, bf16[2,4,16,448]{3,2,1,0:T(8,128)(2,1)S(1)}, u32[]{:S(2)}, u32[]{:S(2)}) collective-permute-start(bf16[2,4,16,448]{3,2,1,0:T(8,128)(2,1)S(1)} %add_convert_fusion.pair), channel_id=1, source_target_pairs={{0,4},{1,5},{2,6},{3,7},{4,0},{5,1},{6,2},{7,3},{8,12},{9,13},{10,... | collective-permute-start | bytes 344072 | tf_op jit(solution)/shard_map/ppermute | solution.py:29
  97.2 0.8 collective-permute-start.25
  98.1 1.5 %collective-permute-done.23.t1 = bf16[2,4,16,448]{3,2,1,0:T(8,128)(2,1)S(1)} collective-permute-done((bf16[2,4,16,448]{3,2,1,0:T(8,128)(2,1)S(1)}, bf16[2,4,16,448]{3,2,1,0:T(8,128)(2,1)S(1)}, u32[]{:S(2)}, u32[]{:S(2)}) %collective-permute-start.23) | collective-permute-done | bytes 114720 | tf_op jit(solution)/shard_map/ppermute | solution.py:29
  99.6 4.0 %collective-permute-done.24.t2 = bf16[2,4,16,448]{3,2,1,0:T(8,128)(2,1)S(1)} collective-permute-done((bf16[2,4,16,448]{3,2,1,0:T(8,128)(2,1)S(1)}, bf16[2,4,16,448]{3,2,1,0:T(8,128)(2,1)S(1)}, u32[]{:S(2)}, u32[]{:S(2)}) %collective-permute-start.24) | collective-permute-done | bytes 114720 | tf_op jit(solution)/shard_map/ppermute | solution.py:29
  103.6 2.2 %collective-permute-done.25.t3 = bf16[2,4,16,448]{3,2,1,0:T(8,128)(2,1)S(1)} collective-permute-done((bf16[2,4,16,448]{3,2,1,0:T(8,128)(2,1)S(1)}, bf16[2,4,16,448]{3,2,1,0:T(8,128)(2,1)S(1)}, u32[]{:S(2)}, u32[]{:S(2)}) %collective-permute-start.25) | collective-permute-done | bytes 114720 | tf_op jit(solution)/shard_map/ppermute | solution.py:29
  105.8 0.6 join.1.half_ref
  106.6 1.3 collective-permute-done.26.other_ref
  107.9 2.0 %ffn.1 = (bf16[16,16,448]{2,1,0:T(8,128)(2,1)S(1)}, bf16[4,16,4736]{2,1,0:T(8,128)(2,1)S(1)}, bf16[4,16,4736]{2,1,0:T(8,128)(2,1)S(1)}, bf16[4,16,4736]{2,1,0:T(8,128)(2,1)S(1)}, bf16[4,16,4736]{2,1,0:T(8,128)(2,1)S(1)}) custom-call(s32[4]{0:T(128)S(1)} %pad_add_fusion.where, bf16[2,4,16,448]{3,2,1,0:T(8,128)(2,1)S(1)} %join.1.half_ref, ...), custom_call_target="tpu_custom_call" | custom-call | tf_op jit(solution)/shard_map/ffn/pallas_call | solution.py:58
  109.9 1.8 %collective-permute-start.27 = (bf16[4,16,4736]{2,1,0:T(8,128)(2,1)S(1)}, bf16[4,16,4736]{2,1,0:T(8,128)(2,1)S(1)}, u32[]{:S(2)}, u32[]{:S(2)}) collective-permute-start(bf16[4,16,4736]{2,1,0:T(8,128)(2,1)S(1)} %get-tuple-element.53), channel_id=1, source_target_pairs={{0,64},{1,17},{2,66},{3,19},{4,68},{5,21},{6,70},{7,23},{8,72},{9,... | collective-permute-start | bytes 1818632 | tf_op jit(solution)/shard_map/ppermute | solution.py:49
  111.7 1.9 %collective-permute-start.28 = (bf16[4,16,4736]{2,1,0:T(8,128)(2,1)S(1)}, bf16[4,16,4736]{2,1,0:T(8,128)(2,1)S(1)}, u32[]{:S(2)}, u32[]{:S(2)}) collective-permute-start(bf16[4,16,4736]{2,1,0:T(8,128)(2,1)S(1)} %get-tuple-element.54), channel_id=1, source_target_pairs={{0,32},{1,9},{2,34},{3,11},{4,36},{5,13},{6,38},{7,15},{8,40},{9,1... | collective-permute-start | bytes 1818632 | tf_op jit(solution)/shard_map/ppermute | solution.py:49
  113.6 1.3 collective-permute-start.29
  114.9 6.7 %collective-permute-done.27.refs_1_ = bf16[4,16,4736]{2,1,0:T(8,128)(2,1)S(1)} collective-permute-done((bf16[4,16,4736]{2,1,0:T(8,128)(2,1)S(1)}, bf16[4,16,4736]{2,1,0:T(8,128)(2,1)S(1)}, u32[]{:S(2)}, u32[]{:S(2)}) %collective-permute-start.27) | collective-permute-done | bytes 606240 | tf_op jit(solution)/shard_map/ppermute | solution.py:49
  121.6 6.4 %collective-permute-done.28.refs_2_ = bf16[4,16,4736]{2,1,0:T(8,128)(2,1)S(1)} collective-permute-done((bf16[4,16,4736]{2,1,0:T(8,128)(2,1)S(1)}, bf16[4,16,4736]{2,1,0:T(8,128)(2,1)S(1)}, u32[]{:S(2)}, u32[]{:S(2)}) %collective-permute-start.28) | collective-permute-done | bytes 606240 | tf_op jit(solution)/shard_map/ppermute | solution.py:49
  128.2 0.5 fold.1
  128.7 1.5 %collective-permute-start.30 = (bf16[16,4736]{1,0:T(8,128)(2,1)S(1)}, bf16[16,4736]{1,0:T(8,128)(2,1)S(1)}, u32[]{:S(2)}, u32[]{:S(2)}) collective-permute-start(bf16[16,4736]{1,0:T(8,128)(2,1)S(1)} %get-tuple-element.57), channel_id=1, source_target_pairs={{0,16},{1,65},{2,18},{3,67},{4,20},{5,69},{6,22},{7,71},{8,24},{9,... | collective-permute-start | bytes 454664 | tf_op jit(solution)/shard_map/ppermute | solution.py:49
  130.2 3.2 %collective-permute-start.32 = (bf16[16,4736]{1,0:T(8,128)(2,1)S(1)}, bf16[16,4736]{1,0:T(8,128)(2,1)S(1)}, u32[]{:S(2)}, u32[]{:S(2)}) collective-permute-start(bf16[16,4736]{1,0:T(8,128)(2,1)S(1)} %get-tuple-element.59), channel_id=1, source_target_pairs={{0,24},{1,97},{2,26},{3,99},{4,28},{5,101},{6,30},{7,103},{8,0},{9... | collective-permute-start | bytes 454664 | tf_op jit(solution)/shard_map/ppermute | solution.py:49
  133.4 0.8 turn.3
  134.3 1.3 collective-permute-done.30.r1
  135.5 1.6 %collective-permute-done.31.r2 = bf16[16,4736]{1,0:T(8,128)(2,1)S(1)} collective-permute-done((bf16[16,4736]{1,0:T(8,128)(2,1)S(1)}, bf16[16,4736]{1,0:T(8,128)(2,1)S(1)}, u32[]{:S(2)}, u32[]{:S(2)}) %collective-permute-start.31) | collective-permute-done | bytes 151584 | tf_op jit(solution)/shard_map/ppermute | solution.py:49
  137.1 0.8 finish.1
  (49 shorter events, 1.7 us)
Async XLA Ops:
  0.6 2.9 %copy-start.7 = (s32[2048]{0:T(1024)S(1)}, s32[2048]{0:T(1024)}, u32[]{:S(2)}) copy-start(s32[2048]{0:T(1024)} %param.15) | copy-start | bytes 24580
  0.6 2.9 %copy-start.6 = (s32[256,32]{0,1:T(8,128)S(1)}, s32[256,32]{0,1:T(8,128)}, u32[]{:S(2)}) copy-start(s32[256,32]{0,1:T(8,128)} %param.17) | copy-start | bytes 98308
  0.7 2.9 %copy-start.9 = (s32[256]{0:T(256)S(1)}, s32[256]{0:T(256)}, u32[]{:S(2)}) copy-start(s32[256]{0:T(256)} %prompts.1) | copy-start | bytes 3076
  0.7 10.8 %copy-start.4 = (bf16[16,9216]{1,0:T(8,128)(2,1)S(1)}, bf16[16,9216]{1,0:T(8,128)(2,1)}, u32[]{:S(2)}) copy-start(bf16[16,9216]{1,0:T(8,128)(2,1)} %queries.1) | copy-start | bytes 884740
  0.7 10.8 %copy-start.8 = (bf16[16,576]{1,0:T(8,128)(2,1)S(1)}, bf16[16,576]{1,0:T(8,128)(2,1)}, u32[]{:S(2)}) copy-start(bf16[16,576]{1,0:T(8,128)(2,1)} %own.1) | copy-start | bytes 55300
  5.7 18.1 %collective-permute-start.3 = (bf16[8,288,128]{2,1,0:T(8,128)(2,1)S(1)}, bf16[8,288,128]{2,1,0:T(8,128)(2,1)S(1)}, u32[]{:S(2)}, u32[]{:S(2)}) collective-permute-start(bf16[8,288,128]{2,1,0:T(8,128)(2,1)S(1)} %get-tuple-element.33), channel_id=1, source_target_pairs={{0,32},{1,9},{2,34},{3,11},{4,36},{5,13},{6,38},{7,15},{8,40},{9,1... | collective-permute-start | bytes 1769480 | tf_op jit(solution)/shard_map/ppermute | solution.py:49
  7.3 16.9 %collective-permute-start.4 = (bf16[8,288,128]{2,1,0:T(8,128)(2,1)S(1)}, bf16[8,288,128]{2,1,0:T(8,128)(2,1)S(1)}, u32[]{:S(2)}, u32[]{:S(2)}) collective-permute-start(bf16[8,288,128]{2,1,0:T(8,128)(2,1)S(1)} %get-tuple-element.34), channel_id=1, source_target_pairs={{0,64},{1,17},{2,66},{3,19},{4,68},{5,21},{6,70},{7,23},{8,72},{9,... | collective-permute-start | bytes 1769480 | tf_op jit(solution)/shard_map/ppermute | solution.py:49
  10.0 14.2 %collective-permute-start.5 = (bf16[8,288,128]{2,1,0:T(8,128)(2,1)S(1)}, bf16[8,288,128]{2,1,0:T(8,128)(2,1)S(1)}, u32[]{:S(2)}, u32[]{:S(2)}) collective-permute-start(bf16[8,288,128]{2,1,0:T(8,128)(2,1)S(1)} %get-tuple-element.35), channel_id=1, source_target_pairs={{0,96},{1,25},{2,98},{3,27},{4,100},{5,29},{6,102},{7,31},{8,104},... | collective-permute-start | bytes 1769480 | tf_op jit(solution)/shard_map/ppermute | solution.py:49
  11.6 12.2 %collective-permute-start = (bf16[256,640]{1,0:T(8,128)(2,1)S(1)}, bf16[256,640]{1,0:T(8,128)(2,1)S(1)}, u32[]{:S(2)}, u32[]{:S(2)}) collective-permute-start(bf16[256,640]{1,0:T(8,128)(2,1)S(1)} %get-tuple-element.32.refs_1_.q_ref), channel_id=1, source_target_pairs={{0,4},{1,5},{2,6},{3,7},{4,0},{5,1},{6,2},{7,3},{8,12},{9,13},{10,... | collective-permute-start | bytes 983048 | tf_op jit(solution)/shard_map/ppermute | solution.py:29
  14.9 16.2 %collective-permute-start.1 = (bf16[256,640]{1,0:T(8,128)(2,1)S(1)}, bf16[256,640]{1,0:T(8,128)(2,1)S(1)}, u32[]{:S(2)}, u32[]{:S(2)}) collective-permute-start(bf16[256,640]{1,0:T(8,128)(2,1)S(1)} %get-tuple-element.32.refs_1_.q_ref), channel_id=1, source_target_pairs={{0,2},{1,3},{2,0},{3,1},{4,6},{5,7},{6,4},{7,5},{8,10},{9,11},{10,... | collective-permute-start | bytes 983048 | tf_op jit(solution)/shard_map/ppermute | solution.py:29
  24.4 16.2 %collective-permute-start.6 = (bf16[8,288,128]{2,1,0:T(8,128)(2,1)S(1)}, bf16[8,288,128]{2,1,0:T(8,128)(2,1)S(1)}, u32[]{:S(2)}, u32[]{:S(2)}) collective-permute-start(bf16[8,288,128]{2,1,0:T(8,128)(2,1)S(1)} %get-tuple-element.36.refs_5_), channel_id=1, source_target_pairs={{0,1},{1,0},{2,3},{3,2},{4,5},{5,4},{6,7},{7,6},{8,9},{9,8},{10,11... | collective-permute-start | bytes 1769480 | tf_op jit(solution)/shard_map/ppermute | solution.py:29
  24.6 19.3 %collective-permute-start.7 = (bf16[8,288,128]{2,1,0:T(8,128)(2,1)S(1)}, bf16[8,288,128]{2,1,0:T(8,128)(2,1)S(1)}, u32[]{:S(2)}, u32[]{:S(2)}) collective-permute-start(bf16[8,288,128]{2,1,0:T(8,128)(2,1)S(1)} %get-tuple-element.38), channel_id=1, source_target_pairs={{0,8},{1,33},{2,10},{3,35},{4,12},{5,37},{6,14},{7,39},{8,16},{9,4... | collective-permute-start | bytes 1769480 | tf_op jit(solution)/shard_map/ppermute | solution.py:49
  26.5 17.8 %collective-permute-start.8 = (bf16[8,288,128]{2,1,0:T(8,128)(2,1)S(1)}, bf16[8,288,128]{2,1,0:T(8,128)(2,1)S(1)}, u32[]{:S(2)}, u32[]{:S(2)}) collective-permute-start(bf16[8,288,128]{2,1,0:T(8,128)(2,1)S(1)} %get-tuple-element.39), channel_id=1, source_target_pairs={{0,16},{1,65},{2,18},{3,67},{4,20},{5,69},{6,22},{7,71},{8,24},{9,... | collective-permute-start | bytes 1769480 | tf_op jit(solution)/shard_map/ppermute | solution.py:49
  30.0 14.2 %collective-permute-start.9 = (bf16[8,288,128]{2,1,0:T(8,128)(2,1)S(1)}, bf16[8,288,128]{2,1,0:T(8,128)(2,1)S(1)}, u32[]{:S(2)}, u32[]{:S(2)}) collective-permute-start(bf16[8,288,128]{2,1,0:T(8,128)(2,1)S(1)} %get-tuple-element.40), channel_id=1, source_target_pairs={{0,24},{1,97},{2,26},{3,99},{4,28},{5,101},{6,30},{7,103},{8,0},{9... | collective-permute-start | bytes 1769480 | tf_op jit(solution)/shard_map/ppermute | solution.py:49
  31.1 9.5 %collective-permute-start.2 = (bf16[256,640]{1,0:T(8,128)(2,1)S(1)}, bf16[256,640]{1,0:T(8,128)(2,1)S(1)}, u32[]{:S(2)}, u32[]{:S(2)}) collective-permute-start(bf16[256,640]{1,0:T(8,128)(2,1)S(1)} %get-tuple-element.32.refs_1_.q_ref), channel_id=1, source_target_pairs={{0,6},{1,7},{2,4},{3,5},{4,2},{5,3},{6,0},{7,1},{8,14},{9,15},{10,... | collective-permute-start | bytes 983048 | tf_op jit(solution)/shard_map/ppermute | solution.py:29
  44.3 5.1 %collective-permute-start.10 = (bf16[8,288,128]{2,1,0:T(8,128)(2,1)S(1)}, bf16[8,288,128]{2,1,0:T(8,128)(2,1)S(1)}, u32[]{:S(2)}, u32[]{:S(2)}) collective-permute-start(bf16[8,288,128]{2,1,0:T(8,128)(2,1)S(1)} %get-tuple-element.41.refs_4_.refs_2_), channel_id=1, source_target_pairs={{0,1},{1,0},{2,3},{3,2},{4,5},{5,4},{6,7},{7,6},{8,9},{9,8},{10,11... | collective-permute-start | bytes 1769480 | tf_op jit(solution)/shard_map/ppermute | solution.py:29
  44.4 5.0 %collective-permute-start.11 = (bf16[8,288,128]{2,1,0:T(8,128)(2,1)S(1)}, bf16[8,288,128]{2,1,0:T(8,128)(2,1)S(1)}, u32[]{:S(2)}, u32[]{:S(2)}) collective-permute-start(bf16[8,288,128]{2,1,0:T(8,128)(2,1)S(1)} %get-tuple-element.42.refs_5_.refs_3_), channel_id=1, source_target_pairs={{0,1},{1,0},{2,3},{3,2},{4,5},{5,4},{6,7},{7,6},{8,9},{9,8},{10,11... | collective-permute-start | bytes 1769480 | tf_op jit(solution)/shard_map/ppermute | solution.py:29
  44.9 4.5 %collective-permute-start.12 = (bf16[8,288,128]{2,1,0:T(8,128)(2,1)S(1)}, bf16[8,288,128]{2,1,0:T(8,128)(2,1)S(1)}, u32[]{:S(2)}, u32[]{:S(2)}) collective-permute-start(bf16[8,288,128]{2,1,0:T(8,128)(2,1)S(1)} %get-tuple-element.43.refs_6_.refs_4_), channel_id=1, source_target_pairs={{0,1},{1,0},{2,3},{3,2},{4,5},{5,4},{6,7},{7,6},{8,9},{9,8},{10,11... | collective-permute-start | bytes 1769480 | tf_op jit(solution)/shard_map/ppermute | solution.py:29
  51.2 11.0 %collective-permute-start.13 = (bf16[272,512]{1,0:T(8,128)(2,1)S(1)}, bf16[272,512]{1,0:T(8,128)(2,1)S(1)}, u32[]{:S(2)}, u32[]{:S(2)}) collective-permute-start(bf16[272,512]{1,0:T(8,128)(2,1)S(1)} %attend.8), channel_id=1, source_target_pairs={{0,4},{1,5},{2,6},{3,7},{4,0},{5,1},{6,2},{7,3},{8,12},{9,13},{10,... | collective-permute-start | bytes 835592 | tf_op jit(solution)/shard_map/ppermute | solution.py:29
  56.1 11.9 %collective-permute-start.14 = (bf16[272,512]{1,0:T(8,128)(2,1)S(1)}, bf16[272,512]{1,0:T(8,128)(2,1)S(1)}, u32[]{:S(2)}, u32[]{:S(2)}) collective-permute-start(bf16[272,512]{1,0:T(8,128)(2,1)S(1)} %attend.9), channel_id=1, source_target_pairs={{0,2},{1,3},{2,0},{3,1},{4,6},{5,7},{6,4},{7,5},{8,10},{9,11},{10,... | collective-permute-start | bytes 835592 | tf_op jit(solution)/shard_map/ppermute | solution.py:29
  58.6 9.7 %copy-start = (bf16[16,512,128]{2,1,0:T(8,128)(2,1)S(1)}, bf16[16,512,128]{2,1,0:T(8,128)(2,1)}, u32[]{:S(2)}) copy-start(bf16[16,512,128]{2,1,0:T(8,128)(2,1)} %up_ref.1) | copy-start | bytes 6291460
  58.6 9.7 %collective-permute-start.15 = (bf16[272,512]{1,0:T(8,128)(2,1)S(1)}, bf16[272,512]{1,0:T(8,128)(2,1)S(1)}, u32[]{:S(2)}, u32[]{:S(2)}) collective-permute-start(bf16[272,512]{1,0:T(8,128)(2,1)S(1)} %attend.10), channel_id=1, source_target_pairs={{0,6},{1,7},{2,4},{3,5},{4,2},{5,3},{6,0},{7,1},{8,14},{9,15},{10,... | collective-permute-start | bytes 835592 | tf_op jit(solution)/shard_map/ppermute | solution.py:29
  68.3 22.1 %copy-start.3 = (bf16[2048,448]{0,1:T(8,128)(2,1)S(1)}, bf16[2048,448]{0,1:T(8,128)(2,1)}, u32[]{:S(2)}) copy-start(bf16[2048,448]{0,1:T(8,128)(2,1)} %param.19) | copy-start | bytes 5505028
  69.1 28.8 %copy-start.5 = (bf16[256,448]{0,1:T(8,128)(2,1)S(1)}, bf16[256,448]{0,1:T(8,128)(2,1)}, u32[]{:S(2)}) copy-start(bf16[256,448]{0,1:T(8,128)(2,1)} %param.20) | copy-start | bytes 688132
  69.1 5.6 %collective-permute-start.18 = (bf16[16,2048]{1,0:T(8,128)(2,1)S(1)}, bf16[16,2048]{1,0:T(8,128)(2,1)S(1)}, u32[]{:S(2)}, u32[]{:S(2)}) collective-permute-start(bf16[16,2048]{1,0:T(8,128)(2,1)S(1)} %merge.1), channel_id=1, source_target_pairs={{0,32},{1,9},{2,34},{3,11},{4,36},{5,13},{6,38},{7,15},{8,40},{9,1... | collective-permute-start | bytes 196616 | tf_op jit(solution)/shard_map/ppermute | solution.py:49
  71.1 5.8 %collective-permute-start.17 = (bf16[16,2048]{1,0:T(8,128)(2,1)S(1)}, bf16[16,2048]{1,0:T(8,128)(2,1)S(1)}, u32[]{:S(2)}, u32[]{:S(2)}) collective-permute-start(bf16[16,2048]{1,0:T(8,128)(2,1)S(1)} %merge.1), channel_id=1, source_target_pairs={{0,64},{1,17},{2,66},{3,19},{4,68},{5,21},{6,70},{7,23},{8,72},{9,... | collective-permute-start | bytes 196616 | tf_op jit(solution)/shard_map/ppermute | solution.py:49
  73.2 4.3 %collective-permute-start.16 = (bf16[16,2048]{1,0:T(8,128)(2,1)S(1)}, bf16[16,2048]{1,0:T(8,128)(2,1)S(1)}, u32[]{:S(2)}, u32[]{:S(2)}) collective-permute-start(bf16[16,2048]{1,0:T(8,128)(2,1)S(1)} %merge.1), channel_id=1, source_target_pairs={{0,96},{1,25},{2,98},{3,27},{4,100},{5,29},{6,102},{7,31},{8,104},... | collective-permute-start | bytes 196616 | tf_op jit(solution)/shard_map/ppermute | solution.py:49
  77.5 9.0 %collective-permute-start.19 = (bf16[64,2048]{1,0:T(8,128)(2,1)S(1)}, bf16[64,2048]{1,0:T(8,128)(2,1)S(1)}, u32[]{:S(2)}, u32[]{:S(2)}) collective-permute-start(bf16[64,2048]{1,0:T(8,128)(2,1)S(1)} %pad_maximum_fusion.p0), channel_id=1, source_target_pairs={{0,24},{1,97},{2,26},{3,99},{4,28},{5,101},{6,30},{7,103},{8,0},{9... | collective-permute-start | bytes 786440 | tf_op jit(solution)/shard_map/ppermute | solution.py:49
  79.7 8.0 %collective-permute-start.20 = (bf16[64,2048]{1,0:T(8,128)(2,1)S(1)}, bf16[64,2048]{1,0:T(8,128)(2,1)S(1)}, u32[]{:S(2)}, u32[]{:S(2)}) collective-permute-start(bf16[64,2048]{1,0:T(8,128)(2,1)S(1)} %pad_maximum_fusion.p0), channel_id=1, source_target_pairs={{0,16},{1,65},{2,18},{3,67},{4,20},{5,69},{6,22},{7,71},{8,24},{9,... | collective-permute-start | bytes 786440 | tf_op jit(solution)/shard_map/ppermute | solution.py:49
  81.2 9.2 %collective-permute-start.21 = (bf16[64,2048]{1,0:T(8,128)(2,1)S(1)}, bf16[64,2048]{1,0:T(8,128)(2,1)S(1)}, u32[]{:S(2)}, u32[]{:S(2)}) collective-permute-start(bf16[64,2048]{1,0:T(8,128)(2,1)S(1)} %pad_maximum_fusion.p0), channel_id=1, source_target_pairs={{0,8},{1,33},{2,10},{3,35},{4,12},{5,37},{6,14},{7,39},{8,16},{9,4... | collective-permute-start | bytes 786440 | tf_op jit(solution)/shard_map/ppermute | solution.py:49
  90.4 16.1 %copy-start.10 = (bf16[448]{0:T(512)(128)(2,1)S(1)}, bf16[448]{0:T(512)(128)(2,1)}, u32[]{:S(2)}) copy-start(bf16[448]{0:T(512)(128)(2,1)} %param.21) | copy-start | bytes 2692
  90.4 17.5 %copy-start.1 = (bf16[448,2304]{1,0:T(8,128)(2,1)S(1)}, bf16[448,2304]{1,0:T(8,128)(2,1)}, u32[]{:S(2)}) copy-start(bf16[448,2304]{1,0:T(8,128)(2,1)} %wg_ref.1) | copy-start | bytes 6193156
  90.4 17.5 %copy-start.2 = (bf16[448,2304]{1,0:T(8,128)(2,1)S(1)}, bf16[448,2304]{1,0:T(8,128)(2,1)}, u32[]{:S(2)}) copy-start(bf16[448,2304]{1,0:T(8,128)(2,1)} %wu_ref.1) | copy-start | bytes 6193156
  91.7 1.4 %collective-permute-start.22 = (bf16[2,4,16,448]{3,2,1,0:T(8,128)(2,1)S(1)}, bf16[2,4,16,448]{3,2,1,0:T(8,128)(2,1)S(1)}, u32[]{:S(2)}, u32[]{:S(2)}) collective-permute-start(bf16[2,4,16,448]{3,2,1,0:T(8,128)(2,1)S(1)} %get-tuple-element.50), channel_id=1, source_target_pairs={{0,1},{1,0},{2,3},{3,2},{4,5},{5,4},{6,7},{7,6},{8,9},{9,8},{10,11... | collective-permute-start | bytes 344072 | tf_op jit(solution)/shard_map/ppermute | solution.py:29
  93.2 6.4 %collective-permute-start.23 = (bf16[2,4,16,448]{3,2,1,0:T(8,128)(2,1)S(1)}, bf16[2,4,16,448]{3,2,1,0:T(8,128)(2,1)S(1)}, u32[]{:S(2)}, u32[]{:S(2)}) collective-permute-start(bf16[2,4,16,448]{3,2,1,0:T(8,128)(2,1)S(1)} %add_convert_fusion.pair), channel_id=1, source_target_pairs={{0,2},{1,3},{2,0},{3,1},{4,6},{5,7},{6,4},{7,5},{8,10},{9,11},{10,... | collective-permute-start | bytes 344072 | tf_op jit(solution)/shard_map/ppermute | solution.py:29
  94.4 9.2 %collective-permute-start.24 = (bf16[2,4,16,448]{3,2,1,0:T(8,128)(2,1)S(1)}, bf16[2,4,16,448]{3,2,1,0:T(8,128)(2,1)S(1)}, u32[]{:S(2)}, u32[]{:S(2)}) collective-permute-start(bf16[2,4,16,448]{3,2,1,0:T(8,128)(2,1)S(1)} %add_convert_fusion.pair), channel_id=1, source_target_pairs={{0,4},{1,5},{2,6},{3,7},{4,0},{5,1},{6,2},{7,3},{8,12},{9,13},{10,... | collective-permute-start | bytes 344072 | tf_op jit(solution)/shard_map/ppermute | solution.py:29
  97.2 8.7 %collective-permute-start.25 = (bf16[2,4,16,448]{3,2,1,0:T(8,128)(2,1)S(1)}, bf16[2,4,16,448]{3,2,1,0:T(8,128)(2,1)S(1)}, u32[]{:S(2)}, u32[]{:S(2)}) collective-permute-start(bf16[2,4,16,448]{3,2,1,0:T(8,128)(2,1)S(1)} %add_convert_fusion.pair), channel_id=1, source_target_pairs={{0,6},{1,7},{2,4},{3,5},{4,2},{5,3},{6,0},{7,1},{8,14},{9,15},{10,... | collective-permute-start | bytes 344072 | tf_op jit(solution)/shard_map/ppermute | solution.py:29
  106.5 1.4 %collective-permute-start.26 = (bf16[2,4,16,448]{3,2,1,0:T(8,128)(2,1)S(1)}, bf16[2,4,16,448]{3,2,1,0:T(8,128)(2,1)S(1)}, u32[]{:S(2)}, u32[]{:S(2)}) collective-permute-start(bf16[2,4,16,448]{3,2,1,0:T(8,128)(2,1)S(1)} %join.1.half_ref), channel_id=1, source_target_pairs={{0,1},{1,0},{2,3},{3,2},{4,5},{5,4},{6,7},{7,6},{8,9},{9,8},{10,11... | collective-permute-start | bytes 344072 | tf_op jit(solution)/shard_map/ppermute | solution.py:29
  109.9 11.7 %collective-permute-start.27 = (bf16[4,16,4736]{2,1,0:T(8,128)(2,1)S(1)}, bf16[4,16,4736]{2,1,0:T(8,128)(2,1)S(1)}, u32[]{:S(2)}, u32[]{:S(2)}) collective-permute-start(bf16[4,16,4736]{2,1,0:T(8,128)(2,1)S(1)} %get-tuple-element.53), channel_id=1, source_target_pairs={{0,64},{1,17},{2,66},{3,19},{4,68},{5,21},{6,70},{7,23},{8,72},{9,... | collective-permute-start | bytes 1818632 | tf_op jit(solution)/shard_map/ppermute | solution.py:49
  111.7 16.3 %collective-permute-start.28 = (bf16[4,16,4736]{2,1,0:T(8,128)(2,1)S(1)}, bf16[4,16,4736]{2,1,0:T(8,128)(2,1)S(1)}, u32[]{:S(2)}, u32[]{:S(2)}) collective-permute-start(bf16[4,16,4736]{2,1,0:T(8,128)(2,1)S(1)} %get-tuple-element.54), channel_id=1, source_target_pairs={{0,32},{1,9},{2,34},{3,11},{4,36},{5,13},{6,38},{7,15},{8,40},{9,1... | collective-permute-start | bytes 1818632 | tf_op jit(solution)/shard_map/ppermute | solution.py:49
  113.6 14.6 %collective-permute-start.29 = (bf16[4,16,4736]{2,1,0:T(8,128)(2,1)S(1)}, bf16[4,16,4736]{2,1,0:T(8,128)(2,1)S(1)}, u32[]{:S(2)}, u32[]{:S(2)}) collective-permute-start(bf16[4,16,4736]{2,1,0:T(8,128)(2,1)S(1)} %get-tuple-element.55), channel_id=1, source_target_pairs={{0,96},{1,25},{2,98},{3,27},{4,100},{5,29},{6,102},{7,31},{8,104},... | collective-permute-start | bytes 1818632 | tf_op jit(solution)/shard_map/ppermute | solution.py:49
  128.7 6.8 %collective-permute-start.30 = (bf16[16,4736]{1,0:T(8,128)(2,1)S(1)}, bf16[16,4736]{1,0:T(8,128)(2,1)S(1)}, u32[]{:S(2)}, u32[]{:S(2)}) collective-permute-start(bf16[16,4736]{1,0:T(8,128)(2,1)S(1)} %get-tuple-element.57), channel_id=1, source_target_pairs={{0,16},{1,65},{2,18},{3,67},{4,20},{5,69},{6,22},{7,71},{8,24},{9,... | collective-permute-start | bytes 454664 | tf_op jit(solution)/shard_map/ppermute | solution.py:49
  130.2 6.9 %collective-permute-start.31 = (bf16[16,4736]{1,0:T(8,128)(2,1)S(1)}, bf16[16,4736]{1,0:T(8,128)(2,1)S(1)}, u32[]{:S(2)}, u32[]{:S(2)}) collective-permute-start(bf16[16,4736]{1,0:T(8,128)(2,1)S(1)} %get-tuple-element.58), channel_id=1, source_target_pairs={{0,8},{1,33},{2,10},{3,35},{4,12},{5,37},{6,14},{7,39},{8,16},{9,4... | collective-permute-start | bytes 454664 | tf_op jit(solution)/shard_map/ppermute | solution.py:49
  130.2 6.9 %collective-permute-start.32 = (bf16[16,4736]{1,0:T(8,128)(2,1)S(1)}, bf16[16,4736]{1,0:T(8,128)(2,1)S(1)}, u32[]{:S(2)}, u32[]{:S(2)}) collective-permute-start(bf16[16,4736]{1,0:T(8,128)(2,1)S(1)} %get-tuple-element.59), channel_id=1, source_target_pairs={{0,24},{1,97},{2,26},{3,99},{4,28},{5,101},{6,30},{7,103},{8,0},{9... | collective-permute-start | bytes 454664 | tf_op jit(solution)/shard_map/ppermute | solution.py:49
